TPU v7x, 32 devices: a whole 2x2x4 slice. The times are simulated.
32 devices in a mesh: grp: 2 (over x), chan: 16 (over z, y, core).
Axes of the slice: x: 2, y: 2, z: 4, core: 2. Of those that a mesh axis runs over, the one named last changes fastest.
Arguments:
- voltages: bfloat16 [2048, 104448], P(('grp', 'chan')), parts along dimension 0, may hold values from -8 to 8
- delays: float32 [4, 2048], P(None, ('grp', 'chan')), parts along dimension 1, may hold values from -2 to 2
- band_feeds: int32 [64, 256], replicated, may hold values from 0 to 1023, as said below
Outputs:
- visibilities: float32 [2048, 2, 256, 256], P(('grp', 'chan')), parts along dimension 0
- beams: float32 [2048, 384], P(('grp', 'chan')), parts along dimension 0
There are 2 independent parts, one for each index of `grp`. A program takes and returns all parts, laid end to end along the dimension named above; an argument that names none is the same for every part. Nothing has to cross between parts.
Inputs may be any that keep to these rules, and one draw needn't show every extreme that they name: `band_feeds`: each row lists 256 distinct feeds in increasing order. Of each aligned block of 64 feeds at most 32 are listed in one row, and every row has a block with exactly 32 listed.
All inputs are finite; a program needn't handle non-finite values.
Results may differ from a plain program's by a relative error of at most 0.0056.
Values may be sent and summed in bfloat16 or wider, within the bound.
No kernel may reach another device: no remote copies, remote signals or barrier semaphores. Data moves between devices by JAX's collectives and lax.ppermute only.
A program may use at most 192 MiB of HBM per device.

v0:
```python
import functools

import jax
import jax.numpy as jnp
import ml_dtypes
import numpy as np
from jax import lax
from jax.experimental import pallas as pl
from jax.experimental.pallas import tpu as pltpu
from jax.sharding import PartitionSpec as P

F = 1024
CHANNELS = 1024
TAPS = 4
BAND_CH = 16
BEAMS = 4
FR = 48
NFFT = 2048
BANDS = 64
FSUB = 256
LANES = 128
CHUNKS = 4
VMEM = 56 * 1024 * 1024

NT = (((1,), (1,)), ((), ()))
TN = (((0,), (0,)), ((), ()))


def fir_window():
    ids = np.arange(TAPS * NFFT, dtype=np.float64)
    centered = (ids - 0.5 * TAPS * NFFT + 0.5) / NFFT
    hann_part = 0.5 - 0.5 * np.cos(2.0 * np.pi * (ids + 0.5) / (TAPS * NFFT))
    return (np.sinc(centered) * hann_part).reshape(TAPS, NFFT)


def dft_rows(chan_ids):
    m = np.arange(NFFT, dtype=np.int64)
    turns = (chan_ids[..., None].astype(np.int64) * m) % NFFT
    table = 2.0 * np.pi * np.arange(NFFT) / NFFT
    cosine = np.cos(table).astype(np.float32).astype(ml_dtypes.bfloat16)
    sine = (-np.sin(table)).astype(np.float32).astype(ml_dtypes.bfloat16)
    return np.stack([cosine[turns], sine[turns]], axis=1)


class Sizes:
    def __init__(self, devices, feed_dev):
        self.devices = devices
        self.feed_dev = feed_dev
        self.cap = feed_dev // 2
        self.lane_frames = LANES // self.cap
        self.quads = FR // self.lane_frames
        self.width = self.lane_frames * feed_dev
        self.steps = 6 if self.quads % 6 == 0 else self.quads
        self.step_frames = FR // self.steps
        self.step_quads = self.quads // self.steps
        self.step_lanes = self.step_frames * feed_dev
        self.chan_dev = CHANNELS // devices
        self.bands_here = BANDS // devices
        self.chunks = min(CHUNKS, self.chan_dev // 8)
        self.chunk_ch = self.chan_dev // self.chunks
        self.rows_dev = 2 * self.chunk_ch
        self.rows = devices * self.rows_dev
        self.groups = devices // self.lane_frames


def pick_rows(z, st_ref, key_ref, send_ref):
    def body(d, carry):
        start = pl.multiple_of(d * z.rows_dev, z.rows_dev)
        parts = []
        for g in range(z.steps):
            for q in range(z.step_quads):
                parts.append(st_ref[g, pl.ds(start, z.rows_dev), q * z.width : (q + 1) * z.width])
        lhs = jnp.concatenate(parts, axis=0)
        key = key_ref[pl.ds(d, 1), :]
        slot = lax.broadcasted_iota(jnp.int32, (LANES, z.width), 0)
        pick = jnp.where(slot == key, 1.0, 0.0).astype(jnp.bfloat16)
        out = lax.dot_general(lhs, pick, NT, preferred_element_type=jnp.float32)
        send_ref[d] = out.astype(jnp.bfloat16).reshape(z.quads, z.rows_dev, LANES)
        return carry

    lax.fori_loop(0, z.devices, body, 0)


def transform(z, scale, filt_ref, basis_ref, key_ref, spec_ref, send_ref, st_ref):
    g = pl.program_id(0)
    spectra = lax.dot_general(
        basis_ref[...], filt_ref[...], NT, preferred_element_type=jnp.float32
    )
    spectra = (spectra * scale).astype(jnp.bfloat16)
    spec_ref[...] = spectra
    st_ref[g] = spectra

    @pl.when(g == z.steps - 1)
    def _():
        pick_rows(z, st_ref, key_ref, send_ref)


def first_kernel(
    z, scale, main_ref, h0_ref, h1_ref, h2_ref, win_ref, basis_ref, key_ref,
    filt_ref, spec_ref, send_ref, st_ref,
):
    halo = (h0_ref, h1_ref, h2_ref)

    def body(i, carry):
        off = pl.multiple_of(i * LANES, LANES)
        taps = [win_ref[k : k + 1, pl.ds(off, LANES)] for k in range(TAPS)]
        for f0 in range(0, z.feed_dev, 16):
            frames = []
            for t in range(z.step_frames + TAPS - 1):
                if t < z.step_frames:
                    x = main_ref[f0 : f0 + 16, pl.ds(t * NFFT + off, LANES)]
                else:
                    x = halo[t - z.step_frames][f0 : f0 + 16, pl.ds(off, LANES)]
                frames.append(x.astype(jnp.float32))
            for t in range(z.step_frames):
                total = taps[0] * frames[t]
                for k in range(1, TAPS):
                    total = total + taps[k] * frames[t + k]
                row = t * z.feed_dev + f0
                filt_ref[row : row + 16, pl.ds(off, LANES)] = total.astype(jnp.bfloat16)
        return carry

    lax.fori_loop(0, NFFT // LANES, body, 0)
    transform(z, scale, filt_ref, basis_ref, key_ref, spec_ref, send_ref, st_ref)


def next_kernel(z, scale, filt_ref, basis_ref, key_ref, spec_ref, send_ref, st_ref):
    transform(z, scale, filt_ref, basis_ref, key_ref, spec_ref, send_ref, st_ref)


def whole_spec(shape):
    return pl.BlockSpec(shape, lambda g: (0,) * len(shape))


def spectra_call(z, scale, basis, key, filt=None, voltages=None, window=None):
    filt_rows = z.step_frames * z.feed_dev
    filt_spec = pl.BlockSpec((filt_rows, NFFT), lambda g: (g, 0))
    spec_shape = jax.ShapeDtypeStruct((z.rows, FR * z.feed_dev), jnp.bfloat16)
    spec_spec = pl.BlockSpec((z.rows, z.step_lanes), lambda g: (0, g))
    send_dims = (z.devices, z.quads, z.rows_dev, LANES)
    send_shape = jax.ShapeDtypeStruct(send_dims, jnp.bfloat16)
    shared = [whole_spec((z.rows, NFFT)), whole_spec((z.devices, z.width))]
    flops = 2 * z.rows * NFFT * FR * z.feed_dev
    common = dict(
        grid=(z.steps,),
        scratch_shapes=[pltpu.VMEM((z.steps, z.rows, z.step_lanes), jnp.bfloat16)],
        compiler_params=pltpu.CompilerParams(vmem_limit_bytes=VMEM),
        cost_estimate=pl.CostEstimate(
            flops=flops, bytes_accessed=20_000_000, transcendentals=0
        ),
    )
    if filt is not None:
        return pl.pallas_call(
            functools.partial(next_kernel, z, scale),
            in_specs=[filt_spec] + shared,
            out_specs=[spec_spec, whole_spec(send_dims)],
            out_shape=[spec_shape, send_shape],
            name="spectra_next",
            **common,
        )(filt, basis, key)

    def halo_spec(h):
        return pl.BlockSpec((z.feed_dev, NFFT), lambda g: (0, z.step_frames * (g + 1) + h))

    return pl.pallas_call(
        functools.partial(first_kernel, z, scale),
        in_specs=[
            pl.BlockSpec((z.feed_dev, z.step_frames * NFFT), lambda g: (0, g)),
            halo_spec(0),
            halo_spec(1),
            halo_spec(2),
            whole_spec((TAPS, NFFT)),
        ]
        + shared,
        out_specs=[filt_spec, spec_spec, whole_spec(send_dims)],
        out_shape=[
            jax.ShapeDtypeStruct((FR * z.feed_dev, NFFT), jnp.bfloat16),
            spec_shape,
            send_shape,
        ],
        name="filter_spectra",
        **common,
    )(voltages, voltages, voltages, voltages, window, basis, key)


def receive_kernel(z, step_ch, arr_ref, key_ref, *refs):
    vis_ref, rows_ref = refs[-2], refs[-1]
    g = pl.program_id(0)
    depth = z.quads * z.rows_dev
    lf = z.lane_frames

    @pl.when(g == 0)
    def _():
        lane_group = lax.broadcasted_iota(jnp.int32, (depth, LANES), 1) // z.cap
        slot = lax.broadcasted_iota(jnp.int32, (z.groups * LANES, FSUB), 0)

        def body(tau, carry):
            tiles = []
            for big in range(z.groups):
                tile = None
                for lane in range(lf):
                    source = big * lf + lax.rem(lane - tau + lf, lf)
                    block = arr_ref[source].reshape(depth, LANES)
                    if tile is None:
                        tile = block
                    else:
                        tile = jnp.where(lane_group == lane, block, tile)
                tiles.append(tile)
            lhs = jnp.concatenate(tiles, axis=1)
            pick = jnp.where(slot == key_ref[pl.ds(tau, 1), :], 1.0, 0.0).astype(jnp.bfloat16)
            start = pl.multiple_of(tau * depth, depth)
            rows = jnp.dot(lhs, pick, preferred_element_type=jnp.float32)
            for half in range(FSUB // LANES):
                rows_ref[half, pl.ds(start, depth), :] = rows[:, half * LANES : (half + 1) * LANES]
            return carry

        lax.fori_loop(0, lf, body, 0)

    for i in range(step_ch):
        ch = g * step_ch + i
        halves = []
        for part in range(2):
            halves.append(
                jnp.concatenate(
                    [
                        rows_ref[half, pl.ds(ch + part * z.chunk_ch, FR, stride=z.rows_dev), :]
                        for half in range(FSUB // LANES)
                    ],
                    axis=1,
                )
            )
        real, imag = halves
        right = jnp.concatenate([real, imag], axis=0)
        swapped = jnp.concatenate([imag, -real], axis=0)
        left = jnp.concatenate([right.T, swapped.T], axis=0).astype(jnp.bfloat16)
        both = jnp.dot(left, right.astype(jnp.bfloat16), preferred_element_type=jnp.float32)
        both = both * (1.0 / FR)
        vis_ref[i, 0] = both[:FSUB]
        vis_ref[i, 1] = both[FSUB:]


def receive_call(z, chunk, arrived, key, vis):
    step_ch = 4
    steps = z.chunk_ch // step_ch
    out_shape = jax.ShapeDtypeStruct((z.chan_dev, 2, FSUB, FSUB), jnp.float32)
    in_specs = [whole_spec(arrived.shape), whole_spec(key.shape)]
    operands = [arrived, key]
    aliases = {}
    if vis is not None:
        in_specs.append(pl.BlockSpec(memory_space=pl.ANY))
        operands.append(vis)
        aliases = {2: 0}
    return pl.pallas_call(
        functools.partial(receive_kernel, z, step_ch),
        grid=(steps,),
        in_specs=in_specs,
        out_specs=pl.BlockSpec(
            (step_ch, 2, FSUB, FSUB), lambda g: (chunk * steps + g, 0, 0, 0)
        ),
        out_shape=out_shape,
        input_output_aliases=aliases,
        scratch_shapes=[
            pltpu.VMEM((FSUB // LANES, FR * z.rows_dev, LANES), jnp.float32)
        ],
        compiler_params=pltpu.CompilerParams(vmem_limit_bytes=VMEM),
        cost_estimate=pl.CostEstimate(
            flops=4_000_000_000, bytes_accessed=10_000_000, transcendentals=0
        ),
        name="correlate",
    )(*operands)


def beam_kernel(z, step_dev, *refs):
    spec_refs = refs[: z.chunks]
    cos_ref, sin_ref, sum_ref, out_ref, prod_ref = refs[z.chunks :]
    count = step_dev * z.chunk_ch
    for k in range(z.chunks):

        def body(q, carry):
            off = pl.multiple_of(q * z.width, z.width)
            x = spec_refs[k][:, pl.ds(off, z.width)].astype(jnp.float32)
            x = x.reshape(step_dev, 2, z.chunk_ch, z.width)
            real = x[:, 0].reshape(count, z.width)
            imag = x[:, 1].reshape(count, z.width)
            for g in range(BEAMS):
                c = cos_ref[k, g].astype(jnp.float32)
                s = sin_ref[k, g].astype(jnp.float32)
                a = (c * real + s * imag).astype(jnp.bfloat16)
                b = (c * imag - s * real).astype(jnp.bfloat16)
                prod_ref[g * count : (g + 1) * count, pl.ds(off, z.width)] = a
                top = (BEAMS + g) * count
                prod_ref[top : top + count, pl.ds(off, z.width)] = b
            return carry

        lax.fori_loop(0, z.quads, body, 0)
        sums = jnp.dot(prod_ref[...], sum_ref[...], preferred_element_type=jnp.float32)
        sums = sums * (1.0 / np.sqrt(F))
        for j in range(2 * BEAMS):
            part = sums[j * count : (j + 1) * count, :FR].reshape(step_dev, z.chunk_ch, FR)
            rows = slice(k * z.chunk_ch, (k + 1) * z.chunk_ch)
            out_ref[:, rows, j * FR : (j + 1) * FR] = part


def beam_call(z, spectra, cos_w, sin_w):
    step_dev = max(1, 64 // z.chunk_ch)
    steps = z.devices // step_dev
    count = step_dev * z.chunk_ch
    lanes = FR * z.feed_dev
    frame = np.arange(lanes) // z.feed_dev
    sums = (frame[:, None] == np.arange(LANES)[None, :]).astype(ml_dtypes.bfloat16)
    weight_spec = pl.BlockSpec((z.chunks, BEAMS, count, z.width), lambda g: (0, 0, g, 0))
    out = pl.pallas_call(
        functools.partial(beam_kernel, z, step_dev),
        grid=(steps,),
        in_specs=[
            pl.BlockSpec((step_dev * z.rows_dev, lanes), lambda g: (g, 0))
            for _ in range(z.chunks)
        ]
        + [weight_spec, weight_spec, whole_spec((lanes, LANES))],
        out_specs=pl.BlockSpec((step_dev, z.chan_dev, 2 * BEAMS * FR), lambda g: (g, 0, 0)),
        out_shape=jax.ShapeDtypeStruct((z.devices, z.chan_dev, 2 * BEAMS * FR), jnp.float32),
        scratch_shapes=[pltpu.VMEM((2 * BEAMS * count, lanes), jnp.bfloat16)],
        compiler_params=pltpu.CompilerParams(vmem_limit_bytes=VMEM),
        cost_estimate=pl.CostEstimate(
            flops=20_000_000_000, bytes_accessed=20_000_000, transcendentals=0
        ),
        name="beam_sums",
    )(*spectra, cos_w, sin_w, jnp.asarray(sums))
    return out.reshape(CHANNELS, 2 * BEAMS * FR)


def on_device(voltages, delays, band_feeds):
    z = Sizes(lax.axis_size("chan"), voltages.shape[0])
    me = lax.axis_index("chan")
    turn = lax.rem(me, z.lane_frames)
    window = fir_window()
    scale = float(np.sqrt(2.0 / np.sum(window * window)))
    window = jnp.asarray(window.astype(np.float32))

    edges = me * z.feed_dev + jnp.arange(z.feed_dev + 1, dtype=jnp.int32)
    below = jnp.sum(
        (band_feeds[:, None, :] < edges[None, :, None]).astype(jnp.int32), axis=2
    )
    rank = below[:, :-1] - below[:, :1]
    listed = below[:, 1:] > below[:, :-1]
    lane = jnp.arange(z.lane_frames, dtype=jnp.int32)
    group = lax.rem(lane + turn, z.lane_frames) * z.cap
    send_key = jnp.where(listed[:, None, :], rank[:, None, :] + group[None, :, None], -1)
    send_key = send_key.reshape(z.devices, z.bands_here, z.width)

    own = lax.dynamic_slice_in_dim(band_feeds, me * z.bands_here, z.bands_here, 0)
    source = own // z.feed_dev
    before = jnp.sum(
        (own[:, None, :] < (source * z.feed_dev)[:, :, None]).astype(jnp.int32), axis=2
    )
    place = jnp.arange(FSUB, dtype=jnp.int32)[None, :] - before
    base = (source // z.lane_frames) * LANES + place
    shift = lax.rem(source, z.lane_frames)
    take_key = base[:, None, :] + z.cap * lax.rem(
        shift[:, None, :] + lane[None, :, None], z.lane_frames
    )

    ids = np.arange(CHANNELS).reshape(z.devices, z.chunks, z.chunk_ch)
    chunk_ids = np.transpose(ids, (1, 0, 2))

    filt = None
    spectra = []
    arrived = []
    for k in range(z.chunks):
        band = k * z.chunk_ch // BAND_CH
        basis = jnp.asarray(dft_rows(chunk_ids[k]).reshape(z.rows, NFFT))
        key = send_key[:, band]
        if k == 0:
            filt, spec, send = spectra_call(
                z, scale, basis, key, voltages=voltages, window=window
            )
        else:
            spec, send = spectra_call(z, scale, basis, key, filt=filt)
        spectra.append(spec)
        arrived.append(lax.all_to_all(send, "chan", split_axis=0, concat_axis=0, tiled=True))

    chan_float = jnp.asarray(chunk_ids.reshape(z.chunks, 1, -1, 1).astype(np.float32))
    phase = 2.0 * jnp.pi / NFFT * (delays[None, :, None, :] * chan_float)
    cos_w = jnp.tile(jnp.cos(phase).astype(jnp.bfloat16), (1, 1, 1, z.lane_frames))
    sin_w = jnp.tile(jnp.sin(phase).astype(jnp.bfloat16), (1, 1, 1, z.lane_frames))
    partial_beams = beam_call(z, spectra, cos_w, sin_w)
    beams = lax.psum_scatter(partial_beams, "chan", scatter_dimension=0, tiled=True)

    vis = None
    for k in range(z.chunks):
        band = k * z.chunk_ch // BAND_CH
        vis = receive_call(z, k, arrived[k], take_key[band], vis)
    return (vis, beams)


def solution(mesh):
    in_specs = (P(("grp", "chan"), None), P(None, ("grp", "chan")), P())
    out_specs = (P(("grp", "chan"), None, None, None), P(("grp", "chan"), None))
    return jax.shard_map(
        on_device, mesh=mesh, in_specs=in_specs, out_specs=out_specs, check_vma=False
    )
```

profile of v0, /device:TPU:5, one launch (start us, length us, event | category | flops | bytes accessed | tf_op | source)
XLA Modules:
  0.0 282.3 jit_solution(8177108707273236305)
XLA Ops:
  7.2 2.1 convert_reduce_fusion
  10.0 0.6 slice_bitcast_fusion
  10.7 24.5 %filter_spectra.1 = (bf16[3072,2048]{1,0:T(8,128)(2,1)}, bf16[512,3072]{1,0:T(8,128)(2,1)}, bf16[16,12,32,128]{3,2,1,0:T(8,128)(2,1)}) custom-call(bf16[64,104448]{1,0:T(8,128)(2,1)} %h2_ref.1, bf16[64,104448]{1,0:T(8,128)(2,1)} %h2_ref.1, bf16[64,104448]{1,0:T(8,128)(2,1)} %h2_ref.1, bf16[64,104448]{1,0:T(8,128)(2,1)} %h2_ref.1, ...), custom_call_target="tpu_custom_call" | custom-call | flops 6442450944 | bytes 20000000 | tf_op jit(solution)/shard_map/filter_spectra/pallas_call | solution.py:165
  35.2 6.7 %all-to-all-start.3 = ((bf16[16,12,32,128]{3,2,1,0:T(8,128)(2,1)}), bf16[16,12,32,128]{3,2,1,0:T(8,128)(2,1)S(1)}, u32[]{:S(2)}, u32[]{:S(2)}) async-start(bf16[16,12,32,128]{3,2,1,0:T(8,128)(2,1)} %get-tuple-element.15), calls=%async_computation.3 | async-start | bytes 3145728 | tf_op jit(solution)/shard_map/all_to_all | solution.py:380
  41.9 15.9 %spectra_next.5 = (bf16[512,3072]{1,0:T(8,128)(2,1)}, bf16[16,12,32,128]{3,2,1,0:T(8,128)(2,1)}) custom-call(bf16[3072,2048]{1,0:T(8,128)(2,1)} %get-tuple-element.11.filt_ref, bf16[512,2048]{1,0:T(8,128)(2,1)} %constant.68.clone.basis_ref, s32[16,256]{1,0:T(8,128)} %get-tuple-element.22.key_ref), custom_call_target="tpu_custom_call" | custom-call | flops 6442450944 | bytes 20000000 | tf_op jit(solution)/shard_map/spectra_next/pallas_call | solution.py:153
  57.8 17.4 %all-to-all-done.3.arr_ref = bf16[16,12,32,128]{3,2,1,0:T(8,128)(2,1)S(1)} async-done(((bf16[16,12,32,128]{3,2,1,0:T(8,128)(2,1)}), bf16[16,12,32,128]{3,2,1,0:T(8,128)(2,1)S(1)}, u32[]{:S(2)}, u32[]{:S(2)}) %all-to-all-start.3) | async-done | bytes 1572896 | tf_op jit(solution)/shard_map/all_to_all | solution.py:380
  75.2 7.8 %all-to-all-start.2 = ((bf16[16,12,32,128]{3,2,1,0:T(8,128)(2,1)}), bf16[16,12,32,128]{3,2,1,0:T(8,128)(2,1)S(1)}, u32[]{:S(2)}, u32[]{:S(2)}) async-start(bf16[16,12,32,128]{3,2,1,0:T(8,128)(2,1)} %get-tuple-element.14), calls=%async_computation.2 | async-start | bytes 3145728 | tf_op jit(solution)/shard_map/all_to_all | solution.py:380
  82.9 16.0 %spectra_next.4 = (bf16[512,3072]{1,0:T(8,128)(2,1)}, bf16[16,12,32,128]{3,2,1,0:T(8,128)(2,1)}) custom-call(bf16[3072,2048]{1,0:T(8,128)(2,1)} %get-tuple-element.11.filt_ref, bf16[512,2048]{1,0:T(8,128)(2,1)} %constant.69.clone.basis_ref, s32[16,256]{1,0:T(8,128)} %get-tuple-element.23.key_ref), custom_call_target="tpu_custom_call" | custom-call | flops 6442450944 | bytes 20000000 | tf_op jit(solution)/shard_map/spectra_next/pallas_call | solution.py:153
  98.9 17.4 %all-to-all-done.2.arr_ref = bf16[16,12,32,128]{3,2,1,0:T(8,128)(2,1)S(1)} async-done(((bf16[16,12,32,128]{3,2,1,0:T(8,128)(2,1)}), bf16[16,12,32,128]{3,2,1,0:T(8,128)(2,1)S(1)}, u32[]{:S(2)}, u32[]{:S(2)}) %all-to-all-start.2) | async-done | bytes 1572896 | tf_op jit(solution)/shard_map/all_to_all | solution.py:380
  116.3 7.8 %all-to-all-start.1 = ((bf16[16,12,32,128]{3,2,1,0:T(8,128)(2,1)}), bf16[16,12,32,128]{3,2,1,0:T(8,128)(2,1)}, u32[]{:S(2)}, u32[]{:S(2)}) async-start(bf16[16,12,32,128]{3,2,1,0:T(8,128)(2,1)} %get-tuple-element.13), calls=%async_computation.1 | async-start | bytes 3145728 | tf_op jit(solution)/shard_map/all_to_all | solution.py:380
  124.1 4.9 %sine_convert_fusion = (bf16[4,4,256,64]{2,3,1,0:T(8,128)(2,1)S(1)}, bf16[4,4,256,64]{2,3,1,0:T(8,128)(2,1)}) fusion(f32[4,256]{1,0:T(4,128)S(1)} %copy-done.4, f32[4,64]{1,0:T(4,128)S(1)} %copy-done.5), kind=kLoop, calls=%fused_computation.1 | loop fusion | flops 1048576 | bytes 1053696 | tf_op jit(solution)/shard_map/convert_element_type | solution.py:385
  129.2 2.4 copy.28.refs_5_
  131.9 2.4 copy.27.refs_4_
  134.3 15.9 %spectra_next.3 = (bf16[512,3072]{1,0:T(8,128)(2,1)}, bf16[16,12,32,128]{3,2,1,0:T(8,128)(2,1)}) custom-call(bf16[3072,2048]{1,0:T(8,128)(2,1)} %get-tuple-element.11.filt_ref, bf16[512,2048]{1,0:T(8,128)(2,1)} %constant.70.clone.basis_ref, s32[16,256]{1,0:T(8,128)} %get-tuple-element.24.key_ref), custom_call_target="tpu_custom_call" | custom-call | flops 6442450944 | bytes 20000000 | tf_op jit(solution)/shard_map/spectra_next/pallas_call | solution.py:153
  150.2 7.3 %all-to-all-done.1.arr_ref = bf16[16,12,32,128]{3,2,1,0:T(8,128)(2,1)} async-done(((bf16[16,12,32,128]{3,2,1,0:T(8,128)(2,1)}), bf16[16,12,32,128]{3,2,1,0:T(8,128)(2,1)}, u32[]{:S(2)}, u32[]{:S(2)}) %all-to-all-start.1) | async-done | bytes 1572896 | tf_op jit(solution)/shard_map/all_to_all | solution.py:380
  157.5 7.8 %all-to-all-start = ((bf16[16,12,32,128]{3,2,1,0:T(8,128)(2,1)}), bf16[16,12,32,128]{3,2,1,0:T(8,128)(2,1)S(1)}, u32[]{:S(2)}, u32[]{:S(2)}) async-start(bf16[16,12,32,128]{3,2,1,0:T(8,128)(2,1)} %get-tuple-element.12), calls=%async_computation | async-start | bytes 3145728 | tf_op jit(solution)/shard_map/all_to_all | solution.py:380
  165.5 51.8 %beam_sums.1 = f32[16,64,384]{2,1,0:T(8,128)} custom-call(bf16[512,3072]{1,0:T(8,128)(2,1)} %get-tuple-element.16.refs_0_, bf16[512,3072]{1,0:T(8,128)(2,1)} %get-tuple-element.17.refs_1_, bf16[512,3072]{1,0:T(8,128)(2,1)} %get-tuple-element.18.refs_2_, bf16[512,3072]{1,0:T(8,128)(2,1)} %get-tuple-element.19.refs_3_, bf16[4,4,256,256]{3,2,1,0:T(8,128)(2,1)} %copy.27.refs_4_, ...), custom_call_target="tpu_custom_call" | custom-call | flops 20000000000 | bytes 20000000 | tf_op jit(solution)/shard_map/beam_sums/pallas_call | solution.py:312
  217.3 0.7 broadcast_multiply_fusion
  219.1 7.1 %correlate.4.refs_0_ = f32[64,2,256,256]{3,2,1,0:T(8,128)} custom-call(bf16[16,12,32,128]{3,2,1,0:T(8,128)(2,1)} %copy-done, s32[4,256]{1,0:T(4,128)} %get-tuple-element.26.key_ref), custom_call_target="tpu_custom_call" | custom-call | flops 4000000000 | bytes 10000000 | tf_op jit(solution)/shard_map/correlate/pallas_call | solution.py:253
  226.2 7.1 %correlate.5.refs_0_ = f32[64,2,256,256]{3,2,1,0:T(8,128)} custom-call(bf16[16,12,32,128]{3,2,1,0:T(8,128)(2,1)} %copy-done.1, s32[4,256]{1,0:T(4,128)} %get-tuple-element.27.key_ref, f32[64,2,256,256]{3,2,1,0:T(8,128)} %correlate.4.refs_0_), custom_call_target="tpu_custom_call", output_to_operand_aliasing={{}: (2, {})} | custom-call | flops 4000000000 | bytes 10000000 | tf_op jit(solution)/shard_map/correlate/pallas_call | solution.py:253
  233.3 7.1 %correlate.6.refs_0_ = f32[64,2,256,256]{3,2,1,0:T(8,128)} custom-call(bf16[16,12,32,128]{3,2,1,0:T(8,128)(2,1)} %all-to-all-done.1.arr_ref, s32[4,256]{1,0:T(4,128)} %get-tuple-element.28.key_ref, f32[64,2,256,256]{3,2,1,0:T(8,128)} %correlate.5.refs_0_), custom_call_target="tpu_custom_call", output_to_operand_aliasing={{}: (2, {})} | custom-call | flops 4000000000 | bytes 10000000 | tf_op jit(solution)/shard_map/correlate/pallas_call | solution.py:253
  240.4 1.2 copy-done.2
  241.6 7.1 %correlate.7 = f32[64,2,256,256]{3,2,1,0:T(8,128)} custom-call(bf16[16,12,32,128]{3,2,1,0:T(8,128)(2,1)} %copy-done.2, s32[4,256]{1,0:T(4,128)} %get-tuple-element.29.key_ref, f32[64,2,256,256]{3,2,1,0:T(8,128)} %correlate.6.refs_0_), custom_call_target="tpu_custom_call", output_to_operand_aliasing={{}: (2, {})} | custom-call | flops 4000000000 | bytes 10000000 | tf_op jit(solution)/shard_map/correlate/pallas_call | solution.py:253
  248.7 26.7 %reduce-scatter.2.cloned.1.call-done = f32[64,384]{1,0:T(8,128)} async-done(((f32[1024,384]{1,0:T(8,128)}), f32[64,384]{1,0:T(8,128)}) %reduce-scatter.2.cloned.1.call-update) | async-done | bytes 98320 | tf_op jit(solution)/shard_map/reduce_scatter | solution.py:387
  (34 shorter events, 2.5 us)
Async XLA Ops:
  35.2 40.0 %all-to-all-start.3 = ((bf16[16,12,32,128]{3,2,1,0:T(8,128)(2,1)}), bf16[16,12,32,128]{3,2,1,0:T(8,128)(2,1)S(1)}, u32[]{:S(2)}, u32[]{:S(2)}) async-start(bf16[16,12,32,128]{3,2,1,0:T(8,128)(2,1)} %get-tuple-element.15), calls=%async_computation.3 | async-start | bytes 3145728 | tf_op jit(solution)/shard_map/all_to_all | solution.py:380
  75.2 23.7 %copy-start = (bf16[16,12,32,128]{3,2,1,0:T(8,128)(2,1)}, bf16[16,12,32,128]{3,2,1,0:T(8,128)(2,1)S(1)}, u32[]{:S(2)}) copy-start(bf16[16,12,32,128]{3,2,1,0:T(8,128)(2,1)S(1)} %all-to-all-done.3.arr_ref) | copy-start | bytes 4718596
  75.2 41.1 %all-to-all-start.2 = ((bf16[16,12,32,128]{3,2,1,0:T(8,128)(2,1)}), bf16[16,12,32,128]{3,2,1,0:T(8,128)(2,1)S(1)}, u32[]{:S(2)}, u32[]{:S(2)}) async-start(bf16[16,12,32,128]{3,2,1,0:T(8,128)(2,1)} %get-tuple-element.14), calls=%async_computation.2 | async-start | bytes 3145728 | tf_op jit(solution)/shard_map/all_to_all | solution.py:380
  98.9 25.1 %copy-start.4 = (f32[4,256]{1,0:T(4,128)S(1)}, f32[4,256]{1,0:T(4,128)}, u32[]{:S(2)}) copy-start(f32[4,256]{1,0:T(4,128)} %constant.73) | copy-start | bytes 12292
  98.9 25.1 %copy-start.5 = (f32[4,64]{1,0:T(4,128)S(1)}, f32[4,64]{1,0:T(4,128)}, u32[]{:S(2)}) copy-start(f32[4,64]{1,0:T(4,128)} %param.11) | copy-start | bytes 3076
  116.3 12.7 %copy-start.1 = (bf16[16,12,32,128]{3,2,1,0:T(8,128)(2,1)}, bf16[16,12,32,128]{3,2,1,0:T(8,128)(2,1)S(1)}, u32[]{:S(2)}) copy-start(bf16[16,12,32,128]{3,2,1,0:T(8,128)(2,1)S(1)} %all-to-all-done.2.arr_ref) | copy-start | bytes 4718596
  116.3 41.2 %all-to-all-start.1 = ((bf16[16,12,32,128]{3,2,1,0:T(8,128)(2,1)}), bf16[16,12,32,128]{3,2,1,0:T(8,128)(2,1)}, u32[]{:S(2)}, u32[]{:S(2)}) async-start(bf16[16,12,32,128]{3,2,1,0:T(8,128)(2,1)} %get-tuple-element.13), calls=%async_computation.1 | async-start | bytes 3145728 | tf_op jit(solution)/shard_map/all_to_all | solution.py:380
  129.2 2.4 copy-start.3
  157.5 83.0 %all-to-all-start = ((bf16[16,12,32,128]{3,2,1,0:T(8,128)(2,1)}), bf16[16,12,32,128]{3,2,1,0:T(8,128)(2,1)S(1)}, u32[]{:S(2)}, u32[]{:S(2)}) async-start(bf16[16,12,32,128]{3,2,1,0:T(8,128)(2,1)} %get-tuple-element.12), calls=%async_computation | async-start | bytes 3145728 | tf_op jit(solution)/shard_map/all_to_all | solution.py:380
  165.2 110.2 %reduce-scatter.2.cloned.1.call-start = ((), (), s32[]{:S(2)}) async-start(), calls=%async_computation.5 | async-start | bytes 1671168 | tf_op jit(solution)/shard_map/reduce_scatter | solution.py:387
  240.4 1.2 copy-start.2
Sparse Core Ops, SparseCore 0:
  217.5 57.9 reduce-scatter.1
where the time goes:
time: 287 us; the launch traced here: 282 us
  Pallas kernels  153 us (53%)
  waiting for transfers between devices  68.8 us (24%)
  starting transfers between devices  30.1 us (10%)
  between operations  14.2 us (5%)
  local copies, waits for them, and re-layouts  8.36 us (3%)
  other arithmetic  8.21 us (3%)
    pallas_call x1, Pallas kernels, beam_call(): pl.pallas_call(functools.partial(beam_kernel, z, step_dev), grid=(steps,)...  51.8 us
    pallas_call x3, Pallas kernels, spectra_call(): pl.pallas_call(functools.partial(next_kernel, z, scale), in_specs=[filt_s...  47.8 us
    all_to_all x4, waiting for transfers between devices, on_device(): lax.all_to_all(send, 'chan', split_axis=0, concat_axis=0, tiled=True)  42.1 us
    all_to_all x4, starting transfers between devices, on_device(): lax.all_to_all(send, 'chan', split_axis=0, concat_axis=0, tiled=True)  29.9 us
    pallas_call x4, Pallas kernels, receive_call(): pl.pallas_call(functools.partial(receive_kernel, z, step_ch), grid=(steps...  28.4 us
    reduce_scatter x1, waiting for transfers between devices, on_device(): lax.psum_scatter(partial_beams, 'chan', scatter_dimension=0, tiled=True)  26.7 us
    pallas_call x1, Pallas kernels, spectra_call(): pl.pallas_call(functools.partial(first_kernel, z, scale), in_specs=[pl.Bl...  24.5 us
  transfers between devices with their start and end apart: 5, of which 4 were waited for; matrix products, arithmetic and copies ran while one was open for 4% of the time, Pallas kernels for 45%

commit v1 on v0

v1 whole, which is shorter than its diff:
```python
import functools

import jax
import jax.numpy as jnp
import ml_dtypes
import numpy as np
from jax import lax
from jax.experimental import pallas as pl
from jax.experimental.pallas import tpu as pltpu
from jax.sharding import PartitionSpec as P

F = 1024
CHANNELS = 1024
TAPS = 4
BAND_CH = 16
BEAMS = 4
FR = 48
NFFT = 2048
BANDS = 64
FSUB = 256
LANES = 128
VMEM = 56 * 1024 * 1024

NT = (((1,), (1,)), ((), ()))


def fir_window():
    ids = np.arange(TAPS * NFFT, dtype=np.float64)
    centered = (ids - 0.5 * TAPS * NFFT + 0.5) / NFFT
    hann_part = 0.5 - 0.5 * np.cos(2.0 * np.pi * (ids + 0.5) / (TAPS * NFFT))
    return (np.sinc(centered) * hann_part).reshape(TAPS, NFFT)


def dft_rows(chan_ids):
    m = np.arange(NFFT, dtype=np.int64)
    turns = (chan_ids[..., None].astype(np.int64) * m) % NFFT
    table = 2.0 * np.pi * np.arange(NFFT) / NFFT
    cosine = np.cos(table).astype(np.float32).astype(ml_dtypes.bfloat16)
    sine = (-np.sin(table)).astype(np.float32).astype(ml_dtypes.bfloat16)
    return np.stack([cosine[turns], sine[turns]], axis=1)


class Sizes:
    def __init__(self, devices, feed_dev):
        self.devices = devices
        self.feed_dev = feed_dev
        self.cap = feed_dev // 2
        self.lane_frames = LANES // self.cap
        self.quads = FR // self.lane_frames
        self.width = self.lane_frames * feed_dev
        self.steps = 6 if self.quads % 6 == 0 else self.quads
        self.step_frames = FR // self.steps
        self.step_quads = self.quads // self.steps
        self.step_lanes = self.step_frames * feed_dev
        self.chan_dev = CHANNELS // devices
        self.bands_here = BANDS // devices
        self.chunks = self.chan_dev // BAND_CH
        self.chunk_ch = BAND_CH
        self.rows_dev = 2 * self.chunk_ch
        self.rows = devices * self.rows_dev
        self.groups = devices // self.lane_frames


def transform(z, scale, count, me_ref, filt_ref, basis_ref, loc_ref, out_refs, st_ref):
    spec_refs, send_refs = out_refs[:count], out_refs[count:]
    me = me_ref[0]
    spectra = lax.dot_general(
        basis_ref[...], filt_ref[...], NT, preferred_element_type=jnp.float32
    )
    spectra = spectra * scale
    st_ref[...] = spectra
    for c in range(count):
        spec_refs[c][...] = spectra[c * z.rows : (c + 1) * z.rows].astype(jnp.bfloat16)
    lane_group = lax.broadcasted_iota(jnp.int32, (z.rows_dev, LANES), 1) // z.cap
    half = z.lane_frames // 2
    for c in range(count):
        for k in range(z.devices):
            owner = me ^ k
            start = pl.multiple_of(c * z.rows + owner * z.rows_dev, z.rows_dev)
            frame = lane_group ^ (k % z.lane_frames)
            lower = frame < half
            index = loc_ref[c, pl.ds(owner, 1), :] + (frame % half) * z.feed_dev
            for q in range(z.step_quads):
                parts = []
                for side in range(2):
                    lane = q * z.width + side * LANES
                    x = st_ref[pl.ds(start, z.rows_dev), lane : lane + LANES]
                    parts.append(
                        jnp.take_along_axis(x, index, axis=1, mode="promise_in_bounds")
                    )
                picked = jnp.where(lower, parts[0], parts[1])
                send_refs[c * z.devices + k][q] = picked.astype(jnp.bfloat16)


def first_kernel(
    z, scale, me_ref, main_ref, h0_ref, h1_ref, h2_ref, win_ref, basis_ref, loc_ref, *refs
):
    filt_ref, out_refs, st_ref = refs[0], refs[1:-1], refs[-1]
    halo = (h0_ref, h1_ref, h2_ref)

    def body(i, carry):
        off = pl.multiple_of(i * LANES, LANES)
        taps = [win_ref[k : k + 1, pl.ds(off, LANES)] for k in range(TAPS)]
        for f0 in range(0, z.feed_dev, 16):
            frames = []
            for t in range(z.step_frames + TAPS - 1):
                if t < z.step_frames:
                    x = main_ref[f0 : f0 + 16, pl.ds(t * NFFT + off, LANES)]
                else:
                    x = halo[t - z.step_frames][f0 : f0 + 16, pl.ds(off, LANES)]
                frames.append(x.astype(jnp.float32))
            for t in range(z.step_frames):
                total = taps[0] * frames[t]
                for k in range(1, TAPS):
                    total = total + taps[k] * frames[t + k]
                row = t * z.feed_dev + f0
                filt_ref[row : row + 16, pl.ds(off, LANES)] = total.astype(jnp.bfloat16)
        return carry

    lax.fori_loop(0, NFFT // LANES, body, 0)
    transform(z, scale, 1, me_ref, filt_ref, basis_ref, loc_ref, out_refs, st_ref)


def next_kernel(z, scale, count, me_ref, filt_ref, basis_ref, loc_ref, *refs):
    transform(z, scale, count, me_ref, filt_ref, basis_ref, loc_ref, refs[:-1], refs[-1])


def whole_spec(shape):
    return pl.BlockSpec(shape, lambda *g: (0,) * len(shape))


def spectra_call(z, scale, me, basis, loc, filt=None, voltages=None, window=None):
    count = loc.shape[0]
    filt_rows = z.step_frames * z.feed_dev
    filt_spec = pl.BlockSpec((filt_rows, NFFT), lambda g: (g, 0))
    spec_shape = jax.ShapeDtypeStruct((z.rows, FR * z.feed_dev), jnp.bfloat16)
    spec_spec = pl.BlockSpec((z.rows, z.step_lanes), lambda g: (0, g))
    send_shape = jax.ShapeDtypeStruct((z.quads, z.rows_dev, LANES), jnp.bfloat16)
    send_spec = pl.BlockSpec((z.step_quads, z.rows_dev, LANES), lambda g: (g, 0, 0))
    me_spec = pl.BlockSpec(memory_space=pltpu.SMEM)
    shared = [whole_spec(basis.shape), whole_spec(loc.shape)]
    out_specs = [spec_spec] * count + [send_spec] * (count * z.devices)
    out_shape = [spec_shape] * count + [send_shape] * (count * z.devices)
    flops = 2 * count * z.rows * NFFT * FR * z.feed_dev
    common = dict(
        grid=(z.steps,),
        scratch_shapes=[pltpu.VMEM((count * z.rows, z.step_lanes), jnp.float32)],
        compiler_params=pltpu.CompilerParams(vmem_limit_bytes=VMEM),
        cost_estimate=pl.CostEstimate(
            flops=flops, bytes_accessed=20_000_000, transcendentals=0
        ),
    )
    if filt is not None:
        outs = pl.pallas_call(
            functools.partial(next_kernel, z, scale, count),
            in_specs=[me_spec, filt_spec] + shared,
            out_specs=out_specs,
            out_shape=out_shape,
            name="spectra_next",
            **common,
        )(me, filt, basis, loc)
        return None, outs[:count], outs[count:]

    def halo_spec(h):
        return pl.BlockSpec((z.feed_dev, NFFT), lambda g: (0, z.step_frames * (g + 1) + h))

    outs = pl.pallas_call(
        functools.partial(first_kernel, z, scale),
        in_specs=[
            me_spec,
            pl.BlockSpec((z.feed_dev, z.step_frames * NFFT), lambda g: (0, g)),
            halo_spec(0),
            halo_spec(1),
            halo_spec(2),
            whole_spec((TAPS, NFFT)),
        ]
        + shared,
        out_specs=[filt_spec] + out_specs,
        out_shape=[jax.ShapeDtypeStruct((FR * z.feed_dev, NFFT), jnp.bfloat16)] + out_shape,
        name="filter_spectra",
        **common,
    )(me, voltages, voltages, voltages, voltages, window, basis, loc)
    return outs[0], outs[1 : 1 + count], outs[1 + count :]


def receive_kernel(z, step_ch, *refs):
    arr_refs, key_ref = refs[: z.devices], refs[z.devices]
    vis_ref, rows_ref = refs[-2], refs[-1]
    g = pl.program_id(0)
    depth = z.quads * z.rows_dev
    lf = z.lane_frames

    @pl.when(g == 0)
    def _():
        lane_group = lax.broadcasted_iota(jnp.int32, (depth, LANES), 1) // z.cap
        slot = lax.broadcasted_iota(jnp.int32, (z.groups * LANES, FSUB), 0)
        for tau in range(lf):
            tiles = []
            for big in range(z.groups):
                tile = arr_refs[big * lf + tau][...].reshape(depth, LANES)
                for lane in range(1, lf):
                    block = arr_refs[big * lf + (lane ^ tau)][...].reshape(depth, LANES)
                    tile = jnp.where(lane_group == lane, block, tile)
                tiles.append(tile)
            lhs = jnp.concatenate(tiles, axis=1)
            pick = jnp.where(slot == key_ref[tau : tau + 1, :], 1.0, 0.0).astype(jnp.bfloat16)
            rows = jnp.dot(lhs, pick, preferred_element_type=jnp.float32)
            for half in range(FSUB // LANES):
                rows_ref[half, tau * depth : (tau + 1) * depth, :] = rows[
                    :, half * LANES : (half + 1) * LANES
                ]

    for i in range(step_ch):
        ch = g * step_ch + i
        halves = []
        for part in range(2):
            halves.append(
                jnp.concatenate(
                    [
                        rows_ref[half, pl.ds(ch + part * z.chunk_ch, FR, stride=z.rows_dev), :]
                        for half in range(FSUB // LANES)
                    ],
                    axis=1,
                )
            )
        real, imag = halves
        right = jnp.concatenate([real, imag], axis=0)
        swapped = jnp.concatenate([imag, -real], axis=0)
        left = jnp.concatenate([right.T, swapped.T], axis=0).astype(jnp.bfloat16)
        both = jnp.dot(left, right.astype(jnp.bfloat16), preferred_element_type=jnp.float32)
        both = both * (1.0 / FR)
        vis_ref[i, 0] = both[:FSUB]
        vis_ref[i, 1] = both[FSUB:]


def receive_call(z, chunk, arrived, key, vis):
    step_ch = 4
    steps = z.chunk_ch // step_ch
    out_shape = jax.ShapeDtypeStruct((z.chan_dev, 2, FSUB, FSUB), jnp.float32)
    in_specs = [whole_spec(x.shape) for x in arrived] + [whole_spec(key.shape)]
    operands = list(arrived) + [key]
    aliases = {}
    if vis is not None:
        in_specs.append(pl.BlockSpec(memory_space=pl.ANY))
        aliases = {len(operands): 0}
        operands.append(vis)
    return pl.pallas_call(
        functools.partial(receive_kernel, z, step_ch),
        grid=(steps,),
        in_specs=in_specs,
        out_specs=pl.BlockSpec(
            (step_ch, 2, FSUB, FSUB), lambda g: (chunk * steps + g, 0, 0, 0)
        ),
        out_shape=out_shape,
        input_output_aliases=aliases,
        scratch_shapes=[
            pltpu.VMEM((FSUB // LANES, FR * z.rows_dev, LANES), jnp.float32)
        ],
        compiler_params=pltpu.CompilerParams(vmem_limit_bytes=VMEM),
        cost_estimate=pl.CostEstimate(
            flops=4_000_000_000, bytes_accessed=10_000_000, transcendentals=0
        ),
        name="correlate",
    )(*operands)


def beam_kernel(z, me_ref, *refs):
    spec_refs = refs[: z.chunks]
    cos_ref, sin_ref, sum_ref, out_ref, acc_ref = refs[z.chunks :]
    count = z.chan_dev
    weights = []
    for g in range(BEAMS):
        weights.append(
            [jnp.concatenate([w[g]] * z.lane_frames, axis=1) for w in (cos_ref, sin_ref)]
        )
    acc_ref[...] = jnp.zeros_like(acc_ref)

    def body(q, carry):
        off = pl.multiple_of(q * z.width, z.width)
        x = [spec_refs[k][:, pl.ds(off, z.width)] for k in range(z.chunks)]
        real = jnp.concatenate([v[: z.chunk_ch] for v in x], axis=0)
        imag = jnp.concatenate([v[z.chunk_ch :] for v in x], axis=0)
        ones = sum_ref[pl.ds(off, z.width), :]
        for g in range(BEAMS):
            c, s = weights[g]
            both = jnp.concatenate([c * real + s * imag, c * imag - s * real], axis=0)
            acc_ref[g] += jnp.dot(both, ones, preferred_element_type=jnp.float32)
        return carry

    lax.fori_loop(0, z.quads, body, 0)
    for g in range(BEAMS):
        sums = acc_ref[g] * (1.0 / np.sqrt(F))
        for part in range(2):
            j = part * BEAMS + g
            out_ref[0, :, j * FR : (j + 1) * FR] = sums[part * count : (part + 1) * count, :FR]


def beam_call(z, me, spectra, cos_w, sin_w):
    bits = z.devices.bit_length() - 1
    lanes = FR * z.feed_dev
    frame = np.arange(lanes) // z.feed_dev
    sums = (frame[:, None] == np.arange(LANES)[None, :]).astype(ml_dtypes.bfloat16)

    def owner(j, me_ref):
        k = 0
        for b in range(bits):
            k = k | (((j >> b) & 1) << (bits - 1 - b))
        return me_ref[0] ^ k

    weight_spec = pl.BlockSpec(
        (BEAMS, z.chan_dev, z.feed_dev), lambda j, me_ref: (0, owner(j, me_ref), 0)
    )
    grid_spec = pltpu.PrefetchScalarGridSpec(
        num_scalar_prefetch=1,
        grid=(z.devices,),
        in_specs=[
            pl.BlockSpec((z.rows_dev, lanes), lambda j, me_ref: (owner(j, me_ref), 0))
            for _ in range(z.chunks)
        ]
        + [weight_spec, weight_spec, whole_spec((lanes, LANES))],
        out_specs=pl.BlockSpec(
            (1, z.chan_dev, 2 * BEAMS * FR), lambda j, me_ref: (j, 0, 0)
        ),
        scratch_shapes=[pltpu.VMEM((BEAMS, 2 * z.chan_dev, LANES), jnp.float32)],
    )
    return pl.pallas_call(
        functools.partial(beam_kernel, z),
        grid_spec=grid_spec,
        out_shape=jax.ShapeDtypeStruct((z.devices, z.chan_dev, 2 * BEAMS * FR), jnp.float32),
        compiler_params=pltpu.CompilerParams(vmem_limit_bytes=VMEM),
        cost_estimate=pl.CostEstimate(
            flops=20_000_000_000, bytes_accessed=20_000_000, transcendentals=0
        ),
        name="beam_sums",
    )(me, *spectra, cos_w, sin_w, jnp.asarray(sums))


def swap(z, x, offset):
    return lax.ppermute(x, "chan", [(i, i ^ offset) for i in range(z.devices)])


def on_device(voltages, delays, band_feeds):
    z = Sizes(lax.axis_size("chan"), voltages.shape[0])
    me = lax.axis_index("chan")
    me_array = me.astype(jnp.int32).reshape(1)
    window = fir_window()
    scale = float(np.sqrt(2.0 / np.sum(window * window)))
    window = jnp.asarray(window.astype(np.float32))

    base = me * z.feed_dev
    edges = base + jnp.arange(z.feed_dev + 1, dtype=jnp.int32)
    below = jnp.sum(
        (band_feeds[:, None, :] < edges[None, :, None]).astype(jnp.int32), axis=2
    )
    rank = below[:, :-1] - below[:, :1]
    listed = below[:, 1:] > below[:, :-1]
    rank = jnp.where(listed, rank, -1)
    slots = jnp.arange(LANES, dtype=jnp.int32) % z.cap
    local = jnp.arange(z.feed_dev, dtype=jnp.int32)
    loc = jnp.sum(
        jnp.where(rank[:, None, :] == slots[None, :, None], local[None, None, :], 0), axis=2
    )
    loc = jnp.swapaxes(loc.reshape(z.devices, z.bands_here, LANES), 0, 1)

    own = lax.dynamic_slice_in_dim(band_feeds, me * z.bands_here, z.bands_here, 0)
    source = own // z.feed_dev
    before = jnp.sum(
        (own[:, None, :] < (source * z.feed_dev)[:, :, None]).astype(jnp.int32), axis=2
    )
    place = jnp.arange(FSUB, dtype=jnp.int32)[None, :] - before
    offset = source ^ me
    tau = jnp.arange(z.lane_frames, dtype=jnp.int32)
    big = (offset // z.lane_frames) * LANES + place
    group = (offset % z.lane_frames)[:, None, :] ^ tau[None, :, None]
    take_key = big[:, None, :] + z.cap * group

    ids = np.arange(CHANNELS).reshape(z.devices, z.chunks, z.chunk_ch)
    chunk_ids = np.transpose(ids, (1, 0, 2))
    basis = [dft_rows(chunk_ids[k]).reshape(z.rows, NFFT) for k in range(z.chunks)]

    calls = [c for c in ([0], [1], [2, 3]) if c[-1] < z.chunks]
    filt = None
    spectra = []
    arrived = []
    for call in calls:
        rows = jnp.asarray(np.concatenate([basis[k] for k in call], axis=0))
        places = loc[call[0] : call[-1] + 1]
        if filt is None:
            filt, spec, send = spectra_call(
                z, scale, me_array, rows, places, voltages=voltages, window=window
            )
        else:
            _, spec, send = spectra_call(z, scale, me_array, rows, places, filt=filt)
        spectra.extend(spec)
        for c in range(len(call)):
            mine = send[c * z.devices : (c + 1) * z.devices]
            got = [mine[0]] + [None] * (z.devices - 1)
            far = z.devices // 2
            for i in range(far):
                for k in (far + i, i):
                    if k > 0:
                        got[k] = swap(z, mine[k], k)
            arrived.append(got)

    chan_float = jnp.arange(CHANNELS, dtype=jnp.int32).astype(jnp.float32)
    phase = 2.0 * jnp.pi / NFFT * (delays[:, None, :] * chan_float[None, :, None])
    cos_w = jnp.cos(phase).astype(jnp.bfloat16)
    sin_w = jnp.sin(phase).astype(jnp.bfloat16)
    beams = beam_call(z, me_array, spectra, cos_w, sin_w)
    bit = 1
    while beams.shape[0] > 1:
        half = beams.shape[0] // 2
        beams = beams[:half] + swap(z, beams[half:], bit)
        bit *= 2
    beams = beams.reshape(z.chan_dev, 2 * BEAMS * FR)

    vis = None
    for k in range(z.chunks):
        vis = receive_call(z, k, arrived[k], take_key[k], vis)
    return (vis, beams)


def solution(mesh):
    in_specs = (P(("grp", "chan"), None), P(None, ("grp", "chan")), P())
    out_specs = (P(("grp", "chan"), None, None, None), P(("grp", "chan"), None))
    return jax.shard_map(
        on_device, mesh=mesh, in_specs=in_specs, out_specs=out_specs, check_vma=False
    )
```

time: 287 us -> 303 us (1.056)
  starting transfers between devices: 30.1 us -> 103 us
  waiting for transfers between devices: 68.8 us -> 42.4 us
  Pallas kernels: 153 us -> 133 us
  between operations: 14.2 us -> 1.7 us
  other arithmetic: 8.21 us -> 13.7 us
  local copies, waits for them, and re-layouts: 8.36 us -> 4.24 us
    ppermute x0 -> x64, starting transfers between devices: none -> 103 us  [swap(): return lax.ppermute(x, 'chan', [(i, i ^ offset) for i in range(z.devices)])]
    ppermute x0 -> x64, waiting for transfers between devices: none -> 42.4 us  [swap(): return lax.ppermute(x, 'chan', [(i, i ^ offset) for i in range(z.devices)])]
    all_to_all x4 -> x0, waiting for transfers between devices: 42.1 us -> none  [on_device(): lax.all_to_all(send, 'chan', split_axis=0, concat_axis=0, tiled=True)]
    all_to_all x4 -> x0, starting transfers between devices: 29.9 us -> none  [on_device(): lax.all_to_all(send, 'chan', split_axis=0, concat_axis=0, tiled=True)]
    reduce_scatter x1 -> x0, waiting for transfers between devices: 26.7 us -> none  [on_device(): lax.psum_scatter(partial_beams, 'chan', scatter_dimension=0, tiled=True)]
    pallas_call x5 -> x4, Pallas kernels: 124 us -> 106 us  [the longest x1 49.6 us: beam_call(): pl.pallas_call(functools.partial(beam_kernel, z), grid_spec=grid_spec, ou...]
    another operation x4 -> x0, local copies, waits for them, and re-layouts: 5.28 us -> none  [the longest x2 2.65 us: on_device(): jnp.tile(jnp.cos(phase).astype(jnp.bfloat16), (1, 1, 1, z.lane_frames))]
    convert_element_type x1 -> x2, other arithmetic: 4.92 us -> 8.93 us  [the longest x1 8.92 us: on_device(): sin_w = jnp.sin(phase).astype(jnp.bfloat16)]
  transfers between devices with their start and end apart: 5 -> 64, of which waited for: 4 -> 13; matrix products, arithmetic and copies ran while one was open for 4% -> 4% of each run, Pallas kernels for 45% -> 37%
where the time goes in v1:
time: 303 us; the launch traced here: 298 us
  Pallas kernels  133 us (44%)
  starting transfers between devices  103 us (34%)
  waiting for transfers between devices  42.4 us (14%)
  other arithmetic  13.7 us (5%)
  local copies, waits for them, and re-layouts  4.24 us (1%)
    ppermute x64, starting transfers between devices, swap(): return lax.ppermute(x, 'chan', [(i, i ^ offset) for i in range(z.devices)])  103 us
    pallas_call x1, Pallas kernels, beam_call(): pl.pallas_call(functools.partial(beam_kernel, z), grid_spec=grid_spec, ou...  49.6 us
    ppermute x64, waiting for transfers between devices, swap(): return lax.ppermute(x, 'chan', [(i, i ^ offset) for i in range(z.devices)])  42.4 us
    pallas_call x2, Pallas kernels, spectra_call(): pl.pallas_call(functools.partial(next_kernel, z, scale, count), in_specs=...  34.3 us
    pallas_call x4, Pallas kernels, receive_call(): pl.pallas_call(functools.partial(receive_kernel, z, step_ch), grid=(steps...  26.9 us
    pallas_call x1, Pallas kernels, spectra_call(): pl.pallas_call(functools.partial(first_kernel, z, scale), in_specs=[me_sp...  22.2 us
    convert_element_type x1, other arithmetic, on_device(): sin_w = jnp.sin(phase).astype(jnp.bfloat16)  8.92 us
  transfers between devices with their start and end apart: 64, of which 13 were waited for; matrix products, arithmetic and copies ran while one was open for 4% of the time, Pallas kernels for 37%

profile of v1, /device:TPU:5, one launch (start us, length us, event | category | flops | bytes accessed | tf_op | source)
XLA Modules:
  0.0 297.8 jit_solution(5963500451938631609)
XLA Ops:
  4.2 22.2 %filter_spectra.1 = (bf16[3072,2048]{1,0:T(8,128)(2,1)}, bf16[512,3072]{1,0:T(8,128)(2,1)}, bf16[12,32,128]{2,1,0:T(8,128)(2,1)}, bf16[12,32,128]{2,1,0:T(8,128)...) custom-call(s32[1]{0:T(128)} %bitcast.me_ref, ...), custom_call_target="tpu_custom_call" | custom-call | flops 6442450944 | bytes 20000000 | tf_op jit(solution)/shard_map/filter_spectra/pallas_call | solution.py:167
  31.3 13.0 %spectra_next.3 = (bf16[512,3072]{1,0:T(8,128)(2,1)}, bf16[12,32,128]{2,1,0:T(8,128)(2,1)}, bf16[12,32,128]{2,1,0:T(8,128)(2,1)}, bf16[12,32,128]{2,1,0:T(8,128)...) custom-call(s32[1]{0:T(128)} %bitcast.me_ref, ...), custom_call_target="tpu_custom_call" | custom-call | flops 6442450944 | bytes 20000000 | tf_op jit(solution)/shard_map/spectra_next/pallas_call | solution.py:154
  44.3 21.3 %spectra_next.2 = (bf16[512,3072]{1,0:T(8,128)(2,1)}, bf16[512,3072]{1,0:T(8,128)(2,1)}, bf16[12,32,128]{2,1,0:T(8,128)(2,1)}, bf16[12,32,128]{2,1,0:T(8,128)(2,...) custom-call(s32[1]{0:T(128)} %bitcast.me_ref, ...), custom_call_target="tpu_custom_call" | custom-call | flops 12884901888 | bytes 20000000 | tf_op jit(solution)/shard_map/spectra_next/pallas_call | solution.py:154
  68.4 8.9 %sine_convert_fusion = (bf16[4,1024,64]{2,1,0:T(8,128)(2,1)}, bf16[4,1024,64]{2,1,0:T(8,128)(2,1)}) fusion(f32[1024]{0:T(1024)S(1)} %iota_convert_fusion, f32[4,64]{1,0:T(4,128)S(1)} %copy-done.61), kind=kLoop, calls=%fused_computation.1 | loop fusion | flops 1048576 | bytes 1053696 | tf_op jit(solution)/shard_map/convert_element_type | solution.py:408
  86.8 49.6 %beam_sums.1 = f32[16,64,384]{2,1,0:T(8,128)} custom-call(s32[1]{0:T(128)} %bitcast.me_ref, bf16[512,3072]{1,0:T(8,128)(2,1)} %get-tuple-element.136.refs_0_, bf16[512,3072]{1,0:T(8,128)(2,1)} %get-tuple-element.137.refs_1_, bf16[512,3072]{1,0:T(8,128)(2,1)} %get-tuple-element.138.refs_2_, bf16[512,3072]{1,0:T(8,128)(2,1)} %get-tuple-element.139.refs_3_, ...), custom_call_target="tpu_custom_call" | custom-call | flops 20000000000 | bytes 20000000 | tf_op jit(solution)/shard_map/beam_sums/pallas_call | solution.py:326
  138.3 3.3 %collective-permute-start.58 = (bf16[12,32,128]{2,1,0:T(8,128)(2,1)}, bf16[12,32,128]{2,1,0:T(8,128)(2,1)S(1)}, u32[]{:S(2)}, u32[]{:S(2)}) collective-permute-start(bf16[12,32,128]{2,1,0:T(8,128)(2,1)} %get-tuple-element.134), channel_id=1, source_target_pairs={{0,14},{1,15},{2,12},{3,13},{4,10},{5,11},{6,8},{7,9},{8,6},{9,7},... | collective-permute-start | bytes 294920 | tf_op jit(solution)/shard_map/ppermute | solution.py:339
  147.0 3.8 %collective-permute-start.33 = (bf16[12,32,128]{2,1,0:T(8,128)(2,1)}, bf16[12,32,128]{2,1,0:T(8,128)(2,1)S(1)}, u32[]{:S(2)}, u32[]{:S(2)}) collective-permute-start(bf16[12,32,128]{2,1,0:T(8,128)(2,1)} %get-tuple-element.108), channel_id=1, source_target_pairs={{0,4},{1,5},{2,6},{3,7},{4,0},{5,1},{6,2},{7,3},{8,12},{9,13},{10,... | collective-permute-start | bytes 294920 | tf_op jit(solution)/shard_map/ppermute | solution.py:339
  166.2 8.2 %collective-permute-done.38.refs_9_ = bf16[12,32,128]{2,1,0:T(8,128)(2,1)S(1)} collective-permute-done((bf16[12,32,128]{2,1,0:T(8,128)(2,1)}, bf16[12,32,128]{2,1,0:T(8,128)(2,1)S(1)}, u32[]{:S(2)}, u32[]{:S(2)}) %collective-permute-start.38) | collective-permute-done | bytes 98336 | tf_op jit(solution)/shard_map/ppermute | solution.py:339
  177.7 6.1 %collective-permute-done.40.refs_11_ = bf16[12,32,128]{2,1,0:T(8,128)(2,1)S(1)} collective-permute-done((bf16[12,32,128]{2,1,0:T(8,128)(2,1)}, bf16[12,32,128]{2,1,0:T(8,128)(2,1)S(1)}, u32[]{:S(2)}, u32[]{:S(2)}) %collective-permute-start.40) | collective-permute-done | bytes 98336 | tf_op jit(solution)/shard_map/ppermute | solution.py:339
  187.7 3.3 %collective-permute-done.44.refs_15_ = bf16[12,32,128]{2,1,0:T(8,128)(2,1)S(1)} collective-permute-done((bf16[12,32,128]{2,1,0:T(8,128)(2,1)}, bf16[12,32,128]{2,1,0:T(8,128)(2,1)S(1)}, u32[]{:S(2)}, u32[]{:S(2)}) %collective-permute-start.44) | collective-permute-done | bytes 98336 | tf_op jit(solution)/shard_map/ppermute | solution.py:339
  190.9 4.2 %collective-permute-start.3 = (bf16[12,32,128]{2,1,0:T(8,128)(2,1)}, bf16[12,32,128]{2,1,0:T(8,128)(2,1)S(1)}, u32[]{:S(2)}, u32[]{:S(2)}) collective-permute-start(bf16[12,32,128]{2,1,0:T(8,128)(2,1)} %get-tuple-element.76), channel_id=1, source_target_pairs={{0,4},{1,5},{2,6},{3,7},{4,0},{5,1},{6,2},{7,3},{8,12},{9,13},{10,... | collective-permute-start | bytes 294920 | tf_op jit(solution)/shard_map/ppermute | solution.py:339
  206.3 6.8 %correlate.4.refs_17_ = f32[64,2,256,256]{3,2,1,0:T(8,128)} custom-call(bf16[12,32,128]{2,1,0:T(8,128)(2,1)} %get-tuple-element.120.refs_0_, bf16[12,32,128]{2,1,0:T(8,128)(2,1)} %copy-done.1, bf16[12,32,128]{2,1,0:T(8,128)(2,1)} %copy-done.2, bf16[12,32,128]{2,1,0:T(8,128)(2,1)} %copy-done.3, bf16[12,32,128]{2,1,0:T(8,128)(2,1)} %copy-done.4, ...), custom_call_target="tpu_custom_call" | custom-call | flops 4000000000 | bytes 10000000 | tf_op jit(solution)/shard_map/correlate/pallas_call | solution.py:247
  218.9 6.8 %correlate.5.refs_17_ = f32[64,2,256,256]{3,2,1,0:T(8,128)} custom-call(bf16[12,32,128]{2,1,0:T(8,128)(2,1)} %get-tuple-element.104.refs_0_, bf16[12,32,128]{2,1,0:T(8,128)(2,1)} %copy-done.19, bf16[12,32,128]{2,1,0:T(8,128)(2,1)} %copy-done.20, bf16[12,32,128]{2,1,0:T(8,128)(2,1)} %copy-done.22, ...), custom_call_target="tpu_custom_call", output_to_operand_aliasing={{}: (17, {})} | custom-call | flops 4000000000 | bytes 10000000 | tf_op jit(solution)/shard_map/correlate/pallas_call | solution.py:247
  225.8 3.5 %collective-permute-start.25 = (bf16[12,32,128]{2,1,0:T(8,128)(2,1)S(1)}, bf16[12,32,128]{2,1,0:T(8,128)(2,1)S(1)}, u32[]{:S(2)}, u32[]{:S(2)}) collective-permute-start(bf16[12,32,128]{2,1,0:T(8,128)(2,1)S(1)} %copy-done.75), channel_id=1, source_target_pairs={{0,11},{1,10},{2,9},{3,8},{4,15},{5,14},{6,13},{7,12},{8,3},{9,2},... | collective-permute-start | bytes 294920 | tf_op jit(solution)/shard_map/ppermute | solution.py:339
  233.0 5.8 %collective-permute-done.24.refs_10_ = bf16[12,32,128]{2,1,0:T(8,128)(2,1)S(1)} collective-permute-done((bf16[12,32,128]{2,1,0:T(8,128)(2,1)S(1)}, bf16[12,32,128]{2,1,0:T(8,128)(2,1)S(1)}, u32[]{:S(2)}, u32[]{:S(2)}) %collective-permute-start.24) | collective-permute-done | bytes 98336 | tf_op jit(solution)/shard_map/ppermute | solution.py:339
  238.9 4.8 %collective-permute-start.29 = (bf16[12,32,128]{2,1,0:T(8,128)(2,1)S(1)}, bf16[12,32,128]{2,1,0:T(8,128)(2,1)S(1)}, u32[]{:S(2)}, u32[]{:S(2)}) collective-permute-start(bf16[12,32,128]{2,1,0:T(8,128)(2,1)S(1)} %copy-done.71), channel_id=1, source_target_pairs={{0,15},{1,14},{2,13},{3,12},{4,11},{5,10},{6,9},{7,8},{8,7},{9,6},... | collective-permute-start | bytes 294920 | tf_op jit(solution)/shard_map/ppermute | solution.py:339
  247.2 5.8 %collective-permute-start.9 = (bf16[12,32,128]{2,1,0:T(8,128)(2,1)S(1)}, bf16[12,32,128]{2,1,0:T(8,128)(2,1)S(1)}, u32[]{:S(2)}, u32[]{:S(2)}) collective-permute-start(bf16[12,32,128]{2,1,0:T(8,128)(2,1)S(1)} %copy-done.67), channel_id=1, source_target_pairs={{0,10},{1,11},{2,8},{3,9},{4,14},{5,15},{6,12},{7,13},{8,2},{9,3},... | collective-permute-start | bytes 294920 | tf_op jit(solution)/shard_map/ppermute | solution.py:339
  252.9 5.1 %collective-permute-start.62 = (f32[2,64,384]{2,1,0:T(8,128)S(1)}, f32[2,64,384]{2,1,0:T(8,128)S(1)}, u32[]{:S(2)}, u32[]{:S(2)}) collective-permute-start(f32[2,64,384]{2,1,0:T(8,128)S(1)} %slice.88), channel_id=1, source_target_pairs={{0,4},{1,5},{2,6},{3,7},{4,0},{5,1},{6,2},{7,3},{8,12},{9,13},{10,... | collective-permute-start | bytes 589832 | tf_op jit(solution)/shard_map/ppermute | solution.py:339
  258.2 6.7 %correlate.6.refs_17_ = f32[64,2,256,256]{3,2,1,0:T(8,128)} custom-call(bf16[12,32,128]{2,1,0:T(8,128)(2,1)} %get-tuple-element.88.refs_0_, bf16[12,32,128]{2,1,0:T(8,128)(2,1)} %copy-done.33, bf16[12,32,128]{2,1,0:T(8,128)(2,1)} %copy-done.35, bf16[12,32,128]{2,1,0:T(8,128)(2,1)} %copy-done.38, ...), custom_call_target="tpu_custom_call", output_to_operand_aliasing={{}: (17, {})} | custom-call | flops 4000000000 | bytes 10000000 | tf_op jit(solution)/shard_map/correlate/pallas_call | solution.py:247
  267.4 3.3 %collective-permute-start.11 = (bf16[12,32,128]{2,1,0:T(8,128)(2,1)S(1)}, bf16[12,32,128]{2,1,0:T(8,128)(2,1)S(1)}, u32[]{:S(2)}, u32[]{:S(2)}) collective-permute-start(bf16[12,32,128]{2,1,0:T(8,128)(2,1)S(1)} %copy-done.65), channel_id=1, source_target_pairs={{0,12},{1,13},{2,14},{3,15},{4,8},{5,9},{6,10},{7,11},{8,4},{9,5},... | collective-permute-start | bytes 294920 | tf_op jit(solution)/shard_map/ppermute | solution.py:339
  272.6 3.8 %collective-permute-start.14 = (bf16[12,32,128]{2,1,0:T(8,128)(2,1)S(1)}, bf16[12,32,128]{2,1,0:T(8,128)(2,1)S(1)}, u32[]{:S(2)}, u32[]{:S(2)}) collective-permute-start(bf16[12,32,128]{2,1,0:T(8,128)(2,1)S(1)} %copy-done.62), channel_id=1, source_target_pairs={{0,15},{1,14},{2,13},{3,12},{4,11},{5,10},{6,9},{7,8},{8,7},{9,6},... | collective-permute-start | bytes 294920 | tf_op jit(solution)/shard_map/ppermute | solution.py:339
  276.5 6.2 %collective-permute-done.10.refs_11_ = bf16[12,32,128]{2,1,0:T(8,128)(2,1)S(1)} collective-permute-done((bf16[12,32,128]{2,1,0:T(8,128)(2,1)S(1)}, bf16[12,32,128]{2,1,0:T(8,128)(2,1)S(1)}, u32[]{:S(2)}, u32[]{:S(2)}) %collective-permute-start.10) | collective-permute-done | bytes 98336 | tf_op jit(solution)/shard_map/ppermute | solution.py:339
  284.5 6.6 %correlate.7 = f32[64,2,256,256]{3,2,1,0:T(8,128)} custom-call(bf16[12,32,128]{2,1,0:T(8,128)(2,1)} %get-tuple-element.72.refs_0_, bf16[12,32,128]{2,1,0:T(8,128)(2,1)} %copy-done.8, bf16[12,32,128]{2,1,0:T(8,128)(2,1)} %copy-done.10, bf16[12,32,128]{2,1,0:T(8,128)(2,1)} %copy-done.12, ...), custom_call_target="tpu_custom_call", output_to_operand_aliasing={{}: (17, {})} | custom-call | flops 4000000000 | bytes 10000000 | tf_op jit(solution)/shard_map/correlate/pallas_call | solution.py:247
  291.1 6.0 %collective-permute-done.63 = f32[1,64,384]{2,1,0:T(8,128)S(1)} collective-permute-done((f32[1,64,384]{2,1,0:T(8,128)S(1)}, f32[1,64,384]{2,1,0:T(8,128)S(1)}, u32[]{:S(2)}, u32[]{:S(2)}) %collective-permute-start.63) | collective-permute-done | bytes 98336 | tf_op jit(solution)/shard_map/ppermute | solution.py:339
  (315 shorter events, 80.8 us)
Async XLA Ops:
  26.4 39.2 %collective-permute-start.45 = (bf16[12,32,128]{2,1,0:T(8,128)(2,1)}, bf16[12,32,128]{2,1,0:T(8,128)(2,1)S(1)}, u32[]{:S(2)}, u32[]{:S(2)}) collective-permute-start(bf16[12,32,128]{2,1,0:T(8,128)(2,1)} %get-tuple-element.121), channel_id=1, source_target_pairs={{0,1},{1,0},{2,3},{3,2},{4,5},{5,4},{6,7},{7,6},{8,9},{9,8},{10,11... | collective-permute-start | bytes 294920 | tf_op jit(solution)/shard_map/ppermute | solution.py:339
  27.1 39.8 %collective-permute-start.46 = (bf16[12,32,128]{2,1,0:T(8,128)(2,1)}, bf16[12,32,128]{2,1,0:T(8,128)(2,1)S(1)}, u32[]{:S(2)}, u32[]{:S(2)}) collective-permute-start(bf16[12,32,128]{2,1,0:T(8,128)(2,1)} %get-tuple-element.122), channel_id=1, source_target_pairs={{0,2},{1,3},{2,0},{3,1},{4,6},{5,7},{6,4},{7,5},{8,10},{9,11},{10,... | collective-permute-start | bytes 294920 | tf_op jit(solution)/shard_map/ppermute | solution.py:339
  27.2 50.1 %collective-permute-start.47 = (bf16[12,32,128]{2,1,0:T(8,128)(2,1)}, bf16[12,32,128]{2,1,0:T(8,128)(2,1)S(1)}, u32[]{:S(2)}, u32[]{:S(2)}) collective-permute-start(bf16[12,32,128]{2,1,0:T(8,128)(2,1)} %get-tuple-element.123), channel_id=1, source_target_pairs={{0,3},{1,2},{2,1},{3,0},{4,7},{5,6},{6,5},{7,4},{8,11},{9,10},{10,... | collective-permute-start | bytes 294920 | tf_op jit(solution)/shard_map/ppermute | solution.py:339
  28.9 50.8 %collective-permute-start.48 = (bf16[12,32,128]{2,1,0:T(8,128)(2,1)}, bf16[12,32,128]{2,1,0:T(8,128)(2,1)S(1)}, u32[]{:S(2)}, u32[]{:S(2)}) collective-permute-start(bf16[12,32,128]{2,1,0:T(8,128)(2,1)} %get-tuple-element.124), channel_id=1, source_target_pairs={{0,4},{1,5},{2,6},{3,7},{4,0},{5,1},{6,2},{7,3},{8,12},{9,13},{10,... | collective-permute-start | bytes 294920 | tf_op jit(solution)/shard_map/ppermute | solution.py:339
  30.2 49.9 %collective-permute-start.49 = (bf16[12,32,128]{2,1,0:T(8,128)(2,1)}, bf16[12,32,128]{2,1,0:T(8,128)(2,1)S(1)}, u32[]{:S(2)}, u32[]{:S(2)}) collective-permute-start(bf16[12,32,128]{2,1,0:T(8,128)(2,1)} %get-tuple-element.125), channel_id=1, source_target_pairs={{0,5},{1,4},{2,7},{3,6},{4,1},{5,0},{6,3},{7,2},{8,13},{9,12},{10,... | collective-permute-start | bytes 294920 | tf_op jit(solution)/shard_map/ppermute | solution.py:339
  77.3 60.6 %collective-permute-start.52 = (bf16[12,32,128]{2,1,0:T(8,128)(2,1)}, bf16[12,32,128]{2,1,0:T(8,128)(2,1)S(1)}, u32[]{:S(2)}, u32[]{:S(2)}) collective-permute-start(bf16[12,32,128]{2,1,0:T(8,128)(2,1)} %get-tuple-element.128), channel_id=1, source_target_pairs={{0,8},{1,9},{2,10},{3,11},{4,12},{5,13},{6,14},{7,15},{8,0},{9,1},... | collective-permute-start | bytes 294920 | tf_op jit(solution)/shard_map/ppermute | solution.py:339
  79.6 58.6 %collective-permute-start.53 = (bf16[12,32,128]{2,1,0:T(8,128)(2,1)}, bf16[12,32,128]{2,1,0:T(8,128)(2,1)S(1)}, u32[]{:S(2)}, u32[]{:S(2)}) collective-permute-start(bf16[12,32,128]{2,1,0:T(8,128)(2,1)} %get-tuple-element.129), channel_id=1, source_target_pairs={{0,9},{1,8},{2,11},{3,10},{4,13},{5,12},{6,15},{7,14},{8,1},{9,0},... | collective-permute-start | bytes 294920 | tf_op jit(solution)/shard_map/ppermute | solution.py:339
  80.0 61.5 %collective-permute-start.54 = (bf16[12,32,128]{2,1,0:T(8,128)(2,1)}, bf16[12,32,128]{2,1,0:T(8,128)(2,1)S(1)}, u32[]{:S(2)}, u32[]{:S(2)}) collective-permute-start(bf16[12,32,128]{2,1,0:T(8,128)(2,1)} %get-tuple-element.130), channel_id=1, source_target_pairs={{0,10},{1,11},{2,8},{3,9},{4,14},{5,15},{6,12},{7,13},{8,2},{9,3},... | collective-permute-start | bytes 294920 | tf_op jit(solution)/shard_map/ppermute | solution.py:339
  82.3 60.6 %collective-permute-start.55 = (bf16[12,32,128]{2,1,0:T(8,128)(2,1)}, bf16[12,32,128]{2,1,0:T(8,128)(2,1)S(1)}, u32[]{:S(2)}, u32[]{:S(2)}) collective-permute-start(bf16[12,32,128]{2,1,0:T(8,128)(2,1)} %get-tuple-element.131), channel_id=1, source_target_pairs={{0,11},{1,10},{2,9},{3,8},{4,15},{5,14},{6,13},{7,12},{8,3},{9,2},... | collective-permute-start | bytes 294920 | tf_op jit(solution)/shard_map/ppermute | solution.py:339
  83.6 59.3 %collective-permute-start.56 = (bf16[12,32,128]{2,1,0:T(8,128)(2,1)}, bf16[12,32,128]{2,1,0:T(8,128)(2,1)S(1)}, u32[]{:S(2)}, u32[]{:S(2)}) collective-permute-start(bf16[12,32,128]{2,1,0:T(8,128)(2,1)} %get-tuple-element.132), channel_id=1, source_target_pairs={{0,12},{1,13},{2,14},{3,15},{4,8},{5,9},{6,10},{7,11},{8,4},{9,5},... | collective-permute-start | bytes 294920 | tf_op jit(solution)/shard_map/ppermute | solution.py:339
  154.2 44.2 %collective-permute-start.60 = (f32[8,64,384]{2,1,0:T(8,128)S(1)}, f32[8,64,384]{2,1,0:T(8,128)S(1)}, u32[]{:S(2)}, u32[]{:S(2)}) collective-permute-start(f32[8,64,384]{2,1,0:T(8,128)S(1)} %slice.84), channel_id=1, source_target_pairs={{0,1},{1,0},{2,3},{3,2},{4,5},{5,4},{6,7},{7,6},{8,9},{9,8},{10,11... | collective-permute-start | bytes 2359304 | tf_op jit(solution)/shard_map/ppermute | solution.py:339
  156.6 17.9 %collective-permute-start.38 = (bf16[12,32,128]{2,1,0:T(8,128)(2,1)}, bf16[12,32,128]{2,1,0:T(8,128)(2,1)S(1)}, u32[]{:S(2)}, u32[]{:S(2)}) collective-permute-start(bf16[12,32,128]{2,1,0:T(8,128)(2,1)} %get-tuple-element.113), channel_id=1, source_target_pairs={{0,9},{1,8},{2,11},{3,10},{4,13},{5,12},{6,15},{7,14},{8,1},{9,0},... | collective-permute-start | bytes 294920 | tf_op jit(solution)/shard_map/ppermute | solution.py:339
  159.7 16.8 %collective-permute-start.39 = (bf16[12,32,128]{2,1,0:T(8,128)(2,1)}, bf16[12,32,128]{2,1,0:T(8,128)(2,1)S(1)}, u32[]{:S(2)}, u32[]{:S(2)}) collective-permute-start(bf16[12,32,128]{2,1,0:T(8,128)(2,1)} %get-tuple-element.114), channel_id=1, source_target_pairs={{0,10},{1,11},{2,8},{3,9},{4,14},{5,15},{6,12},{7,13},{8,2},{9,3},... | collective-permute-start | bytes 294920 | tf_op jit(solution)/shard_map/ppermute | solution.py:339
  163.9 20.0 %collective-permute-start.40 = (bf16[12,32,128]{2,1,0:T(8,128)(2,1)}, bf16[12,32,128]{2,1,0:T(8,128)(2,1)S(1)}, u32[]{:S(2)}, u32[]{:S(2)}) collective-permute-start(bf16[12,32,128]{2,1,0:T(8,128)(2,1)} %get-tuple-element.115), channel_id=1, source_target_pairs={{0,11},{1,10},{2,9},{3,8},{4,15},{5,14},{6,13},{7,12},{8,3},{9,2},... | collective-permute-start | bytes 294920 | tf_op jit(solution)/shard_map/ppermute | solution.py:339
  164.5 19.4 %collective-permute-start.41 = (bf16[12,32,128]{2,1,0:T(8,128)(2,1)}, bf16[12,32,128]{2,1,0:T(8,128)(2,1)S(1)}, u32[]{:S(2)}, u32[]{:S(2)}) collective-permute-start(bf16[12,32,128]{2,1,0:T(8,128)(2,1)} %get-tuple-element.116), channel_id=1, source_target_pairs={{0,12},{1,13},{2,14},{3,15},{4,8},{5,9},{6,10},{7,11},{8,4},{9,5},... | collective-permute-start | bytes 294920 | tf_op jit(solution)/shard_map/ppermute | solution.py:339
  205.8 33.1 %collective-permute-start.61 = (f32[4,64,384]{2,1,0:T(8,128)S(1)}, f32[4,64,384]{2,1,0:T(8,128)S(1)}, u32[]{:S(2)}, u32[]{:S(2)}) collective-permute-start(f32[4,64,384]{2,1,0:T(8,128)S(1)} %slice.86), channel_id=1, source_target_pairs={{0,2},{1,3},{2,0},{3,1},{4,6},{5,7},{6,4},{7,5},{8,10},{9,11},{10,... | collective-permute-start | bytes 1179656 | tf_op jit(solution)/shard_map/ppermute | solution.py:339
  218.7 20.1 %collective-permute-start.24 = (bf16[12,32,128]{2,1,0:T(8,128)(2,1)S(1)}, bf16[12,32,128]{2,1,0:T(8,128)(2,1)S(1)}, u32[]{:S(2)}, u32[]{:S(2)}) collective-permute-start(bf16[12,32,128]{2,1,0:T(8,128)(2,1)S(1)} %copy-done.76), channel_id=1, source_target_pairs={{0,10},{1,11},{2,8},{3,9},{4,14},{5,15},{6,12},{7,13},{8,2},{9,3},... | collective-permute-start | bytes 294920 | tf_op jit(solution)/shard_map/ppermute | solution.py:339
  225.8 18.0 %collective-permute-start.25 = (bf16[12,32,128]{2,1,0:T(8,128)(2,1)S(1)}, bf16[12,32,128]{2,1,0:T(8,128)(2,1)S(1)}, u32[]{:S(2)}, u32[]{:S(2)}) collective-permute-start(bf16[12,32,128]{2,1,0:T(8,128)(2,1)S(1)} %copy-done.75), channel_id=1, source_target_pairs={{0,11},{1,10},{2,9},{3,8},{4,15},{5,14},{6,13},{7,12},{8,3},{9,2},... | collective-permute-start | bytes 294920 | tf_op jit(solution)/shard_map/ppermute | solution.py:339
  243.8 21.2 %collective-permute-start.6 = (bf16[12,32,128]{2,1,0:T(8,128)(2,1)S(1)}, bf16[12,32,128]{2,1,0:T(8,128)(2,1)S(1)}, u32[]{:S(2)}, u32[]{:S(2)}) collective-permute-start(bf16[12,32,128]{2,1,0:T(8,128)(2,1)S(1)} %copy-done.70), channel_id=1, source_target_pairs={{0,7},{1,6},{2,5},{3,4},{4,3},{5,2},{6,1},{7,0},{8,15},{9,14},{10,... | collective-permute-start | bytes 294920 | tf_op jit(solution)/shard_map/ppermute | solution.py:339
  243.9 23.5 %collective-permute-start.7 = (bf16[12,32,128]{2,1,0:T(8,128)(2,1)S(1)}, bf16[12,32,128]{2,1,0:T(8,128)(2,1)S(1)}, u32[]{:S(2)}, u32[]{:S(2)}) collective-permute-start(bf16[12,32,128]{2,1,0:T(8,128)(2,1)S(1)} %copy-done.69), channel_id=1, source_target_pairs={{0,8},{1,9},{2,10},{3,11},{4,12},{5,13},{6,14},{7,15},{8,0},{9,1},... | collective-permute-start | bytes 294920 | tf_op jit(solution)/shard_map/ppermute | solution.py:339
  244.8 26.0 %collective-permute-start.8 = (bf16[12,32,128]{2,1,0:T(8,128)(2,1)S(1)}, bf16[12,32,128]{2,1,0:T(8,128)(2,1)S(1)}, u32[]{:S(2)}, u32[]{:S(2)}) collective-permute-start(bf16[12,32,128]{2,1,0:T(8,128)(2,1)S(1)} %copy-done.68), channel_id=1, source_target_pairs={{0,9},{1,8},{2,11},{3,10},{4,13},{5,12},{6,15},{7,14},{8,1},{9,0},... | collective-permute-start | bytes 294920 | tf_op jit(solution)/shard_map/ppermute | solution.py:339
  247.2 24.5 %collective-permute-start.9 = (bf16[12,32,128]{2,1,0:T(8,128)(2,1)S(1)}, bf16[12,32,128]{2,1,0:T(8,128)(2,1)S(1)}, u32[]{:S(2)}, u32[]{:S(2)}) collective-permute-start(bf16[12,32,128]{2,1,0:T(8,128)(2,1)S(1)} %copy-done.67), channel_id=1, source_target_pairs={{0,10},{1,11},{2,8},{3,9},{4,14},{5,15},{6,12},{7,13},{8,2},{9,3},... | collective-permute-start | bytes 294920 | tf_op jit(solution)/shard_map/ppermute | solution.py:339
  252.9 19.6 %collective-permute-start.62 = (f32[2,64,384]{2,1,0:T(8,128)S(1)}, f32[2,64,384]{2,1,0:T(8,128)S(1)}, u32[]{:S(2)}, u32[]{:S(2)}) collective-permute-start(f32[2,64,384]{2,1,0:T(8,128)S(1)} %slice.88), channel_id=1, source_target_pairs={{0,4},{1,5},{2,6},{3,7},{4,0},{5,1},{6,2},{7,3},{8,12},{9,13},{10,... | collective-permute-start | bytes 589832 | tf_op jit(solution)/shard_map/ppermute | solution.py:339
  265.0 17.8 %collective-permute-start.10 = (bf16[12,32,128]{2,1,0:T(8,128)(2,1)S(1)}, bf16[12,32,128]{2,1,0:T(8,128)(2,1)S(1)}, u32[]{:S(2)}, u32[]{:S(2)}) collective-permute-start(bf16[12,32,128]{2,1,0:T(8,128)(2,1)S(1)} %copy-done.66), channel_id=1, source_target_pairs={{0,11},{1,10},{2,9},{3,8},{4,15},{5,14},{6,13},{7,12},{8,3},{9,2},... | collective-permute-start | bytes 294920 | tf_op jit(solution)/shard_map/ppermute | solution.py:339
  (129 other events, 3380.9 us)

commit v2 on v1

v2 whole, which is shorter than its diff:
```python
import functools

import jax
import jax.numpy as jnp
import ml_dtypes
import numpy as np
from jax import lax
from jax.experimental import pallas as pl
from jax.experimental.pallas import tpu as pltpu
from jax.sharding import PartitionSpec as P

F = 1024
CHANNELS = 1024
TAPS = 4
BAND_CH = 16
BEAMS = 4
FR = 48
NFFT = 2048
BANDS = 64
FSUB = 256
LANES = 128
CALLS = ((0,), (1, 2), (3,))
VMEM = 56 * 1024 * 1024

NT = (((1,), (1,)), ((), ()))


def fir_window():
    ids = np.arange(TAPS * NFFT, dtype=np.float64)
    centered = (ids - 0.5 * TAPS * NFFT + 0.5) / NFFT
    hann_part = 0.5 - 0.5 * np.cos(2.0 * np.pi * (ids + 0.5) / (TAPS * NFFT))
    return (np.sinc(centered) * hann_part).reshape(TAPS, NFFT)


def dft_rows(chan_ids):
    m = np.arange(NFFT, dtype=np.int64)
    turns = (chan_ids[..., None].astype(np.int64) * m) % NFFT
    table = 2.0 * np.pi * np.arange(NFFT) / NFFT
    cosine = np.cos(table).astype(np.float32).astype(ml_dtypes.bfloat16)
    sine = (-np.sin(table)).astype(np.float32).astype(ml_dtypes.bfloat16)
    return np.stack([cosine[turns], sine[turns]], axis=1)


class Sizes:
    def __init__(self, devices, feed_dev):
        self.devices = devices
        self.feed_dev = feed_dev
        self.cap = feed_dev // 2
        self.lane_frames = LANES // self.cap
        self.quads = FR // self.lane_frames
        self.width = self.lane_frames * feed_dev
        self.steps = 6 if self.quads % 6 == 0 else self.quads
        self.step_frames = FR // self.steps
        self.step_quads = self.quads // self.steps
        self.step_lanes = self.step_frames * feed_dev
        self.chan_dev = CHANNELS // devices
        self.bands_here = BANDS // devices
        self.chunks = self.chan_dev // BAND_CH
        self.rows_dev = 2 * BAND_CH
        self.rows = devices * self.rows_dev
        self.groups = devices // self.lane_frames


def emit_spectra(z, scale, count, me_ref, spectra, loc_ref, spec_refs, send_ref):
    spectra = spectra * scale
    for c in range(count):
        spec_refs[c][...] = spectra[c * z.rows : (c + 1) * z.rows].astype(jnp.bfloat16)
    lane = lax.broadcasted_iota(jnp.int32, (z.rows_dev, LANES), 1)
    frame = (lane // z.cap) ^ (me_ref[0] % z.lane_frames)
    start = frame * z.cap
    for c in range(count):
        for owner in range(z.devices):
            loc = loc_ref[c, owner : owner + 1, :]
            index = start + loc % z.cap
            lower = jnp.broadcast_to(loc, index.shape) < z.cap
            row = c * z.rows + owner * z.rows_dev
            for q in range(z.step_quads):
                parts = []
                for side in range(2):
                    left = q * z.width + side * LANES
                    x = spectra[row : row + z.rows_dev, left : left + LANES]
                    parts.append(
                        jnp.take_along_axis(x, index, axis=1, mode="promise_in_bounds")
                    )
                picked = jnp.where(lower, parts[0], parts[1])
                send_ref[owner, c, q] = picked.astype(jnp.bfloat16)


def filter_piece(z, main_ref, halo, win_ref, filt_ref, off):
    lanes = slice(off, off + LANES)
    taps = [win_ref[k : k + 1, lanes] for k in range(TAPS)]
    for f0 in range(0, z.feed_dev, 16):
        frames = []
        for t in range(z.step_frames + TAPS - 1):
            if t < z.step_frames:
                x = main_ref[f0 : f0 + 16, t * NFFT + off : t * NFFT + off + LANES]
            else:
                x = halo[t - z.step_frames][f0 : f0 + 16, lanes]
            frames.append(x.astype(jnp.float32))
        totals = []
        for t in range(z.step_frames):
            total = taps[0] * frames[t]
            for k in range(1, TAPS):
                total = total + taps[k] * frames[t + k]
            totals.append(total)
        if z.cap < 16:
            totals = [
                jnp.concatenate([totals[t][h : h + 8], totals[t + 1][h : h + 8]], axis=0)
                for t in range(0, z.step_frames, 2)
                for h in (0, 8)
            ]
        for i, total in enumerate(totals):
            if z.cap < 16:
                t, half, feed = 2 * (i // 2), i % 2, 0
            else:
                t, half, feed = i, f0 // z.cap, f0 % z.cap
            row = (t // z.lane_frames) * z.width + half * LANES
            row += (t % z.lane_frames) * z.cap + feed
            filt_ref[row : row + 16, lanes] = total.astype(jnp.bfloat16)


def first_kernel(
    z, scale, count, me_ref, main_ref, h0_ref, h1_ref, h2_ref, win_ref, basis_ref, loc_ref,
    filt_ref, *refs,
):
    halo = (h0_ref, h1_ref, h2_ref)
    piece = 512
    spectra = None
    for off in range(0, NFFT, piece):
        for tile in range(off, off + piece, LANES):
            filter_piece(z, main_ref, halo, win_ref, filt_ref, tile)
        part = lax.dot_general(
            basis_ref[:, off : off + piece],
            filt_ref[:, off : off + piece],
            NT,
            preferred_element_type=jnp.float32,
        )
        spectra = part if spectra is None else spectra + part
    emit_spectra(z, scale, count, me_ref, spectra, loc_ref, refs[:-1], refs[-1])


def next_kernel(z, scale, count, me_ref, filt_ref, basis_ref, loc_ref, *refs):
    spectra = lax.dot_general(
        basis_ref[...], filt_ref[...], NT, preferred_element_type=jnp.float32
    )
    emit_spectra(z, scale, count, me_ref, spectra, loc_ref, refs[:-1], refs[-1])


def whole_spec(shape):
    return pl.BlockSpec(shape, lambda *g: (0,) * len(shape))


def spectra_call(z, scale, me, basis, loc, filt=None, voltages=None, window=None):
    count = loc.shape[0]
    filt_rows = z.step_frames * z.feed_dev
    filt_spec = pl.BlockSpec((filt_rows, NFFT), lambda g: (g, 0))
    spec_shape = jax.ShapeDtypeStruct((z.rows, FR * z.feed_dev), jnp.bfloat16)
    spec_spec = pl.BlockSpec((z.rows, z.step_lanes), lambda g: (0, g))
    send_shape = jax.ShapeDtypeStruct(
        (z.devices, count, z.quads, z.rows_dev, LANES), jnp.bfloat16
    )
    send_spec = pl.BlockSpec(
        (z.devices, count, z.step_quads, z.rows_dev, LANES), lambda g: (0, 0, g, 0, 0)
    )
    me_spec = pl.BlockSpec(memory_space=pltpu.SMEM)
    shared = [whole_spec(basis.shape), whole_spec(loc.shape)]
    out_specs = [spec_spec] * count + [send_spec]
    out_shape = [spec_shape] * count + [send_shape]
    flops = 2 * count * z.rows * NFFT * FR * z.feed_dev
    common = dict(
        grid=(z.steps,),
        compiler_params=pltpu.CompilerParams(vmem_limit_bytes=VMEM),
        cost_estimate=pl.CostEstimate(
            flops=flops, bytes_accessed=20_000_000, transcendentals=0
        ),
    )
    if filt is not None:
        outs = pl.pallas_call(
            functools.partial(next_kernel, z, scale, count),
            in_specs=[me_spec, filt_spec] + shared,
            out_specs=out_specs,
            out_shape=out_shape,
            name="spectra_next",
            **common,
        )(me, filt, basis, loc)
        return None, outs[:-1], outs[-1]

    def halo_spec(h):
        return pl.BlockSpec((z.feed_dev, NFFT), lambda g: (0, z.step_frames * (g + 1) + h))

    outs = pl.pallas_call(
        functools.partial(first_kernel, z, scale, count),
        in_specs=[
            me_spec,
            pl.BlockSpec((z.feed_dev, z.step_frames * NFFT), lambda g: (0, g)),
            halo_spec(0),
            halo_spec(1),
            halo_spec(2),
            whole_spec((TAPS, NFFT)),
        ]
        + shared,
        out_specs=[filt_spec] + out_specs,
        out_shape=[jax.ShapeDtypeStruct((FR * z.feed_dev, NFFT), jnp.bfloat16)] + out_shape,
        name="filter_spectra",
        **common,
    )(me, voltages, voltages, voltages, voltages, window, basis, loc)
    return outs[0], outs[1:-1], outs[-1]


def receive_kernel(z, step_ch, arr_ref, key_ref, *refs):
    vis_ref, rows_ref = refs[-2], refs[-1]
    g = pl.program_id(0)
    depth = z.quads * z.rows_dev
    lf = z.lane_frames

    @pl.when(g == 0)
    def _():
        lane_group = lax.broadcasted_iota(jnp.int32, (depth, LANES), 1) // z.cap
        slot = lax.broadcasted_iota(jnp.int32, (z.groups * LANES, FSUB), 0)
        for tau in range(lf):
            tiles = []
            for big in range(z.groups):
                tile = arr_ref[big * lf + tau, 0].reshape(depth, LANES)
                for lane in range(1, lf):
                    block = arr_ref[big * lf + (lane ^ tau), 0].reshape(depth, LANES)
                    tile = jnp.where(lane_group == lane, block, tile)
                tiles.append(tile)
            lhs = jnp.concatenate(tiles, axis=1)
            pick = jnp.where(slot == key_ref[tau : tau + 1, :], 1.0, 0.0).astype(jnp.bfloat16)
            rows = jnp.dot(lhs, pick, preferred_element_type=jnp.float32)
            for half in range(FSUB // LANES):
                rows_ref[half, tau * depth : (tau + 1) * depth, :] = rows[
                    :, half * LANES : (half + 1) * LANES
                ]

    for i in range(step_ch):
        ch = g * step_ch + i
        halves = []
        for part in range(2):
            halves.append(
                jnp.concatenate(
                    [
                        rows_ref[half, pl.ds(ch + part * BAND_CH, FR, stride=z.rows_dev), :]
                        for half in range(FSUB // LANES)
                    ],
                    axis=1,
                )
            )
        real, imag = halves
        right = jnp.concatenate([real, imag], axis=0)
        swapped = jnp.concatenate([imag, -real], axis=0)
        left = jnp.concatenate([right.T, swapped.T], axis=0).astype(jnp.bfloat16)
        both = jnp.dot(left, right.astype(jnp.bfloat16), preferred_element_type=jnp.float32)
        both = both * (1.0 / FR)
        vis_ref[i, 0] = both[:FSUB]
        vis_ref[i, 1] = both[FSUB:]


def receive_call(z, chunk, arrived, at, key, vis):
    step_ch = 4
    steps = BAND_CH // step_ch
    out_shape = jax.ShapeDtypeStruct((z.chan_dev, 2, FSUB, FSUB), jnp.float32)
    block = (z.devices, 1) + arrived.shape[2:]
    in_specs = [pl.BlockSpec(block, lambda g: (0, at, 0, 0, 0)), whole_spec(key.shape)]
    operands = [arrived, key]
    aliases = {}
    if vis is not None:
        in_specs.append(pl.BlockSpec(memory_space=pl.ANY))
        aliases = {len(operands): 0}
        operands.append(vis)
    return pl.pallas_call(
        functools.partial(receive_kernel, z, step_ch),
        grid=(steps,),
        in_specs=in_specs,
        out_specs=pl.BlockSpec(
            (step_ch, 2, FSUB, FSUB), lambda g: (chunk * steps + g, 0, 0, 0)
        ),
        out_shape=out_shape,
        input_output_aliases=aliases,
        scratch_shapes=[
            pltpu.VMEM((FSUB // LANES, FR * z.rows_dev, LANES), jnp.float32)
        ],
        compiler_params=pltpu.CompilerParams(vmem_limit_bytes=VMEM),
        cost_estimate=pl.CostEstimate(
            flops=4_000_000_000, bytes_accessed=10_000_000, transcendentals=0
        ),
        name="correlate",
    )(*operands)


def beam_kernel(z, me_ref, *refs):
    spec_refs = refs[: z.chunks]
    cos_base, sin_base, cos_step, sin_step, sum_ref, out_ref, prod_ref = refs[z.chunks :]
    count = z.chan_dev
    weights = []
    for g in range(BEAMS):
        c0, s0 = cos_base[0, g : g + 1, :], sin_base[0, g : g + 1, :]
        c1, s1 = cos_step[g], sin_step[g]
        weights.append(
            ((c0 * c1 - s0 * s1).astype(jnp.bfloat16), (s0 * c1 + c0 * s1).astype(jnp.bfloat16))
        )
    for q in range(z.quads):
        lanes = slice(q * z.width, (q + 1) * z.width)
        x = [ref[:, lanes] for ref in spec_refs]
        real = jnp.concatenate([v[:BAND_CH] for v in x], axis=0)
        imag = jnp.concatenate([v[BAND_CH:] for v in x], axis=0)
        for g in range(BEAMS):
            c, s = weights[g]
            pair = (c * real + s * imag, c * imag - s * real)
            for part in range(2):
                row = (part * BEAMS + g) * count
                both = pair[part][:, :LANES] + pair[part][:, LANES:]
                prod_ref[row : row + count, q * LANES : (q + 1) * LANES] = both
    sums = jnp.dot(prod_ref[...], sum_ref[...], preferred_element_type=jnp.float32)
    sums = sums * (1.0 / np.sqrt(F))
    for j in range(2 * BEAMS):
        out_ref[0, :, j * FR : (j + 1) * FR] = sums[j * count : (j + 1) * count, :FR]


def beam_call(z, me, spectra, delays):
    bits = z.devices.bit_length() - 1
    lanes = FR * z.feed_dev
    halves = delays.reshape(BEAMS, 2, 1, z.cap)
    spread = jnp.broadcast_to(halves, (BEAMS, 2, z.lane_frames, z.cap)).reshape(BEAMS, z.width)
    unit = 2.0 * jnp.pi / NFFT
    owners = jnp.arange(z.devices, dtype=jnp.int32).astype(jnp.float32) * z.chan_dev
    inner = jnp.arange(z.chan_dev, dtype=jnp.int32).astype(jnp.float32)
    base = unit * (spread[None, :, :] * owners[:, None, None])
    step = unit * (spread[:, None, :] * inner[None, :, None])
    frame = (np.arange(FR * z.cap) // LANES) * z.lane_frames
    frame = frame + (np.arange(FR * z.cap) % LANES) // z.cap
    sums = (frame[:, None] == np.arange(LANES)[None, :]).astype(ml_dtypes.bfloat16)

    def owner(j, me_ref):
        k = 0
        for b in range(bits):
            k = k | (((j >> b) & 1) << (bits - 1 - b))
        return me_ref[0] ^ k

    base_spec = pl.BlockSpec(
        (1, BEAMS, z.width), lambda j, me_ref: (owner(j, me_ref), 0, 0)
    )
    grid_spec = pltpu.PrefetchScalarGridSpec(
        num_scalar_prefetch=1,
        grid=(z.devices,),
        in_specs=[
            pl.BlockSpec((z.rows_dev, lanes), lambda j, me_ref: (owner(j, me_ref), 0))
            for _ in range(z.chunks)
        ]
        + [base_spec, base_spec, whole_spec(step.shape), whole_spec(step.shape)]
        + [whole_spec(sums.shape)],
        out_specs=pl.BlockSpec(
            (1, z.chan_dev, 2 * BEAMS * FR), lambda j, me_ref: (j, 0, 0)
        ),
        scratch_shapes=[pltpu.VMEM((2 * BEAMS * z.chan_dev, FR * z.cap), jnp.bfloat16)],
    )
    return pl.pallas_call(
        functools.partial(beam_kernel, z),
        grid_spec=grid_spec,
        out_shape=jax.ShapeDtypeStruct((z.devices, z.chan_dev, 2 * BEAMS * FR), jnp.float32),
        compiler_params=pltpu.CompilerParams(vmem_limit_bytes=VMEM),
        cost_estimate=pl.CostEstimate(
            flops=20_000_000_000, bytes_accessed=20_000_000, transcendentals=0
        ),
        name="beam_sums",
    )(
        me, *spectra, jnp.cos(base), jnp.sin(base), jnp.cos(step), jnp.sin(step),
        jnp.asarray(sums),
    )


def swap(z, x, offset):
    return lax.ppermute(x, "chan", [(i, i ^ offset) for i in range(z.devices)])


def listed_places(z, me, lists):
    base = me * z.feed_dev
    edges = base + jnp.arange(z.feed_dev + 1, dtype=jnp.int32)
    below = jnp.sum((lists[:, None, :] < edges[None, :, None]).astype(jnp.int32), axis=2)
    rank = below[:, :-1] - below[:, :1]
    rank = jnp.where(below[:, 1:] > below[:, :-1], rank, -1)
    slots = jnp.arange(LANES, dtype=jnp.int32) % z.cap
    local = jnp.arange(z.feed_dev, dtype=jnp.int32)
    return jnp.sum(
        jnp.where(rank[:, None, :] == slots[None, :, None], local[None, None, :], 0), axis=2
    )


def on_device(voltages, delays, band_feeds):
    z = Sizes(lax.axis_size("chan"), voltages.shape[0])
    me = lax.axis_index("chan")
    me_array = me.astype(jnp.int32).reshape(1)
    window = fir_window()
    scale = float(np.sqrt(2.0 / np.sum(window * window)))
    window = jnp.asarray(window.astype(np.float32))
    lists = band_feeds.reshape(z.devices, z.bands_here, FSUB)

    own = lax.dynamic_slice_in_dim(band_feeds, me * z.bands_here, z.bands_here, 0)
    source = own // z.feed_dev
    before = jnp.sum(
        (own[:, None, :] < (source * z.feed_dev)[:, :, None]).astype(jnp.int32), axis=2
    )
    place = jnp.arange(FSUB, dtype=jnp.int32)[None, :] - before
    tau = jnp.arange(z.lane_frames, dtype=jnp.int32)
    big = (source // z.lane_frames) * LANES + place
    group = (source % z.lane_frames)[:, None, :] ^ tau[None, :, None]
    take_key = big[:, None, :] + z.cap * group

    ids = np.arange(CHANNELS).reshape(z.devices, z.chunks, BAND_CH)
    chunk_ids = np.transpose(ids, (1, 0, 2))

    filt = None
    spectra = []
    arrived = []
    for call in CALLS:
        call = [k for k in call if k < z.chunks]
        if not call:
            continue
        basis = np.concatenate([dft_rows(chunk_ids[k]).reshape(z.rows, NFFT) for k in call])
        basis = jnp.asarray(basis)
        places = jnp.stack([listed_places(z, me, lists[:, k]) for k in call])
        if filt is None:
            filt, spec, send = spectra_call(
                z, scale, me_array, basis, places, voltages=voltages, window=window
            )
        else:
            _, spec, send = spectra_call(z, scale, me_array, basis, places, filt=filt)
        spectra.extend(spec)
        got = lax.all_to_all(send, "chan", split_axis=0, concat_axis=0, tiled=True)
        arrived.extend((got, at) for at in range(len(call)))

    beams = beam_call(z, me_array, spectra, delays)
    bit = 1
    while beams.shape[0] > 1:
        half = beams.shape[0] // 2
        beams = beams[:half] + swap(z, beams[half:], bit)
        bit *= 2
    beams = beams.reshape(z.chan_dev, 2 * BEAMS * FR)

    vis = None
    for k in range(z.chunks):
        got, at = arrived[k]
        vis = receive_call(z, k, got, at, take_key[k], vis)
    return (vis, beams)


def solution(mesh):
    in_specs = (P(("grp", "chan"), None), P(None, ("grp", "chan")), P())
    out_specs = (P(("grp", "chan"), None, None, None), P(("grp", "chan"), None))
    return jax.shard_map(
        on_device, mesh=mesh, in_specs=in_specs, out_specs=out_specs, check_vma=False
    )
```

time: 303 us -> 221 us (0.73); the launches traced: 298 us -> 220 us
  starting transfers between devices: 103 us -> 27 us
  Pallas kernels: 133 us -> 95.7 us
  waiting for transfers between devices: 42.4 us -> 78.6 us
    ppermute x64 -> x4, starting transfers between devices: 103 us -> 0.65 us  [swap(): return lax.ppermute(x, 'chan', [(i, i ^ offset) for i in range(z.devices)])]
    all_to_all x0 -> x3, waiting for transfers between devices: none -> 38.2 us  [on_device(): got = lax.all_to_all(send, 'chan', split_axis=0, concat_axis=0, tiled=True)]
    pallas_call x1, Pallas kernels: 49.6 us -> 20.2 us  [beam_call(): pl.pallas_call(functools.partial(beam_kernel, z), grid_spec=grid_spec, ou...]
    all_to_all x0 -> x3, starting transfers between devices: none -> 26.4 us  [on_device(): got = lax.all_to_all(send, 'chan', split_axis=0, concat_axis=0, tiled=True)]
    convert_element_type x2 -> x1, other arithmetic: 8.93 us -> 0.01 us  [beam_call(): inner = jnp.arange(z.chan_dev, dtype=jnp.int32).astype(jnp.float32)]
    pallas_call x1, Pallas kernels: 22.2 us -> 17.8 us  [spectra_call(): pl.pallas_call(functools.partial(first_kernel, z, scale, count), in_specs...]
    reduce_sum x2, other arithmetic: 2.82 us -> 5.85 us  [the longest x1 4.54 us: listed_places(): jnp.sum((lists[:, None, :] < edges[None, :, None]).astype(jnp.int32), axi...]
    ppermute x64 -> x4, waiting for transfers between devices: 42.4 us -> 40.4 us  [swap(): return lax.ppermute(x, 'chan', [(i, i ^ offset) for i in range(z.devices)])]
  transfers between devices with their start and end apart: 64 -> 7, of which waited for: 13 -> 5; matrix products, arithmetic and copies ran while one was open for 4% -> 4% of each run, Pallas kernels for 37% -> 32%
where the time goes in v2:
time: 221 us; the launch traced here: 220 us
  Pallas kernels  95.7 us (43%)
  waiting for transfers between devices  78.6 us (36%)
  starting transfers between devices  27 us (12%)
  other arithmetic  12.8 us (6%)
  local copies, waits for them, and re-layouts  5.3 us (2%)
    ppermute x4, waiting for transfers between devices, swap(): return lax.ppermute(x, 'chan', [(i, i ^ offset) for i in range(z.devices)])  40.4 us
    all_to_all x3, waiting for transfers between devices, on_device(): got = lax.all_to_all(send, 'chan', split_axis=0, concat_axis=0, tiled=True)  38.2 us
    pallas_call x2, Pallas kernels, spectra_call(): pl.pallas_call(functools.partial(next_kernel, z, scale, count), in_specs=...  31.6 us
    all_to_all x3, starting transfers between devices, on_device(): got = lax.all_to_all(send, 'chan', split_axis=0, concat_axis=0, tiled=True)  26.4 us
    pallas_call x4, Pallas kernels, receive_call(): pl.pallas_call(functools.partial(receive_kernel, z, step_ch), grid=(steps...  26.1 us
    pallas_call x1, Pallas kernels, beam_call(): pl.pallas_call(functools.partial(beam_kernel, z), grid_spec=grid_spec, ou...  20.2 us
    pallas_call x1, Pallas kernels, spectra_call(): pl.pallas_call(functools.partial(first_kernel, z, scale, count), in_specs...  17.8 us
    reduce_sum x1, other arithmetic, listed_places(): jnp.sum((lists[:, None, :] < edges[None, :, None]).astype(jnp.int32), axi...  4.54 us
  transfers between devices with their start and end apart: 7, of which 5 were waited for; matrix products, arithmetic and copies ran while one was open for 4% of the time, Pallas kernels for 32%

profile of v2, /device:TPU:5, one launch (start us, length us, event | category | flops | bytes accessed | tf_op | source)
XLA Modules:
  0.0 220.2 jit_solution(5699976935215302726)
XLA Ops:
  0.7 0.9 reshape.48
  1.6 4.5 %convert_reduce_fusion.1 = (s32[16,65]{0,1:T(8,128)S(1)}, s32[16,65]{0,1:T(8,128)S(1)}, s32[16,65]{0,1:T(8,128)S(1)}, s32[16,65]{0,1:T(8,128)S(1)}) fusion(s32[16,256]{1,0:T(8,128)S(1)} %get-tuple-element.44, s32[65]{0:T(128)S(1)} %iota_add_fusion, s32[16,256]{1,0:T(8,128)S(1)} %get-tuple-element.45, s32[16,256]{1,0:T(8,128)S(1)} %get-tuple-element.43, ...), kind=kLoop, calls=%fused_computation.1 | loop fusion | flops 3190720 | bytes 82436 | tf_op jit(solution)/shard_map/reduce_sum | solution.py:379
  6.5 1.3 select_reduce_fusion.1
  7.8 17.8 %filter_spectra.1 = (bf16[3072,2048]{1,0:T(8,128)(2,1)}, bf16[512,3072]{1,0:T(8,128)(2,1)}, bf16[16,1,12,32,128]{4,3,2,1,0:T(8,128)(2,1)}) custom-call(s32[1]{0:T(128)} %bitcast.me_ref, bf16[64,104448]{1,0:T(8,128)(2,1)} %h2_ref.1, bf16[64,104448]{1,0:T(8,128)(2,1)} %h2_ref.1, bf16[64,104448]{1,0:T(8,128)(2,1)} %h2_ref.1, bf16[64,104448]{1,0:T(8,128)(2,1)} %h2_ref.1, ...), custom_call_target="tpu_custom_call" | custom-call | flops 6442450944 | bytes 20000000 | tf_op jit(solution)/shard_map/filter_spectra/pallas_call | solution.py:191
  25.6 6.7 %all-to-all-start.2 = ((bf16[16,1,12,32,128]{4,3,2,1,0:T(8,128)(2,1)}), bf16[16,1,12,32,128]{4,3,2,1,0:T(8,128)(2,1)S(1)}, u32[]{:S(2)}, u32[]{:S(2)}) async-start(bf16[16,1,12,32,128]{4,3,2,1,0:T(8,128)(2,1)} %get-tuple-element.13), calls=%async_computation.2 | async-start | bytes 3145728 | tf_op jit(solution)/shard_map/all_to_all | solution.py:429
  32.9 19.2 %spectra_next.3 = (bf16[512,3072]{1,0:T(8,128)(2,1)}, bf16[512,3072]{1,0:T(8,128)(2,1)}, bf16[16,2,12,32,128]{4,3,2,1,0:T(8,128)(2,1)}) custom-call(s32[1]{0:T(128)} %bitcast.me_ref, bf16[3072,2048]{1,0:T(8,128)(2,1)} %get-tuple-element.10.filt_ref, bf16[1024,2048]{1,0:T(8,128)(2,1)} %constant.91.clone.basis_ref, s32[2,16,128]{2,1,0:T(8,128)} %pad_add_fusion.loc_ref), custom_call_target="tpu_custom_call" | custom-call | flops 12884901888 | bytes 20000000 | tf_op jit(solution)/shard_map/spectra_next/pallas_call | solution.py:178
  52.1 13.5 %all-to-all-done.2.arr_ref = bf16[16,1,12,32,128]{4,3,2,1,0:T(8,128)(2,1)S(1)} async-done(((bf16[16,1,12,32,128]{4,3,2,1,0:T(8,128)(2,1)}), bf16[16,1,12,32,128]{4,3,2,1,0:T(8,128)(2,1)S(1)}, u32[]{:S(2)}, u32[]{:S(2)}) %all-to-all-start.2) | async-done | bytes 1572896 | tf_op jit(solution)/shard_map/all_to_all | solution.py:429
  65.7 1.2 copy-done.1
  66.8 7.8 %all-to-all-start.1 = ((bf16[16,2,12,32,128]{4,3,2,1,0:T(8,128)(2,1)}), bf16[16,2,12,32,128]{4,3,2,1,0:T(8,128)(2,1)S(1)}, u32[]{:S(2)}, u32[]{:S(2)}) async-start(bf16[16,2,12,32,128]{4,3,2,1,0:T(8,128)(2,1)} %get-tuple-element.12), calls=%async_computation.1 | async-start | bytes 6291456 | tf_op jit(solution)/shard_map/all_to_all | solution.py:429
  74.8 1.2 fusion.3
  76.0 1.8 fusion
  77.8 12.4 %spectra_next.2 = (bf16[512,3072]{1,0:T(8,128)(2,1)}, bf16[16,1,12,32,128]{4,3,2,1,0:T(8,128)(2,1)}) custom-call(s32[1]{0:T(128)} %bitcast.me_ref, bf16[3072,2048]{1,0:T(8,128)(2,1)} %get-tuple-element.10.filt_ref, bf16[512,2048]{1,0:T(8,128)(2,1)} %constant.92.clone.basis_ref, s32[1,16,128]{2,1,0:T(8,128)} %bitcast.34), custom_call_target="tpu_custom_call" | custom-call | flops 6442450944 | bytes 20000000 | tf_op jit(solution)/shard_map/spectra_next/pallas_call | solution.py:178
  90.2 20.2 %beam_sums.1 = f32[16,64,384]{2,1,0:T(8,128)} custom-call(s32[1]{0:T(128)} %bitcast.me_ref, bf16[512,3072]{1,0:T(8,128)(2,1)} %get-tuple-element.14.refs_0_, bf16[512,3072]{1,0:T(8,128)(2,1)} %get-tuple-element.15.refs_1_, bf16[512,3072]{1,0:T(8,128)(2,1)} %get-tuple-element.16.refs_2_, bf16[512,3072]{1,0:T(8,128)(2,1)} %get-tuple-element.17.refs_3_, ...), custom_call_target="tpu_custom_call" | custom-call | flops 20000000000 | bytes 20000000 | tf_op jit(solution)/shard_map/beam_sums/pallas_call | solution.py:357
  110.3 2.1 slice.137
  112.8 24.7 %all-to-all-done.1.arr_ref = bf16[16,2,12,32,128]{4,3,2,1,0:T(8,128)(2,1)S(1)} async-done(((bf16[16,2,12,32,128]{4,3,2,1,0:T(8,128)(2,1)}), bf16[16,2,12,32,128]{4,3,2,1,0:T(8,128)(2,1)S(1)}, u32[]{:S(2)}, u32[]{:S(2)}) %all-to-all-start.1) | async-done | bytes 3145760 | tf_op jit(solution)/shard_map/all_to_all | solution.py:429
  137.4 12.0 %all-to-all-start = ((bf16[16,1,12,32,128]{4,3,2,1,0:T(8,128)(2,1)}), bf16[16,1,12,32,128]{4,3,2,1,0:T(8,128)(2,1)}, u32[]{:S(2)}, u32[]{:S(2)}) async-start(bf16[16,1,12,32,128]{4,3,2,1,0:T(8,128)(2,1)} %get-tuple-element.11), calls=%async_computation | async-start | bytes 3145728 | tf_op jit(solution)/shard_map/all_to_all | solution.py:429
  149.4 1.5 slice_add_fusion
  152.2 21.7 %collective-permute-done.1 = f32[4,64,384]{2,1,0:T(8,128)S(1)} collective-permute-done((f32[4,64,384]{2,1,0:T(8,128)S(1)}, f32[4,64,384]{2,1,0:T(8,128)S(1)}, u32[]{:S(2)}, u32[]{:S(2)}) %collective-permute-start.1) | collective-permute-done | bytes 393248 | tf_op jit(solution)/shard_map/ppermute | solution.py:373
  174.0 12.6 %collective-permute-done.2 = f32[2,64,384]{2,1,0:T(8,128)S(1)} collective-permute-done((f32[2,64,384]{2,1,0:T(8,128)S(1)}, f32[2,64,384]{2,1,0:T(8,128)S(1)}, u32[]{:S(2)}, u32[]{:S(2)}) %collective-permute-start.2) | collective-permute-done | bytes 196640 | tf_op jit(solution)/shard_map/ppermute | solution.py:373
  187.4 6.1 %collective-permute-done.3 = f32[1,64,384]{2,1,0:T(8,128)S(1)} collective-permute-done((f32[1,64,384]{2,1,0:T(8,128)S(1)}, f32[1,64,384]{2,1,0:T(8,128)S(1)}, u32[]{:S(2)}, u32[]{:S(2)}) %collective-permute-start.3) | collective-permute-done | bytes 98336 | tf_op jit(solution)/shard_map/ppermute | solution.py:373
  194.1 6.5 %correlate.4.refs_0_ = f32[64,2,256,256]{3,2,1,0:T(8,128)} custom-call(bf16[16,1,12,32,128]{4,3,2,1,0:T(8,128)(2,1)} %copy-done.1, s32[4,256]{1,0:T(4,128)} %get-tuple-element.33.key_ref), custom_call_target="tpu_custom_call" | custom-call | flops 4000000000 | bytes 10000000 | tf_op jit(solution)/shard_map/correlate/pallas_call | solution.py:271
  200.7 6.5 %correlate.5.refs_0_ = f32[64,2,256,256]{3,2,1,0:T(8,128)} custom-call(bf16[16,2,12,32,128]{4,3,2,1,0:T(8,128)(2,1)} %copy-done, s32[4,256]{1,0:T(4,128)} %get-tuple-element.34.key_ref, f32[64,2,256,256]{3,2,1,0:T(8,128)} %correlate.4.refs_0_), custom_call_target="tpu_custom_call", output_to_operand_aliasing={{}: (2, {})} | custom-call | flops 4000000000 | bytes 10000000 | tf_op jit(solution)/shard_map/correlate/pallas_call | solution.py:271
  207.2 6.5 %correlate.6.refs_0_ = f32[64,2,256,256]{3,2,1,0:T(8,128)} custom-call(bf16[16,2,12,32,128]{4,3,2,1,0:T(8,128)(2,1)} %copy-done, s32[4,256]{1,0:T(4,128)} %get-tuple-element.35.key_ref, f32[64,2,256,256]{3,2,1,0:T(8,128)} %correlate.5.refs_0_), custom_call_target="tpu_custom_call", output_to_operand_aliasing={{}: (2, {})} | custom-call | flops 4000000000 | bytes 10000000 | tf_op jit(solution)/shard_map/correlate/pallas_call | solution.py:271
  213.7 6.5 %correlate.7 = f32[64,2,256,256]{3,2,1,0:T(8,128)} custom-call(bf16[16,1,12,32,128]{4,3,2,1,0:T(8,128)(2,1)} %all-to-all-done.arr_ref, s32[4,256]{1,0:T(4,128)} %get-tuple-element.36.key_ref, f32[64,2,256,256]{3,2,1,0:T(8,128)} %correlate.6.refs_0_), custom_call_target="tpu_custom_call", output_to_operand_aliasing={{}: (2, {})} | custom-call | flops 4000000000 | bytes 10000000 | tf_op jit(solution)/shard_map/correlate/pallas_call | solution.py:271
  (45 shorter events, 4.3 us)
Async XLA Ops:
  25.6 40.0 %all-to-all-start.2 = ((bf16[16,1,12,32,128]{4,3,2,1,0:T(8,128)(2,1)}), bf16[16,1,12,32,128]{4,3,2,1,0:T(8,128)(2,1)S(1)}, u32[]{:S(2)}, u32[]{:S(2)}) async-start(bf16[16,1,12,32,128]{4,3,2,1,0:T(8,128)(2,1)} %get-tuple-element.13), calls=%async_computation.2 | async-start | bytes 3145728 | tf_op jit(solution)/shard_map/all_to_all | solution.py:429
  65.7 1.2 copy-start.1
  65.7 8.9 %copy-start.2 = (f32[4,64]{1,0:T(4,128)S(1)}, f32[4,64]{1,0:T(4,128)}, u32[]{:S(2)}) copy-start(f32[4,64]{1,0:T(4,128)} %param.9) | copy-start | bytes 3076
  66.8 70.6 %all-to-all-start.1 = ((bf16[16,2,12,32,128]{4,3,2,1,0:T(8,128)(2,1)}), bf16[16,2,12,32,128]{4,3,2,1,0:T(8,128)(2,1)S(1)}, u32[]{:S(2)}, u32[]{:S(2)}) async-start(bf16[16,2,12,32,128]{4,3,2,1,0:T(8,128)(2,1)} %get-tuple-element.12), calls=%async_computation.1 | async-start | bytes 6291456 | tf_op jit(solution)/shard_map/all_to_all | solution.py:429
  112.4 37.0 %collective-permute-start = (f32[8,64,384]{2,1,0:T(8,128)}, f32[8,64,384]{2,1,0:T(8,128)}, u32[]{:S(2)}, u32[]{:S(2)}) collective-permute-start(f32[8,64,384]{2,1,0:T(8,128)} %slice.137), channel_id=1, source_target_pairs={{0,1},{1,0},{2,3},{3,2},{4,5},{5,4},{6,7},{7,6},{8,9},{9,8},{10,11... | collective-permute-start | bytes 2359304 | tf_op jit(solution)/shard_map/ppermute | solution.py:373
  137.4 13.4 %copy-start = (bf16[16,2,12,32,128]{4,3,2,1,0:T(8,128)(2,1)}, bf16[16,2,12,32,128]{4,3,2,1,0:T(8,128)(2,1)S(1)}, u32[]{:S(2)}) copy-start(bf16[16,2,12,32,128]{4,3,2,1,0:T(8,128)(2,1)S(1)} %all-to-all-done.1.arr_ref) | copy-start | bytes 9437188
  137.4 76.3 %all-to-all-start = ((bf16[16,1,12,32,128]{4,3,2,1,0:T(8,128)(2,1)}), bf16[16,1,12,32,128]{4,3,2,1,0:T(8,128)(2,1)}, u32[]{:S(2)}, u32[]{:S(2)}) async-start(bf16[16,1,12,32,128]{4,3,2,1,0:T(8,128)(2,1)} %get-tuple-element.11), calls=%async_computation | async-start | bytes 3145728 | tf_op jit(solution)/shard_map/all_to_all | solution.py:429
  150.9 23.0 %collective-permute-start.1 = (f32[4,64,384]{2,1,0:T(8,128)S(1)}, f32[4,64,384]{2,1,0:T(8,128)S(1)}, u32[]{:S(2)}, u32[]{:S(2)}) collective-permute-start(f32[4,64,384]{2,1,0:T(8,128)S(1)} %slice.139), channel_id=1, source_target_pairs={{0,2},{1,3},{2,0},{3,1},{4,6},{5,7},{6,4},{7,5},{8,10},{9,11},{10,... | collective-permute-start | bytes 1179656 | tf_op jit(solution)/shard_map/ppermute | solution.py:373
  173.9 12.7 %collective-permute-start.2 = (f32[2,64,384]{2,1,0:T(8,128)S(1)}, f32[2,64,384]{2,1,0:T(8,128)S(1)}, u32[]{:S(2)}, u32[]{:S(2)}) collective-permute-start(f32[2,64,384]{2,1,0:T(8,128)S(1)} %slice.141), channel_id=1, source_target_pairs={{0,4},{1,5},{2,6},{3,7},{4,0},{5,1},{6,2},{7,3},{8,12},{9,13},{10,... | collective-permute-start | bytes 589832 | tf_op jit(solution)/shard_map/ppermute | solution.py:373
  186.7 6.8 %collective-permute-start.3 = (f32[1,64,384]{2,1,0:T(8,128)S(1)}, f32[1,64,384]{2,1,0:T(8,128)S(1)}, u32[]{:S(2)}, u32[]{:S(2)}) collective-permute-start(f32[1,64,384]{2,1,0:T(8,128)S(1)} %slice.143), channel_id=1, source_target_pairs={{0,8},{1,9},{2,10},{3,11},{4,12},{5,13},{6,14},{7,15},{8,0},{9,1},... | collective-permute-start | bytes 294920 | tf_op jit(solution)/shard_map/ppermute | solution.py:373

commit v3 on v2

--- a/solution.py
+++ b/solution.py
@@ -19,7 +19,6 @@
 BANDS = 64
 FSUB = 256
 LANES = 128
-CALLS = ((0,), (1, 2), (3,))
 VMEM = 56 * 1024 * 1024
 
 NT = (((1,), (1,)), ((), ()))
@@ -59,18 +58,36 @@
         self.rows_dev = 2 * BAND_CH
         self.rows = devices * self.rows_dev
         self.groups = devices // self.lane_frames
-
-
-def emit_spectra(z, scale, count, me_ref, spectra, loc_ref, spec_refs, send_ref):
+        self.halves = 2 if self.chunks > 2 and self.steps % 2 == 0 else 1
+
+
+def find_places(z, me, lists):
+    base = me * z.feed_dev
+    first = jnp.sum((lists < base).astype(jnp.int32), axis=1, keepdims=True)
+    lane = lax.broadcasted_iota(jnp.int32, (lists.shape[0], LANES), 1)
+    at = first + lane % z.cap
+    parts = []
+    for side in range(FSUB // LANES):
+        index = jnp.clip(at - side * LANES, 0, LANES - 1)
+        half = lists[:, side * LANES : (side + 1) * LANES]
+        parts.append(jnp.take_along_axis(half, index, axis=1, mode="promise_in_bounds"))
+    loc = jnp.where(at < LANES, parts[0], parts[1]) - base
+    return jnp.clip(loc, 0, z.feed_dev - 1)
+
+
+def emit_spectra(z, scale, chunks, me_ref, spectra, lists_ref, loc_ref, spec_refs, send_refs):
+    loc_ref[...] = find_places(z, me_ref[0], lists_ref[...])
     spectra = spectra * scale
-    for c in range(count):
+    for c in range(len(chunks)):
         spec_refs[c][...] = spectra[c * z.rows : (c + 1) * z.rows].astype(jnp.bfloat16)
     lane = lax.broadcasted_iota(jnp.int32, (z.rows_dev, LANES), 1)
     frame = (lane // z.cap) ^ (me_ref[0] % z.lane_frames)
     start = frame * z.cap
-    for c in range(count):
+    for c, chunk in enumerate(chunks):
+        send_ref, unit = send_refs[c]
         for owner in range(z.devices):
-            loc = loc_ref[c, owner : owner + 1, :]
+            band = owner * z.bands_here + chunk
+            loc = loc_ref[band : band + 1, :]
             index = start + loc % z.cap
             lower = jnp.broadcast_to(loc, index.shape) < z.cap
             row = c * z.rows + owner * z.rows_dev
@@ -83,7 +100,7 @@
                         jnp.take_along_axis(x, index, axis=1, mode="promise_in_bounds")
                     )
                 picked = jnp.where(lower, parts[0], parts[1])
-                send_ref[owner, c, q] = picked.astype(jnp.bfloat16)
+                send_ref[owner, unit, q] = picked.astype(jnp.bfloat16)
 
 
 def filter_piece(z, main_ref, halo, win_ref, filt_ref, off):
@@ -120,9 +137,10 @@
 
 
 def first_kernel(
-    z, scale, count, me_ref, main_ref, h0_ref, h1_ref, h2_ref, win_ref, basis_ref, loc_ref,
-    filt_ref, *refs,
+    z, scale, chunks, held, me_ref, main_ref, h0_ref, h1_ref, h2_ref, win_ref, basis_ref,
+    lists_ref, *refs,
 ):
+    filt_ref, spec_refs, send_ref, loc_ref = refs[held], refs[held + 1 : -2], refs[-2], refs[-1]
     halo = (h0_ref, h1_ref, h2_ref)
     piece = 512
     spectra = None
@@ -136,81 +154,137 @@
             preferred_element_type=jnp.float32,
         )
         spectra = part if spectra is None else spectra + part
-    emit_spectra(z, scale, count, me_ref, spectra, loc_ref, refs[:-1], refs[-1])
-
-
-def next_kernel(z, scale, count, me_ref, filt_ref, basis_ref, loc_ref, *refs):
+    sends = [(send_ref, c) for c in range(len(chunks))]
+    emit_spectra(z, scale, chunks, me_ref, spectra, lists_ref, loc_ref, spec_refs, sends)
+
+
+def next_kernel(z, scale, chunks, me_ref, filt_ref, basis_ref, lists_ref, held_ref, *refs):
     spectra = lax.dot_general(
         basis_ref[...], filt_ref[...], NT, preferred_element_type=jnp.float32
     )
-    emit_spectra(z, scale, count, me_ref, spectra, loc_ref, refs[:-1], refs[-1])
+    count = len(chunks)
+    sends = [(refs[count + c], 0) for c in range(count)]
+    emit_spectra(
+        z, scale, chunks, me_ref, spectra, lists_ref, refs[-1], refs[:count], sends
+    )
 
 
 def whole_spec(shape):
     return pl.BlockSpec(shape, lambda *g: (0,) * len(shape))
 
 
-def spectra_call(z, scale, me, basis, loc, filt=None, voltages=None, window=None):
-    count = loc.shape[0]
-    filt_rows = z.step_frames * z.feed_dev
-    filt_spec = pl.BlockSpec((filt_rows, NFFT), lambda g: (g, 0))
-    spec_shape = jax.ShapeDtypeStruct((z.rows, FR * z.feed_dev), jnp.bfloat16)
-    spec_spec = pl.BlockSpec((z.rows, z.step_lanes), lambda g: (0, g))
-    send_shape = jax.ShapeDtypeStruct(
-        (z.devices, count, z.quads, z.rows_dev, LANES), jnp.bfloat16
-    )
-    send_spec = pl.BlockSpec(
-        (z.devices, count, z.step_quads, z.rows_dev, LANES), lambda g: (0, 0, g, 0, 0)
-    )
-    me_spec = pl.BlockSpec(memory_space=pltpu.SMEM)
-    shared = [whole_spec(basis.shape), whole_spec(loc.shape)]
-    out_specs = [spec_spec] * count + [send_spec]
-    out_shape = [spec_shape] * count + [send_shape]
-    flops = 2 * count * z.rows * NFFT * FR * z.feed_dev
-    common = dict(
-        grid=(z.steps,),
-        compiler_params=pltpu.CompilerParams(vmem_limit_bytes=VMEM),
-        cost_estimate=pl.CostEstimate(
-            flops=flops, bytes_accessed=20_000_000, transcendentals=0
-        ),
-    )
-    if filt is not None:
-        outs = pl.pallas_call(
-            functools.partial(next_kernel, z, scale, count),
-            in_specs=[me_spec, filt_spec] + shared,
-            out_specs=out_specs,
-            out_shape=out_shape,
+class Spectra:
+
+    def __init__(self, z, me, voltages, band_feeds):
+        window = fir_window()
+        self.z = z
+        self.me = me
+        self.scale = float(np.sqrt(2.0 / np.sum(window * window)))
+        self.window = jnp.asarray(window.astype(np.float32))
+        self.voltages = voltages
+        self.lists = band_feeds
+        ids = np.arange(CHANNELS).reshape(z.devices, z.chunks, BAND_CH)
+        self.ids = np.transpose(ids, (1, 0, 2))
+        self.half_quads = z.quads // z.halves
+        self.half_steps = z.steps // z.halves
+        self.me_spec = pl.BlockSpec(memory_space=pltpu.SMEM)
+        self.spec_shape = jax.ShapeDtypeStruct((z.rows, FR * z.feed_dev), jnp.bfloat16)
+        self.filt_shape = jax.ShapeDtypeStruct((FR * z.feed_dev, NFFT), jnp.bfloat16)
+
+    def basis(self, chunks):
+        rows = [dft_rows(self.ids[k]).reshape(self.z.rows, NFFT) for k in chunks]
+        return jnp.asarray(np.concatenate(rows))
+
+    def message(self, units):
+        z = self.z
+        dims = (z.devices, units, self.half_quads, z.rows_dev, LANES)
+        return jax.ShapeDtypeStruct(dims, jnp.bfloat16)
+
+    def common(self, steps, chunks):
+        z = self.z
+        flops = 2 * len(chunks) * z.rows * NFFT * z.step_lanes * steps
+        return dict(
+            grid=(steps,),
+            scratch_shapes=[pltpu.VMEM((BANDS, LANES), jnp.int32)],
+            compiler_params=pltpu.CompilerParams(vmem_limit_bytes=VMEM),
+            cost_estimate=pl.CostEstimate(
+                flops=flops, bytes_accessed=3_000_000 * steps, transcendentals=0
+            ),
+        )
+
+    def first(self, half, chunks, basis, units, held):
+        z = self.z
+        count = len(chunks)
+        steps = self.half_steps
+        begin = half * steps
+
+        def halo_spec(h):
+            return pl.BlockSpec(
+                (z.feed_dev, NFFT), lambda g: (0, z.step_frames * (begin + g + 1) + h)
+            )
+
+        send_block = (z.devices, count, z.step_quads, z.rows_dev, LANES)
+        operands = [self.me] + [self.voltages] * 4 + [self.window, basis, self.lists]
+        aliases = {len(operands) + i: i for i in range(len(held))}
+        return pl.pallas_call(
+            functools.partial(first_kernel, z, self.scale, chunks, len(held)),
+            in_specs=[
+                self.me_spec,
+                pl.BlockSpec((z.feed_dev, z.step_frames * NFFT), lambda g: (0, begin + g)),
+                halo_spec(0),
+                halo_spec(1),
+                halo_spec(2),
+                whole_spec((TAPS, NFFT)),
+                whole_spec(basis.shape),
+                whole_spec(self.lists.shape),
+            ]
+            + [pl.BlockSpec(memory_space=pl.ANY)] * len(held),
+            out_specs=[
+                pl.BlockSpec((z.step_lanes, NFFT), lambda g: (begin + g, 0)),
+            ]
+            + [pl.BlockSpec((z.rows, z.step_lanes), lambda g: (0, begin + g))] * count
+            + [pl.BlockSpec(send_block, lambda g: (0, 0, g, 0, 0))],
+            out_shape=[self.filt_shape] + [self.spec_shape] * count + [self.message(units)],
+            input_output_aliases=aliases,
+            name="filter_spectra",
+            **self.common(steps, chunks),
+        )(*operands, *held)
+
+    def next(self, chunks, filt, held):
+        z = self.z
+        count = len(chunks)
+        per = self.half_steps
+        basis = self.basis(chunks)
+        block = (z.devices, 1, z.step_quads, z.rows_dev, LANES)
+        first_unit = held.shape[1] - z.halves
+        operands = [self.me, filt, basis, self.lists, held]
+        return pl.pallas_call(
+            functools.partial(next_kernel, z, self.scale, chunks),
+            in_specs=[
+                self.me_spec,
+                pl.BlockSpec((z.step_lanes, NFFT), lambda g: (g, 0)),
+                whole_spec(basis.shape),
+                whole_spec(self.lists.shape),
+                pl.BlockSpec(memory_space=pl.ANY),
+            ],
+            out_specs=[pl.BlockSpec((z.rows, z.step_lanes), lambda g: (0, g))] * count
+            + [
+                pl.BlockSpec(block, lambda g: (0, first_unit + g // per, g % per, 0, 0)),
+                pl.BlockSpec(block, lambda g: (0, g // per, g % per, 0, 0)),
+            ],
+            out_shape=[self.spec_shape] * count
+            + [self.message(held.shape[1]), self.message(z.halves)],
+            input_output_aliases={4: count},
             name="spectra_next",
-            **common,
-        )(me, filt, basis, loc)
-        return None, outs[:-1], outs[-1]
-
-    def halo_spec(h):
-        return pl.BlockSpec((z.feed_dev, NFFT), lambda g: (0, z.step_frames * (g + 1) + h))
-
-    outs = pl.pallas_call(
-        functools.partial(first_kernel, z, scale, count),
-        in_specs=[
-            me_spec,
-            pl.BlockSpec((z.feed_dev, z.step_frames * NFFT), lambda g: (0, g)),
-            halo_spec(0),
-            halo_spec(1),
-            halo_spec(2),
-            whole_spec((TAPS, NFFT)),
-        ]
-        + shared,
-        out_specs=[filt_spec] + out_specs,
-        out_shape=[jax.ShapeDtypeStruct((FR * z.feed_dev, NFFT), jnp.bfloat16)] + out_shape,
-        name="filter_spectra",
-        **common,
-    )(me, voltages, voltages, voltages, voltages, window, basis, loc)
-    return outs[0], outs[1:-1], outs[-1]
-
-
-def receive_kernel(z, step_ch, arr_ref, key_ref, *refs):
+            **self.common(z.steps, chunks),
+        )(*operands)
+
+
+def receive_kernel(z, step_ch, *refs):
+    arr_refs, key_ref = refs[: z.halves], refs[z.halves]
     vis_ref, rows_ref = refs[-2], refs[-1]
     g = pl.program_id(0)
-    depth = z.quads * z.rows_dev
+    depth = z.quads // z.halves * z.rows_dev
     lf = z.lane_frames
 
     @pl.when(g == 0)
@@ -218,20 +292,22 @@
         lane_group = lax.broadcasted_iota(jnp.int32, (depth, LANES), 1) // z.cap
         slot = lax.broadcasted_iota(jnp.int32, (z.groups * LANES, FSUB), 0)
         for tau in range(lf):
-            tiles = []
-            for big in range(z.groups):
-                tile = arr_ref[big * lf + tau, 0].reshape(depth, LANES)
-                for lane in range(1, lf):
-                    block = arr_ref[big * lf + (lane ^ tau), 0].reshape(depth, LANES)
-                    tile = jnp.where(lane_group == lane, block, tile)
-                tiles.append(tile)
-            lhs = jnp.concatenate(tiles, axis=1)
             pick = jnp.where(slot == key_ref[tau : tau + 1, :], 1.0, 0.0).astype(jnp.bfloat16)
-            rows = jnp.dot(lhs, pick, preferred_element_type=jnp.float32)
-            for half in range(FSUB // LANES):
-                rows_ref[half, tau * depth : (tau + 1) * depth, :] = rows[
-                    :, half * LANES : (half + 1) * LANES
-                ]
+            for h, arr_ref in enumerate(arr_refs):
+                tiles = []
+                for big in range(z.groups):
+                    tile = arr_ref[big * lf + tau, 0].reshape(depth, LANES)
+                    for lane in range(1, lf):
+                        block = arr_ref[big * lf + (lane ^ tau), 0].reshape(depth, LANES)
+                        tile = jnp.where(lane_group == lane, block, tile)
+                    tiles.append(tile)
+                lhs = jnp.concatenate(tiles, axis=1)
+                rows = jnp.dot(lhs, pick, preferred_element_type=jnp.float32)
+                top = (tau * z.halves + h) * depth
+                for side in range(FSUB // LANES):
+                    rows_ref[side, top : top + depth, :] = rows[
+                        :, side * LANES : (side + 1) * LANES
+                    ]
 
     for i in range(step_ch):
         ch = g * step_ch + i
@@ -240,29 +316,32 @@
             halves.append(
                 jnp.concatenate(
                     [
-                        rows_ref[half, pl.ds(ch + part * BAND_CH, FR, stride=z.rows_dev), :]
-                        for half in range(FSUB // LANES)
+                        rows_ref[side, pl.ds(ch + part * BAND_CH, FR, stride=z.rows_dev), :]
+                        for side in range(FSUB // LANES)
                     ],
                     axis=1,
                 )
             )
         real, imag = halves
-        right = jnp.concatenate([real, imag], axis=0)
-        swapped = jnp.concatenate([imag, -real], axis=0)
-        left = jnp.concatenate([right.T, swapped.T], axis=0).astype(jnp.bfloat16)
-        both = jnp.dot(left, right.astype(jnp.bfloat16), preferred_element_type=jnp.float32)
-        both = both * (1.0 / FR)
-        vis_ref[i, 0] = both[:FSUB]
-        vis_ref[i, 1] = both[FSUB:]
-
-
-def receive_call(z, chunk, arrived, at, key, vis):
+        both = jnp.concatenate([real, imag], axis=0)
+        turned = jnp.concatenate([-imag, real], axis=0)
+        right = jnp.concatenate([both, turned], axis=1).astype(jnp.bfloat16)
+        left = both.astype(jnp.bfloat16).T
+        out = jnp.dot(left, right, preferred_element_type=jnp.float32) * (1.0 / FR)
+        vis_ref[i, 0] = out[:, :FSUB]
+        vis_ref[i, 1] = out[:, FSUB:]
+
+
+def receive_call(z, chunk, arrived, key, vis):
     step_ch = 4
     steps = BAND_CH // step_ch
     out_shape = jax.ShapeDtypeStruct((z.chan_dev, 2, FSUB, FSUB), jnp.float32)
-    block = (z.devices, 1) + arrived.shape[2:]
-    in_specs = [pl.BlockSpec(block, lambda g: (0, at, 0, 0, 0)), whole_spec(key.shape)]
-    operands = [arrived, key]
+
+    def unit_spec(got, unit):
+        return pl.BlockSpec((z.devices, 1) + got.shape[2:], lambda g: (0, unit, 0, 0, 0))
+
+    in_specs = [unit_spec(got, unit) for got, unit in arrived] + [whole_spec(key.shape)]
+    operands = [got for got, _ in arrived] + [key]
     aliases = {}
     if vis is not None:
         in_specs.append(pl.BlockSpec(memory_space=pl.ANY))
@@ -373,27 +452,14 @@
     return lax.ppermute(x, "chan", [(i, i ^ offset) for i in range(z.devices)])
 
 
-def listed_places(z, me, lists):
-    base = me * z.feed_dev
-    edges = base + jnp.arange(z.feed_dev + 1, dtype=jnp.int32)
-    below = jnp.sum((lists[:, None, :] < edges[None, :, None]).astype(jnp.int32), axis=2)
-    rank = below[:, :-1] - below[:, :1]
-    rank = jnp.where(below[:, 1:] > below[:, :-1], rank, -1)
-    slots = jnp.arange(LANES, dtype=jnp.int32) % z.cap
-    local = jnp.arange(z.feed_dev, dtype=jnp.int32)
-    return jnp.sum(
-        jnp.where(rank[:, None, :] == slots[None, :, None], local[None, None, :], 0), axis=2
-    )
+def exchange(x):
+    return lax.all_to_all(x, "chan", split_axis=0, concat_axis=0, tiled=True)
 
 
 def on_device(voltages, delays, band_feeds):
     z = Sizes(lax.axis_size("chan"), voltages.shape[0])
     me = lax.axis_index("chan")
     me_array = me.astype(jnp.int32).reshape(1)
-    window = fir_window()
-    scale = float(np.sqrt(2.0 / np.sum(window * window)))
-    window = jnp.asarray(window.astype(np.float32))
-    lists = band_feeds.reshape(z.devices, z.bands_here, FSUB)
 
     own = lax.dynamic_slice_in_dim(band_feeds, me * z.bands_here, z.bands_here, 0)
     source = own // z.feed_dev
@@ -406,28 +472,24 @@
     group = (source % z.lane_frames)[:, None, :] ^ tau[None, :, None]
     take_key = big[:, None, :] + z.cap * group
 
-    ids = np.arange(CHANNELS).reshape(z.devices, z.chunks, BAND_CH)
-    chunk_ids = np.transpose(ids, (1, 0, 2))
-
-    filt = None
-    spectra = []
-    arrived = []
-    for call in CALLS:
-        call = [k for k in call if k < z.chunks]
-        if not call:
-            continue
-        basis = np.concatenate([dft_rows(chunk_ids[k]).reshape(z.rows, NFFT) for k in call])
-        basis = jnp.asarray(basis)
-        places = jnp.stack([listed_places(z, me, lists[:, k]) for k in call])
-        if filt is None:
-            filt, spec, send = spectra_call(
-                z, scale, me_array, basis, places, voltages=voltages, window=window
-            )
-        else:
-            _, spec, send = spectra_call(z, scale, me_array, basis, places, filt=filt)
-        spectra.extend(spec)
-        got = lax.all_to_all(send, "chan", split_axis=0, concat_axis=0, tiled=True)
-        arrived.extend((got, at) for at in range(len(call)))
+    calls = Spectra(z, me_array, voltages, band_feeds)
+    early = list(range(max(1, z.chunks - 2)))
+    basis = calls.basis(early)
+    filt, *spectra, send = calls.first(0, early, basis, len(early), [])
+    got = exchange(send)
+    arrived = [[(got, c)] for c in early]
+    if z.halves > 1:
+        units = len(early) + z.halves
+        filt, *spectra, send = calls.first(1, early, basis, units, [filt, *spectra])
+        late = [z.chunks - 2, z.chunks - 1]
+        *more, send, last = calls.next(late, filt, send)
+        spectra = spectra + more
+        got = exchange(send)
+        for c in early:
+            arrived[c].append((got, c))
+        arrived.append([(got, len(early) + h) for h in range(z.halves)])
+        got = exchange(last)
+        arrived.append([(got, h) for h in range(z.halves)])
 
     beams = beam_call(z, me_array, spectra, delays)
     bit = 1
@@ -439,8 +501,7 @@
 
     vis = None
     for k in range(z.chunks):
-        got, at = arrived[k]
-        vis = receive_call(z, k, got, at, take_key[k], vis)
+        vis = receive_call(z, k, arrived[k], take_key[k], vis)
     return (vis, beams)
 
 

time: 221 us -> 211 us (0.955)
  other arithmetic: 12.8 us -> 6.32 us
    reduce_sum x2 -> x0, other arithmetic: 5.85 us -> none  [the longest x1 4.54 us: listed_places(): jnp.sum((lists[:, None, :] < edges[None, :, None]).astype(jnp.int32), axi...]
  transfers between devices with their start and end apart: 7 -> 7, of which waited for: 5 -> 4; matrix products, arithmetic and copies ran while one was open for 4% -> 4% of each run, Pallas kernels for 32% -> 35%
where the time goes in v3:
time: 211 us; the launch traced here: 210 us
  Pallas kernels  94.2 us (45%)
  waiting for transfers between devices  77.4 us (37%)
  starting transfers between devices  26.9 us (13%)
  other arithmetic  6.32 us (3%)
  local copies, waits for them, and re-layouts  4.13 us (2%)
    ppermute x4, waiting for transfers between devices, swap(): return lax.ppermute(x, 'chan', [(i, i ^ offset) for i in range(z.devices)])  40.4 us
    all_to_all x3, waiting for transfers between devices, exchange(): return lax.all_to_all(x, 'chan', split_axis=0, concat_axis=0, tiled=True)  37 us
    pallas_call x2, Pallas kernels, first(): pl.pallas_call(functools.partial(first_kernel, z, self.scale, chunks, len...  28.1 us
    pallas_call x4, Pallas kernels, receive_call(): pl.pallas_call(functools.partial(receive_kernel, z, step_ch), grid=(steps...  26.5 us
    all_to_all x3, starting transfers between devices, exchange(): return lax.all_to_all(x, 'chan', split_axis=0, concat_axis=0, tiled=True)  26.3 us
    pallas_call x1, Pallas kernels, beam_call(): pl.pallas_call(functools.partial(beam_kernel, z), grid_spec=grid_spec, ou...  20.2 us
    pallas_call x1, Pallas kernels, next(): pl.pallas_call(functools.partial(next_kernel, z, self.scale, chunks), in_...  19.4 us
  transfers between devices with their start and end apart: 7, of which 4 were waited for; matrix products, arithmetic and copies ran while one was open for 4% of the time, Pallas kernels for 35%

profile of v3, /device:TPU:5, one launch (start us, length us, event | category | flops | bytes accessed | tf_op | source)
XLA Modules:
  0.0 209.6 jit_solution(6516925235534120316)
XLA Ops:
  0.6 14.0 %filter_spectra.2 = (bf16[3072,2048]{1,0:T(8,128)(2,1)}, bf16[512,3072]{1,0:T(8,128)(2,1)}, bf16[512,3072]{1,0:T(8,128)(2,1)}, bf16[16,2,6,32,128]{4,3,2,1,0:T(8,128)(2,1)}) custom-call(s32[1]{0:T(128)} %bitcast.me_ref, bf16[64,104448]{1,0:T(8,128)(2,1)} %h2_ref.3, bf16[64,104448]{1,0:T(8,128)(2,1)} %h2_ref.3, bf16[64,104448]{1,0:T(8,128)(2,1)} %h2_ref.3, ...), custom_call_target="tpu_custom_call" | custom-call | flops 6442450944 | bytes 9000000 | tf_op jit(solution)/shard_map/filter_spectra/pallas_call | solution.py:229
  14.7 6.7 %all-to-all-start.2 = ((bf16[16,2,6,32,128]{4,3,2,1,0:T(8,128)(2,1)}), bf16[16,2,6,32,128]{4,3,2,1,0:T(8,128)(2,1)S(1)}, u32[]{:S(2)}, u32[]{:S(2)}) async-start(bf16[16,2,6,32,128]{4,3,2,1,0:T(8,128)(2,1)} %get-tuple-element.21), calls=%async_computation.2 | async-start | bytes 3145728 | tf_op jit(solution)/shard_map/all_to_all | solution.py:456
  21.3 14.0 %filter_spectra.3 = (bf16[3072,2048]{1,0:T(8,128)(2,1)}, bf16[512,3072]{1,0:T(8,128)(2,1)}, bf16[512,3072]{1,0:T(8,128)(2,1)}, bf16[16,4,6,32,128]{4,3,2,1,0:T(8,128)(2,1)}) custom-call(s32[1]{0:T(128)} %bitcast.me_ref, bf16[64,104448]{1,0:T(8,128)(2,1)} %h2_ref.3, ...), custom_call_target="tpu_custom_call", output_to_operand_aliasing={{0}: (8, {}), {1}: (9, {}), {2}: (10, {})} | custom-call | flops 6442450944 | bytes 9000000 | tf_op jit(solution)/shard_map/filter_spectra/pallas_call | solution.py:229
  35.4 19.4 %spectra_next.1 = (bf16[512,3072]{1,0:T(8,128)(2,1)}, bf16[512,3072]{1,0:T(8,128)(2,1)}, bf16[16,4,6,32,128]{4,3,2,1,0:T(8,128)(2,1)}, bf16[16,2,6,32,128]{4,3,2,1,0:T(8,128)(2,1)}) custom-call(s32[1]{0:T(128)} %bitcast.me_ref, bf16[3072,2048]{1,0:T(8,128)(2,1)} %get-tuple-element.17.filt_ref, ...), custom_call_target="tpu_custom_call", output_to_operand_aliasing={{2}: (4, {})} | custom-call | flops 12884901888 | bytes 18000000 | tf_op jit(solution)/shard_map/spectra_next/pallas_call | solution.py:261
  54.8 1.2 copy-done.1
  56.0 7.6 %all-to-all-start.1 = ((bf16[16,4,6,32,128]{4,3,2,1,0:T(8,128)(2,1)}), bf16[16,4,6,32,128]{4,3,2,1,0:T(8,128)(2,1)S(1)}, u32[]{:S(2)}, u32[]{:S(2)}) async-start(bf16[16,4,6,32,128]{4,3,2,1,0:T(8,128)(2,1)} %get-tuple-element.20), calls=%async_computation.1 | async-start | bytes 6291456 | tf_op jit(solution)/shard_map/all_to_all | solution.py:456
  63.8 1.2 fusion.3
  65.0 1.8 fusion
  66.8 20.2 %beam_sums.1 = f32[16,64,384]{2,1,0:T(8,128)} custom-call(s32[1]{0:T(128)} %bitcast.me_ref, bf16[512,3072]{1,0:T(8,128)(2,1)} %get-tuple-element.22.refs_0_, bf16[512,3072]{1,0:T(8,128)(2,1)} %get-tuple-element.23.refs_1_, bf16[512,3072]{1,0:T(8,128)(2,1)} %get-tuple-element.24.refs_2_, bf16[512,3072]{1,0:T(8,128)(2,1)} %get-tuple-element.25.refs_3_, ...), custom_call_target="tpu_custom_call" | custom-call | flops 20000000000 | bytes 20000000 | tf_op jit(solution)/shard_map/beam_sums/pallas_call | solution.py:436
  87.0 2.1 %slice.53 = f32[8,64,384]{2,1,0:T(8,128)} slice(f32[16,64,384]{2,1,0:T(8,128)} %beam_sums.1), slice={[8:16], [0:64], [0:384]} | slice | bytes 1572864 | tf_op jit(solution)/shard_map/slice | solution.py:498
  89.5 37.0 %all-to-all-done.1.refs_1_.refs_0_ = bf16[16,4,6,32,128]{4,3,2,1,0:T(8,128)(2,1)S(1)} async-done(((bf16[16,4,6,32,128]{4,3,2,1,0:T(8,128)(2,1)}), bf16[16,4,6,32,128]{4,3,2,1,0:T(8,128)(2,1)S(1)}, u32[]{:S(2)}, u32[]{:S(2)}) %all-to-all-start.1) | async-done | bytes 3145760 | tf_op jit(solution)/shard_map/all_to_all | solution.py:456
  126.5 12.0 %all-to-all-start = ((bf16[16,2,6,32,128]{4,3,2,1,0:T(8,128)(2,1)}), bf16[16,2,6,32,128]{4,3,2,1,0:T(8,128)(2,1)}, u32[]{:S(2)}, u32[]{:S(2)}) async-start(bf16[16,2,6,32,128]{4,3,2,1,0:T(8,128)(2,1)} %get-tuple-element.19), calls=%async_computation | async-start | bytes 3145728 | tf_op jit(solution)/shard_map/all_to_all | solution.py:456
  138.4 1.5 slice_add_fusion
  140.1 0.7 broadcast_multiply_fusion
  140.8 0.4 convert_reduce_fusion
  141.2 21.7 %collective-permute-done.1 = f32[4,64,384]{2,1,0:T(8,128)S(1)} collective-permute-done((f32[4,64,384]{2,1,0:T(8,128)S(1)}, f32[4,64,384]{2,1,0:T(8,128)S(1)}, u32[]{:S(2)}, u32[]{:S(2)}) %collective-permute-start.1) | collective-permute-done | bytes 393248 | tf_op jit(solution)/shard_map/ppermute | solution.py:452
  163.0 12.6 %collective-permute-done.2 = f32[2,64,384]{2,1,0:T(8,128)S(1)} collective-permute-done((f32[2,64,384]{2,1,0:T(8,128)S(1)}, f32[2,64,384]{2,1,0:T(8,128)S(1)}, u32[]{:S(2)}, u32[]{:S(2)}) %collective-permute-start.2) | collective-permute-done | bytes 196640 | tf_op jit(solution)/shard_map/ppermute | solution.py:452
  175.8 0.6 slice_bitcast_fusion
  176.4 6.1 %collective-permute-done.3 = f32[1,64,384]{2,1,0:T(8,128)S(1)} collective-permute-done((f32[1,64,384]{2,1,0:T(8,128)S(1)}, f32[1,64,384]{2,1,0:T(8,128)S(1)}, u32[]{:S(2)}, u32[]{:S(2)}) %collective-permute-start.3) | collective-permute-done | bytes 98336 | tf_op jit(solution)/shard_map/ppermute | solution.py:452
  182.5 0.7 fusion.2
  183.1 6.6 %correlate.4.refs_3_ = f32[64,2,256,256]{3,2,1,0:T(8,128)} custom-call(bf16[16,2,6,32,128]{4,3,2,1,0:T(8,128)(2,1)} %copy-done.1, bf16[16,4,6,32,128]{4,3,2,1,0:T(8,128)(2,1)} %copy-done, s32[4,256]{1,0:T(4,128)} %get-tuple-element.29.refs_2_), custom_call_target="tpu_custom_call" | custom-call | flops 4000000000 | bytes 10000000 | tf_op jit(solution)/shard_map/correlate/pallas_call | solution.py:350
  189.8 6.6 %correlate.5.refs_3_ = f32[64,2,256,256]{3,2,1,0:T(8,128)} custom-call(bf16[16,2,6,32,128]{4,3,2,1,0:T(8,128)(2,1)} %copy-done.1, bf16[16,4,6,32,128]{4,3,2,1,0:T(8,128)(2,1)} %copy-done, s32[4,256]{1,0:T(4,128)} %get-tuple-element.30.refs_2_, f32[64,2,256,256]{3,2,1,0:T(8,128)} %correlate.4.refs_3_), custom_call_target="tpu_custom_call", output_to_operand_aliasing={{}: (3, {})} | custom-call | flops 4000000000 | bytes 10000000 | tf_op jit(solution)/shard_map/correlate/pallas_call | solution.py:350
  196.4 6.6 %correlate.6.refs_3_ = f32[64,2,256,256]{3,2,1,0:T(8,128)} custom-call(bf16[16,4,6,32,128]{4,3,2,1,0:T(8,128)(2,1)} %copy-done, bf16[16,4,6,32,128]{4,3,2,1,0:T(8,128)(2,1)} %copy-done, s32[4,256]{1,0:T(4,128)} %get-tuple-element.31.refs_2_, f32[64,2,256,256]{3,2,1,0:T(8,128)} %correlate.5.refs_3_), custom_call_target="tpu_custom_call", output_to_operand_aliasing={{}: (3, {})} | custom-call | flops 4000000000 | bytes 10000000 | tf_op jit(solution)/shard_map/correlate/pallas_call | solution.py:350
  203.0 6.6 %correlate.7 = f32[64,2,256,256]{3,2,1,0:T(8,128)} custom-call(bf16[16,2,6,32,128]{4,3,2,1,0:T(8,128)(2,1)} %all-to-all-done.refs_0_.refs_1_, bf16[16,2,6,32,128]{4,3,2,1,0:T(8,128)(2,1)} %all-to-all-done.refs_0_.refs_1_, s32[4,256]{1,0:T(4,128)} %get-tuple-element.32.refs_2_, f32[64,2,256,256]{3,2,1,0:T(8,128)} %correlate.6.refs_3_), custom_call_target="tpu_custom_call", output_to_operand_aliasing={{}: (3, {})} | custom-call | flops 4000000000 | bytes 10000000 | tf_op jit(solution)/shard_map/correlate/pallas_call | solution.py:350
  (24 shorter events, 1.0 us)
Async XLA Ops:
  14.7 40.1 %all-to-all-start.2 = ((bf16[16,2,6,32,128]{4,3,2,1,0:T(8,128)(2,1)}), bf16[16,2,6,32,128]{4,3,2,1,0:T(8,128)(2,1)S(1)}, u32[]{:S(2)}, u32[]{:S(2)}) async-start(bf16[16,2,6,32,128]{4,3,2,1,0:T(8,128)(2,1)} %get-tuple-element.21), calls=%async_computation.2 | async-start | bytes 3145728 | tf_op jit(solution)/shard_map/all_to_all | solution.py:456
  54.8 1.2 copy-start.1
  54.8 8.8 %copy-start.2 = (f32[4,64]{1,0:T(4,128)S(1)}, f32[4,64]{1,0:T(4,128)}, u32[]{:S(2)}) copy-start(f32[4,64]{1,0:T(4,128)} %param.8) | copy-start | bytes 3076
  56.0 70.5 %all-to-all-start.1 = ((bf16[16,4,6,32,128]{4,3,2,1,0:T(8,128)(2,1)}), bf16[16,4,6,32,128]{4,3,2,1,0:T(8,128)(2,1)S(1)}, u32[]{:S(2)}, u32[]{:S(2)}) async-start(bf16[16,4,6,32,128]{4,3,2,1,0:T(8,128)(2,1)} %get-tuple-element.20), calls=%async_computation.1 | async-start | bytes 6291456 | tf_op jit(solution)/shard_map/all_to_all | solution.py:456
  89.1 49.3 %collective-permute-start = (f32[8,64,384]{2,1,0:T(8,128)}, f32[8,64,384]{2,1,0:T(8,128)}, u32[]{:S(2)}, u32[]{:S(2)}) collective-permute-start(f32[8,64,384]{2,1,0:T(8,128)} %slice.53), channel_id=1, source_target_pairs={{0,1},{1,0},{2,3},{3,2},{4,5},{5,4},{6,7},{7,6},{8,9},{9,8},{10,11... | collective-permute-start | bytes 2359304 | tf_op jit(solution)/shard_map/ppermute | solution.py:452
  126.5 13.5 %copy-start = (bf16[16,4,6,32,128]{4,3,2,1,0:T(8,128)(2,1)}, bf16[16,4,6,32,128]{4,3,2,1,0:T(8,128)(2,1)S(1)}, u32[]{:S(2)}) copy-start(bf16[16,4,6,32,128]{4,3,2,1,0:T(8,128)(2,1)S(1)} %all-to-all-done.1.refs_1_.refs_0_) | copy-start | bytes 9437188
  126.5 76.6 %all-to-all-start = ((bf16[16,2,6,32,128]{4,3,2,1,0:T(8,128)(2,1)}), bf16[16,2,6,32,128]{4,3,2,1,0:T(8,128)(2,1)}, u32[]{:S(2)}, u32[]{:S(2)}) async-start(bf16[16,2,6,32,128]{4,3,2,1,0:T(8,128)(2,1)} %get-tuple-element.19), calls=%async_computation | async-start | bytes 3145728 | tf_op jit(solution)/shard_map/all_to_all | solution.py:456
  139.9 22.9 %collective-permute-start.1 = (f32[4,64,384]{2,1,0:T(8,128)S(1)}, f32[4,64,384]{2,1,0:T(8,128)S(1)}, u32[]{:S(2)}, u32[]{:S(2)}) collective-permute-start(f32[4,64,384]{2,1,0:T(8,128)S(1)} %slice.55), channel_id=1, source_target_pairs={{0,2},{1,3},{2,0},{3,1},{4,6},{5,7},{6,4},{7,5},{8,10},{9,11},{10,... | collective-permute-start | bytes 1179656 | tf_op jit(solution)/shard_map/ppermute | solution.py:452
  162.9 12.7 %collective-permute-start.2 = (f32[2,64,384]{2,1,0:T(8,128)S(1)}, f32[2,64,384]{2,1,0:T(8,128)S(1)}, u32[]{:S(2)}, u32[]{:S(2)}) collective-permute-start(f32[2,64,384]{2,1,0:T(8,128)S(1)} %slice.57), channel_id=1, source_target_pairs={{0,4},{1,5},{2,6},{3,7},{4,0},{5,1},{6,2},{7,3},{8,12},{9,13},{10,... | collective-permute-start | bytes 589832 | tf_op jit(solution)/shard_map/ppermute | solution.py:452
  175.7 6.8 %collective-permute-start.3 = (f32[1,64,384]{2,1,0:T(8,128)S(1)}, f32[1,64,384]{2,1,0:T(8,128)S(1)}, u32[]{:S(2)}, u32[]{:S(2)}) collective-permute-start(f32[1,64,384]{2,1,0:T(8,128)S(1)} %slice.59), channel_id=1, source_target_pairs={{0,8},{1,9},{2,10},{3,11},{4,12},{5,13},{6,14},{7,15},{8,0},{9,1},... | collective-permute-start | bytes 294920 | tf_op jit(solution)/shard_map/ppermute | solution.py:452

commit v4 on v3

--- a/solution.py
+++ b/solution.py
@@ -293,7 +293,8 @@
         slot = lax.broadcasted_iota(jnp.int32, (z.groups * LANES, FSUB), 0)
         for tau in range(lf):
             pick = jnp.where(slot == key_ref[tau : tau + 1, :], 1.0, 0.0).astype(jnp.bfloat16)
-            for h, arr_ref in enumerate(arr_refs):
+            parts = []
+            for arr_ref in arr_refs:
                 tiles = []
                 for big in range(z.groups):
                     tile = arr_ref[big * lf + tau, 0].reshape(depth, LANES)
@@ -301,13 +302,15 @@
                         block = arr_ref[big * lf + (lane ^ tau), 0].reshape(depth, LANES)
                         tile = jnp.where(lane_group == lane, block, tile)
                     tiles.append(tile)
-                lhs = jnp.concatenate(tiles, axis=1)
-                rows = jnp.dot(lhs, pick, preferred_element_type=jnp.float32)
-                top = (tau * z.halves + h) * depth
-                for side in range(FSUB // LANES):
-                    rows_ref[side, top : top + depth, :] = rows[
-                        :, side * LANES : (side + 1) * LANES
-                    ]
+                parts.append(jnp.concatenate(tiles, axis=1))
+            rows = jnp.dot(
+                jnp.concatenate(parts, axis=0), pick, preferred_element_type=jnp.float32
+            )
+            size = z.quads * z.rows_dev
+            for side in range(FSUB // LANES):
+                rows_ref[side, tau * size : (tau + 1) * size, :] = rows[
+                    :, side * LANES : (side + 1) * LANES
+                ]
 
     for i in range(step_ch):
         ch = g * step_ch + i
@@ -452,6 +455,11 @@
     return lax.ppermute(x, "chan", [(i, i ^ offset) for i in range(z.devices)])
 
 
+def halve(z, x, bit):
+    half = x.shape[0] // 2
+    return x[:half] + swap(z, x[half:], bit), 2 * bit
+
+
 def exchange(x):
     return lax.all_to_all(x, "chan", split_axis=0, concat_axis=0, tiled=True)
 
@@ -488,21 +496,24 @@
         for c in early:
             arrived[c].append((got, c))
         arrived.append([(got, len(early) + h) for h in range(z.halves)])
+
+    beams, bit = beam_call(z, me_array, spectra, delays), 1
+    beams, bit = halve(z, beams, bit)
+    beams, bit = halve(z, beams, bit)
+    if z.halves > 1:
+        last, beams = lax.optimization_barrier((last, beams))
         got = exchange(last)
         arrived.append([(got, h) for h in range(z.halves)])
-
-    beams = beam_call(z, me_array, spectra, delays)
-    bit = 1
-    while beams.shape[0] > 1:
-        half = beams.shape[0] // 2
-        beams = beams[:half] + swap(z, beams[half:], bit)
-        bit *= 2
-    beams = beams.reshape(z.chan_dev, 2 * BEAMS * FR)
+    beams, bit = halve(z, beams, bit)
 
     vis = None
     for k in range(z.chunks):
         vis = receive_call(z, k, arrived[k], take_key[k], vis)
-    return (vis, beams)
+        if k == 0:
+            beams, vis = lax.optimization_barrier((beams, vis))
+            while beams.shape[0] > 1:
+                beams, bit = halve(z, beams, bit)
+    return (vis, beams.reshape(z.chan_dev, 2 * BEAMS * FR))
 
 
 def solution(mesh):

time: 211 us -> 202 us (0.957)
  waiting for transfers between devices: 77.4 us -> 63.4 us
  starting transfers between devices: 26.9 us -> 32 us
    all_to_all x3, waiting for transfers between devices: 37 us -> 15.9 us  [exchange(): return lax.all_to_all(x, 'chan', split_axis=0, concat_axis=0, tiled=True)]
    ppermute x4, waiting for transfers between devices: 40.4 us -> 47.5 us  [swap(): return lax.ppermute(x, 'chan', [(i, i ^ offset) for i in range(z.devices)])]
    ppermute x4, starting transfers between devices: 0.65 us -> 5.96 us  [swap(): return lax.ppermute(x, 'chan', [(i, i ^ offset) for i in range(z.devices)])]
  transfers between devices with their start and end apart: 7 -> 7, of which waited for: 4 -> 4; matrix products, arithmetic and copies ran while one was open for 4% -> 4% of each run, Pallas kernels for 35% -> 40%
where the time goes in v4:
time: 202 us; the launch traced here: 199 us
  Pallas kernels  93.8 us (46%)
  waiting for transfers between devices  63.4 us (31%)
  starting transfers between devices  32 us (16%)
  other arithmetic  6.08 us (3%)
  local copies, waits for them, and re-layouts  3.19 us (2%)
    ppermute x4, waiting for transfers between devices, swap(): return lax.ppermute(x, 'chan', [(i, i ^ offset) for i in range(z.devices)])  47.5 us
    pallas_call x2, Pallas kernels, first(): pl.pallas_call(functools.partial(first_kernel, z, self.scale, chunks, len...  28.1 us
    all_to_all x3, starting transfers between devices, exchange(): return lax.all_to_all(x, 'chan', split_axis=0, concat_axis=0, tiled=True)  26.1 us
    pallas_call x4, Pallas kernels, receive_call(): pl.pallas_call(functools.partial(receive_kernel, z, step_ch), grid=(steps...  26 us
    pallas_call x1, Pallas kernels, beam_call(): pl.pallas_call(functools.partial(beam_kernel, z), grid_spec=grid_spec, ou...  20.2 us
    pallas_call x1, Pallas kernels, next(): pl.pallas_call(functools.partial(next_kernel, z, self.scale, chunks), in_...  19.5 us
    all_to_all x3, waiting for transfers between devices, exchange(): return lax.all_to_all(x, 'chan', split_axis=0, concat_axis=0, tiled=True)  15.9 us
    ppermute x4, starting transfers between devices, swap(): return lax.ppermute(x, 'chan', [(i, i ^ offset) for i in range(z.devices)])  5.96 us
  transfers between devices with their start and end apart: 7, of which 4 were waited for; matrix products, arithmetic and copies ran while one was open for 4% of the time, Pallas kernels for 40%

profile of v4, /device:TPU:5, one launch (start us, length us, event | category | flops | bytes accessed | tf_op | source)
XLA Modules:
  0.0 199.2 jit_solution(5962429241917150767)
XLA Ops:
  0.6 14.0 %filter_spectra.2 = (bf16[3072,2048]{1,0:T(8,128)(2,1)}, bf16[512,3072]{1,0:T(8,128)(2,1)}, bf16[512,3072]{1,0:T(8,128)(2,1)}, bf16[16,2,6,32,128]{4,3,2,1,0:T(8,128)(2,1)}) custom-call(s32[1]{0:T(128)} %bitcast.me_ref, bf16[64,104448]{1,0:T(8,128)(2,1)} %h2_ref.3, bf16[64,104448]{1,0:T(8,128)(2,1)} %h2_ref.3, bf16[64,104448]{1,0:T(8,128)(2,1)} %h2_ref.3, ...), custom_call_target="tpu_custom_call" | custom-call | flops 6442450944 | bytes 9000000 | tf_op jit(solution)/shard_map/filter_spectra/pallas_call | solution.py:229
  14.7 6.7 %all-to-all-start.2 = ((bf16[16,2,6,32,128]{4,3,2,1,0:T(8,128)(2,1)}), bf16[16,2,6,32,128]{4,3,2,1,0:T(8,128)(2,1)S(1)}, u32[]{:S(2)}, u32[]{:S(2)}) async-start(bf16[16,2,6,32,128]{4,3,2,1,0:T(8,128)(2,1)} %get-tuple-element.30), calls=%async_computation.2 | async-start | bytes 3145728 | tf_op jit(solution)/shard_map/all_to_all | solution.py:464
  21.3 14.1 %filter_spectra.3 = (bf16[3072,2048]{1,0:T(8,128)(2,1)}, bf16[512,3072]{1,0:T(8,128)(2,1)}, bf16[512,3072]{1,0:T(8,128)(2,1)}, bf16[16,4,6,32,128]{4,3,2,1,0:T(8,128)(2,1)}) custom-call(s32[1]{0:T(128)} %bitcast.me_ref, bf16[64,104448]{1,0:T(8,128)(2,1)} %h2_ref.3, ...), custom_call_target="tpu_custom_call", output_to_operand_aliasing={{0}: (8, {}), {1}: (9, {}), {2}: (10, {})} | custom-call | flops 6442450944 | bytes 9000000 | tf_op jit(solution)/shard_map/filter_spectra/pallas_call | solution.py:229
  35.4 19.5 %spectra_next.1 = (bf16[512,3072]{1,0:T(8,128)(2,1)}, bf16[512,3072]{1,0:T(8,128)(2,1)}, bf16[16,4,6,32,128]{4,3,2,1,0:T(8,128)(2,1)}, bf16[16,2,6,32,128]{4,3,2,1,0:T(8,128)(2,1)}) custom-call(s32[1]{0:T(128)} %bitcast.me_ref, bf16[3072,2048]{1,0:T(8,128)(2,1)} %get-tuple-element.21.filt_ref, ...), custom_call_target="tpu_custom_call", output_to_operand_aliasing={{2}: (4, {})} | custom-call | flops 12884901888 | bytes 18000000 | tf_op jit(solution)/shard_map/spectra_next/pallas_call | solution.py:261
  54.9 1.2 copy-done.1
  56.1 7.5 %all-to-all-start.1 = ((bf16[16,4,6,32,128]{4,3,2,1,0:T(8,128)(2,1)}), bf16[16,4,6,32,128]{4,3,2,1,0:T(8,128)(2,1)S(1)}, u32[]{:S(2)}, u32[]{:S(2)}) async-start(bf16[16,4,6,32,128]{4,3,2,1,0:T(8,128)(2,1)} %get-tuple-element.29), calls=%async_computation.1 | async-start | bytes 6291456 | tf_op jit(solution)/shard_map/all_to_all | solution.py:464
  63.8 1.2 fusion.2
  65.0 1.8 fusion
  66.8 20.2 %beam_sums.1 = f32[16,64,384]{2,1,0:T(8,128)} custom-call(s32[1]{0:T(128)} %bitcast.me_ref, bf16[512,3072]{1,0:T(8,128)(2,1)} %get-tuple-element.24.refs_0_, bf16[512,3072]{1,0:T(8,128)(2,1)} %get-tuple-element.25.refs_1_, bf16[512,3072]{1,0:T(8,128)(2,1)} %get-tuple-element.26.refs_2_, bf16[512,3072]{1,0:T(8,128)(2,1)} %get-tuple-element.27.refs_3_, ...), custom_call_target="tpu_custom_call" | custom-call | flops 20000000000 | bytes 20000000 | tf_op jit(solution)/shard_map/beam_sums/pallas_call | solution.py:439
  87.0 1.2 slice.49
  88.6 1.9 collective-permute-done
  90.5 1.2 slice_add_fusion
  91.9 18.7 %collective-permute-done.1 = f32[4,64,384]{2,1,0:T(8,128)S(1)} collective-permute-done((f32[4,64,384]{2,1,0:T(8,128)S(1)}, f32[4,64,384]{2,1,0:T(8,128)S(1)}, u32[]{:S(2)}, u32[]{:S(2)}) %collective-permute-start.1) | collective-permute-done | bytes 393248 | tf_op jit(solution)/shard_map/ppermute | solution.py:455
  110.7 15.9 %all-to-all-done.1.refs_1_.refs_0_ = bf16[16,4,6,32,128]{4,3,2,1,0:T(8,128)(2,1)S(1)} async-done(((bf16[16,4,6,32,128]{4,3,2,1,0:T(8,128)(2,1)}), bf16[16,4,6,32,128]{4,3,2,1,0:T(8,128)(2,1)S(1)}, u32[]{:S(2)}, u32[]{:S(2)}) %all-to-all-start.1) | async-done | bytes 3145760 | tf_op jit(solution)/shard_map/all_to_all | solution.py:464
  126.5 11.9 %all-to-all-start = ((bf16[16,2,6,32,128]{4,3,2,1,0:T(8,128)(2,1)}), bf16[16,2,6,32,128]{4,3,2,1,0:T(8,128)(2,1)}, u32[]{:S(2)}, u32[]{:S(2)}) async-start(bf16[16,2,6,32,128]{4,3,2,1,0:T(8,128)(2,1)} %get-tuple-element.28), calls=%async_computation | async-start | bytes 3145728 | tf_op jit(solution)/shard_map/all_to_all | solution.py:464
  138.4 0.7 broadcast_multiply_fusion
  139.5 1.2 collective-permute-start.2
  141.4 26.9 %collective-permute-done.2 = f32[2,64,384]{2,1,0:T(8,128)S(1)} collective-permute-done((f32[2,64,384]{2,1,0:T(8,128)S(1)}, f32[2,64,384]{2,1,0:T(8,128)S(1)}, u32[]{:S(2)}, u32[]{:S(2)}) %collective-permute-start.2) | collective-permute-done | bytes 196640 | tf_op jit(solution)/shard_map/ppermute | solution.py:455
  168.4 6.5 %correlate.4.refs_3_ = f32[64,2,256,256]{3,2,1,0:T(8,128)} custom-call(bf16[16,2,6,32,128]{4,3,2,1,0:T(8,128)(2,1)} %copy-done.1, bf16[16,4,6,32,128]{4,3,2,1,0:T(8,128)(2,1)} %copy-done, s32[4,256]{1,0:T(4,128)} %get-tuple-element.37.refs_2_), custom_call_target="tpu_custom_call" | custom-call | flops 4000000000 | bytes 10000000 | tf_op jit(solution)/shard_map/correlate/pallas_call | solution.py:353
  174.9 4.1 %collective-permute-start.3 = (f32[1,64,384]{2,1,0:T(8,128)S(1)}, f32[1,64,384]{2,1,0:T(8,128)S(1)}, u32[]{:S(2)}, u32[]{:S(2)}) collective-permute-start(f32[1,64,384]{2,1,0:T(8,128)S(1)} %slice.47), channel_id=1, source_target_pairs={{0,8},{1,9},{2,10},{3,11},{4,12},{5,13},{6,14},{7,15},{8,0},{9,1},... | collective-permute-start | bytes 294920 | tf_op jit(solution)/shard_map/ppermute | solution.py:455
  179.1 6.5 %correlate.5.refs_3_ = f32[64,2,256,256]{3,2,1,0:T(8,128)} custom-call(bf16[16,2,6,32,128]{4,3,2,1,0:T(8,128)(2,1)} %copy-done.1, bf16[16,4,6,32,128]{4,3,2,1,0:T(8,128)(2,1)} %copy-done, s32[4,256]{1,0:T(4,128)} %get-tuple-element.38.refs_2_, f32[64,2,256,256]{3,2,1,0:T(8,128)} %correlate.4.refs_3_), custom_call_target="tpu_custom_call", output_to_operand_aliasing={{}: (3, {})} | custom-call | flops 4000000000 | bytes 10000000 | tf_op jit(solution)/shard_map/correlate/pallas_call | solution.py:353
  185.5 6.5 %correlate.6.refs_3_ = f32[64,2,256,256]{3,2,1,0:T(8,128)} custom-call(bf16[16,4,6,32,128]{4,3,2,1,0:T(8,128)(2,1)} %copy-done, bf16[16,4,6,32,128]{4,3,2,1,0:T(8,128)(2,1)} %copy-done, s32[4,256]{1,0:T(4,128)} %get-tuple-element.39.refs_2_, f32[64,2,256,256]{3,2,1,0:T(8,128)} %correlate.5.refs_3_), custom_call_target="tpu_custom_call", output_to_operand_aliasing={{}: (3, {})} | custom-call | flops 4000000000 | bytes 10000000 | tf_op jit(solution)/shard_map/correlate/pallas_call | solution.py:353
  192.0 6.5 %correlate.7 = f32[64,2,256,256]{3,2,1,0:T(8,128)} custom-call(bf16[16,2,6,32,128]{4,3,2,1,0:T(8,128)(2,1)} %all-to-all-done.refs_0_.refs_1_, bf16[16,2,6,32,128]{4,3,2,1,0:T(8,128)(2,1)} %all-to-all-done.refs_0_.refs_1_, s32[4,256]{1,0:T(4,128)} %get-tuple-element.40.refs_2_, f32[64,2,256,256]{3,2,1,0:T(8,128)} %correlate.6.refs_3_), custom_call_target="tpu_custom_call", output_to_operand_aliasing={{}: (3, {})} | custom-call | flops 4000000000 | bytes 10000000 | tf_op jit(solution)/shard_map/correlate/pallas_call | solution.py:353
  198.6 0.7 add_bitcast_fusion
  (28 shorter events, 1.9 us)
Async XLA Ops:
  14.7 40.2 %all-to-all-start.2 = ((bf16[16,2,6,32,128]{4,3,2,1,0:T(8,128)(2,1)}), bf16[16,2,6,32,128]{4,3,2,1,0:T(8,128)(2,1)S(1)}, u32[]{:S(2)}, u32[]{:S(2)}) async-start(bf16[16,2,6,32,128]{4,3,2,1,0:T(8,128)(2,1)} %get-tuple-element.30), calls=%async_computation.2 | async-start | bytes 3145728 | tf_op jit(solution)/shard_map/all_to_all | solution.py:464
  54.9 1.2 copy-start.1
  54.9 8.7 %copy-start.4 = (f32[4,64]{1,0:T(4,128)S(1)}, f32[4,64]{1,0:T(4,128)}, u32[]{:S(2)}) copy-start(f32[4,64]{1,0:T(4,128)} %param.8) | copy-start | bytes 3076
  56.1 70.4 %all-to-all-start.1 = ((bf16[16,4,6,32,128]{4,3,2,1,0:T(8,128)(2,1)}), bf16[16,4,6,32,128]{4,3,2,1,0:T(8,128)(2,1)S(1)}, u32[]{:S(2)}, u32[]{:S(2)}) async-start(bf16[16,4,6,32,128]{4,3,2,1,0:T(8,128)(2,1)} %get-tuple-element.29), calls=%async_computation.1 | async-start | bytes 6291456 | tf_op jit(solution)/shard_map/all_to_all | solution.py:464
  88.2 2.4 %collective-permute-start = (f32[8,64,384]{2,1,0:T(8,128)S(1)}, f32[8,64,384]{2,1,0:T(8,128)S(1)}, u32[]{:S(2)}, u32[]{:S(2)}) collective-permute-start(f32[8,64,384]{2,1,0:T(8,128)S(1)} %slice.49), channel_id=1, source_target_pairs={{0,1},{1,0},{2,3},{3,2},{4,5},{5,4},{6,7},{7,6},{8,9},{9,8},{10,11... | collective-permute-start | bytes 2359304 | tf_op jit(solution)/shard_map/ppermute | solution.py:455
  91.8 18.8 %collective-permute-start.1 = (f32[4,64,384]{2,1,0:T(8,128)S(1)}, f32[4,64,384]{2,1,0:T(8,128)S(1)}, u32[]{:S(2)}, u32[]{:S(2)}) collective-permute-start(f32[4,64,384]{2,1,0:T(8,128)S(1)} %slice.51), channel_id=1, source_target_pairs={{0,2},{1,3},{2,0},{3,1},{4,6},{5,7},{6,4},{7,5},{8,10},{9,11},{10,... | collective-permute-start | bytes 1179656 | tf_op jit(solution)/shard_map/ppermute | solution.py:455
  126.5 41.9 %copy-start = (bf16[16,4,6,32,128]{4,3,2,1,0:T(8,128)(2,1)}, bf16[16,4,6,32,128]{4,3,2,1,0:T(8,128)(2,1)S(1)}, u32[]{:S(2)}) copy-start(bf16[16,4,6,32,128]{4,3,2,1,0:T(8,128)(2,1)S(1)} %all-to-all-done.1.refs_1_.refs_0_) | copy-start | bytes 9437188
  126.5 65.5 %all-to-all-start = ((bf16[16,2,6,32,128]{4,3,2,1,0:T(8,128)(2,1)}), bf16[16,2,6,32,128]{4,3,2,1,0:T(8,128)(2,1)}, u32[]{:S(2)}, u32[]{:S(2)}) async-start(bf16[16,2,6,32,128]{4,3,2,1,0:T(8,128)(2,1)} %get-tuple-element.28), calls=%async_computation | async-start | bytes 3145728 | tf_op jit(solution)/shard_map/all_to_all | solution.py:464
  139.5 28.8 %collective-permute-start.2 = (f32[2,64,384]{2,1,0:T(8,128)S(1)}, f32[2,64,384]{2,1,0:T(8,128)S(1)}, u32[]{:S(2)}, u32[]{:S(2)}) collective-permute-start(f32[2,64,384]{2,1,0:T(8,128)S(1)} %slice.44), channel_id=1, source_target_pairs={{0,4},{1,5},{2,6},{3,7},{4,0},{5,1},{6,2},{7,3},{8,12},{9,13},{10,... | collective-permute-start | bytes 589832 | tf_op jit(solution)/shard_map/ppermute | solution.py:455
  168.4 6.6 %copy-start.2 = (f32[2,64,384]{2,1,0:T(8,128)}, f32[2,64,384]{2,1,0:T(8,128)S(1)}, u32[]{:S(2)}) copy-start(f32[2,64,384]{2,1,0:T(8,128)S(1)} %slice_add_fusion.2) | copy-start | bytes 589828
  174.9 23.6 %collective-permute-start.3 = (f32[1,64,384]{2,1,0:T(8,128)S(1)}, f32[1,64,384]{2,1,0:T(8,128)S(1)}, u32[]{:S(2)}, u32[]{:S(2)}) collective-permute-start(f32[1,64,384]{2,1,0:T(8,128)S(1)} %slice.47), channel_id=1, source_target_pairs={{0,8},{1,9},{2,10},{3,11},{4,12},{5,13},{6,14},{7,15},{8,0},{9,1},... | collective-permute-start | bytes 294920 | tf_op jit(solution)/shard_map/ppermute | solution.py:455
  192.0 6.6 %copy-start.3 = (f32[2,64,384]{2,1,0:T(8,128)S(1)}, f32[2,64,384]{2,1,0:T(8,128)}, u32[]{:S(2)}) copy-start(f32[2,64,384]{2,1,0:T(8,128)} %copy-done.2) | copy-start | bytes 589828

commit v5 on v4

--- a/solution.py
+++ b/solution.py
@@ -1,4 +1,5 @@
 import functools
+import math
 
 import jax
 import jax.numpy as jnp
@@ -31,8 +32,11 @@
     return (np.sinc(centered) * hann_part).reshape(TAPS, NFFT)
 
 
+ORDER = np.concatenate([np.arange(0, BAND_CH, 2), np.arange(1, BAND_CH, 2)])
+
+
 def dft_rows(chan_ids):
-    m = np.arange(NFFT, dtype=np.int64)
+    m = np.arange(NFFT // 2, dtype=np.int64)
     turns = (chan_ids[..., None].astype(np.int64) * m) % NFFT
     table = 2.0 * np.pi * np.arange(NFFT) / NFFT
     cosine = np.cos(table).astype(np.float32).astype(ml_dtypes.bfloat16)
@@ -58,7 +62,11 @@
         self.rows_dev = 2 * BAND_CH
         self.rows = devices * self.rows_dev
         self.groups = devices // self.lane_frames
-        self.halves = 2 if self.chunks > 2 and self.steps % 2 == 0 else 1
+        self.early = min(2, self.chunks)
+        if self.chunks == 4:
+            self.parts = (self.steps // 3, self.steps - self.steps // 3)
+        else:
+            self.early, self.parts = self.chunks, (self.steps,)
 
 
 def find_places(z, me, lists):
@@ -77,63 +85,91 @@
 
 def emit_spectra(z, scale, chunks, me_ref, spectra, lists_ref, loc_ref, spec_refs, send_refs):
     loc_ref[...] = find_places(z, me_ref[0], lists_ref[...])
-    spectra = spectra * scale
-    for c in range(len(chunks)):
-        spec_refs[c][...] = spectra[c * z.rows : (c + 1) * z.rows].astype(jnp.bfloat16)
     lane = lax.broadcasted_iota(jnp.int32, (z.rows_dev, LANES), 1)
     frame = (lane // z.cap) ^ (me_ref[0] % z.lane_frames)
     start = frame * z.cap
+    few = BAND_CH // 2
     for c, chunk in enumerate(chunks):
         send_ref, unit = send_refs[c]
         for owner in range(z.devices):
+            top = (c * z.devices + owner) * BAND_CH
+            rows = [x[top + p : top + p + few] for p in (0, few) for x in spectra]
+            rows = jnp.concatenate(rows, axis=0) * scale
+            spec_refs[c][owner * z.rows_dev : (owner + 1) * z.rows_dev, :] = rows.astype(
+                jnp.bfloat16
+            )
             band = owner * z.bands_here + chunk
             loc = loc_ref[band : band + 1, :]
             index = start + loc % z.cap
             lower = jnp.broadcast_to(loc, index.shape) < z.cap
-            row = c * z.rows + owner * z.rows_dev
             for q in range(z.step_quads):
                 parts = []
                 for side in range(2):
                     left = q * z.width + side * LANES
-                    x = spectra[row : row + z.rows_dev, left : left + LANES]
                     parts.append(
-                        jnp.take_along_axis(x, index, axis=1, mode="promise_in_bounds")
+                        jnp.take_along_axis(
+                            rows[:, left : left + LANES], index, axis=1,
+                            mode="promise_in_bounds",
+                        )
                     )
                 picked = jnp.where(lower, parts[0], parts[1])
-                send_ref[owner, unit, q] = picked.astype(jnp.bfloat16)
-
-
-def filter_piece(z, main_ref, halo, win_ref, filt_ref, off):
+                send_ref[owner, unit + q] = picked.astype(jnp.bfloat16)
+
+
+def filter_tile(z, main_ref, halo, win_ref, off, f0):
     lanes = slice(off, off + LANES)
     taps = [win_ref[k : k + 1, lanes] for k in range(TAPS)]
+    frames = []
+    for t in range(z.step_frames + TAPS - 1):
+        if t < z.step_frames:
+            x = main_ref[f0 : f0 + 16, t * NFFT + off : t * NFFT + off + LANES]
+        else:
+            x = halo[t - z.step_frames][f0 : f0 + 16, lanes]
+        frames.append(x.astype(jnp.float32))
+    totals = []
+    for t in range(z.step_frames):
+        total = taps[0] * frames[t]
+        for k in range(1, TAPS):
+            total = total + taps[k] * frames[t + k]
+        totals.append(total)
+    if z.cap < 16:
+        totals = [
+            jnp.concatenate([totals[t][h : h + 8], totals[t + 1][h : h + 8]], axis=0)
+            for t in range(0, z.step_frames, 2)
+            for h in (0, 8)
+        ]
+    out = []
+    for i, total in enumerate(totals):
+        if z.cap < 16:
+            t, half, feed = 2 * (i // 2), i % 2, 0
+        else:
+            t, half, feed = i, f0 // z.cap, f0 % z.cap
+        row = (t // z.lane_frames) * z.width + half * LANES
+        row += (t % z.lane_frames) * z.cap + feed
+        out.append((row, total.astype(jnp.bfloat16)))
+    return out
+
+
+def filter_fold(z, main_ref, halo, win_ref, filt_ref, off):
+    far = off + NFFT // 2
     for f0 in range(0, z.feed_dev, 16):
-        frames = []
-        for t in range(z.step_frames + TAPS - 1):
-            if t < z.step_frames:
-                x = main_ref[f0 : f0 + 16, t * NFFT + off : t * NFFT + off + LANES]
-            else:
-                x = halo[t - z.step_frames][f0 : f0 + 16, lanes]
-            frames.append(x.astype(jnp.float32))
-        totals = []
-        for t in range(z.step_frames):
-            total = taps[0] * frames[t]
-            for k in range(1, TAPS):
-                total = total + taps[k] * frames[t + k]
-            totals.append(total)
-        if z.cap < 16:
-            totals = [
-                jnp.concatenate([totals[t][h : h + 8], totals[t + 1][h : h + 8]], axis=0)
-                for t in range(0, z.step_frames, 2)
-                for h in (0, 8)
-            ]
-        for i, total in enumerate(totals):
-            if z.cap < 16:
-                t, half, feed = 2 * (i // 2), i % 2, 0
-            else:
-                t, half, feed = i, f0 // z.cap, f0 % z.cap
-            row = (t // z.lane_frames) * z.width + half * LANES
-            row += (t % z.lane_frames) * z.cap + feed
-            filt_ref[row : row + 16, lanes] = total.astype(jnp.bfloat16)
+        low = filter_tile(z, main_ref, halo, win_ref, off, f0)
+        high = filter_tile(z, main_ref, halo, win_ref, far, f0)
+        for (row, a), (_, b) in zip(low, high):
+            filt_ref[row : row + 16, off : off + LANES] = a + b
+            filt_ref[row : row + 16, far : far + LANES] = a - b
+
+
+def transform(basis_ref, filt_ref, begin, end):
+    return [
+        lax.dot_general(
+            basis_ref[parity, :, begin:end],
+            filt_ref[:, parity * (NFFT // 2) + begin : parity * (NFFT // 2) + end],
+            NT,
+            preferred_element_type=jnp.float32,
+        )
+        for parity in range(2)
+    ]
 
 
 def first_kernel(
@@ -144,24 +180,17 @@
     halo = (h0_ref, h1_ref, h2_ref)
     piece = 512
     spectra = None
-    for off in range(0, NFFT, piece):
+    for off in range(0, NFFT // 2, piece):
         for tile in range(off, off + piece, LANES):
-            filter_piece(z, main_ref, halo, win_ref, filt_ref, tile)
-        part = lax.dot_general(
-            basis_ref[:, off : off + piece],
-            filt_ref[:, off : off + piece],
-            NT,
-            preferred_element_type=jnp.float32,
-        )
-        spectra = part if spectra is None else spectra + part
-    sends = [(send_ref, c) for c in range(len(chunks))]
+            filter_fold(z, main_ref, halo, win_ref, filt_ref, tile)
+        part = transform(basis_ref, filt_ref, off, off + piece)
+        spectra = part if spectra is None else [x + y for x, y in zip(spectra, part)]
+    sends = [(send_ref, c * z.step_quads) for c in range(len(chunks))]
     emit_spectra(z, scale, chunks, me_ref, spectra, lists_ref, loc_ref, spec_refs, sends)
 
 
 def next_kernel(z, scale, chunks, me_ref, filt_ref, basis_ref, lists_ref, held_ref, *refs):
-    spectra = lax.dot_general(
-        basis_ref[...], filt_ref[...], NT, preferred_element_type=jnp.float32
-    )
+    spectra = transform(basis_ref, filt_ref, 0, NFFT // 2)
     count = len(chunks)
     sends = [(refs[count + c], 0) for c in range(count)]
     emit_spectra(
@@ -183,26 +212,27 @@
         self.window = jnp.asarray(window.astype(np.float32))
         self.voltages = voltages
         self.lists = band_feeds
-        ids = np.arange(CHANNELS).reshape(z.devices, z.chunks, BAND_CH)
-        self.ids = np.transpose(ids, (1, 0, 2))
-        self.half_quads = z.quads // z.halves
-        self.half_steps = z.steps // z.halves
+        self.ids = np.arange(CHANNELS).reshape(z.devices, z.chunks, BAND_CH)
         self.me_spec = pl.BlockSpec(memory_space=pltpu.SMEM)
         self.spec_shape = jax.ShapeDtypeStruct((z.rows, FR * z.feed_dev), jnp.bfloat16)
         self.filt_shape = jax.ShapeDtypeStruct((FR * z.feed_dev, NFFT), jnp.bfloat16)
 
     def basis(self, chunks):
-        rows = [dft_rows(self.ids[k]).reshape(self.z.rows, NFFT) for k in chunks]
-        return jnp.asarray(np.concatenate(rows))
-
-    def message(self, units):
+        sides = []
+        for parity in range(2):
+            rows = [dft_rows(self.ids[:, k, parity::2].reshape(-1)) for k in chunks]
+            rows = np.stack(rows).reshape(len(chunks), self.z.devices, BAND_CH // 2, 2, -1)
+            rows = np.transpose(rows, (0, 1, 3, 2, 4))
+            sides.append(rows.reshape(len(chunks) * self.z.rows // 2, NFFT // 2))
+        return jnp.asarray(np.stack(sides))
+
+    def message(self, quads):
         z = self.z
-        dims = (z.devices, units, self.half_quads, z.rows_dev, LANES)
-        return jax.ShapeDtypeStruct(dims, jnp.bfloat16)
+        return jax.ShapeDtypeStruct((z.devices, quads, z.rows_dev, LANES), jnp.bfloat16)
 
     def common(self, steps, chunks):
         z = self.z
-        flops = 2 * len(chunks) * z.rows * NFFT * z.step_lanes * steps
+        flops = len(chunks) * z.rows * NFFT * z.step_lanes * steps
         return dict(
             grid=(steps,),
             scratch_shapes=[pltpu.VMEM((BANDS, LANES), jnp.int32)],
@@ -212,18 +242,16 @@
             ),
         )
 
-    def first(self, half, chunks, basis, units, held):
+    def first(self, begin, steps, chunks, basis, quads, held):
         z = self.z
         count = len(chunks)
-        steps = self.half_steps
-        begin = half * steps
 
         def halo_spec(h):
             return pl.BlockSpec(
                 (z.feed_dev, NFFT), lambda g: (0, z.step_frames * (begin + g + 1) + h)
             )
 
-        send_block = (z.devices, count, z.step_quads, z.rows_dev, LANES)
+        send_block = (z.devices, count * z.step_quads, z.rows_dev, LANES)
         operands = [self.me] + [self.voltages] * 4 + [self.window, basis, self.lists]
         aliases = {len(operands) + i: i for i in range(len(held))}
         return pl.pallas_call(
@@ -243,8 +271,8 @@
                 pl.BlockSpec((z.step_lanes, NFFT), lambda g: (begin + g, 0)),
             ]
             + [pl.BlockSpec((z.rows, z.step_lanes), lambda g: (0, begin + g))] * count
-            + [pl.BlockSpec(send_block, lambda g: (0, 0, g, 0, 0))],
-            out_shape=[self.filt_shape] + [self.spec_shape] * count + [self.message(units)],
+            + [pl.BlockSpec(send_block, lambda g: (0, g, 0, 0))],
+            out_shape=[self.filt_shape] + [self.spec_shape] * count + [self.message(quads)],
             input_output_aliases=aliases,
             name="filter_spectra",
             **self.common(steps, chunks),
@@ -253,10 +281,9 @@
     def next(self, chunks, filt, held):
         z = self.z
         count = len(chunks)
-        per = self.half_steps
         basis = self.basis(chunks)
-        block = (z.devices, 1, z.step_quads, z.rows_dev, LANES)
-        first_unit = held.shape[1] - z.halves
+        block = (z.devices, z.step_quads, z.rows_dev, LANES)
+        base = (held.shape[1] - z.quads) // z.step_quads
         operands = [self.me, filt, basis, self.lists, held]
         return pl.pallas_call(
             functools.partial(next_kernel, z, self.scale, chunks),
@@ -269,51 +296,56 @@
             ],
             out_specs=[pl.BlockSpec((z.rows, z.step_lanes), lambda g: (0, g))] * count
             + [
-                pl.BlockSpec(block, lambda g: (0, first_unit + g // per, g % per, 0, 0)),
-                pl.BlockSpec(block, lambda g: (0, g // per, g % per, 0, 0)),
+                pl.BlockSpec(block, lambda g: (0, base + g, 0, 0)),
+                pl.BlockSpec(block, lambda g: (0, g, 0, 0)),
             ],
             out_shape=[self.spec_shape] * count
-            + [self.message(held.shape[1]), self.message(z.halves)],
+            + [self.message(held.shape[1]), self.message(z.quads)],
             input_output_aliases={4: count},
             name="spectra_next",
             **self.common(z.steps, chunks),
         )(*operands)
 
 
-def receive_kernel(z, step_ch, *refs):
-    arr_refs, key_ref = refs[: z.halves], refs[z.halves]
+def receive_kernel(z, step_ch, runs, *refs):
+    arr_refs, key_ref = refs[: len(runs)], refs[len(runs)]
     vis_ref, rows_ref = refs[-2], refs[-1]
     g = pl.program_id(0)
-    depth = z.quads // z.halves * z.rows_dev
     lf = z.lane_frames
 
     @pl.when(g == 0)
     def _():
-        lane_group = lax.broadcasted_iota(jnp.int32, (depth, LANES), 1) // z.cap
         slot = lax.broadcasted_iota(jnp.int32, (z.groups * LANES, FSUB), 0)
+        size = z.quads * z.rows_dev
         for tau in range(lf):
             pick = jnp.where(slot == key_ref[tau : tau + 1, :], 1.0, 0.0).astype(jnp.bfloat16)
             parts = []
-            for arr_ref in arr_refs:
-                tiles = []
-                for big in range(z.groups):
-                    tile = arr_ref[big * lf + tau, 0].reshape(depth, LANES)
-                    for lane in range(1, lf):
-                        block = arr_ref[big * lf + (lane ^ tau), 0].reshape(depth, LANES)
-                        tile = jnp.where(lane_group == lane, block, tile)
-                    tiles.append(tile)
-                parts.append(jnp.concatenate(tiles, axis=1))
+            for arr_ref, places in zip(arr_refs, runs):
+                for first, count in places:
+                    depth = count * z.rows_dev
+                    lane_group = lax.broadcasted_iota(jnp.int32, (depth, LANES), 1) // z.cap
+                    tiles = []
+                    for big in range(z.groups):
+                        tile = None
+                        for lane in range(lf):
+                            block = arr_ref[big * lf + (lane ^ tau), first : first + count]
+                            block = block.reshape(depth, LANES)
+                            if tile is None:
+                                tile = block
+                            else:
+                                tile = jnp.where(lane_group == lane, block, tile)
+                        tiles.append(tile)
+                    parts.append(jnp.concatenate(tiles, axis=1))
             rows = jnp.dot(
                 jnp.concatenate(parts, axis=0), pick, preferred_element_type=jnp.float32
             )
-            size = z.quads * z.rows_dev
             for side in range(FSUB // LANES):
                 rows_ref[side, tau * size : (tau + 1) * size, :] = rows[
                     :, side * LANES : (side + 1) * LANES
                 ]
 
     for i in range(step_ch):
-        ch = g * step_ch + i
+        ch = (i % 2) * (BAND_CH // 2) + g * (step_ch // 2) + i // 2
         halves = []
         for part in range(2):
             halves.append(
@@ -340,18 +372,20 @@
     steps = BAND_CH // step_ch
     out_shape = jax.ShapeDtypeStruct((z.chan_dev, 2, FSUB, FSUB), jnp.float32)
 
-    def unit_spec(got, unit):
-        return pl.BlockSpec((z.devices, 1) + got.shape[2:], lambda g: (0, unit, 0, 0, 0))
-
-    in_specs = [unit_spec(got, unit) for got, unit in arrived] + [whole_spec(key.shape)]
-    operands = [got for got, _ in arrived] + [key]
+    def block_spec(got, quads, at, places):
+        shape = (z.devices, quads) + got.shape[2:]
+        return pl.BlockSpec(shape, lambda g: (0, at, 0, 0))
+
+    in_specs = [block_spec(*x) for x in arrived] + [whole_spec(key.shape)]
+    operands = [x[0] for x in arrived] + [key]
+    runs = [x[3] for x in arrived]
     aliases = {}
     if vis is not None:
         in_specs.append(pl.BlockSpec(memory_space=pl.ANY))
         aliases = {len(operands): 0}
         operands.append(vis)
     return pl.pallas_call(
-        functools.partial(receive_kernel, z, step_ch),
+        functools.partial(receive_kernel, z, step_ch, runs),
         grid=(steps,),
         in_specs=in_specs,
         out_specs=pl.BlockSpec(
@@ -406,7 +440,8 @@
     spread = jnp.broadcast_to(halves, (BEAMS, 2, z.lane_frames, z.cap)).reshape(BEAMS, z.width)
     unit = 2.0 * jnp.pi / NFFT
     owners = jnp.arange(z.devices, dtype=jnp.int32).astype(jnp.float32) * z.chan_dev
-    inner = jnp.arange(z.chan_dev, dtype=jnp.int32).astype(jnp.float32)
+    inner = np.arange(z.chunks)[:, None] * BAND_CH + ORDER[None, :]
+    inner = jnp.asarray(inner.reshape(-1).astype(np.float32))
     base = unit * (spread[None, :, :] * owners[:, None, None])
     step = unit * (spread[:, None, :] * inner[None, :, None])
     frame = (np.arange(FR * z.cap) // LANES) * z.lane_frames
@@ -455,11 +490,6 @@
     return lax.ppermute(x, "chan", [(i, i ^ offset) for i in range(z.devices)])
 
 
-def halve(z, x, bit):
-    half = x.shape[0] // 2
-    return x[:half] + swap(z, x[half:], bit), 2 * bit
-
-
 def exchange(x):
     return lax.all_to_all(x, "chan", split_axis=0, concat_axis=0, tiled=True)
 
@@ -481,39 +511,47 @@
     take_key = big[:, None, :] + z.cap * group
 
     calls = Spectra(z, me_array, voltages, band_feeds)
-    early = list(range(max(1, z.chunks - 2)))
+    early = list(range(z.early))
     basis = calls.basis(early)
-    filt, *spectra, send = calls.first(0, early, basis, len(early), [])
-    got = exchange(send)
-    arrived = [[(got, c)] for c in early]
-    if z.halves > 1:
-        units = len(early) + z.halves
-        filt, *spectra, send = calls.first(1, early, basis, units, [filt, *spectra])
-        late = [z.chunks - 2, z.chunks - 1]
-        *more, send, last = calls.next(late, filt, send)
+    step = z.early * z.step_quads
+    arrived = [[] for _ in range(z.chunks)]
+
+    def early_places(got, steps):
+        for c in early:
+            places = [(g * step + c * z.step_quads, z.step_quads) for g in range(steps)]
+            arrived[c].append((got, steps * step, 0, places))
+
+    steps = z.parts[0]
+    filt, *spectra, send = calls.first(0, steps, early, basis, steps * step, [])
+    early_places(exchange(send), steps)
+    if len(z.parts) > 1:
+        begin, steps = steps, z.parts[1]
+        base = steps * step
+        filt, *spectra, send = calls.first(
+            begin, steps, early, basis, base + z.quads, [filt, *spectra]
+        )
+        *more, send, last = calls.next([z.chunks - 2, z.chunks - 1], filt, send)
         spectra = spectra + more
         got = exchange(send)
-        for c in early:
-            arrived[c].append((got, c))
-        arrived.append([(got, len(early) + h) for h in range(z.halves)])
+        early_places(got, steps)
+        block = math.gcd(base, z.quads)
+        for i in range(z.quads // block):
+            arrived[-2].append((got, block, base // block + i, [(0, block)]))
 
     beams, bit = beam_call(z, me_array, spectra, delays), 1
-    beams, bit = halve(z, beams, bit)
-    beams, bit = halve(z, beams, bit)
-    if z.halves > 1:
+    while beams.shape[0] > 1:
+        half = beams.shape[0] // 2
+        beams, bit = beams[:half] + swap(z, beams[half:], bit), 2 * bit
+    beams = beams.reshape(z.chunks, 2, BAND_CH // 2, 2 * BEAMS * FR)
+    beams = jnp.swapaxes(beams, 1, 2).reshape(z.chan_dev, 2 * BEAMS * FR)
+    if len(z.parts) > 1:
         last, beams = lax.optimization_barrier((last, beams))
-        got = exchange(last)
-        arrived.append([(got, h) for h in range(z.halves)])
-    beams, bit = halve(z, beams, bit)
+        arrived[-1].append((exchange(last), z.quads, 0, [(0, z.quads)]))
 
     vis = None
     for k in range(z.chunks):
         vis = receive_call(z, k, arrived[k], take_key[k], vis)
-        if k == 0:
-            beams, vis = lax.optimization_barrier((beams, vis))
-            while beams.shape[0] > 1:
-                beams, bit = halve(z, beams, bit)
-    return (vis, beams.reshape(z.chan_dev, 2 * BEAMS * FR))
+    return (vis, beams)
 
 
 def solution(mesh):

time: 202 us -> 192 us (0.950)
  starting transfers between devices: 32 us -> 21.2 us
  Pallas kernels: 93.8 us -> 88.4 us
  waiting for transfers between devices: 63.4 us -> 67.3 us
    all_to_all x3, starting transfers between devices: 26.1 us -> 17.3 us  [exchange(): return lax.all_to_all(x, 'chan', split_axis=0, concat_axis=0, tiled=True)]
    ppermute x4, waiting for transfers between devices: 47.5 us -> 56.3 us  [swap(): return lax.ppermute(x, 'chan', [(i, i ^ offset) for i in range(z.devices)])]
    pallas_call x1, Pallas kernels: 19.5 us -> 13.3 us  [next(): pl.pallas_call(functools.partial(next_kernel, z, self.scale, chunks), in_...]
    all_to_all x3, waiting for transfers between devices: 15.9 us -> 11.1 us  [exchange(): return lax.all_to_all(x, 'chan', split_axis=0, concat_axis=0, tiled=True)]
    ppermute x4, starting transfers between devices: 5.96 us -> 3.91 us  [swap(): return lax.ppermute(x, 'chan', [(i, i ^ offset) for i in range(z.devices)])]
  transfers between devices with their start and end apart: 7 -> 7, of which waited for: 4 -> 5; matrix products, arithmetic and copies ran while one was open for 4% -> 4% of each run, Pallas kernels for 40% -> 38%
where the time goes in v5:
time: 192 us; the launch traced here: 188 us
  Pallas kernels  88.4 us (46%)
  waiting for transfers between devices  67.3 us (35%)
  starting transfers between devices  21.2 us (11%)
  other arithmetic  5.41 us (3%)
  local copies, waits for them, and re-layouts  4.97 us (3%)
    ppermute x4, waiting for transfers between devices, swap(): return lax.ppermute(x, 'chan', [(i, i ^ offset) for i in range(z.devices)])  56.3 us
    pallas_call x2, Pallas kernels, first(): pl.pallas_call(functools.partial(first_kernel, z, self.scale, chunks, len...  27.9 us
    pallas_call x4, Pallas kernels, receive_call(): pl.pallas_call(functools.partial(receive_kernel, z, step_ch, runs), grid=...  27 us
    pallas_call x1, Pallas kernels, beam_call(): pl.pallas_call(functools.partial(beam_kernel, z), grid_spec=grid_spec, ou...  20.2 us
    all_to_all x3, starting transfers between devices, exchange(): return lax.all_to_all(x, 'chan', split_axis=0, concat_axis=0, tiled=True)  17.3 us
    pallas_call x1, Pallas kernels, next(): pl.pallas_call(functools.partial(next_kernel, z, self.scale, chunks), in_...  13.3 us
    all_to_all x3, waiting for transfers between devices, exchange(): return lax.all_to_all(x, 'chan', split_axis=0, concat_axis=0, tiled=True)  11.1 us
    ppermute x4, starting transfers between devices, swap(): return lax.ppermute(x, 'chan', [(i, i ^ offset) for i in range(z.devices)])  3.91 us
  transfers between devices with their start and end apart: 7, of which 5 were waited for; matrix products, arithmetic and copies ran while one was open for 4% of the time, Pallas kernels for 38%

profile of v5, /device:TPU:5, one launch (start us, length us, event | category | flops | bytes accessed | tf_op | source)
XLA Modules:
  0.0 188.1 jit_solution(4795161437850656411)
XLA Ops:
  0.6 10.6 %filter_spectra.2 = (bf16[3072,2048]{1,0:T(8,128)(2,1)}, bf16[512,3072]{1,0:T(8,128)(2,1)}, bf16[512,3072]{1,0:T(8,128)(2,1)}, bf16[16,8,32,128]{3,2,1,0:T(8,128)(2,1)}) custom-call(s32[1]{0:T(128)} %bitcast.me_ref, bf16[64,104448]{1,0:T(8,128)(2,1)} %h2_ref.3, bf16[64,104448]{1,0:T(8,128)(2,1)} %h2_ref.3, bf16[64,104448]{1,0:T(8,128)(2,1)} %h2_ref.3, ...), custom_call_target="tpu_custom_call" | custom-call | flops 2147483648 | bytes 6000000 | tf_op jit(solution)/shard_map/filter_spectra/pallas_call | solution.py:257
  11.2 6.7 %all-to-all-start.2 = ((bf16[16,8,32,128]{3,2,1,0:T(8,128)(2,1)}), bf16[16,8,32,128]{3,2,1,0:T(8,128)(2,1)S(1)}, u32[]{:S(2)}, u32[]{:S(2)}) async-start(bf16[16,8,32,128]{3,2,1,0:T(8,128)(2,1)} %get-tuple-element.28), calls=%async_computation.2 | async-start | bytes 2097152 | tf_op jit(solution)/shard_map/all_to_all | solution.py:494
  17.9 17.4 %filter_spectra.3 = (bf16[3072,2048]{1,0:T(8,128)(2,1)}, bf16[512,3072]{1,0:T(8,128)(2,1)}, bf16[512,3072]{1,0:T(8,128)(2,1)}, bf16[16,28,32,128]{3,2,1,0:T(8,128)(2,1)}) custom-call(s32[1]{0:T(128)} %bitcast.me_ref, bf16[64,104448]{1,0:T(8,128)(2,1)} %h2_ref.3, ...), custom_call_target="tpu_custom_call", output_to_operand_aliasing={{0}: (8, {}), {1}: (9, {}), {2}: (10, {})} | custom-call | flops 4294967296 | bytes 12000000 | tf_op jit(solution)/shard_map/filter_spectra/pallas_call | solution.py:257
  35.2 13.3 %spectra_next.1 = (bf16[512,3072]{1,0:T(8,128)(2,1)}, bf16[512,3072]{1,0:T(8,128)(2,1)}, bf16[16,28,32,128]{3,2,1,0:T(8,128)(2,1)}, bf16[16,12,32,128]{3,2,1,0:T(8,128)(2,1)}) custom-call(s32[1]{0:T(128)} %bitcast.me_ref, bf16[3072,2048]{1,0:T(8,128)(2,1)} %get-tuple-element.19.filt_ref, ...), custom_call_target="tpu_custom_call", output_to_operand_aliasing={{2}: (4, {})} | custom-call | flops 6442450944 | bytes 18000000 | tf_op jit(solution)/shard_map/spectra_next/pallas_call | solution.py:288
  48.6 1.0 copy-done
  49.6 6.0 %all-to-all-start.1 = ((bf16[16,28,32,128]{3,2,1,0:T(8,128)(2,1)}), bf16[16,28,32,128]{3,2,1,0:T(8,128)(2,1)}, u32[]{:S(2)}, u32[]{:S(2)}) async-start(bf16[16,28,32,128]{3,2,1,0:T(8,128)(2,1)} %get-tuple-element.27), calls=%async_computation.1 | async-start | bytes 7340032 | tf_op jit(solution)/shard_map/all_to_all | solution.py:494
  55.8 1.2 fusion.2
  57.0 1.8 fusion
  58.8 20.2 %beam_sums.1 = f32[16,64,384]{2,1,0:T(8,128)} custom-call(s32[1]{0:T(128)} %bitcast.me_ref, bf16[512,3072]{1,0:T(8,128)(2,1)} %get-tuple-element.22.refs_0_, bf16[512,3072]{1,0:T(8,128)(2,1)} %get-tuple-element.23.refs_1_, bf16[512,3072]{1,0:T(8,128)(2,1)} %get-tuple-element.24.refs_2_, bf16[512,3072]{1,0:T(8,128)(2,1)} %get-tuple-element.25.refs_3_, ...), custom_call_target="tpu_custom_call" | custom-call | flops 20000000000 | bytes 20000000 | tf_op jit(solution)/shard_map/beam_sums/pallas_call | solution.py:474
  78.9 1.2 slice.49
  80.6 1.9 %collective-permute-done = f32[8,64,384]{2,1,0:T(8,128)S(1)} collective-permute-done((f32[8,64,384]{2,1,0:T(8,128)S(1)}, f32[8,64,384]{2,1,0:T(8,128)S(1)}, u32[]{:S(2)}, u32[]{:S(2)}) %collective-permute-start) | collective-permute-done | bytes 786464 | tf_op jit(solution)/shard_map/ppermute | solution.py:490
  82.5 1.2 slice_add_fusion
  83.9 18.4 %collective-permute-done.1 = f32[4,64,384]{2,1,0:T(8,128)S(1)} collective-permute-done((f32[4,64,384]{2,1,0:T(8,128)S(1)}, f32[4,64,384]{2,1,0:T(8,128)S(1)}, u32[]{:S(2)}, u32[]{:S(2)}) %collective-permute-start.1) | collective-permute-done | bytes 393248 | tf_op jit(solution)/shard_map/ppermute | solution.py:490
  102.4 17.8 %collective-permute-done.2 = f32[2,64,384]{2,1,0:T(8,128)S(1)} collective-permute-done((f32[2,64,384]{2,1,0:T(8,128)S(1)}, f32[2,64,384]{2,1,0:T(8,128)S(1)}, u32[]{:S(2)}, u32[]{:S(2)}) %collective-permute-start.2) | collective-permute-done | bytes 196640 | tf_op jit(solution)/shard_map/ppermute | solution.py:490
  120.3 3.3 %collective-permute-start.3 = (f32[1,64,384]{2,1,0:T(8,128)S(1)}, f32[1,64,384]{2,1,0:T(8,128)S(1)}, u32[]{:S(2)}, u32[]{:S(2)}) collective-permute-start(f32[1,64,384]{2,1,0:T(8,128)S(1)} %slice.55), channel_id=1, source_target_pairs={{0,8},{1,9},{2,10},{3,11},{4,12},{5,13},{6,14},{7,15},{8,0},{9,1},... | collective-permute-start | bytes 294920 | tf_op jit(solution)/shard_map/ppermute | solution.py:490
  123.6 18.1 %collective-permute-done.3 = f32[1,64,384]{2,1,0:T(8,128)S(1)} collective-permute-done((f32[1,64,384]{2,1,0:T(8,128)S(1)}, f32[1,64,384]{2,1,0:T(8,128)S(1)}, u32[]{:S(2)}, u32[]{:S(2)}) %collective-permute-start.3) | collective-permute-done | bytes 98336 | tf_op jit(solution)/shard_map/ppermute | solution.py:490
  142.5 4.6 %all-to-all-start = ((bf16[16,12,32,128]{3,2,1,0:T(8,128)(2,1)}), bf16[16,12,32,128]{3,2,1,0:T(8,128)(2,1)S(1)}, u32[]{:S(2)}, u32[]{:S(2)}) async-start(bf16[16,12,32,128]{3,2,1,0:T(8,128)(2,1)} %get-tuple-element.26), calls=%async_computation | async-start | bytes 3145728 | tf_op jit(solution)/shard_map/all_to_all | solution.py:494
  147.1 0.7 broadcast_multiply_fusion
  148.9 7.0 %correlate.4.refs_3_ = f32[64,2,256,256]{3,2,1,0:T(8,128)} custom-call(bf16[16,8,32,128]{3,2,1,0:T(8,128)(2,1)} %copy-done, bf16[16,28,32,128]{3,2,1,0:T(8,128)(2,1)} %all-to-all-done.1.refs_1_.refs_0_.refs_2_, s32[4,256]{1,0:T(4,128)} %get-tuple-element.33.refs_2_), custom_call_target="tpu_custom_call" | custom-call | flops 4000000000 | bytes 10000000 | tf_op jit(solution)/shard_map/correlate/pallas_call | solution.py:387
  155.9 7.0 %correlate.5.refs_4_ = f32[64,2,256,256]{3,2,1,0:T(8,128)} custom-call(bf16[16,8,32,128]{3,2,1,0:T(8,128)(2,1)} %copy-done, bf16[16,28,32,128]{3,2,1,0:T(8,128)(2,1)} %all-to-all-done.1.refs_1_.refs_0_.refs_2_, s32[4,256]{1,0:T(4,128)} %get-tuple-element.34.refs_2_, f32[64,2,256,256]{3,2,1,0:T(8,128)} %correlate.4.refs_3_), custom_call_target="tpu_custom_call", output_to_operand_aliasing={{}: (3, {})} | custom-call | flops 4000000000 | bytes 10000000 | tf_op jit(solution)/shard_map/correlate/pallas_call | solution.py:387
  162.9 6.5 %correlate.6.refs_2_ = f32[64,2,256,256]{3,2,1,0:T(8,128)} custom-call(bf16[16,28,32,128]{3,2,1,0:T(8,128)(2,1)} %all-to-all-done.1.refs_1_.refs_0_.refs_2_, bf16[16,28,32,128]{3,2,1,0:T(8,128)(2,1)} %all-to-all-done.1.refs_1_.refs_0_.refs_2_, bf16[16,28,32,128]{3,2,1,0:T(8,128)(2,1)} %all-to-all-done.1.refs_1_.refs_0_.refs_2_, ...), custom_call_target="tpu_custom_call", output_to_operand_aliasing={{}: (4, {})} | custom-call | flops 4000000000 | bytes 10000000 | tf_op jit(solution)/shard_map/correlate/pallas_call | solution.py:387
  169.4 11.1 %all-to-all-done.refs_0_ = bf16[16,12,32,128]{3,2,1,0:T(8,128)(2,1)S(1)} async-done(((bf16[16,12,32,128]{3,2,1,0:T(8,128)(2,1)}), bf16[16,12,32,128]{3,2,1,0:T(8,128)(2,1)S(1)}, u32[]{:S(2)}, u32[]{:S(2)}) %all-to-all-start) | async-done | bytes 1572896 | tf_op jit(solution)/shard_map/all_to_all | solution.py:494
  180.4 1.2 copy-done.1
  181.6 6.5 %correlate.7 = f32[64,2,256,256]{3,2,1,0:T(8,128)} custom-call(bf16[16,12,32,128]{3,2,1,0:T(8,128)(2,1)} %copy-done.1, s32[4,256]{1,0:T(4,128)} %get-tuple-element.36.refs_1_, f32[64,2,256,256]{3,2,1,0:T(8,128)} %correlate.6.refs_2_), custom_call_target="tpu_custom_call", output_to_operand_aliasing={{}: (2, {})} | custom-call | flops 4000000000 | bytes 10000000 | tf_op jit(solution)/shard_map/correlate/pallas_call | solution.py:387
  (27 shorter events, 2.8 us)
Async XLA Ops:
  11.2 37.3 %all-to-all-start.2 = ((bf16[16,8,32,128]{3,2,1,0:T(8,128)(2,1)}), bf16[16,8,32,128]{3,2,1,0:T(8,128)(2,1)S(1)}, u32[]{:S(2)}, u32[]{:S(2)}) async-start(bf16[16,8,32,128]{3,2,1,0:T(8,128)(2,1)} %get-tuple-element.28), calls=%async_computation.2 | async-start | bytes 2097152 | tf_op jit(solution)/shard_map/all_to_all | solution.py:494
  48.6 1.0 copy-start
  48.6 7.0 %copy-start.2 = (f32[4,64]{1,0:T(4,128)S(1)}, f32[4,64]{1,0:T(4,128)}, u32[]{:S(2)}) copy-start(f32[4,64]{1,0:T(4,128)} %param.9) | copy-start | bytes 3076
  48.6 8.4 %copy-start.3 = (f32[64]{0:T(128)S(1)}, f32[64]{0:T(128)}, u32[]{:S(2)}) copy-start(f32[64]{0:T(128)} %constant.68.clone) | copy-start | bytes 772
  49.6 92.9 %all-to-all-start.1 = ((bf16[16,28,32,128]{3,2,1,0:T(8,128)(2,1)}), bf16[16,28,32,128]{3,2,1,0:T(8,128)(2,1)}, u32[]{:S(2)}, u32[]{:S(2)}) async-start(bf16[16,28,32,128]{3,2,1,0:T(8,128)(2,1)} %get-tuple-element.27), calls=%async_computation.1 | async-start | bytes 7340032 | tf_op jit(solution)/shard_map/all_to_all | solution.py:494
  80.1 2.4 %collective-permute-start = (f32[8,64,384]{2,1,0:T(8,128)S(1)}, f32[8,64,384]{2,1,0:T(8,128)S(1)}, u32[]{:S(2)}, u32[]{:S(2)}) collective-permute-start(f32[8,64,384]{2,1,0:T(8,128)S(1)} %slice.49), channel_id=1, source_target_pairs={{0,1},{1,0},{2,3},{3,2},{4,5},{5,4},{6,7},{7,6},{8,9},{9,8},{10,11... | collective-permute-start | bytes 2359304 | tf_op jit(solution)/shard_map/ppermute | solution.py:490
  83.7 18.5 %collective-permute-start.1 = (f32[4,64,384]{2,1,0:T(8,128)S(1)}, f32[4,64,384]{2,1,0:T(8,128)S(1)}, u32[]{:S(2)}, u32[]{:S(2)}) collective-permute-start(f32[4,64,384]{2,1,0:T(8,128)S(1)} %slice.51), channel_id=1, source_target_pairs={{0,2},{1,3},{2,0},{3,1},{4,6},{5,7},{6,4},{7,5},{8,10},{9,11},{10,... | collective-permute-start | bytes 1179656 | tf_op jit(solution)/shard_map/ppermute | solution.py:490
  102.3 17.9 %collective-permute-start.2 = (f32[2,64,384]{2,1,0:T(8,128)S(1)}, f32[2,64,384]{2,1,0:T(8,128)S(1)}, u32[]{:S(2)}, u32[]{:S(2)}) collective-permute-start(f32[2,64,384]{2,1,0:T(8,128)S(1)} %slice.53), channel_id=1, source_target_pairs={{0,4},{1,5},{2,6},{3,7},{4,0},{5,1},{6,2},{7,3},{8,12},{9,13},{10,... | collective-permute-start | bytes 589832 | tf_op jit(solution)/shard_map/ppermute | solution.py:490
  120.3 21.4 %collective-permute-start.3 = (f32[1,64,384]{2,1,0:T(8,128)S(1)}, f32[1,64,384]{2,1,0:T(8,128)S(1)}, u32[]{:S(2)}, u32[]{:S(2)}) collective-permute-start(f32[1,64,384]{2,1,0:T(8,128)S(1)} %slice.55), channel_id=1, source_target_pairs={{0,8},{1,9},{2,10},{3,11},{4,12},{5,13},{6,14},{7,15},{8,0},{9,1},... | collective-permute-start | bytes 294920 | tf_op jit(solution)/shard_map/ppermute | solution.py:490
  142.5 38.0 %all-to-all-start = ((bf16[16,12,32,128]{3,2,1,0:T(8,128)(2,1)}), bf16[16,12,32,128]{3,2,1,0:T(8,128)(2,1)S(1)}, u32[]{:S(2)}, u32[]{:S(2)}) async-start(bf16[16,12,32,128]{3,2,1,0:T(8,128)(2,1)} %get-tuple-element.26), calls=%async_computation | async-start | bytes 3145728 | tf_op jit(solution)/shard_map/all_to_all | solution.py:494
  180.4 1.2 copy-start.1

commit v6 on v5

--- a/solution.py
+++ b/solution.py
@@ -1,5 +1,4 @@
 import functools
-import math
 
 import jax
 import jax.numpy as jnp
@@ -64,7 +63,7 @@
         self.groups = devices // self.lane_frames
         self.early = min(2, self.chunks)
         if self.chunks == 4:
-            self.parts = (self.steps // 3, self.steps - self.steps // 3)
+            self.parts = (self.steps // 2, self.steps - self.steps // 2)
         else:
             self.early, self.parts = self.chunks, (self.steps,)
 
@@ -90,7 +89,6 @@
     start = frame * z.cap
     few = BAND_CH // 2
     for c, chunk in enumerate(chunks):
-        send_ref, unit = send_refs[c]
         for owner in range(z.devices):
             top = (c * z.devices + owner) * BAND_CH
             rows = [x[top + p : top + p + few] for p in (0, few) for x in spectra]
@@ -113,7 +111,13 @@
                         )
                     )
                 picked = jnp.where(lower, parts[0], parts[1])
-                send_ref[owner, unit + q] = picked.astype(jnp.bfloat16)
+                for parity, (send_ref, unit, stride) in enumerate(send_refs[c]):
+                    half = [
+                        picked[p * BAND_CH + parity * few : p * BAND_CH + parity * few + few]
+                        for p in range(2)
+                    ]
+                    half = jnp.concatenate(half, axis=0).astype(jnp.bfloat16)
+                    send_ref[owner, unit + q * stride] = half
 
 
 def filter_tile(z, main_ref, halo, win_ref, off, f0):
@@ -185,17 +189,21 @@
             filter_fold(z, main_ref, halo, win_ref, filt_ref, tile)
         part = transform(basis_ref, filt_ref, off, off + piece)
         spectra = part if spectra is None else [x + y for x, y in zip(spectra, part)]
-    sends = [(send_ref, c * z.step_quads) for c in range(len(chunks))]
+    sends = []
+    for c in range(len(chunks)):
+        unit = c * 2 * z.step_quads
+        sends.append([(send_ref, unit, 2), (send_ref, unit + 1, 2)])
     emit_spectra(z, scale, chunks, me_ref, spectra, lists_ref, loc_ref, spec_refs, sends)
 
 
 def next_kernel(z, scale, chunks, me_ref, filt_ref, basis_ref, lists_ref, held_ref, *refs):
     spectra = transform(basis_ref, filt_ref, 0, NFFT // 2)
-    count = len(chunks)
-    sends = [(refs[count + c], 0) for c in range(count)]
-    emit_spectra(
-        z, scale, chunks, me_ref, spectra, lists_ref, refs[-1], refs[:count], sends
-    )
+    begun_ref, last_ref = refs[2], refs[3]
+    sends = [
+        [(begun_ref, 0, 2), (begun_ref, 1, 2)],
+        [(begun_ref, 2 * z.step_quads, 1), (last_ref, 0, 1)],
+    ]
+    emit_spectra(z, scale, chunks, me_ref, spectra, lists_ref, refs[-1], refs[:2], sends)
 
 
 def whole_spec(shape):
@@ -226,9 +234,8 @@
             sides.append(rows.reshape(len(chunks) * self.z.rows // 2, NFFT // 2))
         return jnp.asarray(np.stack(sides))
 
-    def message(self, quads):
-        z = self.z
-        return jax.ShapeDtypeStruct((z.devices, quads, z.rows_dev, LANES), jnp.bfloat16)
+    def message(self, units):
+        return jax.ShapeDtypeStruct((self.z.devices, units, BAND_CH, LANES), jnp.bfloat16)
 
     def common(self, steps, chunks):
         z = self.z
@@ -242,7 +249,7 @@
             ),
         )
 
-    def first(self, begin, steps, chunks, basis, quads, held):
+    def first(self, begin, steps, chunks, basis, units, held):
         z = self.z
         count = len(chunks)
 
@@ -251,7 +258,7 @@
                 (z.feed_dev, NFFT), lambda g: (0, z.step_frames * (begin + g + 1) + h)
             )
 
-        send_block = (z.devices, count * z.step_quads, z.rows_dev, LANES)
+        send_block = (z.devices, count * 2 * z.step_quads, BAND_CH, LANES)
         operands = [self.me] + [self.voltages] * 4 + [self.window, basis, self.lists]
         aliases = {len(operands) + i: i for i in range(len(held))}
         return pl.pallas_call(
@@ -272,7 +279,7 @@
             ]
             + [pl.BlockSpec((z.rows, z.step_lanes), lambda g: (0, begin + g))] * count
             + [pl.BlockSpec(send_block, lambda g: (0, g, 0, 0))],
-            out_shape=[self.filt_shape] + [self.spec_shape] * count + [self.message(quads)],
+            out_shape=[self.filt_shape] + [self.spec_shape] * count + [self.message(units)],
             input_output_aliases=aliases,
             name="filter_spectra",
             **self.common(steps, chunks),
@@ -280,10 +287,9 @@
 
     def next(self, chunks, filt, held):
         z = self.z
-        count = len(chunks)
         basis = self.basis(chunks)
-        block = (z.devices, z.step_quads, z.rows_dev, LANES)
-        base = (held.shape[1] - z.quads) // z.step_quads
+        begun = 3 * z.step_quads
+        base = held.shape[1] // begun - z.steps
         operands = [self.me, filt, basis, self.lists, held]
         return pl.pallas_call(
             functools.partial(next_kernel, z, self.scale, chunks),
@@ -294,111 +300,124 @@
                 whole_spec(self.lists.shape),
                 pl.BlockSpec(memory_space=pl.ANY),
             ],
-            out_specs=[pl.BlockSpec((z.rows, z.step_lanes), lambda g: (0, g))] * count
+            out_specs=[pl.BlockSpec((z.rows, z.step_lanes), lambda g: (0, g))] * 2
             + [
-                pl.BlockSpec(block, lambda g: (0, base + g, 0, 0)),
-                pl.BlockSpec(block, lambda g: (0, g, 0, 0)),
+                pl.BlockSpec((z.devices, begun, BAND_CH, LANES), lambda g: (0, base + g, 0, 0)),
+                pl.BlockSpec((z.devices, z.step_quads, BAND_CH, LANES), lambda g: (0, g, 0, 0)),
             ],
-            out_shape=[self.spec_shape] * count
+            out_shape=[self.spec_shape] * 2
             + [self.message(held.shape[1]), self.message(z.quads)],
-            input_output_aliases={4: count},
+            input_output_aliases={4: 2},
             name="spectra_next",
             **self.common(z.steps, chunks),
         )(*operands)
 
 
-def receive_kernel(z, step_ch, runs, *refs):
-    arr_refs, key_ref = refs[: len(runs)], refs[len(runs)]
-    vis_ref, rows_ref = refs[-2], refs[-1]
+def receive_kernel(z, parities, step_pairs, runs, arrays, *refs):
+    arr_refs, key_ref = refs[:arrays], refs[arrays]
+    vis_ref, buf_ref, rows_ref, sems = refs[-4:]
     g = pl.program_id(0)
     lf = z.lane_frames
+    few = BAND_CH // 2
+    depth = buf_ref.shape[1] * BAND_CH
 
     @pl.when(g == 0)
     def _():
+        copies = []
+        place = 0
+        for i, (array, first, count) in enumerate(runs):
+            copy = pltpu.make_async_copy(
+                arr_refs[array].at[:, first : first + count],
+                buf_ref.at[:, place : place + count],
+                sems.at[i],
+            )
+            copy.start()
+            copies.append(copy)
+            place += count
+        for copy in copies:
+            copy.wait()
         slot = lax.broadcasted_iota(jnp.int32, (z.groups * LANES, FSUB), 0)
-        size = z.quads * z.rows_dev
+        lane_group = lax.broadcasted_iota(jnp.int32, (depth, LANES), 1) // z.cap
         for tau in range(lf):
+            tiles = []
+            for big in range(z.groups):
+                tile = buf_ref[big * lf + tau].reshape(depth, LANES)
+                for lane in range(1, lf):
+                    block = buf_ref[big * lf + (lane ^ tau)].reshape(depth, LANES)
+                    tile = jnp.where(lane_group == lane, block, tile)
+                tiles.append(tile)
             pick = jnp.where(slot == key_ref[tau : tau + 1, :], 1.0, 0.0).astype(jnp.bfloat16)
-            parts = []
-            for arr_ref, places in zip(arr_refs, runs):
-                for first, count in places:
-                    depth = count * z.rows_dev
-                    lane_group = lax.broadcasted_iota(jnp.int32, (depth, LANES), 1) // z.cap
-                    tiles = []
-                    for big in range(z.groups):
-                        tile = None
-                        for lane in range(lf):
-                            block = arr_ref[big * lf + (lane ^ tau), first : first + count]
-                            block = block.reshape(depth, LANES)
-                            if tile is None:
-                                tile = block
-                            else:
-                                tile = jnp.where(lane_group == lane, block, tile)
-                        tiles.append(tile)
-                    parts.append(jnp.concatenate(tiles, axis=1))
             rows = jnp.dot(
-                jnp.concatenate(parts, axis=0), pick, preferred_element_type=jnp.float32
+                jnp.concatenate(tiles, axis=1), pick, preferred_element_type=jnp.float32
             )
             for side in range(FSUB // LANES):
-                rows_ref[side, tau * size : (tau + 1) * size, :] = rows[
+                rows_ref[side, tau * depth : (tau + 1) * depth, :] = rows[
                     :, side * LANES : (side + 1) * LANES
                 ]
 
-    for i in range(step_ch):
-        ch = (i % 2) * (BAND_CH // 2) + g * (step_ch // 2) + i // 2
-        halves = []
-        for part in range(2):
-            halves.append(
-                jnp.concatenate(
-                    [
-                        rows_ref[side, pl.ds(ch + part * BAND_CH, FR, stride=z.rows_dev), :]
-                        for side in range(FSUB // LANES)
-                    ],
-                    axis=1,
+    for i in range(step_pairs):
+        for p in range(parities):
+            halves = []
+            for part in range(2):
+                first = p * BAND_CH + part * few + g * step_pairs + i
+                halves.append(
+                    jnp.concatenate(
+                        [
+                            rows_ref[side, pl.ds(first, FR, stride=parities * BAND_CH), :]
+                            for side in range(FSUB // LANES)
+                        ],
+                        axis=1,
+                    )
                 )
-            )
-        real, imag = halves
-        both = jnp.concatenate([real, imag], axis=0)
-        turned = jnp.concatenate([-imag, real], axis=0)
-        right = jnp.concatenate([both, turned], axis=1).astype(jnp.bfloat16)
-        left = both.astype(jnp.bfloat16).T
-        out = jnp.dot(left, right, preferred_element_type=jnp.float32) * (1.0 / FR)
-        vis_ref[i, 0] = out[:, :FSUB]
-        vis_ref[i, 1] = out[:, FSUB:]
-
-
-def receive_call(z, chunk, arrived, key, vis):
-    step_ch = 4
-    steps = BAND_CH // step_ch
-    out_shape = jax.ShapeDtypeStruct((z.chan_dev, 2, FSUB, FSUB), jnp.float32)
-
-    def block_spec(got, quads, at, places):
-        shape = (z.devices, quads) + got.shape[2:]
-        return pl.BlockSpec(shape, lambda g: (0, at, 0, 0))
-
-    in_specs = [block_spec(*x) for x in arrived] + [whole_spec(key.shape)]
-    operands = [x[0] for x in arrived] + [key]
-    runs = [x[3] for x in arrived]
+            real, imag = halves
+            both = jnp.concatenate([real, imag], axis=0)
+            turned = jnp.concatenate([-imag, real], axis=0)
+            right = jnp.concatenate([both, turned], axis=1).astype(jnp.bfloat16)
+            left = both.astype(jnp.bfloat16).T
+            out = jnp.dot(left, right, preferred_element_type=jnp.float32) * (1.0 / FR)
+            vis_ref[i, p, 0] = out[:, :FSUB]
+            vis_ref[i, p, 1] = out[:, FSUB:]
+
+
+def receive_call(z, chunk, parity, arrived, key, vis):
+    parities = 2 if parity is None else 1
+    step_pairs = 4 // parities
+    steps = BAND_CH // 2 // step_pairs
+    at = 0 if parity is None else parity
+    out_shape = jax.ShapeDtypeStruct((z.chan_dev // 2, 2, 2, FSUB, FSUB), jnp.float32)
+    arrays = []
+    runs = []
+    for got, first, count in arrived:
+        if not any(got is x for x in arrays):
+            arrays.append(got)
+        runs.append(([got is x for x in arrays].index(True), first, count))
+    units = sum(count for _, _, count in runs)
+    operands = arrays + [key]
+    in_specs = [pl.BlockSpec(memory_space=pl.ANY)] * len(arrays) + [whole_spec(key.shape)]
     aliases = {}
     if vis is not None:
         in_specs.append(pl.BlockSpec(memory_space=pl.ANY))
         aliases = {len(operands): 0}
         operands.append(vis)
     return pl.pallas_call(
-        functools.partial(receive_kernel, z, step_ch, runs),
+        functools.partial(receive_kernel, z, parities, step_pairs, runs, len(arrays)),
         grid=(steps,),
         in_specs=in_specs,
         out_specs=pl.BlockSpec(
-            (step_ch, 2, FSUB, FSUB), lambda g: (chunk * steps + g, 0, 0, 0)
+            (step_pairs, parities, 2, FSUB, FSUB),
+            lambda g: (chunk * steps + g, at, 0, 0, 0),
         ),
         out_shape=out_shape,
         input_output_aliases=aliases,
         scratch_shapes=[
-            pltpu.VMEM((FSUB // LANES, FR * z.rows_dev, LANES), jnp.float32)
+            pltpu.VMEM((z.devices, units, BAND_CH, LANES), jnp.bfloat16),
+            pltpu.VMEM((FSUB // LANES, z.lane_frames * units * BAND_CH, LANES), jnp.float32),
+            pltpu.SemaphoreType.DMA((len(runs),)),
         ],
-        compiler_params=pltpu.CompilerParams(vmem_limit_bytes=VMEM),
+        compiler_params=pltpu.CompilerParams(vmem_limit_bytes=VMEM // 2),
         cost_estimate=pl.CostEstimate(
-            flops=4_000_000_000, bytes_accessed=10_000_000, transcendentals=0
+            flops=2_000_000_000 * parities, bytes_accessed=5_000_000 * parities,
+            transcendentals=0,
         ),
         name="correlate",
     )(*operands)
@@ -513,30 +532,28 @@
     calls = Spectra(z, me_array, voltages, band_feeds)
     early = list(range(z.early))
     basis = calls.basis(early)
-    step = z.early * z.step_quads
+    share = 2 * z.step_quads
+    step = z.early * share
     arrived = [[] for _ in range(z.chunks)]
-
-    def early_places(got, steps):
-        for c in early:
-            places = [(g * step + c * z.step_quads, z.step_quads) for g in range(steps)]
-            arrived[c].append((got, steps * step, 0, places))
-
     steps = z.parts[0]
     filt, *spectra, send = calls.first(0, steps, early, basis, steps * step, [])
-    early_places(exchange(send), steps)
+    got = exchange(send)
+    for c in early:
+        arrived[c] += [(got, g * step + c * share, share) for g in range(steps)]
     if len(z.parts) > 1:
         begin, steps = steps, z.parts[1]
         base = steps * step
+        begun = 3 * z.step_quads
         filt, *spectra, send = calls.first(
-            begin, steps, early, basis, base + z.quads, [filt, *spectra]
+            begin, steps, early, basis, base + z.steps * begun, [filt, *spectra]
         )
         *more, send, last = calls.next([z.chunks - 2, z.chunks - 1], filt, send)
         spectra = spectra + more
         got = exchange(send)
-        early_places(got, steps)
-        block = math.gcd(base, z.quads)
-        for i in range(z.quads // block):
-            arrived[-2].append((got, block, base // block + i, [(0, block)]))
+        for c in early:
+            arrived[c] += [(got, g * step + c * share, share) for g in range(steps)]
+        arrived[-2] += [(got, base + g * begun, share) for g in range(z.steps)]
+        arrived[-1] += [(got, base + g * begun + share, z.step_quads) for g in range(z.steps)]
 
     beams, bit = beam_call(z, me_array, spectra, delays), 1
     while beams.shape[0] > 1:
@@ -544,14 +561,17 @@
         beams, bit = beams[:half] + swap(z, beams[half:], bit), 2 * bit
     beams = beams.reshape(z.chunks, 2, BAND_CH // 2, 2 * BEAMS * FR)
     beams = jnp.swapaxes(beams, 1, 2).reshape(z.chan_dev, 2 * BEAMS * FR)
+    wanted = [(k, None, arrived[k]) for k in range(z.chunks)]
     if len(z.parts) > 1:
         last, beams = lax.optimization_barrier((last, beams))
-        arrived[-1].append((exchange(last), z.quads, 0, [(0, z.quads)]))
+        got = exchange(last)
+        k = z.chunks - 1
+        wanted = wanted[:-1] + [(k, 0, arrived[k]), (k, 1, [(got, 0, z.quads)])]
 
     vis = None
-    for k in range(z.chunks):
-        vis = receive_call(z, k, arrived[k], take_key[k], vis)
-    return (vis, beams)
+    for k, parity, runs in wanted:
+        vis = receive_call(z, k, parity, runs, take_key[k], vis)
+    return (vis.reshape(z.chan_dev, 2, FSUB, FSUB), beams)
 
 
 def solution(mesh):

time: 192 us -> 188 us (0.979); the launches traced: 188 us -> 186 us
  local copies, waits for them, and re-layouts: 4.97 us -> 2.19 us
    all_to_all x3, waiting for transfers between devices: 11.1 us -> 6.07 us  [exchange(): return lax.all_to_all(x, 'chan', split_axis=0, concat_axis=0, tiled=True)]
    ppermute x4, waiting for transfers between devices: 56.3 us -> 60.8 us  [swap(): return lax.ppermute(x, 'chan', [(i, i ^ offset) for i in range(z.devices)])]
    unnamed x8 -> x4, local copies, waits for them, and re-layouts: 2.17 us -> 0.01 us
    pallas_call x4 -> x5, Pallas kernels: 27 us -> 26.5 us  [receive_call(): pl.pallas_call(functools.partial(receive_kernel, z, parities, step_pairs,...]
where the time goes in v6:
time: 188 us; the launch traced here: 186 us
  Pallas kernels  87.9 us (47%)
  waiting for transfers between devices  66.9 us (36%)
  starting transfers between devices  23 us (12%)
  other arithmetic  5.4 us (3%)
  local copies, waits for them, and re-layouts  2.19 us (1%)
    ppermute x4, waiting for transfers between devices, swap(): return lax.ppermute(x, 'chan', [(i, i ^ offset) for i in range(z.devices)])  60.8 us
    pallas_call x2, Pallas kernels, first(): pl.pallas_call(functools.partial(first_kernel, z, self.scale, chunks, len...  27.9 us
    pallas_call x5, Pallas kernels, receive_call(): pl.pallas_call(functools.partial(receive_kernel, z, parities, step_pairs,...  26.5 us
    pallas_call x1, Pallas kernels, beam_call(): pl.pallas_call(functools.partial(beam_kernel, z), grid_spec=grid_spec, ou...  20.2 us
    all_to_all x3, starting transfers between devices, exchange(): return lax.all_to_all(x, 'chan', split_axis=0, concat_axis=0, tiled=True)  19.1 us
    pallas_call x1, Pallas kernels, next(): pl.pallas_call(functools.partial(next_kernel, z, self.scale, chunks), in_...  13.3 us
    all_to_all x3, waiting for transfers between devices, exchange(): return lax.all_to_all(x, 'chan', split_axis=0, concat_axis=0, tiled=True)  6.07 us
    ppermute x4, starting transfers between devices, swap(): return lax.ppermute(x, 'chan', [(i, i ^ offset) for i in range(z.devices)])  3.86 us
  transfers between devices with their start and end apart: 7, of which 5 were waited for; matrix products, arithmetic and copies ran while one was open for 4% of the time, Pallas kernels for 38%

profile of v6, /device:TPU:5, one launch (start us, length us, event | category | flops | bytes accessed | tf_op | source)
XLA Modules:
  0.0 186.2 jit_solution(4209605930370044633)
XLA Ops:
  0.6 14.0 %filter_spectra.2 = (bf16[3072,2048]{1,0:T(8,128)(2,1)}, bf16[512,3072]{1,0:T(8,128)(2,1)}, bf16[512,3072]{1,0:T(8,128)(2,1)}, bf16[16,24,16,128]{3,2,1,0:T(8,128)(2,1)}) custom-call(s32[1]{0:T(128)} %bitcast.me_ref, bf16[64,104448]{1,0:T(8,128)(2,1)} %h2_ref.3, bf16[64,104448]{1,0:T(8,128)(2,1)} %h2_ref.3, bf16[64,104448]{1,0:T(8,128)(2,1)} %h2_ref.3, ...), custom_call_target="tpu_custom_call" | custom-call | flops 3221225472 | bytes 9000000 | tf_op jit(solution)/shard_map/filter_spectra/pallas_call | solution.py:264
  14.6 6.7 %all-to-all-start.2 = ((bf16[16,24,16,128]{3,2,1,0:T(8,128)(2,1)}), bf16[16,24,16,128]{3,2,1,0:T(8,128)(2,1)S(1)}, u32[]{:S(2)}, u32[]{:S(2)}) async-start(bf16[16,24,16,128]{3,2,1,0:T(8,128)(2,1)} %get-tuple-element.28), calls=%async_computation.2 | async-start | bytes 3145728 | tf_op jit(solution)/shard_map/all_to_all | solution.py:513
  21.3 14.0 %filter_spectra.3 = (bf16[3072,2048]{1,0:T(8,128)(2,1)}, bf16[512,3072]{1,0:T(8,128)(2,1)}, bf16[512,3072]{1,0:T(8,128)(2,1)}, bf16[16,60,16,128]{3,2,1,0:T(8,128)(2,1)}) custom-call(s32[1]{0:T(128)} %bitcast.me_ref, bf16[64,104448]{1,0:T(8,128)(2,1)} %h2_ref.3, ...), custom_call_target="tpu_custom_call", output_to_operand_aliasing={{0}: (8, {}), {1}: (9, {}), {2}: (10, {})} | custom-call | flops 3221225472 | bytes 9000000 | tf_op jit(solution)/shard_map/filter_spectra/pallas_call | solution.py:264
  35.2 13.3 %spectra_next.1 = (bf16[512,3072]{1,0:T(8,128)(2,1)}, bf16[512,3072]{1,0:T(8,128)(2,1)}, bf16[16,60,16,128]{3,2,1,0:T(8,128)(2,1)}, bf16[16,12,16,128]{3,2,1,0:T(8,128)(2,1)}) custom-call(s32[1]{0:T(128)} %bitcast.me_ref, bf16[3072,2048]{1,0:T(8,128)(2,1)} %get-tuple-element.19.filt_ref, ...), custom_call_target="tpu_custom_call", output_to_operand_aliasing={{2}: (4, {})} | custom-call | flops 6442450944 | bytes 18000000 | tf_op jit(solution)/shard_map/spectra_next/pallas_call | solution.py:294
  48.5 6.1 %all-to-all-done.2.refs_0_ = bf16[16,24,16,128]{3,2,1,0:T(8,128)(2,1)S(1)} async-done(((bf16[16,24,16,128]{3,2,1,0:T(8,128)(2,1)}), bf16[16,24,16,128]{3,2,1,0:T(8,128)(2,1)S(1)}, u32[]{:S(2)}, u32[]{:S(2)}) %all-to-all-start.2) | async-done | bytes 1572896 | tf_op jit(solution)/shard_map/all_to_all | solution.py:513
  54.6 7.9 %all-to-all-start.1 = ((bf16[16,60,16,128]{3,2,1,0:T(8,128)(2,1)}), bf16[16,60,16,128]{3,2,1,0:T(8,128)(2,1)}, u32[]{:S(2)}, u32[]{:S(2)}) async-start(bf16[16,60,16,128]{3,2,1,0:T(8,128)(2,1)} %get-tuple-element.27), calls=%async_computation.1 | async-start | bytes 7864320 | tf_op jit(solution)/shard_map/all_to_all | solution.py:513
  62.7 1.2 fusion.2
  63.9 1.8 fusion
  65.7 20.2 %beam_sums.1 = f32[16,64,384]{2,1,0:T(8,128)} custom-call(s32[1]{0:T(128)} %bitcast.me_ref, bf16[512,3072]{1,0:T(8,128)(2,1)} %get-tuple-element.22.refs_0_, bf16[512,3072]{1,0:T(8,128)(2,1)} %get-tuple-element.23.refs_1_, bf16[512,3072]{1,0:T(8,128)(2,1)} %get-tuple-element.24.refs_2_, bf16[512,3072]{1,0:T(8,128)(2,1)} %get-tuple-element.25.refs_3_, ...), custom_call_target="tpu_custom_call" | custom-call | flops 20000000000 | bytes 20000000 | tf_op jit(solution)/shard_map/beam_sums/pallas_call | solution.py:493
  85.8 1.2 slice.50
  87.5 1.9 %collective-permute-done = f32[8,64,384]{2,1,0:T(8,128)S(1)} collective-permute-done((f32[8,64,384]{2,1,0:T(8,128)S(1)}, f32[8,64,384]{2,1,0:T(8,128)S(1)}, u32[]{:S(2)}, u32[]{:S(2)}) %collective-permute-start) | collective-permute-done | bytes 786464 | tf_op jit(solution)/shard_map/ppermute | solution.py:509
  89.4 1.2 slice_add_fusion
  90.8 0.7 broadcast_multiply_fusion
  91.9 19.6 %collective-permute-done.1 = f32[4,64,384]{2,1,0:T(8,128)S(1)} collective-permute-done((f32[4,64,384]{2,1,0:T(8,128)S(1)}, f32[4,64,384]{2,1,0:T(8,128)S(1)}, u32[]{:S(2)}, u32[]{:S(2)}) %collective-permute-start.1) | collective-permute-done | bytes 393248 | tf_op jit(solution)/shard_map/ppermute | solution.py:509
  111.7 19.7 %collective-permute-done.2 = f32[2,64,384]{2,1,0:T(8,128)S(1)} collective-permute-done((f32[2,64,384]{2,1,0:T(8,128)S(1)}, f32[2,64,384]{2,1,0:T(8,128)S(1)}, u32[]{:S(2)}, u32[]{:S(2)}) %collective-permute-start.2) | collective-permute-done | bytes 196640 | tf_op jit(solution)/shard_map/ppermute | solution.py:509
  131.5 3.2 %collective-permute-start.3 = (f32[1,64,384]{2,1,0:T(8,128)S(1)}, f32[1,64,384]{2,1,0:T(8,128)S(1)}, u32[]{:S(2)}, u32[]{:S(2)}) collective-permute-start(f32[1,64,384]{2,1,0:T(8,128)S(1)} %slice.56), channel_id=1, source_target_pairs={{0,8},{1,9},{2,10},{3,11},{4,12},{5,13},{6,14},{7,15},{8,0},{9,1},... | collective-permute-start | bytes 294920 | tf_op jit(solution)/shard_map/ppermute | solution.py:509
  134.7 19.5 %collective-permute-done.3 = f32[1,64,384]{2,1,0:T(8,128)S(1)} collective-permute-done((f32[1,64,384]{2,1,0:T(8,128)S(1)}, f32[1,64,384]{2,1,0:T(8,128)S(1)}, u32[]{:S(2)}, u32[]{:S(2)}) %collective-permute-start.3) | collective-permute-done | bytes 98336 | tf_op jit(solution)/shard_map/ppermute | solution.py:509
  154.3 0.7 reshape.32
  155.0 4.6 %all-to-all-start = ((bf16[16,12,16,128]{3,2,1,0:T(8,128)(2,1)}), bf16[16,12,16,128]{3,2,1,0:T(8,128)(2,1)S(1)}, u32[]{:S(2)}, u32[]{:S(2)}) async-start(bf16[16,12,16,128]{3,2,1,0:T(8,128)(2,1)} %get-tuple-element.26), calls=%async_computation | async-start | bytes 1572864 | tf_op jit(solution)/shard_map/all_to_all | solution.py:513
  159.6 6.3 %correlate.5.refs_3_ = f32[32,2,2,256,256]{4,3,2,1,0:T(8,128)} custom-call(bf16[16,24,16,128]{3,2,1,0:T(8,128)(2,1)S(1)} %all-to-all-done.2.refs_0_, bf16[16,60,16,128]{3,2,1,0:T(8,128)(2,1)} %all-to-all-done.1.refs_1_.refs_0_, s32[4,256]{1,0:T(4,128)S(1)} %get-tuple-element.33.refs_2_), custom_call_target="tpu_custom_call" | custom-call | flops 4000000000 | bytes 10000000 | tf_op jit(solution)/shard_map/correlate/pallas_call | solution.py:402
  165.9 6.3 %correlate.6.refs_2_ = f32[32,2,2,256,256]{4,3,2,1,0:T(8,128)} custom-call(bf16[16,24,16,128]{3,2,1,0:T(8,128)(2,1)S(1)} %all-to-all-done.2.refs_0_, bf16[16,60,16,128]{3,2,1,0:T(8,128)(2,1)} %all-to-all-done.1.refs_1_.refs_0_, s32[4,256]{1,0:T(4,128)S(1)} %get-tuple-element.34.refs_2_, ...), custom_call_target="tpu_custom_call", output_to_operand_aliasing={{}: (3, {})} | custom-call | flops 4000000000 | bytes 10000000 | tf_op jit(solution)/shard_map/correlate/pallas_call | solution.py:402
  172.3 6.5 %correlate.7.refs_2_ = f32[32,2,2,256,256]{4,3,2,1,0:T(8,128)} custom-call(bf16[16,60,16,128]{3,2,1,0:T(8,128)(2,1)} %all-to-all-done.1.refs_1_.refs_0_, s32[4,256]{1,0:T(4,128)S(1)} %get-tuple-element.35.refs_1_, f32[32,2,2,256,256]{4,3,2,1,0:T(8,128)} %correlate.6.refs_2_), custom_call_target="tpu_custom_call", output_to_operand_aliasing={{}: (2, {})} | custom-call | flops 4000000000 | bytes 10000000 | tf_op jit(solution)/shard_map/correlate/pallas_call | solution.py:402
  178.8 4.2 %correlate.8.refs_2_ = f32[32,2,2,256,256]{4,3,2,1,0:T(8,128)} custom-call(bf16[16,60,16,128]{3,2,1,0:T(8,128)(2,1)} %all-to-all-done.1.refs_1_.refs_0_, s32[4,256]{1,0:T(4,128)S(1)} %get-tuple-element.36.refs_1_, f32[32,2,2,256,256]{4,3,2,1,0:T(8,128)} %correlate.7.refs_2_), custom_call_target="tpu_custom_call", output_to_operand_aliasing={{}: (2, {})} | custom-call | flops 2000000000 | bytes 5000000 | tf_op jit(solution)/shard_map/correlate/pallas_call | solution.py:402
  183.1 3.0 %correlate.9 = f32[32,2,2,256,256]{4,3,2,1,0:T(8,128)} custom-call(bf16[16,12,16,128]{3,2,1,0:T(8,128)(2,1)S(1)} %all-to-all-done.refs_0_, s32[4,256]{1,0:T(4,128)S(1)} %get-tuple-element.36.refs_1_, f32[32,2,2,256,256]{4,3,2,1,0:T(8,128)} %correlate.8.refs_2_), custom_call_target="tpu_custom_call", output_to_operand_aliasing={{}: (2, {})} | custom-call | flops 2000000000 | bytes 5000000 | tf_op jit(solution)/shard_map/correlate/pallas_call | solution.py:402
  (24 shorter events, 1.4 us)
Async XLA Ops:
  14.6 40.0 %all-to-all-start.2 = ((bf16[16,24,16,128]{3,2,1,0:T(8,128)(2,1)}), bf16[16,24,16,128]{3,2,1,0:T(8,128)(2,1)S(1)}, u32[]{:S(2)}, u32[]{:S(2)}) async-start(bf16[16,24,16,128]{3,2,1,0:T(8,128)(2,1)} %get-tuple-element.28), calls=%async_computation.2 | async-start | bytes 3145728 | tf_op jit(solution)/shard_map/all_to_all | solution.py:513
  54.6 7.9 %copy-start = (f32[4,64]{1,0:T(4,128)S(1)}, f32[4,64]{1,0:T(4,128)}, u32[]{:S(2)}) copy-start(f32[4,64]{1,0:T(4,128)} %param.9) | copy-start | bytes 3076
  54.6 9.3 %copy-start.1 = (f32[64]{0:T(128)S(1)}, f32[64]{0:T(128)}, u32[]{:S(2)}) copy-start(f32[64]{0:T(128)} %constant.68.clone) | copy-start | bytes 772
  54.6 100.4 %all-to-all-start.1 = ((bf16[16,60,16,128]{3,2,1,0:T(8,128)(2,1)}), bf16[16,60,16,128]{3,2,1,0:T(8,128)(2,1)}, u32[]{:S(2)}, u32[]{:S(2)}) async-start(bf16[16,60,16,128]{3,2,1,0:T(8,128)(2,1)} %get-tuple-element.27), calls=%async_computation.1 | async-start | bytes 7864320 | tf_op jit(solution)/shard_map/all_to_all | solution.py:513
  87.0 2.4 %collective-permute-start = (f32[8,64,384]{2,1,0:T(8,128)S(1)}, f32[8,64,384]{2,1,0:T(8,128)S(1)}, u32[]{:S(2)}, u32[]{:S(2)}) collective-permute-start(f32[8,64,384]{2,1,0:T(8,128)S(1)} %slice.50), channel_id=1, source_target_pairs={{0,1},{1,0},{2,3},{3,2},{4,5},{5,4},{6,7},{7,6},{8,9},{9,8},{10,11... | collective-permute-start | bytes 2359304 | tf_op jit(solution)/shard_map/ppermute | solution.py:509
  90.7 20.9 %collective-permute-start.1 = (f32[4,64,384]{2,1,0:T(8,128)S(1)}, f32[4,64,384]{2,1,0:T(8,128)S(1)}, u32[]{:S(2)}, u32[]{:S(2)}) collective-permute-start(f32[4,64,384]{2,1,0:T(8,128)S(1)} %slice.52), channel_id=1, source_target_pairs={{0,2},{1,3},{2,0},{3,1},{4,6},{5,7},{6,4},{7,5},{8,10},{9,11},{10,... | collective-permute-start | bytes 1179656 | tf_op jit(solution)/shard_map/ppermute | solution.py:509
  111.6 19.8 %collective-permute-start.2 = (f32[2,64,384]{2,1,0:T(8,128)S(1)}, f32[2,64,384]{2,1,0:T(8,128)S(1)}, u32[]{:S(2)}, u32[]{:S(2)}) collective-permute-start(f32[2,64,384]{2,1,0:T(8,128)S(1)} %slice.54), channel_id=1, source_target_pairs={{0,4},{1,5},{2,6},{3,7},{4,0},{5,1},{6,2},{7,3},{8,12},{9,13},{10,... | collective-permute-start | bytes 589832 | tf_op jit(solution)/shard_map/ppermute | solution.py:509
  131.5 22.7 %collective-permute-start.3 = (f32[1,64,384]{2,1,0:T(8,128)S(1)}, f32[1,64,384]{2,1,0:T(8,128)S(1)}, u32[]{:S(2)}, u32[]{:S(2)}) collective-permute-start(f32[1,64,384]{2,1,0:T(8,128)S(1)} %slice.56), channel_id=1, source_target_pairs={{0,8},{1,9},{2,10},{3,11},{4,12},{5,13},{6,14},{7,15},{8,0},{9,1},... | collective-permute-start | bytes 294920 | tf_op jit(solution)/shard_map/ppermute | solution.py:509
  155.0 28.1 %all-to-all-start = ((bf16[16,12,16,128]{3,2,1,0:T(8,128)(2,1)}), bf16[16,12,16,128]{3,2,1,0:T(8,128)(2,1)S(1)}, u32[]{:S(2)}, u32[]{:S(2)}) async-start(bf16[16,12,16,128]{3,2,1,0:T(8,128)(2,1)} %get-tuple-element.26), calls=%async_computation | async-start | bytes 1572864 | tf_op jit(solution)/shard_map/all_to_all | solution.py:513

commit v7 on v6

--- a/solution.py
+++ b/solution.py
@@ -319,34 +319,53 @@
     g = pl.program_id(0)
     lf = z.lane_frames
     few = BAND_CH // 2
-    depth = buf_ref.shape[1] * BAND_CH
-
-    @pl.when(g == 0)
+    steps = few // step_pairs
+    depth = buf_ref.shape[2] * BAND_CH
+    slots = buf_ref.shape[0]
+    at = g % steps
+
+    def copies(c):
+        place = 0
+        out = []
+        for i, (array, first, count) in enumerate(runs[c]):
+            out.append(
+                pltpu.make_async_copy(
+                    arr_refs[array].at[:, first : first + count],
+                    buf_ref.at[c % slots, :, place : place + count],
+                    sems.at[c % slots, i],
+                )
+            )
+            place += count
+        return out
+
+    for c in range(len(runs)):
+
+        @pl.when(g == c * steps)
+        def _():
+            if c == 0:
+                for copy in copies(c):
+                    copy.start()
+            for copy in copies(c):
+                copy.wait()
+            if c + 1 < len(runs):
+                for copy in copies(c + 1):
+                    copy.start()
+
+    @pl.when(at == 0)
     def _():
-        copies = []
-        place = 0
-        for i, (array, first, count) in enumerate(runs):
-            copy = pltpu.make_async_copy(
-                arr_refs[array].at[:, first : first + count],
-                buf_ref.at[:, place : place + count],
-                sems.at[i],
-            )
-            copy.start()
-            copies.append(copy)
-            place += count
-        for copy in copies:
-            copy.wait()
+        c = g // steps
         slot = lax.broadcasted_iota(jnp.int32, (z.groups * LANES, FSUB), 0)
         lane_group = lax.broadcasted_iota(jnp.int32, (depth, LANES), 1) // z.cap
         for tau in range(lf):
             tiles = []
             for big in range(z.groups):
-                tile = buf_ref[big * lf + tau].reshape(depth, LANES)
+                tile = buf_ref[c % slots, big * lf + tau].reshape(depth, LANES)
                 for lane in range(1, lf):
-                    block = buf_ref[big * lf + (lane ^ tau)].reshape(depth, LANES)
+                    block = buf_ref[c % slots, big * lf + (lane ^ tau)].reshape(depth, LANES)
                     tile = jnp.where(lane_group == lane, block, tile)
                 tiles.append(tile)
-            pick = jnp.where(slot == key_ref[tau : tau + 1, :], 1.0, 0.0).astype(jnp.bfloat16)
+            key = key_ref[c, tau : tau + 1, :]
+            pick = jnp.where(slot == key, 1.0, 0.0).astype(jnp.bfloat16)
             rows = jnp.dot(
                 jnp.concatenate(tiles, axis=1), pick, preferred_element_type=jnp.float32
             )
@@ -355,31 +374,36 @@
                     :, side * LANES : (side + 1) * LANES
                 ]
 
-    for i in range(step_pairs):
-        for p in range(parities):
-            halves = []
-            for part in range(2):
-                first = p * BAND_CH + part * few + g * step_pairs + i
-                halves.append(
-                    jnp.concatenate(
-                        [
-                            rows_ref[side, pl.ds(first, FR, stride=parities * BAND_CH), :]
-                            for side in range(FSUB // LANES)
-                        ],
-                        axis=1,
-                    )
+    todo = [(i, p) for i in range(step_pairs) for p in range(parities)]
+    operands = []
+    for i, p in todo:
+        halves = []
+        for part in range(2):
+            first = p * BAND_CH + part * few + at * step_pairs + i
+            halves.append(
+                jnp.concatenate(
+                    [
+                        rows_ref[side, pl.ds(first, FR, stride=parities * BAND_CH), :]
+                        for side in range(FSUB // LANES)
+                    ],
+                    axis=1,
                 )
-            real, imag = halves
-            both = jnp.concatenate([real, imag], axis=0)
-            turned = jnp.concatenate([-imag, real], axis=0)
-            right = jnp.concatenate([both, turned], axis=1).astype(jnp.bfloat16)
-            left = both.astype(jnp.bfloat16).T
-            out = jnp.dot(left, right, preferred_element_type=jnp.float32) * (1.0 / FR)
-            vis_ref[i, p, 0] = out[:, :FSUB]
-            vis_ref[i, p, 1] = out[:, FSUB:]
-
-
-def receive_call(z, chunk, parity, arrived, key, vis):
+            )
+        real, imag = halves
+        both = jnp.concatenate([real, imag], axis=0)
+        turned = jnp.concatenate([-imag, real], axis=0)
+        right = jnp.concatenate([both, turned], axis=1).astype(jnp.bfloat16)
+        operands.append((both.astype(jnp.bfloat16).T, right))
+    outs = [
+        jnp.dot(left, right, preferred_element_type=jnp.float32) for left, right in operands
+    ]
+    for (i, p), out in zip(todo, outs):
+        out = out * (1.0 / FR)
+        vis_ref[i, p, 0] = out[:, :FSUB]
+        vis_ref[i, p, 1] = out[:, FSUB:]
+
+
+def receive_call(z, chunk, parity, arrived, keys, vis):
     parities = 2 if parity is None else 1
     step_pairs = 4 // parities
     steps = BAND_CH // 2 // step_pairs
@@ -387,21 +411,25 @@
     out_shape = jax.ShapeDtypeStruct((z.chan_dev // 2, 2, 2, FSUB, FSUB), jnp.float32)
     arrays = []
     runs = []
-    for got, first, count in arrived:
-        if not any(got is x for x in arrays):
-            arrays.append(got)
-        runs.append(([got is x for x in arrays].index(True), first, count))
-    units = sum(count for _, _, count in runs)
-    operands = arrays + [key]
-    in_specs = [pl.BlockSpec(memory_space=pl.ANY)] * len(arrays) + [whole_spec(key.shape)]
+    for one in arrived:
+        runs.append([])
+        for got, first, count in one:
+            if not any(got is x for x in arrays):
+                arrays.append(got)
+            runs[-1].append(([got is x for x in arrays].index(True), first, count))
+    units = sum(count for _, _, count in runs[0])
+    slots = min(2, len(runs))
+    operands = arrays + [keys]
+    in_specs = [pl.BlockSpec(memory_space=pl.ANY)] * len(arrays) + [whole_spec(keys.shape)]
     aliases = {}
     if vis is not None:
         in_specs.append(pl.BlockSpec(memory_space=pl.ANY))
         aliases = {len(operands): 0}
         operands.append(vis)
+    share = parities * len(runs)
     return pl.pallas_call(
         functools.partial(receive_kernel, z, parities, step_pairs, runs, len(arrays)),
-        grid=(steps,),
+        grid=(len(runs) * steps,),
         in_specs=in_specs,
         out_specs=pl.BlockSpec(
             (step_pairs, parities, 2, FSUB, FSUB),
@@ -410,14 +438,13 @@
         out_shape=out_shape,
         input_output_aliases=aliases,
         scratch_shapes=[
-            pltpu.VMEM((z.devices, units, BAND_CH, LANES), jnp.bfloat16),
+            pltpu.VMEM((slots, z.devices, units, BAND_CH, LANES), jnp.bfloat16),
             pltpu.VMEM((FSUB // LANES, z.lane_frames * units * BAND_CH, LANES), jnp.float32),
-            pltpu.SemaphoreType.DMA((len(runs),)),
+            pltpu.SemaphoreType.DMA((slots, max(len(x) for x in runs))),
         ],
         compiler_params=pltpu.CompilerParams(vmem_limit_bytes=VMEM // 2),
         cost_estimate=pl.CostEstimate(
-            flops=2_000_000_000 * parities, bytes_accessed=5_000_000 * parities,
-            transcendentals=0,
+            flops=2_000_000_000 * share, bytes_accessed=5_000_000 * share, transcendentals=0
         ),
         name="correlate",
     )(*operands)
@@ -561,16 +588,15 @@
         beams, bit = beams[:half] + swap(z, beams[half:], bit), 2 * bit
     beams = beams.reshape(z.chunks, 2, BAND_CH // 2, 2 * BEAMS * FR)
     beams = jnp.swapaxes(beams, 1, 2).reshape(z.chan_dev, 2 * BEAMS * FR)
-    wanted = [(k, None, arrived[k]) for k in range(z.chunks)]
     if len(z.parts) > 1:
         last, beams = lax.optimization_barrier((last, beams))
         got = exchange(last)
         k = z.chunks - 1
-        wanted = wanted[:-1] + [(k, 0, arrived[k]), (k, 1, [(got, 0, z.quads)])]
-
-    vis = None
-    for k, parity, runs in wanted:
-        vis = receive_call(z, k, parity, runs, take_key[k], vis)
+        vis = receive_call(z, 0, None, arrived[:k], take_key[:k], None)
+        vis = receive_call(z, k, 0, arrived[k:], take_key[k:], vis)
+        vis = receive_call(z, k, 1, [[(got, 0, z.quads)]], take_key[k:], vis)
+    else:
+        vis = receive_call(z, 0, None, arrived, take_key, None)
     return (vis.reshape(z.chan_dev, 2, FSUB, FSUB), beams)
 
 

time: 188 us -> 184 us (0.979)
  Pallas kernels: 87.9 us -> 84 us
    pallas_call x5 -> x3, Pallas kernels: 26.5 us -> 22.6 us  [receive_call(): pl.pallas_call(functools.partial(receive_kernel, z, parities, step_pairs,...]
  transfers between devices with their start and end apart: 7 -> 7, of which waited for: 5 -> 5; matrix products, arithmetic and copies ran while one was open for 4% -> 4% of each run, Pallas kernels for 38% -> 37%
where the time goes in v7:
time: 184 us; the launch traced here: 182 us
  Pallas kernels  84 us (46%)
  waiting for transfers between devices  66.8 us (36%)
  starting transfers between devices  23 us (12%)
  other arithmetic  5.44 us (3%)
  local copies, waits for them, and re-layouts  2.19 us (1%)
    ppermute x4, waiting for transfers between devices, swap(): return lax.ppermute(x, 'chan', [(i, i ^ offset) for i in range(z.devices)])  60.8 us
    pallas_call x2, Pallas kernels, first(): pl.pallas_call(functools.partial(first_kernel, z, self.scale, chunks, len...  28 us
    pallas_call x3, Pallas kernels, receive_call(): pl.pallas_call(functools.partial(receive_kernel, z, parities, step_pairs,...  22.6 us
    pallas_call x1, Pallas kernels, beam_call(): pl.pallas_call(functools.partial(beam_kernel, z), grid_spec=grid_spec, ou...  20.2 us
    all_to_all x3, starting transfers between devices, exchange(): return lax.all_to_all(x, 'chan', split_axis=0, concat_axis=0, tiled=True)  19.1 us
    pallas_call x1, Pallas kernels, next(): pl.pallas_call(functools.partial(next_kernel, z, self.scale, chunks), in_...  13.3 us
    all_to_all x3, waiting for transfers between devices, exchange(): return lax.all_to_all(x, 'chan', split_axis=0, concat_axis=0, tiled=True)  6.06 us
    ppermute x4, starting transfers between devices, swap(): return lax.ppermute(x, 'chan', [(i, i ^ offset) for i in range(z.devices)])  3.86 us
  transfers between devices with their start and end apart: 7, of which 5 were waited for; matrix products, arithmetic and copies ran while one was open for 4% of the time, Pallas kernels for 37%

profile of v7, /device:TPU:5, one launch (start us, length us, event | category | flops | bytes accessed | tf_op | source)
XLA Modules:
  0.0 182.4 jit_solution(18117283951994177739)
XLA Ops:
  0.6 14.0 %filter_spectra.2 = (bf16[3072,2048]{1,0:T(8,128)(2,1)}, bf16[512,3072]{1,0:T(8,128)(2,1)}, bf16[512,3072]{1,0:T(8,128)(2,1)}, bf16[16,24,16,128]{3,2,1,0:T(8,128)(2,1)}) custom-call(s32[1]{0:T(128)} %bitcast.me_ref, bf16[64,104448]{1,0:T(8,128)(2,1)} %h2_ref.3, bf16[64,104448]{1,0:T(8,128)(2,1)} %h2_ref.3, bf16[64,104448]{1,0:T(8,128)(2,1)} %h2_ref.3, ...), custom_call_target="tpu_custom_call" | custom-call | flops 3221225472 | bytes 9000000 | tf_op jit(solution)/shard_map/filter_spectra/pallas_call | solution.py:264
  14.6 6.7 %all-to-all-start.2 = ((bf16[16,24,16,128]{3,2,1,0:T(8,128)(2,1)}), bf16[16,24,16,128]{3,2,1,0:T(8,128)(2,1)S(1)}, u32[]{:S(2)}, u32[]{:S(2)}) async-start(bf16[16,24,16,128]{3,2,1,0:T(8,128)(2,1)} %get-tuple-element.28), calls=%async_computation.2 | async-start | bytes 3145728 | tf_op jit(solution)/shard_map/all_to_all | solution.py:540
  21.3 14.0 %filter_spectra.3 = (bf16[3072,2048]{1,0:T(8,128)(2,1)}, bf16[512,3072]{1,0:T(8,128)(2,1)}, bf16[512,3072]{1,0:T(8,128)(2,1)}, bf16[16,60,16,128]{3,2,1,0:T(8,128)(2,1)}) custom-call(s32[1]{0:T(128)} %bitcast.me_ref, bf16[64,104448]{1,0:T(8,128)(2,1)} %h2_ref.3, ...), custom_call_target="tpu_custom_call", output_to_operand_aliasing={{0}: (8, {}), {1}: (9, {}), {2}: (10, {})} | custom-call | flops 3221225472 | bytes 9000000 | tf_op jit(solution)/shard_map/filter_spectra/pallas_call | solution.py:264
  35.3 13.3 %spectra_next.1 = (bf16[512,3072]{1,0:T(8,128)(2,1)}, bf16[512,3072]{1,0:T(8,128)(2,1)}, bf16[16,60,16,128]{3,2,1,0:T(8,128)(2,1)}, bf16[16,12,16,128]{3,2,1,0:T(8,128)(2,1)}) custom-call(s32[1]{0:T(128)} %bitcast.me_ref, bf16[3072,2048]{1,0:T(8,128)(2,1)} %get-tuple-element.19.filt_ref, ...), custom_call_target="tpu_custom_call", output_to_operand_aliasing={{2}: (4, {})} | custom-call | flops 6442450944 | bytes 18000000 | tf_op jit(solution)/shard_map/spectra_next/pallas_call | solution.py:294
  48.5 6.1 %all-to-all-done.2.refs_0_ = bf16[16,24,16,128]{3,2,1,0:T(8,128)(2,1)S(1)} async-done(((bf16[16,24,16,128]{3,2,1,0:T(8,128)(2,1)}), bf16[16,24,16,128]{3,2,1,0:T(8,128)(2,1)S(1)}, u32[]{:S(2)}, u32[]{:S(2)}) %all-to-all-start.2) | async-done | bytes 1572896 | tf_op jit(solution)/shard_map/all_to_all | solution.py:540
  54.6 7.9 %all-to-all-start.1 = ((bf16[16,60,16,128]{3,2,1,0:T(8,128)(2,1)}), bf16[16,60,16,128]{3,2,1,0:T(8,128)(2,1)}, u32[]{:S(2)}, u32[]{:S(2)}) async-start(bf16[16,60,16,128]{3,2,1,0:T(8,128)(2,1)} %get-tuple-element.27), calls=%async_computation.1 | async-start | bytes 7864320 | tf_op jit(solution)/shard_map/all_to_all | solution.py:540
  62.7 1.2 fusion.2
  63.9 1.8 fusion
  65.7 20.2 %beam_sums.1 = f32[16,64,384]{2,1,0:T(8,128)} custom-call(s32[1]{0:T(128)} %bitcast.me_ref, bf16[512,3072]{1,0:T(8,128)(2,1)} %get-tuple-element.22.refs_0_, bf16[512,3072]{1,0:T(8,128)(2,1)} %get-tuple-element.23.refs_1_, bf16[512,3072]{1,0:T(8,128)(2,1)} %get-tuple-element.24.refs_2_, bf16[512,3072]{1,0:T(8,128)(2,1)} %get-tuple-element.25.refs_3_, ...), custom_call_target="tpu_custom_call" | custom-call | flops 20000000000 | bytes 20000000 | tf_op jit(solution)/shard_map/beam_sums/pallas_call | solution.py:520
  85.9 1.2 slice.42
  87.1 0.4 collective-permute-start
  87.5 1.9 %collective-permute-done = f32[8,64,384]{2,1,0:T(8,128)S(1)} collective-permute-done((f32[8,64,384]{2,1,0:T(8,128)S(1)}, f32[8,64,384]{2,1,0:T(8,128)S(1)}, u32[]{:S(2)}, u32[]{:S(2)}) %collective-permute-start) | collective-permute-done | bytes 786464 | tf_op jit(solution)/shard_map/ppermute | solution.py:536
  89.4 1.2 slice_add_fusion
  90.8 20.7 %collective-permute-done.1 = f32[4,64,384]{2,1,0:T(8,128)S(1)} collective-permute-done((f32[4,64,384]{2,1,0:T(8,128)S(1)}, f32[4,64,384]{2,1,0:T(8,128)S(1)}, u32[]{:S(2)}, u32[]{:S(2)}) %collective-permute-start.1) | collective-permute-done | bytes 393248 | tf_op jit(solution)/shard_map/ppermute | solution.py:536
  111.7 0.7 broadcast_multiply_fusion
  112.4 0.4 convert_reduce_fusion
  112.8 18.6 %collective-permute-done.2 = f32[2,64,384]{2,1,0:T(8,128)S(1)} collective-permute-done((f32[2,64,384]{2,1,0:T(8,128)S(1)}, f32[2,64,384]{2,1,0:T(8,128)S(1)}, u32[]{:S(2)}, u32[]{:S(2)}) %collective-permute-start.2) | collective-permute-done | bytes 196640 | tf_op jit(solution)/shard_map/ppermute | solution.py:536
  131.5 3.2 %collective-permute-start.3 = (f32[1,64,384]{2,1,0:T(8,128)S(1)}, f32[1,64,384]{2,1,0:T(8,128)S(1)}, u32[]{:S(2)}, u32[]{:S(2)}) collective-permute-start(f32[1,64,384]{2,1,0:T(8,128)S(1)} %slice.48), channel_id=1, source_target_pairs={{0,8},{1,9},{2,10},{3,11},{4,12},{5,13},{6,14},{7,15},{8,0},{9,1},... | collective-permute-start | bytes 294920 | tf_op jit(solution)/shard_map/ppermute | solution.py:536
  134.7 19.5 %collective-permute-done.3 = f32[1,64,384]{2,1,0:T(8,128)S(1)} collective-permute-done((f32[1,64,384]{2,1,0:T(8,128)S(1)}, f32[1,64,384]{2,1,0:T(8,128)S(1)}, u32[]{:S(2)}, u32[]{:S(2)}) %collective-permute-start.3) | collective-permute-done | bytes 98336 | tf_op jit(solution)/shard_map/ppermute | solution.py:536
  154.3 0.7 reshape.32
  155.0 4.6 %all-to-all-start = ((bf16[16,12,16,128]{3,2,1,0:T(8,128)(2,1)}), bf16[16,12,16,128]{3,2,1,0:T(8,128)(2,1)S(1)}, u32[]{:S(2)}, u32[]{:S(2)}) async-start(bf16[16,12,16,128]{3,2,1,0:T(8,128)(2,1)} %get-tuple-element.26), calls=%async_computation | async-start | bytes 1572864 | tf_op jit(solution)/shard_map/all_to_all | solution.py:540
  159.6 15.3 %correlate.3.refs_2_ = f32[32,2,2,256,256]{4,3,2,1,0:T(8,128)} custom-call(bf16[16,24,16,128]{3,2,1,0:T(8,128)(2,1)S(1)} %all-to-all-done.2.refs_0_, bf16[16,60,16,128]{3,2,1,0:T(8,128)(2,1)} %all-to-all-done.1.refs_1_.refs_0_, s32[3,4,256]{2,1,0:T(4,128)S(1)} %slice.50.refs_2_), custom_call_target="tpu_custom_call" | custom-call | flops 12000000000 | bytes 30000000 | tf_op jit(solution)/shard_map/correlate/pallas_call | solution.py:430
  175.0 4.2 %correlate.4.refs_2_ = f32[32,2,2,256,256]{4,3,2,1,0:T(8,128)} custom-call(bf16[16,60,16,128]{3,2,1,0:T(8,128)(2,1)} %all-to-all-done.1.refs_1_.refs_0_, s32[1,4,256]{2,1,0:T(4,128)S(1)} %slice.49.refs_1_, f32[32,2,2,256,256]{4,3,2,1,0:T(8,128)} %correlate.3.refs_2_), custom_call_target="tpu_custom_call", output_to_operand_aliasing={{}: (2, {})} | custom-call | flops 2000000000 | bytes 5000000 | tf_op jit(solution)/shard_map/correlate/pallas_call | solution.py:430
  179.2 3.0 %correlate.5 = f32[32,2,2,256,256]{4,3,2,1,0:T(8,128)} custom-call(bf16[16,12,16,128]{3,2,1,0:T(8,128)(2,1)S(1)} %all-to-all-done.refs_0_, s32[1,4,256]{2,1,0:T(4,128)S(1)} %slice.49.refs_1_, f32[32,2,2,256,256]{4,3,2,1,0:T(8,128)} %correlate.4.refs_2_), custom_call_target="tpu_custom_call", output_to_operand_aliasing={{}: (2, {})} | custom-call | flops 2000000000 | bytes 5000000 | tf_op jit(solution)/shard_map/correlate/pallas_call | solution.py:430
  (23 shorter events, 0.6 us)
Async XLA Ops:
  14.6 40.0 %all-to-all-start.2 = ((bf16[16,24,16,128]{3,2,1,0:T(8,128)(2,1)}), bf16[16,24,16,128]{3,2,1,0:T(8,128)(2,1)S(1)}, u32[]{:S(2)}, u32[]{:S(2)}) async-start(bf16[16,24,16,128]{3,2,1,0:T(8,128)(2,1)} %get-tuple-element.28), calls=%async_computation.2 | async-start | bytes 3145728 | tf_op jit(solution)/shard_map/all_to_all | solution.py:540
  54.6 7.9 %copy-start = (f32[4,64]{1,0:T(4,128)S(1)}, f32[4,64]{1,0:T(4,128)}, u32[]{:S(2)}) copy-start(f32[4,64]{1,0:T(4,128)} %param.9) | copy-start | bytes 3076
  54.6 9.3 %copy-start.1 = (f32[64]{0:T(128)S(1)}, f32[64]{0:T(128)}, u32[]{:S(2)}) copy-start(f32[64]{0:T(128)} %constant.68.clone) | copy-start | bytes 772
  54.6 100.4 %all-to-all-start.1 = ((bf16[16,60,16,128]{3,2,1,0:T(8,128)(2,1)}), bf16[16,60,16,128]{3,2,1,0:T(8,128)(2,1)}, u32[]{:S(2)}, u32[]{:S(2)}) async-start(bf16[16,60,16,128]{3,2,1,0:T(8,128)(2,1)} %get-tuple-element.27), calls=%async_computation.1 | async-start | bytes 7864320 | tf_op jit(solution)/shard_map/all_to_all | solution.py:540
  87.1 2.4 %collective-permute-start = (f32[8,64,384]{2,1,0:T(8,128)S(1)}, f32[8,64,384]{2,1,0:T(8,128)S(1)}, u32[]{:S(2)}, u32[]{:S(2)}) collective-permute-start(f32[8,64,384]{2,1,0:T(8,128)S(1)} %slice.42), channel_id=1, source_target_pairs={{0,1},{1,0},{2,3},{3,2},{4,5},{5,4},{6,7},{7,6},{8,9},{9,8},{10,11... | collective-permute-start | bytes 2359304 | tf_op jit(solution)/shard_map/ppermute | solution.py:536
  90.7 20.8 %collective-permute-start.1 = (f32[4,64,384]{2,1,0:T(8,128)S(1)}, f32[4,64,384]{2,1,0:T(8,128)S(1)}, u32[]{:S(2)}, u32[]{:S(2)}) collective-permute-start(f32[4,64,384]{2,1,0:T(8,128)S(1)} %slice.44), channel_id=1, source_target_pairs={{0,2},{1,3},{2,0},{3,1},{4,6},{5,7},{6,4},{7,5},{8,10},{9,11},{10,... | collective-permute-start | bytes 1179656 | tf_op jit(solution)/shard_map/ppermute | solution.py:536
  111.6 19.8 %collective-permute-start.2 = (f32[2,64,384]{2,1,0:T(8,128)S(1)}, f32[2,64,384]{2,1,0:T(8,128)S(1)}, u32[]{:S(2)}, u32[]{:S(2)}) collective-permute-start(f32[2,64,384]{2,1,0:T(8,128)S(1)} %slice.46), channel_id=1, source_target_pairs={{0,4},{1,5},{2,6},{3,7},{4,0},{5,1},{6,2},{7,3},{8,12},{9,13},{10,... | collective-permute-start | bytes 589832 | tf_op jit(solution)/shard_map/ppermute | solution.py:536
  131.5 22.7 %collective-permute-start.3 = (f32[1,64,384]{2,1,0:T(8,128)S(1)}, f32[1,64,384]{2,1,0:T(8,128)S(1)}, u32[]{:S(2)}, u32[]{:S(2)}) collective-permute-start(f32[1,64,384]{2,1,0:T(8,128)S(1)} %slice.48), channel_id=1, source_target_pairs={{0,8},{1,9},{2,10},{3,11},{4,12},{5,13},{6,14},{7,15},{8,0},{9,1},... | collective-permute-start | bytes 294920 | tf_op jit(solution)/shard_map/ppermute | solution.py:536
  155.0 24.2 %all-to-all-start = ((bf16[16,12,16,128]{3,2,1,0:T(8,128)(2,1)}), bf16[16,12,16,128]{3,2,1,0:T(8,128)(2,1)S(1)}, u32[]{:S(2)}, u32[]{:S(2)}) async-start(bf16[16,12,16,128]{3,2,1,0:T(8,128)(2,1)} %get-tuple-element.26), calls=%async_computation | async-start | bytes 1572864 | tf_op jit(solution)/shard_map/all_to_all | solution.py:540

commit v8 on v7

--- a/solution.py
+++ b/solution.py
@@ -156,22 +156,16 @@
 
 def filter_fold(z, main_ref, halo, win_ref, filt_ref, off):
     far = off + NFFT // 2
+    folded = {}
     for f0 in range(0, z.feed_dev, 16):
         low = filter_tile(z, main_ref, halo, win_ref, off, f0)
         high = filter_tile(z, main_ref, halo, win_ref, far, f0)
         for (row, a), (_, b) in zip(low, high):
-            filt_ref[row : row + 16, off : off + LANES] = a + b
-            filt_ref[row : row + 16, far : far + LANES] = a - b
-
-
-def transform(basis_ref, filt_ref, begin, end):
+            folded[row] = (a + b, a - b)
+            filt_ref[row : row + 16, off : off + LANES] = folded[row][0]
+            filt_ref[row : row + 16, far : far + LANES] = folded[row][1]
     return [
-        lax.dot_general(
-            basis_ref[parity, :, begin:end],
-            filt_ref[:, parity * (NFFT // 2) + begin : parity * (NFFT // 2) + end],
-            NT,
-            preferred_element_type=jnp.float32,
-        )
+        jnp.concatenate([folded[row][parity] for row in sorted(folded)], axis=0)
         for parity in range(2)
     ]
 
@@ -185,9 +179,19 @@
     piece = 512
     spectra = None
     for off in range(0, NFFT // 2, piece):
-        for tile in range(off, off + piece, LANES):
+        tiles = [
             filter_fold(z, main_ref, halo, win_ref, filt_ref, tile)
-        part = transform(basis_ref, filt_ref, off, off + piece)
+            for tile in range(off, off + piece, LANES)
+        ]
+        part = [
+            lax.dot_general(
+                basis_ref[parity, :, off : off + piece],
+                jnp.concatenate([tile[parity] for tile in tiles], axis=1),
+                NT,
+                preferred_element_type=jnp.float32,
+            )
+            for parity in range(2)
+        ]
         spectra = part if spectra is None else [x + y for x, y in zip(spectra, part)]
     sends = []
     for c in range(len(chunks)):
@@ -197,7 +201,16 @@
 
 
 def next_kernel(z, scale, chunks, me_ref, filt_ref, basis_ref, lists_ref, held_ref, *refs):
-    spectra = transform(basis_ref, filt_ref, 0, NFFT // 2)
+    half = NFFT // 2
+    spectra = [
+        lax.dot_general(
+            basis_ref[parity],
+            filt_ref[:, parity * half : (parity + 1) * half],
+            NT,
+            preferred_element_type=jnp.float32,
+        )
+        for parity in range(2)
+    ]
     begun_ref, last_ref = refs[2], refs[3]
     sends = [
         [(begun_ref, 0, 2), (begun_ref, 1, 2)],
@@ -585,9 +598,8 @@
     beams, bit = beam_call(z, me_array, spectra, delays), 1
     while beams.shape[0] > 1:
         half = beams.shape[0] // 2
-        beams, bit = beams[:half] + swap(z, beams[half:], bit), 2 * bit
-    beams = beams.reshape(z.chunks, 2, BAND_CH // 2, 2 * BEAMS * FR)
-    beams = jnp.swapaxes(beams, 1, 2).reshape(z.chan_dev, 2 * BEAMS * FR)
+        away = beams[half:].astype(jnp.bfloat16) if half == 1 else beams[half:]
+        beams, bit = beams[:half] + swap(z, away, bit).astype(jnp.float32), 2 * bit
     if len(z.parts) > 1:
         last, beams = lax.optimization_barrier((last, beams))
         got = exchange(last)
@@ -597,6 +609,8 @@
         vis = receive_call(z, k, 1, [[(got, 0, z.quads)]], take_key[k:], vis)
     else:
         vis = receive_call(z, 0, None, arrived, take_key, None)
+    beams = beams.reshape(z.chunks, 2, BAND_CH // 2, 2 * BEAMS * FR)
+    beams = jnp.swapaxes(beams, 1, 2).reshape(z.chan_dev, 2 * BEAMS * FR)
     return (vis.reshape(z.chan_dev, 2, FSUB, FSUB), beams)
 
 

time: 184 us -> 181 us (0.984)
  Pallas kernels: 84 us -> 81 us
    pallas_call x2, Pallas kernels: 28 us -> 25 us  [first(): pl.pallas_call(functools.partial(first_kernel, z, self.scale, chunks, len...]
    ppermute x4, waiting for transfers between devices: 60.8 us -> 58.7 us  [swap(): return lax.ppermute(x, 'chan', [(i, i ^ offset) for i in range(z.devices)])]
where the time goes in v8:
time: 181 us; the launch traced here: 179 us
  Pallas kernels  81 us (45%)
  waiting for transfers between devices  66.2 us (37%)
  starting transfers between devices  23 us (13%)
  other arithmetic  5.44 us (3%)
  local copies, waits for them, and re-layouts  2.19 us (1%)
    ppermute x4, waiting for transfers between devices, swap(): return lax.ppermute(x, 'chan', [(i, i ^ offset) for i in range(z.devices)])  58.7 us
    pallas_call x2, Pallas kernels, first(): pl.pallas_call(functools.partial(first_kernel, z, self.scale, chunks, len...  25 us
    pallas_call x3, Pallas kernels, receive_call(): pl.pallas_call(functools.partial(receive_kernel, z, parities, step_pairs,...  22.6 us
    pallas_call x1, Pallas kernels, beam_call(): pl.pallas_call(functools.partial(beam_kernel, z), grid_spec=grid_spec, ou...  20.2 us
    all_to_all x3, starting transfers between devices, exchange(): return lax.all_to_all(x, 'chan', split_axis=0, concat_axis=0, tiled=True)  19.1 us
    pallas_call x1, Pallas kernels, next(): pl.pallas_call(functools.partial(next_kernel, z, self.scale, chunks), in_...  13.3 us
    all_to_all x3, waiting for transfers between devices, exchange(): return lax.all_to_all(x, 'chan', split_axis=0, concat_axis=0, tiled=True)  7.56 us
    ppermute x4, starting transfers between devices, swap(): return lax.ppermute(x, 'chan', [(i, i ^ offset) for i in range(z.devices)])  3.86 us
  transfers between devices with their start and end apart: 7, of which 5 were waited for; matrix products, arithmetic and copies ran while one was open for 4% of the time, Pallas kernels for 37%

profile of v8, /device:TPU:5, one launch (start us, length us, event | category | flops | bytes accessed | tf_op | source)
XLA Modules:
  0.0 178.8 jit_solution(15232734160240022454)
XLA Ops:
  0.6 12.5 %filter_spectra.2 = (bf16[3072,2048]{1,0:T(8,128)(2,1)}, bf16[512,3072]{1,0:T(8,128)(2,1)}, bf16[512,3072]{1,0:T(8,128)(2,1)}, bf16[16,24,16,128]{3,2,1,0:T(8,128)(2,1)}) custom-call(s32[1]{0:T(128)} %bitcast.me_ref, bf16[64,104448]{1,0:T(8,128)(2,1)} %h2_ref.3, bf16[64,104448]{1,0:T(8,128)(2,1)} %h2_ref.3, bf16[64,104448]{1,0:T(8,128)(2,1)} %h2_ref.3, ...), custom_call_target="tpu_custom_call" | custom-call | flops 3221225472 | bytes 9000000 | tf_op jit(solution)/shard_map/filter_spectra/pallas_call | solution.py:277
  13.1 6.6 %all-to-all-start.2 = ((bf16[16,24,16,128]{3,2,1,0:T(8,128)(2,1)}), bf16[16,24,16,128]{3,2,1,0:T(8,128)(2,1)S(1)}, u32[]{:S(2)}, u32[]{:S(2)}) async-start(bf16[16,24,16,128]{3,2,1,0:T(8,128)(2,1)} %get-tuple-element.28), calls=%async_computation.2 | async-start | bytes 3145728 | tf_op jit(solution)/shard_map/all_to_all | solution.py:553
  19.7 12.5 %filter_spectra.3 = (bf16[3072,2048]{1,0:T(8,128)(2,1)}, bf16[512,3072]{1,0:T(8,128)(2,1)}, bf16[512,3072]{1,0:T(8,128)(2,1)}, bf16[16,60,16,128]{3,2,1,0:T(8,128)(2,1)}) custom-call(s32[1]{0:T(128)} %bitcast.me_ref, bf16[64,104448]{1,0:T(8,128)(2,1)} %h2_ref.3, ...), custom_call_target="tpu_custom_call", output_to_operand_aliasing={{0}: (8, {}), {1}: (9, {}), {2}: (10, {})} | custom-call | flops 3221225472 | bytes 9000000 | tf_op jit(solution)/shard_map/filter_spectra/pallas_call | solution.py:277
  32.3 13.3 %spectra_next.1 = (bf16[512,3072]{1,0:T(8,128)(2,1)}, bf16[512,3072]{1,0:T(8,128)(2,1)}, bf16[16,60,16,128]{3,2,1,0:T(8,128)(2,1)}, bf16[16,12,16,128]{3,2,1,0:T(8,128)(2,1)}) custom-call(s32[1]{0:T(128)} %bitcast.me_ref, bf16[3072,2048]{1,0:T(8,128)(2,1)} %get-tuple-element.19.filt_ref, ...), custom_call_target="tpu_custom_call", output_to_operand_aliasing={{2}: (4, {})} | custom-call | flops 6442450944 | bytes 18000000 | tf_op jit(solution)/shard_map/spectra_next/pallas_call | solution.py:307
  45.5 7.6 %all-to-all-done.2.refs_0_ = bf16[16,24,16,128]{3,2,1,0:T(8,128)(2,1)S(1)} async-done(((bf16[16,24,16,128]{3,2,1,0:T(8,128)(2,1)}), bf16[16,24,16,128]{3,2,1,0:T(8,128)(2,1)S(1)}, u32[]{:S(2)}, u32[]{:S(2)}) %all-to-all-start.2) | async-done | bytes 1572896 | tf_op jit(solution)/shard_map/all_to_all | solution.py:553
  53.1 7.9 %all-to-all-start.1 = ((bf16[16,60,16,128]{3,2,1,0:T(8,128)(2,1)}), bf16[16,60,16,128]{3,2,1,0:T(8,128)(2,1)}, u32[]{:S(2)}, u32[]{:S(2)}) async-start(bf16[16,60,16,128]{3,2,1,0:T(8,128)(2,1)} %get-tuple-element.27), calls=%async_computation.1 | async-start | bytes 7864320 | tf_op jit(solution)/shard_map/all_to_all | solution.py:553
  61.2 1.2 fusion.2
  62.4 1.8 %fusion = (f32[4,64,256]{2,1,0:T(8,128)}, f32[4,64,256]{2,1,0:T(8,128)}) fusion(f32[64]{0:T(128)S(1)} %copy-done.1, f32[4,256]{1,0:T(4,128)S(1)} %mul.66), kind=kLoop, calls=%fused_computation.4 | loop fusion | flops 131072 | bytes 528640 | tf_op jit(solution)/shard_map/sin | solution.py:543
  64.2 20.2 %beam_sums.1 = f32[16,64,384]{2,1,0:T(8,128)} custom-call(s32[1]{0:T(128)} %bitcast.me_ref, bf16[512,3072]{1,0:T(8,128)(2,1)} %get-tuple-element.22.refs_0_, bf16[512,3072]{1,0:T(8,128)(2,1)} %get-tuple-element.23.refs_1_, bf16[512,3072]{1,0:T(8,128)(2,1)} %get-tuple-element.24.refs_2_, bf16[512,3072]{1,0:T(8,128)(2,1)} %get-tuple-element.25.refs_3_, ...), custom_call_target="tpu_custom_call" | custom-call | flops 20000000000 | bytes 20000000 | tf_op jit(solution)/shard_map/beam_sums/pallas_call | solution.py:533
  84.4 1.2 slice.43
  85.5 0.4 collective-permute-start
  86.0 1.9 %collective-permute-done = f32[8,64,384]{2,1,0:T(8,128)S(1)} collective-permute-done((f32[8,64,384]{2,1,0:T(8,128)S(1)}, f32[8,64,384]{2,1,0:T(8,128)S(1)}, u32[]{:S(2)}, u32[]{:S(2)}) %collective-permute-start) | collective-permute-done | bytes 786464 | tf_op jit(solution)/shard_map/ppermute | solution.py:549
  87.9 1.2 slice_add_fusion
  89.3 20.7 %collective-permute-done.1 = f32[4,64,384]{2,1,0:T(8,128)S(1)} collective-permute-done((f32[4,64,384]{2,1,0:T(8,128)S(1)}, f32[4,64,384]{2,1,0:T(8,128)S(1)}, u32[]{:S(2)}, u32[]{:S(2)}) %collective-permute-start.1) | collective-permute-done | bytes 393248 | tf_op jit(solution)/shard_map/ppermute | solution.py:549
  110.2 0.7 broadcast_multiply_fusion
  110.9 0.4 convert_reduce_fusion
  111.3 18.6 %collective-permute-done.2 = f32[2,64,384]{2,1,0:T(8,128)S(1)} collective-permute-done((f32[2,64,384]{2,1,0:T(8,128)S(1)}, f32[2,64,384]{2,1,0:T(8,128)S(1)}, u32[]{:S(2)}, u32[]{:S(2)}) %collective-permute-start.2) | collective-permute-done | bytes 196640 | tf_op jit(solution)/shard_map/ppermute | solution.py:549
  129.9 3.2 %collective-permute-start.3 = (bf16[1,64,384]{2,1,0:T(8,128)(2,1)S(1)}, bf16[1,64,384]{2,1,0:T(8,128)(2,1)S(1)}, u32[]{:S(2)}, u32[]{:S(2)}) collective-permute-start(bf16[1,64,384]{2,1,0:T(8,128)(2,1)S(1)} %slice.57), channel_id=1, source_target_pairs={{0,8},{1,9},{2,10},{3,11},{4,12},{5,13},{6,14},{7,15},{8,0},{9,1},... | collective-permute-start | bytes 147464 | tf_op jit(solution)/shard_map/ppermute | solution.py:549
  133.2 17.4 %collective-permute-done.3 = bf16[1,64,384]{2,1,0:T(8,128)(2,1)S(1)} collective-permute-done((bf16[1,64,384]{2,1,0:T(8,128)(2,1)S(1)}, bf16[1,64,384]{2,1,0:T(8,128)(2,1)S(1)}, u32[]{:S(2)}, u32[]{:S(2)}) %collective-permute-start.3) | collective-permute-done | bytes 49184 | tf_op jit(solution)/shard_map/ppermute | solution.py:549
  150.6 4.6 %all-to-all-start = ((bf16[16,12,16,128]{3,2,1,0:T(8,128)(2,1)}), bf16[16,12,16,128]{3,2,1,0:T(8,128)(2,1)S(1)}, u32[]{:S(2)}, u32[]{:S(2)}) async-start(bf16[16,12,16,128]{3,2,1,0:T(8,128)(2,1)} %get-tuple-element.26), calls=%async_computation | async-start | bytes 1572864 | tf_op jit(solution)/shard_map/all_to_all | solution.py:553
  155.3 0.7 reshape.33
  156.0 15.3 %correlate.3.refs_2_ = f32[32,2,2,256,256]{4,3,2,1,0:T(8,128)} custom-call(bf16[16,24,16,128]{3,2,1,0:T(8,128)(2,1)S(1)} %all-to-all-done.2.refs_0_, bf16[16,60,16,128]{3,2,1,0:T(8,128)(2,1)} %all-to-all-done.1.refs_1_.refs_0_, s32[3,4,256]{2,1,0:T(4,128)S(1)} %slice.51.refs_2_), custom_call_target="tpu_custom_call" | custom-call | flops 12000000000 | bytes 30000000 | tf_op jit(solution)/shard_map/correlate/pallas_call | solution.py:443
  171.3 4.2 %correlate.4.refs_2_ = f32[32,2,2,256,256]{4,3,2,1,0:T(8,128)} custom-call(bf16[16,60,16,128]{3,2,1,0:T(8,128)(2,1)} %all-to-all-done.1.refs_1_.refs_0_, s32[1,4,256]{2,1,0:T(4,128)S(1)} %slice.50.refs_1_, f32[32,2,2,256,256]{4,3,2,1,0:T(8,128)} %correlate.3.refs_2_), custom_call_target="tpu_custom_call", output_to_operand_aliasing={{}: (2, {})} | custom-call | flops 2000000000 | bytes 5000000 | tf_op jit(solution)/shard_map/correlate/pallas_call | solution.py:443
  175.5 3.0 %correlate.5 = f32[32,2,2,256,256]{4,3,2,1,0:T(8,128)} custom-call(bf16[16,12,16,128]{3,2,1,0:T(8,128)(2,1)S(1)} %all-to-all-done.refs_0_, s32[1,4,256]{2,1,0:T(4,128)S(1)} %slice.50.refs_1_, f32[32,2,2,256,256]{4,3,2,1,0:T(8,128)} %correlate.4.refs_2_), custom_call_target="tpu_custom_call", output_to_operand_aliasing={{}: (2, {})} | custom-call | flops 2000000000 | bytes 5000000 | tf_op jit(solution)/shard_map/correlate/pallas_call | solution.py:443
  (23 shorter events, 0.6 us)
Async XLA Ops:
  13.1 40.0 %all-to-all-start.2 = ((bf16[16,24,16,128]{3,2,1,0:T(8,128)(2,1)}), bf16[16,24,16,128]{3,2,1,0:T(8,128)(2,1)S(1)}, u32[]{:S(2)}, u32[]{:S(2)}) async-start(bf16[16,24,16,128]{3,2,1,0:T(8,128)(2,1)} %get-tuple-element.28), calls=%async_computation.2 | async-start | bytes 3145728 | tf_op jit(solution)/shard_map/all_to_all | solution.py:553
  53.1 7.9 %copy-start = (f32[4,64]{1,0:T(4,128)S(1)}, f32[4,64]{1,0:T(4,128)}, u32[]{:S(2)}) copy-start(f32[4,64]{1,0:T(4,128)} %param.9) | copy-start | bytes 3076
  53.1 9.3 %copy-start.1 = (f32[64]{0:T(128)S(1)}, f32[64]{0:T(128)}, u32[]{:S(2)}) copy-start(f32[64]{0:T(128)} %constant.68.clone) | copy-start | bytes 772
  53.1 97.5 %all-to-all-start.1 = ((bf16[16,60,16,128]{3,2,1,0:T(8,128)(2,1)}), bf16[16,60,16,128]{3,2,1,0:T(8,128)(2,1)}, u32[]{:S(2)}, u32[]{:S(2)}) async-start(bf16[16,60,16,128]{3,2,1,0:T(8,128)(2,1)} %get-tuple-element.27), calls=%async_computation.1 | async-start | bytes 7864320 | tf_op jit(solution)/shard_map/all_to_all | solution.py:553
  85.5 2.4 %collective-permute-start = (f32[8,64,384]{2,1,0:T(8,128)S(1)}, f32[8,64,384]{2,1,0:T(8,128)S(1)}, u32[]{:S(2)}, u32[]{:S(2)}) collective-permute-start(f32[8,64,384]{2,1,0:T(8,128)S(1)} %slice.43), channel_id=1, source_target_pairs={{0,1},{1,0},{2,3},{3,2},{4,5},{5,4},{6,7},{7,6},{8,9},{9,8},{10,11... | collective-permute-start | bytes 2359304 | tf_op jit(solution)/shard_map/ppermute | solution.py:549
  89.2 20.8 %collective-permute-start.1 = (f32[4,64,384]{2,1,0:T(8,128)S(1)}, f32[4,64,384]{2,1,0:T(8,128)S(1)}, u32[]{:S(2)}, u32[]{:S(2)}) collective-permute-start(f32[4,64,384]{2,1,0:T(8,128)S(1)} %slice.45), channel_id=1, source_target_pairs={{0,2},{1,3},{2,0},{3,1},{4,6},{5,7},{6,4},{7,5},{8,10},{9,11},{10,... | collective-permute-start | bytes 1179656 | tf_op jit(solution)/shard_map/ppermute | solution.py:549
  110.1 19.8 %collective-permute-start.2 = (f32[2,64,384]{2,1,0:T(8,128)S(1)}, f32[2,64,384]{2,1,0:T(8,128)S(1)}, u32[]{:S(2)}, u32[]{:S(2)}) collective-permute-start(f32[2,64,384]{2,1,0:T(8,128)S(1)} %slice.47), channel_id=1, source_target_pairs={{0,4},{1,5},{2,6},{3,7},{4,0},{5,1},{6,2},{7,3},{8,12},{9,13},{10,... | collective-permute-start | bytes 589832 | tf_op jit(solution)/shard_map/ppermute | solution.py:549
  129.9 20.6 %collective-permute-start.3 = (bf16[1,64,384]{2,1,0:T(8,128)(2,1)S(1)}, bf16[1,64,384]{2,1,0:T(8,128)(2,1)S(1)}, u32[]{:S(2)}, u32[]{:S(2)}) collective-permute-start(bf16[1,64,384]{2,1,0:T(8,128)(2,1)S(1)} %slice.57), channel_id=1, source_target_pairs={{0,8},{1,9},{2,10},{3,11},{4,12},{5,13},{6,14},{7,15},{8,0},{9,1},... | collective-permute-start | bytes 147464 | tf_op jit(solution)/shard_map/ppermute | solution.py:549
  150.6 24.9 %all-to-all-start = ((bf16[16,12,16,128]{3,2,1,0:T(8,128)(2,1)}), bf16[16,12,16,128]{3,2,1,0:T(8,128)(2,1)S(1)}, u32[]{:S(2)}, u32[]{:S(2)}) async-start(bf16[16,12,16,128]{3,2,1,0:T(8,128)(2,1)} %get-tuple-element.26), calls=%async_computation | async-start | bytes 1572864 | tf_op jit(solution)/shard_map/all_to_all | solution.py:553

commit v9 on v8

--- a/solution.py
+++ b/solution.py
@@ -82,42 +82,44 @@
     return jnp.clip(loc, 0, z.feed_dev - 1)
 
 
-def emit_spectra(z, scale, chunks, me_ref, spectra, lists_ref, loc_ref, spec_refs, send_refs):
-    loc_ref[...] = find_places(z, me_ref[0], lists_ref[...])
+def emit_spectra(z, scale, chunk, me_ref, spectra, loc_ref, spec_ref, sends):
     lane = lax.broadcasted_iota(jnp.int32, (z.rows_dev, LANES), 1)
     frame = (lane // z.cap) ^ (me_ref[0] % z.lane_frames)
     start = frame * z.cap
     few = BAND_CH // 2
-    for c, chunk in enumerate(chunks):
-        for owner in range(z.devices):
-            top = (c * z.devices + owner) * BAND_CH
-            rows = [x[top + p : top + p + few] for p in (0, few) for x in spectra]
-            rows = jnp.concatenate(rows, axis=0) * scale
-            spec_refs[c][owner * z.rows_dev : (owner + 1) * z.rows_dev, :] = rows.astype(
-                jnp.bfloat16
-            )
-            band = owner * z.bands_here + chunk
-            loc = loc_ref[band : band + 1, :]
-            index = start + loc % z.cap
-            lower = jnp.broadcast_to(loc, index.shape) < z.cap
-            for q in range(z.step_quads):
-                parts = []
-                for side in range(2):
-                    left = q * z.width + side * LANES
-                    parts.append(
-                        jnp.take_along_axis(
-                            rows[:, left : left + LANES], index, axis=1,
-                            mode="promise_in_bounds",
-                        )
+    for owner in range(z.devices):
+        top = owner * BAND_CH
+        rows = [x[top + p : top + p + few] for p in (0, few) for x in spectra]
+        rows = jnp.concatenate(rows, axis=0) * scale
+        spec_ref[owner * z.rows_dev : (owner + 1) * z.rows_dev, :] = rows.astype(jnp.bfloat16)
+        band = owner * z.bands_here + chunk
+        loc = loc_ref[band : band + 1, :]
+        index = start + loc % z.cap
+        lower = jnp.broadcast_to(loc, index.shape) < z.cap
+        for q in range(z.step_quads):
+            parts = []
+            for side in range(2):
+                left = q * z.width + side * LANES
+                parts.append(
+                    jnp.take_along_axis(
+                        rows[:, left : left + LANES], index, axis=1, mode="promise_in_bounds"
                     )
-                picked = jnp.where(lower, parts[0], parts[1])
-                for parity, (send_ref, unit, stride) in enumerate(send_refs[c]):
-                    half = [
-                        picked[p * BAND_CH + parity * few : p * BAND_CH + parity * few + few]
-                        for p in range(2)
-                    ]
-                    half = jnp.concatenate(half, axis=0).astype(jnp.bfloat16)
-                    send_ref[owner, unit + q * stride] = half
+                )
+            picked = jnp.where(lower, parts[0], parts[1])
+            for parity, (send_ref, unit, stride) in enumerate(sends):
+                half = [
+                    picked[p * BAND_CH + parity * few : p * BAND_CH + parity * few + few]
+                    for p in range(2)
+                ]
+                half = jnp.concatenate(half, axis=0).astype(jnp.bfloat16)
+                send_ref[owner, unit + q * stride] = half
+
+
+def product(z, basis_ref, parity, c, begin, end, samples):
+    rows = slice(c * z.rows // 2, (c + 1) * z.rows // 2)
+    return lax.dot_general(
+        basis_ref[parity, rows, begin:end], samples, NT, preferred_element_type=jnp.float32
+    )
 
 
 def filter_tile(z, main_ref, halo, win_ref, off, f0):
@@ -176,47 +178,44 @@
 ):
     filt_ref, spec_refs, send_ref, loc_ref = refs[held], refs[held + 1 : -2], refs[-2], refs[-1]
     halo = (h0_ref, h1_ref, h2_ref)
+    loc_ref[...] = find_places(z, me_ref[0], lists_ref[...])
     piece = 512
-    spectra = None
+    count = len(chunks)
+    spectra = [[None, None] for _ in chunks]
     for off in range(0, NFFT // 2, piece):
         tiles = [
             filter_fold(z, main_ref, halo, win_ref, filt_ref, tile)
             for tile in range(off, off + piece, LANES)
         ]
-        part = [
-            lax.dot_general(
-                basis_ref[parity, :, off : off + piece],
-                jnp.concatenate([tile[parity] for tile in tiles], axis=1),
-                NT,
-                preferred_element_type=jnp.float32,
-            )
-            for parity in range(2)
-        ]
-        spectra = part if spectra is None else [x + y for x, y in zip(spectra, part)]
-    sends = []
-    for c in range(len(chunks)):
+        for parity in range(2):
+            samples = jnp.concatenate([tile[parity] for tile in tiles], axis=1)
+            for c in range(count):
+                part = product(z, basis_ref, parity, c, off, off + piece, samples)
+                old = spectra[c][parity]
+                spectra[c][parity] = part if old is None else old + part
+    for c, chunk in enumerate(chunks):
         unit = c * 2 * z.step_quads
-        sends.append([(send_ref, unit, 2), (send_ref, unit + 1, 2)])
-    emit_spectra(z, scale, chunks, me_ref, spectra, lists_ref, loc_ref, spec_refs, sends)
+        sends = [(send_ref, unit, 2), (send_ref, unit + 1, 2)]
+        emit_spectra(z, scale, chunk, me_ref, spectra[c], loc_ref, spec_refs[c], sends)
 
 
 def next_kernel(z, scale, chunks, me_ref, filt_ref, basis_ref, lists_ref, held_ref, *refs):
+    begun_ref, last_ref, loc_ref = refs[2], refs[3], refs[-1]
+    loc_ref[...] = find_places(z, me_ref[0], lists_ref[...])
     half = NFFT // 2
     spectra = [
-        lax.dot_general(
-            basis_ref[parity],
-            filt_ref[:, parity * half : (parity + 1) * half],
-            NT,
-            preferred_element_type=jnp.float32,
-        )
-        for parity in range(2)
+        [
+            product(z, basis_ref, p, c, 0, half, filt_ref[:, p * half : (p + 1) * half])
+            for p in range(2)
+        ]
+        for c in range(2)
     ]
-    begun_ref, last_ref = refs[2], refs[3]
     sends = [
         [(begun_ref, 0, 2), (begun_ref, 1, 2)],
         [(begun_ref, 2 * z.step_quads, 1), (last_ref, 0, 1)],
     ]
-    emit_spectra(z, scale, chunks, me_ref, spectra, lists_ref, refs[-1], refs[:2], sends)
+    for c, chunk in enumerate(chunks):
+        emit_spectra(z, scale, chunk, me_ref, spectra[c], loc_ref, refs[c], sends[c])
 
 
 def whole_spec(shape):
@@ -326,7 +325,7 @@
         )(*operands)
 
 
-def receive_kernel(z, parities, step_pairs, runs, arrays, *refs):
+def receive_kernel(z, parities, step_pairs, runs, arrays, even_steps, *refs):
     arr_refs, key_ref = refs[:arrays], refs[arrays]
     vis_ref, buf_ref, rows_ref, sems = refs[-4:]
     g = pl.program_id(0)
@@ -338,18 +337,14 @@
     at = g % steps
 
     def copies(c):
-        place = 0
-        out = []
-        for i, (array, first, count) in enumerate(runs[c]):
-            out.append(
-                pltpu.make_async_copy(
-                    arr_refs[array].at[:, first : first + count],
-                    buf_ref.at[c % slots, :, place : place + count],
-                    sems.at[c % slots, i],
-                )
+        return [
+            pltpu.make_async_copy(
+                arr_refs[array].at[:, first : first + count],
+                buf_ref.at[c % slots, :, place : place + count],
+                sems.at[c % slots, i],
             )
-            place += count
-        return out
+            for i, (array, first, count, place) in enumerate(runs[c])
+        ]
 
     for c in range(len(runs)):
 
@@ -387,36 +382,52 @@
                     :, side * LANES : (side + 1) * LANES
                 ]
 
-    todo = [(i, p) for i in range(step_pairs) for p in range(parities)]
-    operands = []
-    for i, p in todo:
-        halves = []
-        for part in range(2):
-            first = p * BAND_CH + part * few + at * step_pairs + i
-            halves.append(
-                jnp.concatenate(
-                    [
-                        rows_ref[side, pl.ds(first, FR, stride=parities * BAND_CH), :]
-                        for side in range(FSUB // LANES)
-                    ],
-                    axis=1,
+    def correlate(todo):
+        operands = []
+        for i, p in todo:
+            halves = []
+            for part in range(2):
+                first = p * BAND_CH + part * few + at * step_pairs + i
+                halves.append(
+                    jnp.concatenate(
+                        [
+                            rows_ref[side, pl.ds(first, FR, stride=parities * BAND_CH), :]
+                            for side in range(FSUB // LANES)
+                        ],
+                        axis=1,
+                    )
                 )
-            )
-        real, imag = halves
-        both = jnp.concatenate([real, imag], axis=0)
-        turned = jnp.concatenate([-imag, real], axis=0)
-        right = jnp.concatenate([both, turned], axis=1).astype(jnp.bfloat16)
-        operands.append((both.astype(jnp.bfloat16).T, right))
-    outs = [
-        jnp.dot(left, right, preferred_element_type=jnp.float32) for left, right in operands
-    ]
-    for (i, p), out in zip(todo, outs):
-        out = out * (1.0 / FR)
-        vis_ref[i, p, 0] = out[:, :FSUB]
-        vis_ref[i, p, 1] = out[:, FSUB:]
-
-
-def receive_call(z, chunk, parity, arrived, keys, vis):
+            real, imag = halves
+            both = jnp.concatenate([real, imag], axis=0)
+            turned = jnp.concatenate([-imag, real], axis=0)
+            right = jnp.concatenate([both, turned], axis=1).astype(jnp.bfloat16)
+            operands.append((both.astype(jnp.bfloat16).T, right))
+        outs = [
+            jnp.dot(left, right, preferred_element_type=jnp.float32)
+            for left, right in operands
+        ]
+        for (i, p), out in zip(todo, outs):
+            out = out * (1.0 / FR)
+            vis_ref[i, p, 0] = out[:, :FSUB]
+            vis_ref[i, p, 1] = out[:, FSUB:]
+
+    every = [(i, p) for i in range(step_pairs) for p in range(parities)]
+    if even_steps:
+        begin = len(runs) * steps - even_steps
+
+        @pl.when(g < begin)
+        def _():
+            correlate(every)
+
+        @pl.when(g >= begin)
+        def _():
+            correlate([(i, p) for i, p in every if p == 0])
+
+    else:
+        correlate(every)
+
+
+def receive_call(z, chunk, parity, arrived, keys, vis, even_last=False):
     parities = 2 if parity is None else 1
     step_pairs = 4 // parities
     steps = BAND_CH // 2 // step_pairs
@@ -426,11 +437,12 @@
     runs = []
     for one in arrived:
         runs.append([])
-        for got, first, count in one:
+        for got, first, count, place in one:
             if not any(got is x for x in arrays):
                 arrays.append(got)
-            runs[-1].append(([got is x for x in arrays].index(True), first, count))
-    units = sum(count for _, _, count in runs[0])
+            index = [got is x for x in arrays].index(True)
+            runs[-1].append((index, first, count, place))
+    units = parities * z.quads
     slots = min(2, len(runs))
     operands = arrays + [keys]
     in_specs = [pl.BlockSpec(memory_space=pl.ANY)] * len(arrays) + [whole_spec(keys.shape)]
@@ -441,7 +453,9 @@
         operands.append(vis)
     share = parities * len(runs)
     return pl.pallas_call(
-        functools.partial(receive_kernel, z, parities, step_pairs, runs, len(arrays)),
+        functools.partial(
+            receive_kernel, z, parities, step_pairs, runs, len(arrays), steps if even_last else 0
+        ),
         grid=(len(runs) * steps,),
         in_specs=in_specs,
         out_specs=pl.BlockSpec(
@@ -465,7 +479,7 @@
 
 def beam_kernel(z, me_ref, *refs):
     spec_refs = refs[: z.chunks]
-    cos_base, sin_base, cos_step, sin_step, sum_ref, out_ref, prod_ref = refs[z.chunks :]
+    cos_base, sin_base, cos_step, sin_step, sum_ref, out_ref, prod_ref, row_ref = refs[z.chunks :]
     count = z.chan_dev
     weights = []
     for g in range(BEAMS):
@@ -488,8 +502,13 @@
                 prod_ref[row : row + count, q * LANES : (q + 1) * LANES] = both
     sums = jnp.dot(prod_ref[...], sum_ref[...], preferred_element_type=jnp.float32)
     sums = sums * (1.0 / np.sqrt(F))
+    few = BAND_CH // 2
     for j in range(2 * BEAMS):
-        out_ref[0, :, j * FR : (j + 1) * FR] = sums[j * count : (j + 1) * count, :FR]
+        for i in range(count // few):
+            first = i // 2 * BAND_CH + i % 2
+            top = j * count + i * few
+            row_ref[j, pl.ds(first, few, stride=2), :] = sums[top : top + few]
+        out_ref[0, :, j * FR : (j + 1) * FR] = row_ref[j][:, :FR]
 
 
 def beam_call(z, me, spectra, delays):
@@ -528,7 +547,10 @@
         out_specs=pl.BlockSpec(
             (1, z.chan_dev, 2 * BEAMS * FR), lambda j, me_ref: (j, 0, 0)
         ),
-        scratch_shapes=[pltpu.VMEM((2 * BEAMS * z.chan_dev, FR * z.cap), jnp.bfloat16)],
+        scratch_shapes=[
+            pltpu.VMEM((2 * BEAMS * z.chan_dev, FR * z.cap), jnp.bfloat16),
+            pltpu.VMEM((2 * BEAMS, z.chan_dev, LANES), jnp.float32),
+        ],
     )
     return pl.pallas_call(
         functools.partial(beam_kernel, z),
@@ -579,7 +601,7 @@
     filt, *spectra, send = calls.first(0, steps, early, basis, steps * step, [])
     got = exchange(send)
     for c in early:
-        arrived[c] += [(got, g * step + c * share, share) for g in range(steps)]
+        arrived[c] += [(got, g * step + c * share, share, g * share) for g in range(steps)]
     if len(z.parts) > 1:
         begin, steps = steps, z.parts[1]
         base = steps * step
@@ -591,9 +613,15 @@
         spectra = spectra + more
         got = exchange(send)
         for c in early:
-            arrived[c] += [(got, g * step + c * share, share) for g in range(steps)]
-        arrived[-2] += [(got, base + g * begun, share) for g in range(z.steps)]
-        arrived[-1] += [(got, base + g * begun + share, z.step_quads) for g in range(z.steps)]
+            arrived[c] += [
+                (got, g * step + c * share, share, (begin + g) * share) for g in range(steps)
+            ]
+        for g in range(z.steps):
+            first = base + g * begun
+            arrived[-2].append((got, first, share, g * share))
+            arrived[-1] += [
+                (got, first + share + q, 1, g * share + 2 * q) for q in range(z.step_quads)
+            ]
 
     beams, bit = beam_call(z, me_array, spectra, delays), 1
     while beams.shape[0] > 1:
@@ -604,13 +632,11 @@
         last, beams = lax.optimization_barrier((last, beams))
         got = exchange(last)
         k = z.chunks - 1
-        vis = receive_call(z, 0, None, arrived[:k], take_key[:k], None)
-        vis = receive_call(z, k, 0, arrived[k:], take_key[k:], vis)
-        vis = receive_call(z, k, 1, [[(got, 0, z.quads)]], take_key[k:], vis)
+        vis = receive_call(z, 0, None, arrived, take_key, None, even_last=True)
+        vis = receive_call(z, k, 1, [[(got, 0, z.quads, 0)]], take_key[k:], vis)
     else:
         vis = receive_call(z, 0, None, arrived, take_key, None)
-    beams = beams.reshape(z.chunks, 2, BAND_CH // 2, 2 * BEAMS * FR)
-    beams = jnp.swapaxes(beams, 1, 2).reshape(z.chan_dev, 2 * BEAMS * FR)
+    beams = beams.reshape(z.chan_dev, 2 * BEAMS * FR)
     return (vis.reshape(z.chan_dev, 2, FSUB, FSUB), beams)
 
 

time: 181 us -> 180 us (level)
    pallas_call x3 -> x2, Pallas kernels: 22.6 us -> 22.6 us  [receive_call(): pl.pallas_call(functools.partial(receive_kernel, z, parities, step_pairs,...]
  transfers between devices with their start and end apart: 7 -> 7, of which waited for: 5 -> 5; matrix products, arithmetic and copies ran while one was open for 4% -> 4% of each run, Pallas kernels for 37% -> 36%
where the time goes in v9:
time: 180 us; the launch traced here: 178 us
  Pallas kernels  79.9 us (44%)
  waiting for transfers between devices  67 us (37%)
  starting transfers between devices  23 us (13%)
  other arithmetic  6.07 us (3%)
    ppermute x4, waiting for transfers between devices, swap(): return lax.ppermute(x, 'chan', [(i, i ^ offset) for i in range(z.devices)])  58.6 us
    pallas_call x2, Pallas kernels, first(): pl.pallas_call(functools.partial(first_kernel, z, self.scale, chunks, len...  24.2 us
    pallas_call x2, Pallas kernels, receive_call(): pl.pallas_call(functools.partial(receive_kernel, z, parities, step_pairs,...  22.6 us
    pallas_call x1, Pallas kernels, beam_call(): pl.pallas_call(functools.partial(beam_kernel, z), grid_spec=grid_spec, ou...  20.2 us
    all_to_all x3, starting transfers between devices, exchange(): return lax.all_to_all(x, 'chan', split_axis=0, concat_axis=0, tiled=True)  19.1 us
    pallas_call x1, Pallas kernels, next(): pl.pallas_call(functools.partial(next_kernel, z, self.scale, chunks), in_...  12.8 us
    all_to_all x3, waiting for transfers between devices, exchange(): return lax.all_to_all(x, 'chan', split_axis=0, concat_axis=0, tiled=True)  8.35 us
    ppermute x4, starting transfers between devices, swap(): return lax.ppermute(x, 'chan', [(i, i ^ offset) for i in range(z.devices)])  3.86 us
  transfers between devices with their start and end apart: 7, of which 5 were waited for; matrix products, arithmetic and copies ran while one was open for 4% of the time, Pallas kernels for 36%

profile of v9, /device:TPU:5, one launch (start us, length us, event | category | flops | bytes accessed | tf_op | source)
XLA Modules:
  0.0 178.3 jit_solution(96897892143925381)
XLA Ops:
  0.6 12.1 %filter_spectra.2 = (bf16[3072,2048]{1,0:T(8,128)(2,1)}, bf16[512,3072]{1,0:T(8,128)(2,1)}, bf16[512,3072]{1,0:T(8,128)(2,1)}, bf16[16,24,16,128]{3,2,1,0:T(8,128)(2,1)}) custom-call(s32[1]{0:T(128)} %bitcast.me_ref, bf16[64,104448]{1,0:T(8,128)(2,1)} %h2_ref.3, bf16[64,104448]{1,0:T(8,128)(2,1)} %h2_ref.3, bf16[64,104448]{1,0:T(8,128)(2,1)} %h2_ref.3, ...), custom_call_target="tpu_custom_call" | custom-call | flops 3221225472 | bytes 9000000 | tf_op jit(solution)/shard_map/filter_spectra/pallas_call | solution.py:276
  12.7 6.7 %all-to-all-start.1 = ((bf16[16,24,16,128]{3,2,1,0:T(8,128)(2,1)}), bf16[16,24,16,128]{3,2,1,0:T(8,128)(2,1)S(1)}, u32[]{:S(2)}, u32[]{:S(2)}) async-start(bf16[16,24,16,128]{3,2,1,0:T(8,128)(2,1)} %get-tuple-element.27), calls=%async_computation.1 | async-start | bytes 3145728 | tf_op jit(solution)/shard_map/all_to_all | solution.py:575
  19.4 12.1 %filter_spectra.3 = (bf16[3072,2048]{1,0:T(8,128)(2,1)}, bf16[512,3072]{1,0:T(8,128)(2,1)}, bf16[512,3072]{1,0:T(8,128)(2,1)}, bf16[16,60,16,128]{3,2,1,0:T(8,128)(2,1)}) custom-call(s32[1]{0:T(128)} %bitcast.me_ref, bf16[64,104448]{1,0:T(8,128)(2,1)} %h2_ref.3, ...), custom_call_target="tpu_custom_call", output_to_operand_aliasing={{0}: (8, {}), {1}: (9, {}), {2}: (10, {})} | custom-call | flops 3221225472 | bytes 9000000 | tf_op jit(solution)/shard_map/filter_spectra/pallas_call | solution.py:276
  31.5 12.8 %spectra_next.1 = (bf16[512,3072]{1,0:T(8,128)(2,1)}, bf16[512,3072]{1,0:T(8,128)(2,1)}, bf16[16,60,16,128]{3,2,1,0:T(8,128)(2,1)}, bf16[16,12,16,128]{3,2,1,0:T(8,128)(2,1)}) custom-call(s32[1]{0:T(128)} %bitcast.me_ref, bf16[3072,2048]{1,0:T(8,128)(2,1)} %get-tuple-element.19.filt_ref, ...), custom_call_target="tpu_custom_call", output_to_operand_aliasing={{2}: (4, {})} | custom-call | flops 6442450944 | bytes 18000000 | tf_op jit(solution)/shard_map/spectra_next/pallas_call | solution.py:306
  44.4 8.3 %all-to-all-done.1.refs_0_ = bf16[16,24,16,128]{3,2,1,0:T(8,128)(2,1)S(1)} async-done(((bf16[16,24,16,128]{3,2,1,0:T(8,128)(2,1)}), bf16[16,24,16,128]{3,2,1,0:T(8,128)(2,1)S(1)}, u32[]{:S(2)}, u32[]{:S(2)}) %all-to-all-start.1) | async-done | bytes 1572896 | tf_op jit(solution)/shard_map/all_to_all | solution.py:575
  52.7 7.9 %all-to-all-start.2 = ((bf16[16,60,16,128]{3,2,1,0:T(8,128)(2,1)}), bf16[16,60,16,128]{3,2,1,0:T(8,128)(2,1)}, u32[]{:S(2)}, u32[]{:S(2)}) async-start(bf16[16,60,16,128]{3,2,1,0:T(8,128)(2,1)} %get-tuple-element.28), calls=%async_computation.2 | async-start | bytes 7864320 | tf_op jit(solution)/shard_map/all_to_all | solution.py:575
  60.8 1.2 fusion.2
  62.0 1.8 %fusion = (f32[4,64,256]{2,1,0:T(8,128)}, f32[4,64,256]{2,1,0:T(8,128)}) fusion(f32[64]{0:T(128)S(1)} %copy-done.1, f32[4,256]{1,0:T(4,128)S(1)} %mul.66), kind=kLoop, calls=%fused_computation.4 | loop fusion | flops 131072 | bytes 528640 | tf_op jit(solution)/shard_map/sin | solution.py:565
  63.8 20.2 %beam_sums.1 = f32[16,64,384]{2,1,0:T(8,128)} custom-call(s32[1]{0:T(128)} %bitcast.me_ref, bf16[512,3072]{1,0:T(8,128)(2,1)} %get-tuple-element.22.refs_0_, bf16[512,3072]{1,0:T(8,128)(2,1)} %get-tuple-element.23.refs_1_, bf16[512,3072]{1,0:T(8,128)(2,1)} %get-tuple-element.24.refs_2_, bf16[512,3072]{1,0:T(8,128)(2,1)} %get-tuple-element.25.refs_3_, ...), custom_call_target="tpu_custom_call" | custom-call | flops 20000000000 | bytes 20000000 | tf_op jit(solution)/shard_map/beam_sums/pallas_call | solution.py:555
  84.0 1.2 slice.38
  85.2 0.4 collective-permute-start
  85.7 1.9 %collective-permute-done = f32[8,64,384]{2,1,0:T(8,128)S(1)} collective-permute-done((f32[8,64,384]{2,1,0:T(8,128)S(1)}, f32[8,64,384]{2,1,0:T(8,128)S(1)}, u32[]{:S(2)}, u32[]{:S(2)}) %collective-permute-start) | collective-permute-done | bytes 786464 | tf_op jit(solution)/shard_map/ppermute | solution.py:571
  87.6 1.2 slice_add_fusion
  88.8 0.1 collective-permute-start.1
  89.0 0.7 broadcast_multiply_fusion
  89.7 0.4 convert_reduce_fusion
  90.1 19.6 %collective-permute-done.1 = f32[4,64,384]{2,1,0:T(8,128)S(1)} collective-permute-done((f32[4,64,384]{2,1,0:T(8,128)S(1)}, f32[4,64,384]{2,1,0:T(8,128)S(1)}, u32[]{:S(2)}, u32[]{:S(2)}) %collective-permute-start.1) | collective-permute-done | bytes 393248 | tf_op jit(solution)/shard_map/ppermute | solution.py:571
  109.8 19.7 %collective-permute-done.2 = f32[2,64,384]{2,1,0:T(8,128)S(1)} collective-permute-done((f32[2,64,384]{2,1,0:T(8,128)S(1)}, f32[2,64,384]{2,1,0:T(8,128)S(1)}, u32[]{:S(2)}, u32[]{:S(2)}) %collective-permute-start.2) | collective-permute-done | bytes 196640 | tf_op jit(solution)/shard_map/ppermute | solution.py:571
  129.6 3.2 %collective-permute-start.3 = (bf16[1,64,384]{2,1,0:T(8,128)(2,1)S(1)}, bf16[1,64,384]{2,1,0:T(8,128)(2,1)S(1)}, u32[]{:S(2)}, u32[]{:S(2)}) collective-permute-start(bf16[1,64,384]{2,1,0:T(8,128)(2,1)S(1)} %slice.51), channel_id=1, source_target_pairs={{0,8},{1,9},{2,10},{3,11},{4,12},{5,13},{6,14},{7,15},{8,0},{9,1},... | collective-permute-start | bytes 147464 | tf_op jit(solution)/shard_map/ppermute | solution.py:571
  132.8 17.4 %collective-permute-done.3 = bf16[1,64,384]{2,1,0:T(8,128)(2,1)S(1)} collective-permute-done((bf16[1,64,384]{2,1,0:T(8,128)(2,1)S(1)}, bf16[1,64,384]{2,1,0:T(8,128)(2,1)S(1)}, u32[]{:S(2)}, u32[]{:S(2)}) %collective-permute-start.3) | collective-permute-done | bytes 49184 | tf_op jit(solution)/shard_map/ppermute | solution.py:571
  150.2 0.7 slice_add_fusion.3
  150.9 4.6 %all-to-all-start = ((bf16[16,12,16,128]{3,2,1,0:T(8,128)(2,1)}), bf16[16,12,16,128]{3,2,1,0:T(8,128)(2,1)S(1)}, u32[]{:S(2)}, u32[]{:S(2)}) async-start(bf16[16,12,16,128]{3,2,1,0:T(8,128)(2,1)} %get-tuple-element.26), calls=%async_computation | async-start | bytes 1572864 | tf_op jit(solution)/shard_map/all_to_all | solution.py:575
  155.5 19.6 %correlate.2.refs_2_ = f32[32,2,2,256,256]{4,3,2,1,0:T(8,128)} custom-call(bf16[16,24,16,128]{3,2,1,0:T(8,128)(2,1)S(1)} %all-to-all-done.1.refs_0_, bf16[16,60,16,128]{3,2,1,0:T(8,128)(2,1)} %all-to-all-done.2.refs_1_, s32[4,4,256]{2,1,0:T(4,128)S(1)} %multiply_add_fusion.refs_2_), custom_call_target="tpu_custom_call" | custom-call | flops 16000000000 | bytes 40000000 | tf_op jit(solution)/shard_map/correlate/pallas_call | solution.py:455
  175.1 3.0 %correlate.3 = f32[32,2,2,256,256]{4,3,2,1,0:T(8,128)} custom-call(bf16[16,12,16,128]{3,2,1,0:T(8,128)(2,1)S(1)} %all-to-all-done.refs_0_, s32[1,4,256]{2,1,0:T(4,128)S(1)} %slice.45.refs_1_, f32[32,2,2,256,256]{4,3,2,1,0:T(8,128)} %correlate.2.refs_2_), custom_call_target="tpu_custom_call", output_to_operand_aliasing={{}: (2, {})} | custom-call | flops 2000000000 | bytes 5000000 | tf_op jit(solution)/shard_map/correlate/pallas_call | solution.py:455
  (19 shorter events, 0.4 us)
Async XLA Ops:
  12.7 40.0 %all-to-all-start.1 = ((bf16[16,24,16,128]{3,2,1,0:T(8,128)(2,1)}), bf16[16,24,16,128]{3,2,1,0:T(8,128)(2,1)S(1)}, u32[]{:S(2)}, u32[]{:S(2)}) async-start(bf16[16,24,16,128]{3,2,1,0:T(8,128)(2,1)} %get-tuple-element.27), calls=%async_computation.1 | async-start | bytes 3145728 | tf_op jit(solution)/shard_map/all_to_all | solution.py:575
  52.7 7.9 %copy-start = (f32[4,64]{1,0:T(4,128)S(1)}, f32[4,64]{1,0:T(4,128)}, u32[]{:S(2)}) copy-start(f32[4,64]{1,0:T(4,128)} %param.9) | copy-start | bytes 3076
  52.7 9.3 %copy-start.1 = (f32[64]{0:T(128)S(1)}, f32[64]{0:T(128)}, u32[]{:S(2)}) copy-start(f32[64]{0:T(128)} %constant.68.clone) | copy-start | bytes 772
  52.7 98.1 %all-to-all-start.2 = ((bf16[16,60,16,128]{3,2,1,0:T(8,128)(2,1)}), bf16[16,60,16,128]{3,2,1,0:T(8,128)(2,1)}, u32[]{:S(2)}, u32[]{:S(2)}) async-start(bf16[16,60,16,128]{3,2,1,0:T(8,128)(2,1)} %get-tuple-element.28), calls=%async_computation.2 | async-start | bytes 7864320 | tf_op jit(solution)/shard_map/all_to_all | solution.py:575
  85.2 2.4 %collective-permute-start = (f32[8,64,384]{2,1,0:T(8,128)S(1)}, f32[8,64,384]{2,1,0:T(8,128)S(1)}, u32[]{:S(2)}, u32[]{:S(2)}) collective-permute-start(f32[8,64,384]{2,1,0:T(8,128)S(1)} %slice.38), channel_id=1, source_target_pairs={{0,1},{1,0},{2,3},{3,2},{4,5},{5,4},{6,7},{7,6},{8,9},{9,8},{10,11... | collective-permute-start | bytes 2359304 | tf_op jit(solution)/shard_map/ppermute | solution.py:571
  88.8 20.8 %collective-permute-start.1 = (f32[4,64,384]{2,1,0:T(8,128)S(1)}, f32[4,64,384]{2,1,0:T(8,128)S(1)}, u32[]{:S(2)}, u32[]{:S(2)}) collective-permute-start(f32[4,64,384]{2,1,0:T(8,128)S(1)} %slice.40), channel_id=1, source_target_pairs={{0,2},{1,3},{2,0},{3,1},{4,6},{5,7},{6,4},{7,5},{8,10},{9,11},{10,... | collective-permute-start | bytes 1179656 | tf_op jit(solution)/shard_map/ppermute | solution.py:571
  109.7 19.8 %collective-permute-start.2 = (f32[2,64,384]{2,1,0:T(8,128)S(1)}, f32[2,64,384]{2,1,0:T(8,128)S(1)}, u32[]{:S(2)}, u32[]{:S(2)}) collective-permute-start(f32[2,64,384]{2,1,0:T(8,128)S(1)} %slice.42), channel_id=1, source_target_pairs={{0,4},{1,5},{2,6},{3,7},{4,0},{5,1},{6,2},{7,3},{8,12},{9,13},{10,... | collective-permute-start | bytes 589832 | tf_op jit(solution)/shard_map/ppermute | solution.py:571
  129.6 20.6 %collective-permute-start.3 = (bf16[1,64,384]{2,1,0:T(8,128)(2,1)S(1)}, bf16[1,64,384]{2,1,0:T(8,128)(2,1)S(1)}, u32[]{:S(2)}, u32[]{:S(2)}) collective-permute-start(bf16[1,64,384]{2,1,0:T(8,128)(2,1)S(1)} %slice.51), channel_id=1, source_target_pairs={{0,8},{1,9},{2,10},{3,11},{4,12},{5,13},{6,14},{7,15},{8,0},{9,1},... | collective-permute-start | bytes 147464 | tf_op jit(solution)/shard_map/ppermute | solution.py:571
  150.9 24.2 %all-to-all-start = ((bf16[16,12,16,128]{3,2,1,0:T(8,128)(2,1)}), bf16[16,12,16,128]{3,2,1,0:T(8,128)(2,1)S(1)}, u32[]{:S(2)}, u32[]{:S(2)}) async-start(bf16[16,12,16,128]{3,2,1,0:T(8,128)(2,1)} %get-tuple-element.26), calls=%async_computation | async-start | bytes 1572864 | tf_op jit(solution)/shard_map/all_to_all | solution.py:575

commit v10 on v9

--- a/solution.py
+++ b/solution.py
@@ -363,15 +363,15 @@
     def _():
         c = g // steps
         slot = lax.broadcasted_iota(jnp.int32, (z.groups * LANES, FSUB), 0)
-        lane_group = lax.broadcasted_iota(jnp.int32, (depth, LANES), 1) // z.cap
+        lane_group = lax.broadcasted_iota(jnp.int32, (BAND_CH, LANES), 1) // z.cap
+        masks = [jnp.where(lane_group == i, 1.0, 0.0).astype(jnp.bfloat16) for i in range(lf)]
         for tau in range(lf):
             tiles = []
             for big in range(z.groups):
-                tile = buf_ref[c % slots, big * lf + tau].reshape(depth, LANES)
+                tile = buf_ref[c % slots, big * lf + tau] * masks[0]
                 for lane in range(1, lf):
-                    block = buf_ref[c % slots, big * lf + (lane ^ tau)].reshape(depth, LANES)
-                    tile = jnp.where(lane_group == lane, block, tile)
-                tiles.append(tile)
+                    tile = tile + buf_ref[c % slots, big * lf + (lane ^ tau)] * masks[lane]
+                tiles.append(tile.reshape(depth, LANES))
             key = key_ref[c, tau : tau + 1, :]
             pick = jnp.where(slot == key, 1.0, 0.0).astype(jnp.bfloat16)
             rows = jnp.dot(

time: 180 us -> 182 us (1.011)
  transfers between devices with their start and end apart: 7 -> 7, of which waited for: 5 -> 5; matrix products, arithmetic and copies ran while one was open for 4% -> 4% of each run, Pallas kernels for 36% -> 37%
where the time goes in v10:
time: 182 us; the launch traced here: 180 us
  Pallas kernels  81.5 us (45%)
  waiting for transfers between devices  67 us (37%)
  starting transfers between devices  23 us (13%)
  other arithmetic  6.07 us (3%)
    ppermute x4, waiting for transfers between devices, swap(): return lax.ppermute(x, 'chan', [(i, i ^ offset) for i in range(z.devices)])  58.6 us
    pallas_call x2, Pallas kernels, receive_call(): pl.pallas_call(functools.partial(receive_kernel, z, parities, step_pairs,...  24.2 us
    pallas_call x2, Pallas kernels, first(): pl.pallas_call(functools.partial(first_kernel, z, self.scale, chunks, len...  24.2 us
    pallas_call x1, Pallas kernels, beam_call(): pl.pallas_call(functools.partial(beam_kernel, z), grid_spec=grid_spec, ou...  20.2 us
    all_to_all x3, starting transfers between devices, exchange(): return lax.all_to_all(x, 'chan', split_axis=0, concat_axis=0, tiled=True)  19.1 us
    pallas_call x1, Pallas kernels, next(): pl.pallas_call(functools.partial(next_kernel, z, self.scale, chunks), in_...  12.8 us
    all_to_all x3, waiting for transfers between devices, exchange(): return lax.all_to_all(x, 'chan', split_axis=0, concat_axis=0, tiled=True)  8.35 us
    ppermute x4, starting transfers between devices, swap(): return lax.ppermute(x, 'chan', [(i, i ^ offset) for i in range(z.devices)])  3.86 us
  transfers between devices with their start and end apart: 7, of which 5 were waited for; matrix products, arithmetic and copies ran while one was open for 4% of the time, Pallas kernels for 37%

profile of v10, /device:TPU:5, one launch (start us, length us, event | category | flops | bytes accessed | tf_op | source)
XLA Modules:
  0.0 179.9 jit_solution(1722978861725110388)
XLA Ops:
  0.6 12.1 %filter_spectra.2 = (bf16[3072,2048]{1,0:T(8,128)(2,1)}, bf16[512,3072]{1,0:T(8,128)(2,1)}, bf16[512,3072]{1,0:T(8,128)(2,1)}, bf16[16,24,16,128]{3,2,1,0:T(8,128)(2,1)}) custom-call(s32[1]{0:T(128)} %bitcast.me_ref, bf16[64,104448]{1,0:T(8,128)(2,1)} %h2_ref.3, bf16[64,104448]{1,0:T(8,128)(2,1)} %h2_ref.3, bf16[64,104448]{1,0:T(8,128)(2,1)} %h2_ref.3, ...), custom_call_target="tpu_custom_call" | custom-call | flops 3221225472 | bytes 9000000 | tf_op jit(solution)/shard_map/filter_spectra/pallas_call | solution.py:276
  12.7 6.7 %all-to-all-start.1 = ((bf16[16,24,16,128]{3,2,1,0:T(8,128)(2,1)}), bf16[16,24,16,128]{3,2,1,0:T(8,128)(2,1)S(1)}, u32[]{:S(2)}, u32[]{:S(2)}) async-start(bf16[16,24,16,128]{3,2,1,0:T(8,128)(2,1)} %get-tuple-element.27), calls=%async_computation.1 | async-start | bytes 3145728 | tf_op jit(solution)/shard_map/all_to_all | solution.py:575
  19.4 12.1 %filter_spectra.3 = (bf16[3072,2048]{1,0:T(8,128)(2,1)}, bf16[512,3072]{1,0:T(8,128)(2,1)}, bf16[512,3072]{1,0:T(8,128)(2,1)}, bf16[16,60,16,128]{3,2,1,0:T(8,128)(2,1)}) custom-call(s32[1]{0:T(128)} %bitcast.me_ref, bf16[64,104448]{1,0:T(8,128)(2,1)} %h2_ref.3, ...), custom_call_target="tpu_custom_call", output_to_operand_aliasing={{0}: (8, {}), {1}: (9, {}), {2}: (10, {})} | custom-call | flops 3221225472 | bytes 9000000 | tf_op jit(solution)/shard_map/filter_spectra/pallas_call | solution.py:276
  31.5 12.8 %spectra_next.1 = (bf16[512,3072]{1,0:T(8,128)(2,1)}, bf16[512,3072]{1,0:T(8,128)(2,1)}, bf16[16,60,16,128]{3,2,1,0:T(8,128)(2,1)}, bf16[16,12,16,128]{3,2,1,0:T(8,128)(2,1)}) custom-call(s32[1]{0:T(128)} %bitcast.me_ref, bf16[3072,2048]{1,0:T(8,128)(2,1)} %get-tuple-element.19.filt_ref, ...), custom_call_target="tpu_custom_call", output_to_operand_aliasing={{2}: (4, {})} | custom-call | flops 6442450944 | bytes 18000000 | tf_op jit(solution)/shard_map/spectra_next/pallas_call | solution.py:306
  44.4 8.3 %all-to-all-done.1.refs_0_ = bf16[16,24,16,128]{3,2,1,0:T(8,128)(2,1)S(1)} async-done(((bf16[16,24,16,128]{3,2,1,0:T(8,128)(2,1)}), bf16[16,24,16,128]{3,2,1,0:T(8,128)(2,1)S(1)}, u32[]{:S(2)}, u32[]{:S(2)}) %all-to-all-start.1) | async-done | bytes 1572896 | tf_op jit(solution)/shard_map/all_to_all | solution.py:575
  52.7 7.9 %all-to-all-start.2 = ((bf16[16,60,16,128]{3,2,1,0:T(8,128)(2,1)}), bf16[16,60,16,128]{3,2,1,0:T(8,128)(2,1)}, u32[]{:S(2)}, u32[]{:S(2)}) async-start(bf16[16,60,16,128]{3,2,1,0:T(8,128)(2,1)} %get-tuple-element.28), calls=%async_computation.2 | async-start | bytes 7864320 | tf_op jit(solution)/shard_map/all_to_all | solution.py:575
  60.8 1.2 fusion.2
  62.0 1.8 %fusion = (f32[4,64,256]{2,1,0:T(8,128)}, f32[4,64,256]{2,1,0:T(8,128)}) fusion(f32[64]{0:T(128)S(1)} %copy-done.1, f32[4,256]{1,0:T(4,128)S(1)} %mul.66), kind=kLoop, calls=%fused_computation.4 | loop fusion | flops 131072 | bytes 528640 | tf_op jit(solution)/shard_map/sin | solution.py:565
  63.8 20.2 %beam_sums.1 = f32[16,64,384]{2,1,0:T(8,128)} custom-call(s32[1]{0:T(128)} %bitcast.me_ref, bf16[512,3072]{1,0:T(8,128)(2,1)} %get-tuple-element.22.refs_0_, bf16[512,3072]{1,0:T(8,128)(2,1)} %get-tuple-element.23.refs_1_, bf16[512,3072]{1,0:T(8,128)(2,1)} %get-tuple-element.24.refs_2_, bf16[512,3072]{1,0:T(8,128)(2,1)} %get-tuple-element.25.refs_3_, ...), custom_call_target="tpu_custom_call" | custom-call | flops 20000000000 | bytes 20000000 | tf_op jit(solution)/shard_map/beam_sums/pallas_call | solution.py:555
  84.0 1.2 slice.38
  85.2 0.4 collective-permute-start
  85.7 1.9 %collective-permute-done = f32[8,64,384]{2,1,0:T(8,128)S(1)} collective-permute-done((f32[8,64,384]{2,1,0:T(8,128)S(1)}, f32[8,64,384]{2,1,0:T(8,128)S(1)}, u32[]{:S(2)}, u32[]{:S(2)}) %collective-permute-start) | collective-permute-done | bytes 786464 | tf_op jit(solution)/shard_map/ppermute | solution.py:571
  87.6 1.2 slice_add_fusion
  88.8 0.1 collective-permute-start.1
  89.0 0.7 broadcast_multiply_fusion
  89.7 0.4 convert_reduce_fusion
  90.1 19.6 %collective-permute-done.1 = f32[4,64,384]{2,1,0:T(8,128)S(1)} collective-permute-done((f32[4,64,384]{2,1,0:T(8,128)S(1)}, f32[4,64,384]{2,1,0:T(8,128)S(1)}, u32[]{:S(2)}, u32[]{:S(2)}) %collective-permute-start.1) | collective-permute-done | bytes 393248 | tf_op jit(solution)/shard_map/ppermute | solution.py:571
  109.8 19.7 %collective-permute-done.2 = f32[2,64,384]{2,1,0:T(8,128)S(1)} collective-permute-done((f32[2,64,384]{2,1,0:T(8,128)S(1)}, f32[2,64,384]{2,1,0:T(8,128)S(1)}, u32[]{:S(2)}, u32[]{:S(2)}) %collective-permute-start.2) | collective-permute-done | bytes 196640 | tf_op jit(solution)/shard_map/ppermute | solution.py:571
  129.6 3.2 %collective-permute-start.3 = (bf16[1,64,384]{2,1,0:T(8,128)(2,1)S(1)}, bf16[1,64,384]{2,1,0:T(8,128)(2,1)S(1)}, u32[]{:S(2)}, u32[]{:S(2)}) collective-permute-start(bf16[1,64,384]{2,1,0:T(8,128)(2,1)S(1)} %slice.51), channel_id=1, source_target_pairs={{0,8},{1,9},{2,10},{3,11},{4,12},{5,13},{6,14},{7,15},{8,0},{9,1},... | collective-permute-start | bytes 147464 | tf_op jit(solution)/shard_map/ppermute | solution.py:571
  132.8 17.4 %collective-permute-done.3 = bf16[1,64,384]{2,1,0:T(8,128)(2,1)S(1)} collective-permute-done((bf16[1,64,384]{2,1,0:T(8,128)(2,1)S(1)}, bf16[1,64,384]{2,1,0:T(8,128)(2,1)S(1)}, u32[]{:S(2)}, u32[]{:S(2)}) %collective-permute-start.3) | collective-permute-done | bytes 49184 | tf_op jit(solution)/shard_map/ppermute | solution.py:571
  150.2 0.7 slice_add_fusion.3
  150.9 4.6 %all-to-all-start = ((bf16[16,12,16,128]{3,2,1,0:T(8,128)(2,1)}), bf16[16,12,16,128]{3,2,1,0:T(8,128)(2,1)S(1)}, u32[]{:S(2)}, u32[]{:S(2)}) async-start(bf16[16,12,16,128]{3,2,1,0:T(8,128)(2,1)} %get-tuple-element.26), calls=%async_computation | async-start | bytes 1572864 | tf_op jit(solution)/shard_map/all_to_all | solution.py:575
  155.5 21.0 %correlate.2.refs_2_ = f32[32,2,2,256,256]{4,3,2,1,0:T(8,128)} custom-call(bf16[16,24,16,128]{3,2,1,0:T(8,128)(2,1)S(1)} %all-to-all-done.1.refs_0_, bf16[16,60,16,128]{3,2,1,0:T(8,128)(2,1)} %all-to-all-done.2.refs_1_, s32[4,4,256]{2,1,0:T(4,128)S(1)} %multiply_add_fusion.refs_2_), custom_call_target="tpu_custom_call" | custom-call | flops 16000000000 | bytes 40000000 | tf_op jit(solution)/shard_map/correlate/pallas_call | solution.py:455
  176.5 3.2 %correlate.3 = f32[32,2,2,256,256]{4,3,2,1,0:T(8,128)} custom-call(bf16[16,12,16,128]{3,2,1,0:T(8,128)(2,1)S(1)} %all-to-all-done.refs_0_, s32[1,4,256]{2,1,0:T(4,128)S(1)} %slice.45.refs_1_, f32[32,2,2,256,256]{4,3,2,1,0:T(8,128)} %correlate.2.refs_2_), custom_call_target="tpu_custom_call", output_to_operand_aliasing={{}: (2, {})} | custom-call | flops 2000000000 | bytes 5000000 | tf_op jit(solution)/shard_map/correlate/pallas_call | solution.py:455
  (19 shorter events, 0.4 us)
Async XLA Ops:
  12.7 40.0 %all-to-all-start.1 = ((bf16[16,24,16,128]{3,2,1,0:T(8,128)(2,1)}), bf16[16,24,16,128]{3,2,1,0:T(8,128)(2,1)S(1)}, u32[]{:S(2)}, u32[]{:S(2)}) async-start(bf16[16,24,16,128]{3,2,1,0:T(8,128)(2,1)} %get-tuple-element.27), calls=%async_computation.1 | async-start | bytes 3145728 | tf_op jit(solution)/shard_map/all_to_all | solution.py:575
  52.7 7.9 %copy-start = (f32[4,64]{1,0:T(4,128)S(1)}, f32[4,64]{1,0:T(4,128)}, u32[]{:S(2)}) copy-start(f32[4,64]{1,0:T(4,128)} %param.9) | copy-start | bytes 3076
  52.7 9.3 %copy-start.1 = (f32[64]{0:T(128)S(1)}, f32[64]{0:T(128)}, u32[]{:S(2)}) copy-start(f32[64]{0:T(128)} %constant.68.clone) | copy-start | bytes 772
  52.7 98.1 %all-to-all-start.2 = ((bf16[16,60,16,128]{3,2,1,0:T(8,128)(2,1)}), bf16[16,60,16,128]{3,2,1,0:T(8,128)(2,1)}, u32[]{:S(2)}, u32[]{:S(2)}) async-start(bf16[16,60,16,128]{3,2,1,0:T(8,128)(2,1)} %get-tuple-element.28), calls=%async_computation.2 | async-start | bytes 7864320 | tf_op jit(solution)/shard_map/all_to_all | solution.py:575
  85.2 2.4 %collective-permute-start = (f32[8,64,384]{2,1,0:T(8,128)S(1)}, f32[8,64,384]{2,1,0:T(8,128)S(1)}, u32[]{:S(2)}, u32[]{:S(2)}) collective-permute-start(f32[8,64,384]{2,1,0:T(8,128)S(1)} %slice.38), channel_id=1, source_target_pairs={{0,1},{1,0},{2,3},{3,2},{4,5},{5,4},{6,7},{7,6},{8,9},{9,8},{10,11... | collective-permute-start | bytes 2359304 | tf_op jit(solution)/shard_map/ppermute | solution.py:571
  88.8 20.8 %collective-permute-start.1 = (f32[4,64,384]{2,1,0:T(8,128)S(1)}, f32[4,64,384]{2,1,0:T(8,128)S(1)}, u32[]{:S(2)}, u32[]{:S(2)}) collective-permute-start(f32[4,64,384]{2,1,0:T(8,128)S(1)} %slice.40), channel_id=1, source_target_pairs={{0,2},{1,3},{2,0},{3,1},{4,6},{5,7},{6,4},{7,5},{8,10},{9,11},{10,... | collective-permute-start | bytes 1179656 | tf_op jit(solution)/shard_map/ppermute | solution.py:571
  109.7 19.8 %collective-permute-start.2 = (f32[2,64,384]{2,1,0:T(8,128)S(1)}, f32[2,64,384]{2,1,0:T(8,128)S(1)}, u32[]{:S(2)}, u32[]{:S(2)}) collective-permute-start(f32[2,64,384]{2,1,0:T(8,128)S(1)} %slice.42), channel_id=1, source_target_pairs={{0,4},{1,5},{2,6},{3,7},{4,0},{5,1},{6,2},{7,3},{8,12},{9,13},{10,... | collective-permute-start | bytes 589832 | tf_op jit(solution)/shard_map/ppermute | solution.py:571
  129.6 20.6 %collective-permute-start.3 = (bf16[1,64,384]{2,1,0:T(8,128)(2,1)S(1)}, bf16[1,64,384]{2,1,0:T(8,128)(2,1)S(1)}, u32[]{:S(2)}, u32[]{:S(2)}) collective-permute-start(bf16[1,64,384]{2,1,0:T(8,128)(2,1)S(1)} %slice.51), channel_id=1, source_target_pairs={{0,8},{1,9},{2,10},{3,11},{4,12},{5,13},{6,14},{7,15},{8,0},{9,1},... | collective-permute-start | bytes 147464 | tf_op jit(solution)/shard_map/ppermute | solution.py:571
  150.9 25.6 %all-to-all-start = ((bf16[16,12,16,128]{3,2,1,0:T(8,128)(2,1)}), bf16[16,12,16,128]{3,2,1,0:T(8,128)(2,1)S(1)}, u32[]{:S(2)}, u32[]{:S(2)}) async-start(bf16[16,12,16,128]{3,2,1,0:T(8,128)(2,1)} %get-tuple-element.26), calls=%async_computation | async-start | bytes 1572864 | tf_op jit(solution)/shard_map/all_to_all | solution.py:575

commit v11 on v9

--- a/solution.py
+++ b/solution.py
@@ -327,7 +327,7 @@
 
 def receive_kernel(z, parities, step_pairs, runs, arrays, even_steps, *refs):
     arr_refs, key_ref = refs[:arrays], refs[arrays]
-    vis_ref, buf_ref, rows_ref, sems = refs[-4:]
+    vis_ref, buf_ref, rows_ref, pick_ref, sems = refs[-5:]
     g = pl.program_id(0)
     lf = z.lane_frames
     few = BAND_CH // 2
@@ -346,13 +346,22 @@
             for i, (array, first, count, place) in enumerate(runs[c])
         ]
 
+    @pl.when(g == 0)
+    def _():
+        for copy in copies(0):
+            copy.start()
+
+    @pl.when(at == 0)
+    def _():
+        slot = lax.broadcasted_iota(jnp.int32, (z.groups * LANES, FSUB), 0)
+        for tau in range(lf):
+            key = key_ref[g // steps, tau : tau + 1, :]
+            pick_ref[tau] = jnp.where(slot == key, 1.0, 0.0).astype(jnp.bfloat16)
+
     for c in range(len(runs)):
 
         @pl.when(g == c * steps)
         def _():
-            if c == 0:
-                for copy in copies(c):
-                    copy.start()
             for copy in copies(c):
                 copy.wait()
             if c + 1 < len(runs):
@@ -362,7 +371,6 @@
     @pl.when(at == 0)
     def _():
         c = g // steps
-        slot = lax.broadcasted_iota(jnp.int32, (z.groups * LANES, FSUB), 0)
         lane_group = lax.broadcasted_iota(jnp.int32, (depth, LANES), 1) // z.cap
         for tau in range(lf):
             tiles = []
@@ -372,10 +380,8 @@
                     block = buf_ref[c % slots, big * lf + (lane ^ tau)].reshape(depth, LANES)
                     tile = jnp.where(lane_group == lane, block, tile)
                 tiles.append(tile)
-            key = key_ref[c, tau : tau + 1, :]
-            pick = jnp.where(slot == key, 1.0, 0.0).astype(jnp.bfloat16)
             rows = jnp.dot(
-                jnp.concatenate(tiles, axis=1), pick, preferred_element_type=jnp.float32
+                jnp.concatenate(tiles, axis=1), pick_ref[tau], preferred_element_type=jnp.float32
             )
             for side in range(FSUB // LANES):
                 rows_ref[side, tau * depth : (tau + 1) * depth, :] = rows[
@@ -429,7 +435,7 @@
 
 def receive_call(z, chunk, parity, arrived, keys, vis, even_last=False):
     parities = 2 if parity is None else 1
-    step_pairs = 4 // parities
+    step_pairs = 4
     steps = BAND_CH // 2 // step_pairs
     at = 0 if parity is None else parity
     out_shape = jax.ShapeDtypeStruct((z.chan_dev // 2, 2, 2, FSUB, FSUB), jnp.float32)
@@ -467,6 +473,7 @@
         scratch_shapes=[
             pltpu.VMEM((slots, z.devices, units, BAND_CH, LANES), jnp.bfloat16),
             pltpu.VMEM((FSUB // LANES, z.lane_frames * units * BAND_CH, LANES), jnp.float32),
+            pltpu.VMEM((z.lane_frames, z.groups * LANES, FSUB), jnp.bfloat16),
             pltpu.SemaphoreType.DMA((slots, max(len(x) for x in runs))),
         ],
         compiler_params=pltpu.CompilerParams(vmem_limit_bytes=VMEM // 2),
@@ -626,17 +633,20 @@
     beams, bit = beam_call(z, me_array, spectra, delays), 1
     while beams.shape[0] > 1:
         half = beams.shape[0] // 2
-        away = beams[half:].astype(jnp.bfloat16) if half == 1 else beams[half:]
-        beams, bit = beams[:half] + swap(z, away, bit).astype(jnp.float32), 2 * bit
+        kept, away = beams[:half], beams[half:]
+        if half > 1:
+            beams, bit = kept + swap(z, away, bit), 2 * bit
+        else:
+            beams = away = swap(z, away.astype(jnp.bfloat16), bit)
     if len(z.parts) > 1:
-        last, beams = lax.optimization_barrier((last, beams))
+        last, kept, away = lax.optimization_barrier((last, kept, away))
         got = exchange(last)
         k = z.chunks - 1
         vis = receive_call(z, 0, None, arrived, take_key, None, even_last=True)
         vis = receive_call(z, k, 1, [[(got, 0, z.quads, 0)]], take_key[k:], vis)
     else:
         vis = receive_call(z, 0, None, arrived, take_key, None)
-    beams = beams.reshape(z.chan_dev, 2 * BEAMS * FR)
+    beams = (kept + away.astype(jnp.float32)).reshape(z.chan_dev, 2 * BEAMS * FR)
     return (vis.reshape(z.chan_dev, 2, FSUB, FSUB), beams)
 
 

time: 180 us -> 179 us (level)
  Pallas kernels: 79.9 us -> 78.1 us
    pallas_call x2, Pallas kernels: 22.6 us -> 20.8 us  [receive_call(): pl.pallas_call(functools.partial(receive_kernel, z, parities, step_pairs,...]
  transfers between devices with their start and end apart: 7 -> 7, of which waited for: 5 -> 6; matrix products, arithmetic and copies ran while one was open for 4% -> 4% of each run, Pallas kernels for 36% -> 35%
where the time goes in v11:
time: 179 us; the launch traced here: 177 us
  Pallas kernels  78.1 us (44%)
  waiting for transfers between devices  67.8 us (38%)
  starting transfers between devices  23 us (13%)
  other arithmetic  6.07 us (3%)
    ppermute x4, waiting for transfers between devices, swap(): return lax.ppermute(x, 'chan', [(i, i ^ offset) for i in range(z.devices)])  58.6 us
    pallas_call x2, Pallas kernels, first(): pl.pallas_call(functools.partial(first_kernel, z, self.scale, chunks, len...  24.2 us
    pallas_call x2, Pallas kernels, receive_call(): pl.pallas_call(functools.partial(receive_kernel, z, parities, step_pairs,...  20.8 us
    pallas_call x1, Pallas kernels, beam_call(): pl.pallas_call(functools.partial(beam_kernel, z), grid_spec=grid_spec, ou...  20.2 us
    all_to_all x3, starting transfers between devices, exchange(): return lax.all_to_all(x, 'chan', split_axis=0, concat_axis=0, tiled=True)  19.1 us
    pallas_call x1, Pallas kernels, next(): pl.pallas_call(functools.partial(next_kernel, z, self.scale, chunks), in_...  12.8 us
    all_to_all x3, waiting for transfers between devices, exchange(): return lax.all_to_all(x, 'chan', split_axis=0, concat_axis=0, tiled=True)  9.17 us
    ppermute x4, starting transfers between devices, swap(): return lax.ppermute(x, 'chan', [(i, i ^ offset) for i in range(z.devices)])  3.86 us
  transfers between devices with their start and end apart: 7, of which 6 were waited for; matrix products, arithmetic and copies ran while one was open for 4% of the time, Pallas kernels for 35%

profile of v11, /device:TPU:5, one launch (start us, length us, event | category | flops | bytes accessed | tf_op | source)
XLA Modules:
  0.0 177.3 jit_solution(4709653839299369220)
XLA Ops:
  0.6 12.1 %filter_spectra.2 = (bf16[3072,2048]{1,0:T(8,128)(2,1)}, bf16[512,3072]{1,0:T(8,128)(2,1)}, bf16[512,3072]{1,0:T(8,128)(2,1)}, bf16[16,24,16,128]{3,2,1,0:T(8,128)(2,1)}) custom-call(s32[1]{0:T(128)} %bitcast.me_ref, bf16[64,104448]{1,0:T(8,128)(2,1)} %h2_ref.3, bf16[64,104448]{1,0:T(8,128)(2,1)} %h2_ref.3, bf16[64,104448]{1,0:T(8,128)(2,1)} %h2_ref.3, ...), custom_call_target="tpu_custom_call" | custom-call | flops 3221225472 | bytes 9000000 | tf_op jit(solution)/shard_map/filter_spectra/pallas_call | solution.py:276
  12.7 6.7 %all-to-all-start.1 = ((bf16[16,24,16,128]{3,2,1,0:T(8,128)(2,1)}), bf16[16,24,16,128]{3,2,1,0:T(8,128)(2,1)S(1)}, u32[]{:S(2)}, u32[]{:S(2)}) async-start(bf16[16,24,16,128]{3,2,1,0:T(8,128)(2,1)} %get-tuple-element.28), calls=%async_computation.1 | async-start | bytes 3145728 | tf_op jit(solution)/shard_map/all_to_all | solution.py:582
  19.4 12.1 %filter_spectra.3 = (bf16[3072,2048]{1,0:T(8,128)(2,1)}, bf16[512,3072]{1,0:T(8,128)(2,1)}, bf16[512,3072]{1,0:T(8,128)(2,1)}, bf16[16,60,16,128]{3,2,1,0:T(8,128)(2,1)}) custom-call(s32[1]{0:T(128)} %bitcast.me_ref, bf16[64,104448]{1,0:T(8,128)(2,1)} %h2_ref.3, ...), custom_call_target="tpu_custom_call", output_to_operand_aliasing={{0}: (8, {}), {1}: (9, {}), {2}: (10, {})} | custom-call | flops 3221225472 | bytes 9000000 | tf_op jit(solution)/shard_map/filter_spectra/pallas_call | solution.py:276
  31.5 12.8 %spectra_next.1 = (bf16[512,3072]{1,0:T(8,128)(2,1)}, bf16[512,3072]{1,0:T(8,128)(2,1)}, bf16[16,60,16,128]{3,2,1,0:T(8,128)(2,1)}, bf16[16,12,16,128]{3,2,1,0:T(8,128)(2,1)}) custom-call(s32[1]{0:T(128)} %bitcast.me_ref, bf16[3072,2048]{1,0:T(8,128)(2,1)} %get-tuple-element.20.filt_ref, ...), custom_call_target="tpu_custom_call", output_to_operand_aliasing={{2}: (4, {})} | custom-call | flops 6442450944 | bytes 18000000 | tf_op jit(solution)/shard_map/spectra_next/pallas_call | solution.py:306
  44.4 8.3 %all-to-all-done.1.refs_0_ = bf16[16,24,16,128]{3,2,1,0:T(8,128)(2,1)S(1)} async-done(((bf16[16,24,16,128]{3,2,1,0:T(8,128)(2,1)}), bf16[16,24,16,128]{3,2,1,0:T(8,128)(2,1)S(1)}, u32[]{:S(2)}, u32[]{:S(2)}) %all-to-all-start.1) | async-done | bytes 1572896 | tf_op jit(solution)/shard_map/all_to_all | solution.py:582
  52.7 7.9 %all-to-all-start.2 = ((bf16[16,60,16,128]{3,2,1,0:T(8,128)(2,1)}), bf16[16,60,16,128]{3,2,1,0:T(8,128)(2,1)}, u32[]{:S(2)}, u32[]{:S(2)}) async-start(bf16[16,60,16,128]{3,2,1,0:T(8,128)(2,1)} %get-tuple-element.29), calls=%async_computation.2 | async-start | bytes 7864320 | tf_op jit(solution)/shard_map/all_to_all | solution.py:582
  60.8 1.2 fusion.2
  62.0 1.8 %fusion = (f32[4,64,256]{2,1,0:T(8,128)}, f32[4,64,256]{2,1,0:T(8,128)}) fusion(f32[64]{0:T(128)S(1)} %copy-done.1, f32[4,256]{1,0:T(4,128)S(1)} %mul.66), kind=kLoop, calls=%fused_computation.4 | loop fusion | flops 131072 | bytes 528640 | tf_op jit(solution)/shard_map/sin | solution.py:572
  63.8 20.2 %beam_sums.1 = f32[16,64,384]{2,1,0:T(8,128)} custom-call(s32[1]{0:T(128)} %bitcast.me_ref, bf16[512,3072]{1,0:T(8,128)(2,1)} %get-tuple-element.23.refs_0_, bf16[512,3072]{1,0:T(8,128)(2,1)} %get-tuple-element.24.refs_1_, bf16[512,3072]{1,0:T(8,128)(2,1)} %get-tuple-element.25.refs_2_, bf16[512,3072]{1,0:T(8,128)(2,1)} %get-tuple-element.26.refs_3_, ...), custom_call_target="tpu_custom_call" | custom-call | flops 20000000000 | bytes 20000000 | tf_op jit(solution)/shard_map/beam_sums/pallas_call | solution.py:562
  84.0 1.2 slice.38
  85.2 0.4 collective-permute-start
  85.7 1.9 %collective-permute-done = f32[8,64,384]{2,1,0:T(8,128)S(1)} collective-permute-done((f32[8,64,384]{2,1,0:T(8,128)S(1)}, f32[8,64,384]{2,1,0:T(8,128)S(1)}, u32[]{:S(2)}, u32[]{:S(2)}) %collective-permute-start) | collective-permute-done | bytes 786464 | tf_op jit(solution)/shard_map/ppermute | solution.py:578
  87.6 1.2 slice_add_fusion
  89.0 0.7 broadcast_multiply_fusion
  89.7 0.4 convert_reduce_fusion
  90.1 19.6 %collective-permute-done.1 = f32[4,64,384]{2,1,0:T(8,128)S(1)} collective-permute-done((f32[4,64,384]{2,1,0:T(8,128)S(1)}, f32[4,64,384]{2,1,0:T(8,128)S(1)}, u32[]{:S(2)}, u32[]{:S(2)}) %collective-permute-start.1) | collective-permute-done | bytes 393248 | tf_op jit(solution)/shard_map/ppermute | solution.py:578
  109.8 19.7 %collective-permute-done.2 = f32[2,64,384]{2,1,0:T(8,128)S(1)} collective-permute-done((f32[2,64,384]{2,1,0:T(8,128)S(1)}, f32[2,64,384]{2,1,0:T(8,128)S(1)}, u32[]{:S(2)}, u32[]{:S(2)}) %collective-permute-start.2) | collective-permute-done | bytes 196640 | tf_op jit(solution)/shard_map/ppermute | solution.py:578
  129.6 3.2 %collective-permute-start.3 = (bf16[1,64,384]{2,1,0:T(8,128)(2,1)S(1)}, bf16[1,64,384]{2,1,0:T(8,128)(2,1)S(1)}, u32[]{:S(2)}, u32[]{:S(2)}) collective-permute-start(bf16[1,64,384]{2,1,0:T(8,128)(2,1)S(1)} %slice.50), channel_id=1, source_target_pairs={{0,8},{1,9},{2,10},{3,11},{4,12},{5,13},{6,14},{7,15},{8,0},{9,1},... | collective-permute-start | bytes 147464 | tf_op jit(solution)/shard_map/ppermute | solution.py:578
  132.8 17.4 %collective-permute-done.3 = bf16[1,64,384]{2,1,0:T(8,128)(2,1)S(1)} collective-permute-done((bf16[1,64,384]{2,1,0:T(8,128)(2,1)S(1)}, bf16[1,64,384]{2,1,0:T(8,128)(2,1)S(1)}, u32[]{:S(2)}, u32[]{:S(2)}) %collective-permute-start.3) | collective-permute-done | bytes 49184 | tf_op jit(solution)/shard_map/ppermute | solution.py:578
  150.2 0.7 add_bitcast_fusion
  150.9 4.6 %all-to-all-start = ((bf16[16,12,16,128]{3,2,1,0:T(8,128)(2,1)}), bf16[16,12,16,128]{3,2,1,0:T(8,128)(2,1)S(1)}, u32[]{:S(2)}, u32[]{:S(2)}) async-start(bf16[16,12,16,128]{3,2,1,0:T(8,128)(2,1)} %get-tuple-element.27), calls=%async_computation | async-start | bytes 1572864 | tf_op jit(solution)/shard_map/all_to_all | solution.py:582
  155.5 17.7 %correlate.2.refs_2_ = f32[32,2,2,256,256]{4,3,2,1,0:T(8,128)} custom-call(bf16[16,24,16,128]{3,2,1,0:T(8,128)(2,1)S(1)} %all-to-all-done.1.refs_0_, bf16[16,60,16,128]{3,2,1,0:T(8,128)(2,1)} %all-to-all-done.2.refs_1_, s32[4,4,256]{2,1,0:T(4,128)S(1)} %multiply_add_fusion.refs_2_), custom_call_target="tpu_custom_call" | custom-call | flops 16000000000 | bytes 40000000 | tf_op jit(solution)/shard_map/correlate/pallas_call | solution.py:461
  173.1 0.8 all-to-all-done.refs_0_
  174.0 3.1 %correlate.3 = f32[32,2,2,256,256]{4,3,2,1,0:T(8,128)} custom-call(bf16[16,12,16,128]{3,2,1,0:T(8,128)(2,1)S(1)} %all-to-all-done.refs_0_, s32[1,4,256]{2,1,0:T(4,128)S(1)} %slice.45.refs_1_, f32[32,2,2,256,256]{4,3,2,1,0:T(8,128)} %correlate.2.refs_2_), custom_call_target="tpu_custom_call", output_to_operand_aliasing={{}: (2, {})} | custom-call | flops 2000000000 | bytes 5000000 | tf_op jit(solution)/shard_map/correlate/pallas_call | solution.py:461
  (20 shorter events, 0.6 us)
Async XLA Ops:
  12.7 40.0 %all-to-all-start.1 = ((bf16[16,24,16,128]{3,2,1,0:T(8,128)(2,1)}), bf16[16,24,16,128]{3,2,1,0:T(8,128)(2,1)S(1)}, u32[]{:S(2)}, u32[]{:S(2)}) async-start(bf16[16,24,16,128]{3,2,1,0:T(8,128)(2,1)} %get-tuple-element.28), calls=%async_computation.1 | async-start | bytes 3145728 | tf_op jit(solution)/shard_map/all_to_all | solution.py:582
  52.7 7.9 %copy-start = (f32[4,64]{1,0:T(4,128)S(1)}, f32[4,64]{1,0:T(4,128)}, u32[]{:S(2)}) copy-start(f32[4,64]{1,0:T(4,128)} %param.9) | copy-start | bytes 3076
  52.7 9.3 %copy-start.1 = (f32[64]{0:T(128)S(1)}, f32[64]{0:T(128)}, u32[]{:S(2)}) copy-start(f32[64]{0:T(128)} %constant.68.clone) | copy-start | bytes 772
  52.7 98.1 %all-to-all-start.2 = ((bf16[16,60,16,128]{3,2,1,0:T(8,128)(2,1)}), bf16[16,60,16,128]{3,2,1,0:T(8,128)(2,1)}, u32[]{:S(2)}, u32[]{:S(2)}) async-start(bf16[16,60,16,128]{3,2,1,0:T(8,128)(2,1)} %get-tuple-element.29), calls=%async_computation.2 | async-start | bytes 7864320 | tf_op jit(solution)/shard_map/all_to_all | solution.py:582
  85.2 2.4 %collective-permute-start = (f32[8,64,384]{2,1,0:T(8,128)S(1)}, f32[8,64,384]{2,1,0:T(8,128)S(1)}, u32[]{:S(2)}, u32[]{:S(2)}) collective-permute-start(f32[8,64,384]{2,1,0:T(8,128)S(1)} %slice.38), channel_id=1, source_target_pairs={{0,1},{1,0},{2,3},{3,2},{4,5},{5,4},{6,7},{7,6},{8,9},{9,8},{10,11... | collective-permute-start | bytes 2359304 | tf_op jit(solution)/shard_map/ppermute | solution.py:578
  88.8 20.8 %collective-permute-start.1 = (f32[4,64,384]{2,1,0:T(8,128)S(1)}, f32[4,64,384]{2,1,0:T(8,128)S(1)}, u32[]{:S(2)}, u32[]{:S(2)}) collective-permute-start(f32[4,64,384]{2,1,0:T(8,128)S(1)} %slice.40), channel_id=1, source_target_pairs={{0,2},{1,3},{2,0},{3,1},{4,6},{5,7},{6,4},{7,5},{8,10},{9,11},{10,... | collective-permute-start | bytes 1179656 | tf_op jit(solution)/shard_map/ppermute | solution.py:578
  109.7 19.8 %collective-permute-start.2 = (f32[2,64,384]{2,1,0:T(8,128)S(1)}, f32[2,64,384]{2,1,0:T(8,128)S(1)}, u32[]{:S(2)}, u32[]{:S(2)}) collective-permute-start(f32[2,64,384]{2,1,0:T(8,128)S(1)} %slice.42), channel_id=1, source_target_pairs={{0,4},{1,5},{2,6},{3,7},{4,0},{5,1},{6,2},{7,3},{8,12},{9,13},{10,... | collective-permute-start | bytes 589832 | tf_op jit(solution)/shard_map/ppermute | solution.py:578
  129.6 20.6 %collective-permute-start.3 = (bf16[1,64,384]{2,1,0:T(8,128)(2,1)S(1)}, bf16[1,64,384]{2,1,0:T(8,128)(2,1)S(1)}, u32[]{:S(2)}, u32[]{:S(2)}) collective-permute-start(bf16[1,64,384]{2,1,0:T(8,128)(2,1)S(1)} %slice.50), channel_id=1, source_target_pairs={{0,8},{1,9},{2,10},{3,11},{4,12},{5,13},{6,14},{7,15},{8,0},{9,1},... | collective-permute-start | bytes 147464 | tf_op jit(solution)/shard_map/ppermute | solution.py:578
  150.9 23.1 %all-to-all-start = ((bf16[16,12,16,128]{3,2,1,0:T(8,128)(2,1)}), bf16[16,12,16,128]{3,2,1,0:T(8,128)(2,1)S(1)}, u32[]{:S(2)}, u32[]{:S(2)}) async-start(bf16[16,12,16,128]{3,2,1,0:T(8,128)(2,1)} %get-tuple-element.27), calls=%async_computation | async-start | bytes 1572864 | tf_op jit(solution)/shard_map/all_to_all | solution.py:582

commit v12 on v11

--- a/solution.py
+++ b/solution.py
@@ -82,7 +82,7 @@
     return jnp.clip(loc, 0, z.feed_dev - 1)
 
 
-def emit_spectra(z, scale, chunk, me_ref, spectra, loc_ref, spec_ref, sends):
+def emit_spectra(z, scale, chunk, me_ref, spectra, loc_ref, spec_ref, sends, quads, base=0):
     lane = lax.broadcasted_iota(jnp.int32, (z.rows_dev, LANES), 1)
     frame = (lane // z.cap) ^ (me_ref[0] % z.lane_frames)
     start = frame * z.cap
@@ -91,12 +91,15 @@
         top = owner * BAND_CH
         rows = [x[top + p : top + p + few] for p in (0, few) for x in spectra]
         rows = jnp.concatenate(rows, axis=0) * scale
-        spec_ref[owner * z.rows_dev : (owner + 1) * z.rows_dev, :] = rows.astype(jnp.bfloat16)
+        columns = slice(base * z.width, (base + quads) * z.width)
+        spec_ref[owner * z.rows_dev : (owner + 1) * z.rows_dev, columns] = rows.astype(
+            jnp.bfloat16
+        )
         band = owner * z.bands_here + chunk
         loc = loc_ref[band : band + 1, :]
         index = start + loc % z.cap
         lower = jnp.broadcast_to(loc, index.shape) < z.cap
-        for q in range(z.step_quads):
+        for q in range(quads):
             parts = []
             for side in range(2):
                 left = q * z.width + side * LANES
@@ -112,28 +115,21 @@
                     for p in range(2)
                 ]
                 half = jnp.concatenate(half, axis=0).astype(jnp.bfloat16)
-                send_ref[owner, unit + q * stride] = half
-
-
-def product(z, basis_ref, parity, c, begin, end, samples):
-    rows = slice(c * z.rows // 2, (c + 1) * z.rows // 2)
-    return lax.dot_general(
-        basis_ref[parity, rows, begin:end], samples, NT, preferred_element_type=jnp.float32
-    )
-
-
-def filter_tile(z, main_ref, halo, win_ref, off, f0):
+                send_ref[owner, unit + (base + q) * stride] = half
+
+
+def filter_tile(z, main_ref, halo, win_ref, off, f0, begin):
     lanes = slice(off, off + LANES)
     taps = [win_ref[k : k + 1, lanes] for k in range(TAPS)]
     frames = []
-    for t in range(z.step_frames + TAPS - 1):
+    for t in range(begin, begin + z.lane_frames + TAPS - 1):
         if t < z.step_frames:
             x = main_ref[f0 : f0 + 16, t * NFFT + off : t * NFFT + off + LANES]
         else:
             x = halo[t - z.step_frames][f0 : f0 + 16, lanes]
         frames.append(x.astype(jnp.float32))
     totals = []
-    for t in range(z.step_frames):
+    for t in range(z.lane_frames):
         total = taps[0] * frames[t]
         for k in range(1, TAPS):
             total = total + taps[k] * frames[t + k]
@@ -141,7 +137,7 @@
     if z.cap < 16:
         totals = [
             jnp.concatenate([totals[t][h : h + 8], totals[t + 1][h : h + 8]], axis=0)
-            for t in range(0, z.step_frames, 2)
+            for t in range(0, z.lane_frames, 2)
             for h in (0, 8)
         ]
     out = []
@@ -150,26 +146,33 @@
             t, half, feed = 2 * (i // 2), i % 2, 0
         else:
             t, half, feed = i, f0 // z.cap, f0 % z.cap
-        row = (t // z.lane_frames) * z.width + half * LANES
-        row += (t % z.lane_frames) * z.cap + feed
-        out.append((row, total.astype(jnp.bfloat16)))
+        out.append((half * LANES + t * z.cap + feed, total.astype(jnp.bfloat16)))
     return out
 
 
-def filter_fold(z, main_ref, halo, win_ref, filt_ref, off):
+def filter_fold(z, main_ref, halo, win_ref, filt_ref, off, quad):
     far = off + NFFT // 2
+    begin = quad * z.lane_frames
     folded = {}
     for f0 in range(0, z.feed_dev, 16):
-        low = filter_tile(z, main_ref, halo, win_ref, off, f0)
-        high = filter_tile(z, main_ref, halo, win_ref, far, f0)
+        low = filter_tile(z, main_ref, halo, win_ref, off, f0, begin)
+        high = filter_tile(z, main_ref, halo, win_ref, far, f0, begin)
         for (row, a), (_, b) in zip(low, high):
             folded[row] = (a + b, a - b)
-            filt_ref[row : row + 16, off : off + LANES] = folded[row][0]
-            filt_ref[row : row + 16, far : far + LANES] = folded[row][1]
+            top = quad * z.width + row
+            filt_ref[top : top + 16, off : off + LANES] = folded[row][0]
+            filt_ref[top : top + 16, far : far + LANES] = folded[row][1]
     return [
         jnp.concatenate([folded[row][parity] for row in sorted(folded)], axis=0)
         for parity in range(2)
     ]
+
+
+def product(z, basis_ref, parity, c, samples):
+    rows = slice(c * z.rows // 2, (c + 1) * z.rows // 2)
+    return lax.dot_general(
+        basis_ref[parity, rows, :], samples, NT, preferred_element_type=jnp.float32
+    )
 
 
 def first_kernel(
@@ -179,24 +182,29 @@
     filt_ref, spec_refs, send_ref, loc_ref = refs[held], refs[held + 1 : -2], refs[-2], refs[-1]
     halo = (h0_ref, h1_ref, h2_ref)
     loc_ref[...] = find_places(z, me_ref[0], lists_ref[...])
-    piece = 512
-    count = len(chunks)
-    spectra = [[None, None] for _ in chunks]
-    for off in range(0, NFFT // 2, piece):
+
+    def emit(quad, spectra):
+        for c, chunk in enumerate(chunks):
+            unit = c * 2 * z.step_quads
+            sends = [(send_ref, unit, 2), (send_ref, unit + 1, 2)]
+            emit_spectra(
+                z, scale, chunk, me_ref, spectra[c], loc_ref, spec_refs[c], sends, 1, quad
+            )
+
+    before = None
+    for quad in range(z.step_quads):
         tiles = [
-            filter_fold(z, main_ref, halo, win_ref, filt_ref, tile)
-            for tile in range(off, off + piece, LANES)
+            filter_fold(z, main_ref, halo, win_ref, filt_ref, off, quad)
+            for off in range(0, NFFT // 2, LANES)
         ]
-        for parity in range(2):
-            samples = jnp.concatenate([tile[parity] for tile in tiles], axis=1)
-            for c in range(count):
-                part = product(z, basis_ref, parity, c, off, off + piece, samples)
-                old = spectra[c][parity]
-                spectra[c][parity] = part if old is None else old + part
-    for c, chunk in enumerate(chunks):
-        unit = c * 2 * z.step_quads
-        sends = [(send_ref, unit, 2), (send_ref, unit + 1, 2)]
-        emit_spectra(z, scale, chunk, me_ref, spectra[c], loc_ref, spec_refs[c], sends)
+        samples = [jnp.concatenate([tile[p] for tile in tiles], axis=1) for p in range(2)]
+        if before is not None:
+            emit(quad - 1, before)
+        before = [
+            [product(z, basis_ref, p, c, samples[p]) for p in range(2)]
+            for c in range(len(chunks))
+        ]
+    emit(z.step_quads - 1, before)
 
 
 def next_kernel(z, scale, chunks, me_ref, filt_ref, basis_ref, lists_ref, held_ref, *refs):
@@ -205,7 +213,7 @@
     half = NFFT // 2
     spectra = [
         [
-            product(z, basis_ref, p, c, 0, half, filt_ref[:, p * half : (p + 1) * half])
+            product(z, basis_ref, p, c, filt_ref[:, p * half : (p + 1) * half])
             for p in range(2)
         ]
         for c in range(2)
@@ -215,7 +223,9 @@
         [(begun_ref, 2 * z.step_quads, 1), (last_ref, 0, 1)],
     ]
     for c, chunk in enumerate(chunks):
-        emit_spectra(z, scale, chunk, me_ref, spectra[c], loc_ref, refs[c], sends[c])
+        emit_spectra(
+            z, scale, chunk, me_ref, spectra[c], loc_ref, refs[c], sends[c], z.step_quads
+        )
 
 
 def whole_spec(shape):

time: 179 us -> 179 us (level)
  no operation moved by 1% of the time
where the time goes in v12:
time: 179 us; the launch traced here: 177 us
  Pallas kernels  78.1 us (44%)
  waiting for transfers between devices  67.7 us (38%)
  starting transfers between devices  23 us (13%)
  other arithmetic  6.07 us (3%)
    ppermute x4, waiting for transfers between devices, swap(): return lax.ppermute(x, 'chan', [(i, i ^ offset) for i in range(z.devices)])  58.6 us
    pallas_call x2, Pallas kernels, first(): pl.pallas_call(functools.partial(first_kernel, z, self.scale, chunks, len...  24.3 us
    pallas_call x2, Pallas kernels, receive_call(): pl.pallas_call(functools.partial(receive_kernel, z, parities, step_pairs,...  20.8 us
    pallas_call x1, Pallas kernels, beam_call(): pl.pallas_call(functools.partial(beam_kernel, z), grid_spec=grid_spec, ou...  20.2 us
    all_to_all x3, starting transfers between devices, exchange(): return lax.all_to_all(x, 'chan', split_axis=0, concat_axis=0, tiled=True)  19.1 us
    pallas_call x1, Pallas kernels, next(): pl.pallas_call(functools.partial(next_kernel, z, self.scale, chunks), in_...  12.8 us
    all_to_all x3, waiting for transfers between devices, exchange(): return lax.all_to_all(x, 'chan', split_axis=0, concat_axis=0, tiled=True)  9.15 us
    ppermute x4, starting transfers between devices, swap(): return lax.ppermute(x, 'chan', [(i, i ^ offset) for i in range(z.devices)])  3.86 us
  transfers between devices with their start and end apart: 7, of which 6 were waited for; matrix products, arithmetic and copies ran while one was open for 4% of the time, Pallas kernels for 35%

profile of v12, /device:TPU:5, one launch (start us, length us, event | category | flops | bytes accessed | tf_op | source)
XLA Modules:
  0.0 177.3 jit_solution(1983445278266883510)
XLA Ops:
  0.6 12.1 %filter_spectra.2 = (bf16[3072,2048]{1,0:T(8,128)(2,1)}, bf16[512,3072]{1,0:T(8,128)(2,1)}, bf16[512,3072]{1,0:T(8,128)(2,1)}, bf16[16,24,16,128]{3,2,1,0:T(8,128)(2,1)}) custom-call(s32[1]{0:T(128)} %bitcast.me_ref, bf16[64,104448]{1,0:T(8,128)(2,1)} %h2_ref.3, bf16[64,104448]{1,0:T(8,128)(2,1)} %h2_ref.3, bf16[64,104448]{1,0:T(8,128)(2,1)} %h2_ref.3, ...), custom_call_target="tpu_custom_call" | custom-call | flops 3221225472 | bytes 9000000 | tf_op jit(solution)/shard_map/filter_spectra/pallas_call | solution.py:286
  12.7 6.7 %all-to-all-start.1 = ((bf16[16,24,16,128]{3,2,1,0:T(8,128)(2,1)}), bf16[16,24,16,128]{3,2,1,0:T(8,128)(2,1)S(1)}, u32[]{:S(2)}, u32[]{:S(2)}) async-start(bf16[16,24,16,128]{3,2,1,0:T(8,128)(2,1)} %get-tuple-element.28), calls=%async_computation.1 | async-start | bytes 3145728 | tf_op jit(solution)/shard_map/all_to_all | solution.py:592
  19.4 12.2 %filter_spectra.3 = (bf16[3072,2048]{1,0:T(8,128)(2,1)}, bf16[512,3072]{1,0:T(8,128)(2,1)}, bf16[512,3072]{1,0:T(8,128)(2,1)}, bf16[16,60,16,128]{3,2,1,0:T(8,128)(2,1)}) custom-call(s32[1]{0:T(128)} %bitcast.me_ref, bf16[64,104448]{1,0:T(8,128)(2,1)} %h2_ref.3, ...), custom_call_target="tpu_custom_call", output_to_operand_aliasing={{0}: (8, {}), {1}: (9, {}), {2}: (10, {})} | custom-call | flops 3221225472 | bytes 9000000 | tf_op jit(solution)/shard_map/filter_spectra/pallas_call | solution.py:286
  31.6 12.8 %spectra_next.1 = (bf16[512,3072]{1,0:T(8,128)(2,1)}, bf16[512,3072]{1,0:T(8,128)(2,1)}, bf16[16,60,16,128]{3,2,1,0:T(8,128)(2,1)}, bf16[16,12,16,128]{3,2,1,0:T(8,128)(2,1)}) custom-call(s32[1]{0:T(128)} %bitcast.me_ref, bf16[3072,2048]{1,0:T(8,128)(2,1)} %get-tuple-element.20.filt_ref, ...), custom_call_target="tpu_custom_call", output_to_operand_aliasing={{2}: (4, {})} | custom-call | flops 6442450944 | bytes 18000000 | tf_op jit(solution)/shard_map/spectra_next/pallas_call | solution.py:316
  44.4 8.3 %all-to-all-done.1.refs_0_ = bf16[16,24,16,128]{3,2,1,0:T(8,128)(2,1)S(1)} async-done(((bf16[16,24,16,128]{3,2,1,0:T(8,128)(2,1)}), bf16[16,24,16,128]{3,2,1,0:T(8,128)(2,1)S(1)}, u32[]{:S(2)}, u32[]{:S(2)}) %all-to-all-start.1) | async-done | bytes 1572896 | tf_op jit(solution)/shard_map/all_to_all | solution.py:592
  52.8 7.9 %all-to-all-start.2 = ((bf16[16,60,16,128]{3,2,1,0:T(8,128)(2,1)}), bf16[16,60,16,128]{3,2,1,0:T(8,128)(2,1)}, u32[]{:S(2)}, u32[]{:S(2)}) async-start(bf16[16,60,16,128]{3,2,1,0:T(8,128)(2,1)} %get-tuple-element.29), calls=%async_computation.2 | async-start | bytes 7864320 | tf_op jit(solution)/shard_map/all_to_all | solution.py:592
  60.8 1.2 fusion.2
  62.0 1.8 %fusion = (f32[4,64,256]{2,1,0:T(8,128)}, f32[4,64,256]{2,1,0:T(8,128)}) fusion(f32[64]{0:T(128)S(1)} %copy-done.1, f32[4,256]{1,0:T(4,128)S(1)} %mul.66), kind=kLoop, calls=%fused_computation.4 | loop fusion | flops 131072 | bytes 528640 | tf_op jit(solution)/shard_map/sin | solution.py:582
  63.8 20.2 %beam_sums.1 = f32[16,64,384]{2,1,0:T(8,128)} custom-call(s32[1]{0:T(128)} %bitcast.me_ref, bf16[512,3072]{1,0:T(8,128)(2,1)} %get-tuple-element.23.refs_0_, bf16[512,3072]{1,0:T(8,128)(2,1)} %get-tuple-element.24.refs_1_, bf16[512,3072]{1,0:T(8,128)(2,1)} %get-tuple-element.25.refs_2_, bf16[512,3072]{1,0:T(8,128)(2,1)} %get-tuple-element.26.refs_3_, ...), custom_call_target="tpu_custom_call" | custom-call | flops 20000000000 | bytes 20000000 | tf_op jit(solution)/shard_map/beam_sums/pallas_call | solution.py:572
  84.1 1.2 slice.38
  85.2 0.4 collective-permute-start
  85.7 1.9 %collective-permute-done = f32[8,64,384]{2,1,0:T(8,128)S(1)} collective-permute-done((f32[8,64,384]{2,1,0:T(8,128)S(1)}, f32[8,64,384]{2,1,0:T(8,128)S(1)}, u32[]{:S(2)}, u32[]{:S(2)}) %collective-permute-start) | collective-permute-done | bytes 786464 | tf_op jit(solution)/shard_map/ppermute | solution.py:588
  87.6 1.2 slice_add_fusion
  89.0 0.7 broadcast_multiply_fusion
  89.7 0.4 convert_reduce_fusion
  90.1 19.6 %collective-permute-done.1 = f32[4,64,384]{2,1,0:T(8,128)S(1)} collective-permute-done((f32[4,64,384]{2,1,0:T(8,128)S(1)}, f32[4,64,384]{2,1,0:T(8,128)S(1)}, u32[]{:S(2)}, u32[]{:S(2)}) %collective-permute-start.1) | collective-permute-done | bytes 393248 | tf_op jit(solution)/shard_map/ppermute | solution.py:588
  109.9 19.7 %collective-permute-done.2 = f32[2,64,384]{2,1,0:T(8,128)S(1)} collective-permute-done((f32[2,64,384]{2,1,0:T(8,128)S(1)}, f32[2,64,384]{2,1,0:T(8,128)S(1)}, u32[]{:S(2)}, u32[]{:S(2)}) %collective-permute-start.2) | collective-permute-done | bytes 196640 | tf_op jit(solution)/shard_map/ppermute | solution.py:588
  129.6 3.2 %collective-permute-start.3 = (bf16[1,64,384]{2,1,0:T(8,128)(2,1)S(1)}, bf16[1,64,384]{2,1,0:T(8,128)(2,1)S(1)}, u32[]{:S(2)}, u32[]{:S(2)}) collective-permute-start(bf16[1,64,384]{2,1,0:T(8,128)(2,1)S(1)} %slice.50), channel_id=1, source_target_pairs={{0,8},{1,9},{2,10},{3,11},{4,12},{5,13},{6,14},{7,15},{8,0},{9,1},... | collective-permute-start | bytes 147464 | tf_op jit(solution)/shard_map/ppermute | solution.py:588
  132.9 17.4 %collective-permute-done.3 = bf16[1,64,384]{2,1,0:T(8,128)(2,1)S(1)} collective-permute-done((bf16[1,64,384]{2,1,0:T(8,128)(2,1)S(1)}, bf16[1,64,384]{2,1,0:T(8,128)(2,1)S(1)}, u32[]{:S(2)}, u32[]{:S(2)}) %collective-permute-start.3) | collective-permute-done | bytes 49184 | tf_op jit(solution)/shard_map/ppermute | solution.py:588
  150.2 0.7 add_bitcast_fusion
  150.9 4.6 %all-to-all-start = ((bf16[16,12,16,128]{3,2,1,0:T(8,128)(2,1)}), bf16[16,12,16,128]{3,2,1,0:T(8,128)(2,1)S(1)}, u32[]{:S(2)}, u32[]{:S(2)}) async-start(bf16[16,12,16,128]{3,2,1,0:T(8,128)(2,1)} %get-tuple-element.27), calls=%async_computation | async-start | bytes 1572864 | tf_op jit(solution)/shard_map/all_to_all | solution.py:592
  155.5 17.7 %correlate.2.refs_2_ = f32[32,2,2,256,256]{4,3,2,1,0:T(8,128)} custom-call(bf16[16,24,16,128]{3,2,1,0:T(8,128)(2,1)S(1)} %all-to-all-done.1.refs_0_, bf16[16,60,16,128]{3,2,1,0:T(8,128)(2,1)} %all-to-all-done.2.refs_1_, s32[4,4,256]{2,1,0:T(4,128)S(1)} %multiply_add_fusion.refs_2_), custom_call_target="tpu_custom_call" | custom-call | flops 16000000000 | bytes 40000000 | tf_op jit(solution)/shard_map/correlate/pallas_call | solution.py:471
  173.2 0.8 all-to-all-done.refs_0_
  174.0 3.1 %correlate.3 = f32[32,2,2,256,256]{4,3,2,1,0:T(8,128)} custom-call(bf16[16,12,16,128]{3,2,1,0:T(8,128)(2,1)S(1)} %all-to-all-done.refs_0_, s32[1,4,256]{2,1,0:T(4,128)S(1)} %slice.45.refs_1_, f32[32,2,2,256,256]{4,3,2,1,0:T(8,128)} %correlate.2.refs_2_), custom_call_target="tpu_custom_call", output_to_operand_aliasing={{}: (2, {})} | custom-call | flops 2000000000 | bytes 5000000 | tf_op jit(solution)/shard_map/correlate/pallas_call | solution.py:471
  (20 shorter events, 0.6 us)
Async XLA Ops:
  12.7 40.0 %all-to-all-start.1 = ((bf16[16,24,16,128]{3,2,1,0:T(8,128)(2,1)}), bf16[16,24,16,128]{3,2,1,0:T(8,128)(2,1)S(1)}, u32[]{:S(2)}, u32[]{:S(2)}) async-start(bf16[16,24,16,128]{3,2,1,0:T(8,128)(2,1)} %get-tuple-element.28), calls=%async_computation.1 | async-start | bytes 3145728 | tf_op jit(solution)/shard_map/all_to_all | solution.py:592
  52.7 7.9 %copy-start = (f32[4,64]{1,0:T(4,128)S(1)}, f32[4,64]{1,0:T(4,128)}, u32[]{:S(2)}) copy-start(f32[4,64]{1,0:T(4,128)} %param.9) | copy-start | bytes 3076
  52.8 9.3 %copy-start.1 = (f32[64]{0:T(128)S(1)}, f32[64]{0:T(128)}, u32[]{:S(2)}) copy-start(f32[64]{0:T(128)} %constant.68.clone) | copy-start | bytes 772
  52.8 98.1 %all-to-all-start.2 = ((bf16[16,60,16,128]{3,2,1,0:T(8,128)(2,1)}), bf16[16,60,16,128]{3,2,1,0:T(8,128)(2,1)}, u32[]{:S(2)}, u32[]{:S(2)}) async-start(bf16[16,60,16,128]{3,2,1,0:T(8,128)(2,1)} %get-tuple-element.29), calls=%async_computation.2 | async-start | bytes 7864320 | tf_op jit(solution)/shard_map/all_to_all | solution.py:592
  85.2 2.4 %collective-permute-start = (f32[8,64,384]{2,1,0:T(8,128)S(1)}, f32[8,64,384]{2,1,0:T(8,128)S(1)}, u32[]{:S(2)}, u32[]{:S(2)}) collective-permute-start(f32[8,64,384]{2,1,0:T(8,128)S(1)} %slice.38), channel_id=1, source_target_pairs={{0,1},{1,0},{2,3},{3,2},{4,5},{5,4},{6,7},{7,6},{8,9},{9,8},{10,11... | collective-permute-start | bytes 2359304 | tf_op jit(solution)/shard_map/ppermute | solution.py:588
  88.9 20.8 %collective-permute-start.1 = (f32[4,64,384]{2,1,0:T(8,128)S(1)}, f32[4,64,384]{2,1,0:T(8,128)S(1)}, u32[]{:S(2)}, u32[]{:S(2)}) collective-permute-start(f32[4,64,384]{2,1,0:T(8,128)S(1)} %slice.40), channel_id=1, source_target_pairs={{0,2},{1,3},{2,0},{3,1},{4,6},{5,7},{6,4},{7,5},{8,10},{9,11},{10,... | collective-permute-start | bytes 1179656 | tf_op jit(solution)/shard_map/ppermute | solution.py:588
  109.8 19.8 %collective-permute-start.2 = (f32[2,64,384]{2,1,0:T(8,128)S(1)}, f32[2,64,384]{2,1,0:T(8,128)S(1)}, u32[]{:S(2)}, u32[]{:S(2)}) collective-permute-start(f32[2,64,384]{2,1,0:T(8,128)S(1)} %slice.42), channel_id=1, source_target_pairs={{0,4},{1,5},{2,6},{3,7},{4,0},{5,1},{6,2},{7,3},{8,12},{9,13},{10,... | collective-permute-start | bytes 589832 | tf_op jit(solution)/shard_map/ppermute | solution.py:588
  129.6 20.6 %collective-permute-start.3 = (bf16[1,64,384]{2,1,0:T(8,128)(2,1)S(1)}, bf16[1,64,384]{2,1,0:T(8,128)(2,1)S(1)}, u32[]{:S(2)}, u32[]{:S(2)}) collective-permute-start(bf16[1,64,384]{2,1,0:T(8,128)(2,1)S(1)} %slice.50), channel_id=1, source_target_pairs={{0,8},{1,9},{2,10},{3,11},{4,12},{5,13},{6,14},{7,15},{8,0},{9,1},... | collective-permute-start | bytes 147464 | tf_op jit(solution)/shard_map/ppermute | solution.py:588
  150.9 23.1 %all-to-all-start = ((bf16[16,12,16,128]{3,2,1,0:T(8,128)(2,1)}), bf16[16,12,16,128]{3,2,1,0:T(8,128)(2,1)S(1)}, u32[]{:S(2)}, u32[]{:S(2)}) async-start(bf16[16,12,16,128]{3,2,1,0:T(8,128)(2,1)} %get-tuple-element.27), calls=%async_computation | async-start | bytes 1572864 | tf_op jit(solution)/shard_map/all_to_all | solution.py:592

commit v13 on v12

--- a/solution.py
+++ b/solution.py
@@ -1,3 +1,4 @@
+import copy
 import functools
 
 import jax
@@ -51,10 +52,7 @@
         self.lane_frames = LANES // self.cap
         self.quads = FR // self.lane_frames
         self.width = self.lane_frames * feed_dev
-        self.steps = 6 if self.quads % 6 == 0 else self.quads
-        self.step_frames = FR // self.steps
-        self.step_quads = self.quads // self.steps
-        self.step_lanes = self.step_frames * feed_dev
+        self.set_steps(6 if self.quads % 6 == 0 else self.quads)
         self.chan_dev = CHANNELS // devices
         self.bands_here = BANDS // devices
         self.chunks = self.chan_dev // BAND_CH
@@ -63,9 +61,15 @@
         self.groups = devices // self.lane_frames
         self.early = min(2, self.chunks)
         if self.chunks == 4:
-            self.parts = (self.steps // 2, self.steps - self.steps // 2)
+            self.parts = (self.quads * 5 // 12, self.quads - self.quads * 5 // 12)
         else:
-            self.early, self.parts = self.chunks, (self.steps,)
+            self.early, self.parts = self.chunks, (self.quads,)
+
+    def set_steps(self, steps):
+        self.steps = steps
+        self.step_frames = FR // steps
+        self.step_quads = self.quads // steps
+        self.step_lanes = self.step_frames * self.feed_dev
 
 
 def find_places(z, me, lists):
@@ -237,6 +241,8 @@
     def __init__(self, z, me, voltages, band_feeds):
         window = fir_window()
         self.z = z
+        self.fine = copy.copy(z)
+        self.fine.set_steps(z.quads)
         self.me = me
         self.scale = float(np.sqrt(2.0 / np.sum(window * window)))
         self.window = jnp.asarray(window.astype(np.float32))
@@ -271,9 +277,10 @@
             ),
         )
 
-    def first(self, begin, steps, chunks, basis, units, held):
-        z = self.z
+    def first(self, begin, steps, chunks, basis, units, base, held):
+        z = self.fine
         count = len(chunks)
+        base = base // (count * 2 * z.step_quads)
 
         def halo_spec(h):
             return pl.BlockSpec(
@@ -300,7 +307,7 @@
                 pl.BlockSpec((z.step_lanes, NFFT), lambda g: (begin + g, 0)),
             ]
             + [pl.BlockSpec((z.rows, z.step_lanes), lambda g: (0, begin + g))] * count
-            + [pl.BlockSpec(send_block, lambda g: (0, g, 0, 0))],
+            + [pl.BlockSpec(send_block, lambda g: (0, base + g, 0, 0))],
             out_shape=[self.filt_shape] + [self.spec_shape] * count + [self.message(units)],
             input_output_aliases=aliases,
             name="filter_spectra",
@@ -311,7 +318,6 @@
         z = self.z
         basis = self.basis(chunks)
         begun = 3 * z.step_quads
-        base = held.shape[1] // begun - z.steps
         operands = [self.me, filt, basis, self.lists, held]
         return pl.pallas_call(
             functools.partial(next_kernel, z, self.scale, chunks),
@@ -324,7 +330,7 @@
             ],
             out_specs=[pl.BlockSpec((z.rows, z.step_lanes), lambda g: (0, g))] * 2
             + [
-                pl.BlockSpec((z.devices, begun, BAND_CH, LANES), lambda g: (0, base + g, 0, 0)),
+                pl.BlockSpec((z.devices, begun, BAND_CH, LANES), lambda g: (0, g, 0, 0)),
                 pl.BlockSpec((z.devices, z.step_quads, BAND_CH, LANES), lambda g: (0, g, 0, 0)),
             ],
             out_shape=[self.spec_shape] * 2
@@ -358,8 +364,8 @@
 
     @pl.when(g == 0)
     def _():
-        for copy in copies(0):
-            copy.start()
+        for one in copies(0):
+            one.start()
 
     @pl.when(at == 0)
     def _():
@@ -372,11 +378,11 @@
 
         @pl.when(g == c * steps)
         def _():
-            for copy in copies(c):
-                copy.wait()
+            for one in copies(c):
+                one.wait()
             if c + 1 < len(runs):
-                for copy in copies(c + 1):
-                    copy.start()
+                for one in copies(c + 1):
+                    one.start()
 
     @pl.when(at == 0)
     def _():
@@ -611,33 +617,34 @@
     calls = Spectra(z, me_array, voltages, band_feeds)
     early = list(range(z.early))
     basis = calls.basis(early)
-    share = 2 * z.step_quads
+    share = 2 * calls.fine.step_quads
     step = z.early * share
     arrived = [[] for _ in range(z.chunks)]
     steps = z.parts[0]
-    filt, *spectra, send = calls.first(0, steps, early, basis, steps * step, [])
+    filt, *spectra, send = calls.first(0, steps, early, basis, steps * step, 0, [])
     got = exchange(send)
     for c in early:
         arrived[c] += [(got, g * step + c * share, share, g * share) for g in range(steps)]
     if len(z.parts) > 1:
         begin, steps = steps, z.parts[1]
-        base = steps * step
-        begun = 3 * z.step_quads
+        late, begun = 2 * z.step_quads, 3 * z.step_quads
+        base = z.steps * begun
         filt, *spectra, send = calls.first(
-            begin, steps, early, basis, base + z.steps * begun, [filt, *spectra]
+            begin, steps, early, basis, base + steps * step, base, [filt, *spectra]
         )
         *more, send, last = calls.next([z.chunks - 2, z.chunks - 1], filt, send)
         spectra = spectra + more
         got = exchange(send)
         for c in early:
             arrived[c] += [
-                (got, g * step + c * share, share, (begin + g) * share) for g in range(steps)
+                (got, base + g * step + c * share, share, (begin + g) * share)
+                for g in range(steps)
             ]
         for g in range(z.steps):
-            first = base + g * begun
-            arrived[-2].append((got, first, share, g * share))
+            first = g * begun
+            arrived[-2].append((got, first, late, g * late))
             arrived[-1] += [
-                (got, first + share + q, 1, g * share + 2 * q) for q in range(z.step_quads)
+                (got, first + late + q, 1, g * late + 2 * q) for q in range(z.step_quads)
             ]
 
     beams, bit = beam_call(z, me_array, spectra, delays), 1

time: 179 us -> 178 us (level)
    all_to_all x3, waiting for transfers between devices: 9.15 us -> 2.36 us  [exchange(): return lax.all_to_all(x, 'chan', split_axis=0, concat_axis=0, tiled=True)]
    ppermute x4, waiting for transfers between devices: 58.6 us -> 64 us  [swap(): return lax.ppermute(x, 'chan', [(i, i ^ offset) for i in range(z.devices)])]
  transfers between devices with their start and end apart: 7 -> 7, of which waited for: 6 -> 6; matrix products, arithmetic and copies ran while one was open for 4% -> 4% of each run, Pallas kernels for 35% -> 37%
where the time goes in v13:
time: 178 us; the launch traced here: 176 us
  Pallas kernels  78.6 us (44%)
  waiting for transfers between devices  66.3 us (37%)
  starting transfers between devices  22.5 us (13%)
  other arithmetic  6.1 us (3%)
    ppermute x4, waiting for transfers between devices, swap(): return lax.ppermute(x, 'chan', [(i, i ^ offset) for i in range(z.devices)])  64 us
    pallas_call x2, Pallas kernels, first(): pl.pallas_call(functools.partial(first_kernel, z, self.scale, chunks, len...  24.6 us
    pallas_call x2, Pallas kernels, receive_call(): pl.pallas_call(functools.partial(receive_kernel, z, parities, step_pairs,...  21 us
    pallas_call x1, Pallas kernels, beam_call(): pl.pallas_call(functools.partial(beam_kernel, z), grid_spec=grid_spec, ou...  20.2 us
    all_to_all x3, starting transfers between devices, exchange(): return lax.all_to_all(x, 'chan', split_axis=0, concat_axis=0, tiled=True)  18.4 us
    pallas_call x1, Pallas kernels, next(): pl.pallas_call(functools.partial(next_kernel, z, self.scale, chunks), in_...  12.8 us
    ppermute x4, starting transfers between devices, swap(): return lax.ppermute(x, 'chan', [(i, i ^ offset) for i in range(z.devices)])  4.09 us
  transfers between devices with their start and end apart: 7, of which 6 were waited for; matrix products, arithmetic and copies ran while one was open for 4% of the time, Pallas kernels for 37%

profile of v13, /device:TPU:5, one launch (start us, length us, event | category | flops | bytes accessed | tf_op | source)
XLA Modules:
  0.0 175.7 jit_solution(14863064812557379018)
XLA Ops:
  0.6 10.7 %filter_spectra.2 = (bf16[3072,2048]{1,0:T(8,128)(2,1)}, bf16[512,3072]{1,0:T(8,128)(2,1)}, bf16[512,3072]{1,0:T(8,128)(2,1)}, bf16[16,20,16,128]{3,2,1,0:T(8,128)(2,1)}) custom-call(s32[1]{0:T(128)} %bitcast.me_ref, bf16[64,104448]{1,0:T(8,128)(2,1)} %h2_ref.3, bf16[64,104448]{1,0:T(8,128)(2,1)} %h2_ref.3, bf16[64,104448]{1,0:T(8,128)(2,1)} %h2_ref.3, ...), custom_call_target="tpu_custom_call" | custom-call | flops 5368709120 | bytes 15000000 | tf_op jit(solution)/shard_map/filter_spectra/pallas_call | solution.py:293
  11.4 6.7 %all-to-all-start.1 = ((bf16[16,20,16,128]{3,2,1,0:T(8,128)(2,1)}), bf16[16,20,16,128]{3,2,1,0:T(8,128)(2,1)S(1)}, u32[]{:S(2)}, u32[]{:S(2)}) async-start(bf16[16,20,16,128]{3,2,1,0:T(8,128)(2,1)} %get-tuple-element.28), calls=%async_computation.1 | async-start | bytes 2621440 | tf_op jit(solution)/shard_map/all_to_all | solution.py:598
  18.0 13.8 %filter_spectra.3 = (bf16[3072,2048]{1,0:T(8,128)(2,1)}, bf16[512,3072]{1,0:T(8,128)(2,1)}, bf16[512,3072]{1,0:T(8,128)(2,1)}, bf16[16,64,16,128]{3,2,1,0:T(8,128)(2,1)}) custom-call(s32[1]{0:T(128)} %bitcast.me_ref, bf16[64,104448]{1,0:T(8,128)(2,1)} %h2_ref.3, ...), custom_call_target="tpu_custom_call", output_to_operand_aliasing={{0}: (8, {}), {1}: (9, {}), {2}: (10, {})} | custom-call | flops 7516192768 | bytes 21000000 | tf_op jit(solution)/shard_map/filter_spectra/pallas_call | solution.py:293
  31.9 12.8 %spectra_next.1 = (bf16[512,3072]{1,0:T(8,128)(2,1)}, bf16[512,3072]{1,0:T(8,128)(2,1)}, bf16[16,64,16,128]{3,2,1,0:T(8,128)(2,1)}, bf16[16,12,16,128]{3,2,1,0:T(8,128)(2,1)}) custom-call(s32[1]{0:T(128)} %bitcast.me_ref, bf16[3072,2048]{1,0:T(8,128)(2,1)} %get-tuple-element.20.filt_ref, ...), custom_call_target="tpu_custom_call", output_to_operand_aliasing={{2}: (4, {})} | custom-call | flops 6442450944 | bytes 18000000 | tf_op jit(solution)/shard_map/spectra_next/pallas_call | solution.py:322
  44.7 1.8 %all-to-all-done.1.refs_0_ = bf16[16,20,16,128]{3,2,1,0:T(8,128)(2,1)S(1)} async-done(((bf16[16,20,16,128]{3,2,1,0:T(8,128)(2,1)}), bf16[16,20,16,128]{3,2,1,0:T(8,128)(2,1)S(1)}, u32[]{:S(2)}, u32[]{:S(2)}) %all-to-all-start.1) | async-done | bytes 1310752 | tf_op jit(solution)/shard_map/all_to_all | solution.py:598
  46.5 7.1 %all-to-all-start.2 = ((bf16[16,64,16,128]{3,2,1,0:T(8,128)(2,1)}), bf16[16,64,16,128]{3,2,1,0:T(8,128)(2,1)}, u32[]{:S(2)}, u32[]{:S(2)}) async-start(bf16[16,64,16,128]{3,2,1,0:T(8,128)(2,1)} %get-tuple-element.29), calls=%async_computation.2 | async-start | bytes 8388608 | tf_op jit(solution)/shard_map/all_to_all | solution.py:598
  53.8 1.2 fusion.2
  55.0 1.8 %fusion = (f32[4,64,256]{2,1,0:T(8,128)}, f32[4,64,256]{2,1,0:T(8,128)}) fusion(f32[64]{0:T(128)S(1)} %copy-done.1, f32[4,256]{1,0:T(4,128)S(1)} %mul.66), kind=kLoop, calls=%fused_computation.4 | loop fusion | flops 131072 | bytes 528640 | tf_op jit(solution)/shard_map/sin | solution.py:588
  56.8 20.2 %beam_sums.1 = f32[16,64,384]{2,1,0:T(8,128)} custom-call(s32[1]{0:T(128)} %bitcast.me_ref, bf16[512,3072]{1,0:T(8,128)(2,1)} %get-tuple-element.23.refs_0_, bf16[512,3072]{1,0:T(8,128)(2,1)} %get-tuple-element.24.refs_1_, bf16[512,3072]{1,0:T(8,128)(2,1)} %get-tuple-element.25.refs_2_, bf16[512,3072]{1,0:T(8,128)(2,1)} %get-tuple-element.26.refs_3_, ...), custom_call_target="tpu_custom_call" | custom-call | flops 20000000000 | bytes 20000000 | tf_op jit(solution)/shard_map/beam_sums/pallas_call | solution.py:578
  77.0 1.2 slice.38
  78.2 0.4 collective-permute-start
  78.7 1.9 %collective-permute-done = f32[8,64,384]{2,1,0:T(8,128)S(1)} collective-permute-done((f32[8,64,384]{2,1,0:T(8,128)S(1)}, f32[8,64,384]{2,1,0:T(8,128)S(1)}, u32[]{:S(2)}, u32[]{:S(2)}) %collective-permute-start) | collective-permute-done | bytes 786464 | tf_op jit(solution)/shard_map/ppermute | solution.py:594
  80.6 1.2 slice_add_fusion
  82.0 0.7 broadcast_multiply_fusion
  82.7 0.4 convert_reduce_fusion
  83.1 20.7 %collective-permute-done.1 = f32[4,64,384]{2,1,0:T(8,128)S(1)} collective-permute-done((f32[4,64,384]{2,1,0:T(8,128)S(1)}, f32[4,64,384]{2,1,0:T(8,128)S(1)}, u32[]{:S(2)}, u32[]{:S(2)}) %collective-permute-start.1) | collective-permute-done | bytes 393248 | tf_op jit(solution)/shard_map/ppermute | solution.py:594
  104.2 22.6 %collective-permute-done.2 = f32[2,64,384]{2,1,0:T(8,128)S(1)} collective-permute-done((f32[2,64,384]{2,1,0:T(8,128)S(1)}, f32[2,64,384]{2,1,0:T(8,128)S(1)}, u32[]{:S(2)}, u32[]{:S(2)}) %collective-permute-start.2) | collective-permute-done | bytes 196640 | tf_op jit(solution)/shard_map/ppermute | solution.py:594
  126.8 3.2 %collective-permute-start.3 = (bf16[1,64,384]{2,1,0:T(8,128)(2,1)S(1)}, bf16[1,64,384]{2,1,0:T(8,128)(2,1)S(1)}, u32[]{:S(2)}, u32[]{:S(2)}) collective-permute-start(bf16[1,64,384]{2,1,0:T(8,128)(2,1)S(1)} %slice.50), channel_id=1, source_target_pairs={{0,8},{1,9},{2,10},{3,11},{4,12},{5,13},{6,14},{7,15},{8,0},{9,1},... | collective-permute-start | bytes 147464 | tf_op jit(solution)/shard_map/ppermute | solution.py:594
  130.0 18.8 %collective-permute-done.3 = bf16[1,64,384]{2,1,0:T(8,128)(2,1)S(1)} collective-permute-done((bf16[1,64,384]{2,1,0:T(8,128)(2,1)S(1)}, bf16[1,64,384]{2,1,0:T(8,128)(2,1)S(1)}, u32[]{:S(2)}, u32[]{:S(2)}) %collective-permute-start.3) | collective-permute-done | bytes 49184 | tf_op jit(solution)/shard_map/ppermute | solution.py:594
  148.8 0.7 add_bitcast_fusion
  149.5 4.6 %all-to-all-start = ((bf16[16,12,16,128]{3,2,1,0:T(8,128)(2,1)}), bf16[16,12,16,128]{3,2,1,0:T(8,128)(2,1)S(1)}, u32[]{:S(2)}, u32[]{:S(2)}) async-start(bf16[16,12,16,128]{3,2,1,0:T(8,128)(2,1)} %get-tuple-element.27), calls=%async_computation | async-start | bytes 1572864 | tf_op jit(solution)/shard_map/all_to_all | solution.py:598
  154.1 17.9 %correlate.2.refs_2_ = f32[32,2,2,256,256]{4,3,2,1,0:T(8,128)} custom-call(bf16[16,20,16,128]{3,2,1,0:T(8,128)(2,1)S(1)} %all-to-all-done.1.refs_0_, bf16[16,64,16,128]{3,2,1,0:T(8,128)(2,1)} %all-to-all-done.2.refs_1_, s32[4,4,256]{2,1,0:T(4,128)S(1)} %multiply_add_fusion.refs_2_), custom_call_target="tpu_custom_call" | custom-call | flops 16000000000 | bytes 40000000 | tf_op jit(solution)/shard_map/correlate/pallas_call | solution.py:477
  172.0 0.6 all-to-all-done.refs_0_
  172.6 3.1 %correlate.3 = f32[32,2,2,256,256]{4,3,2,1,0:T(8,128)} custom-call(bf16[16,12,16,128]{3,2,1,0:T(8,128)(2,1)S(1)} %all-to-all-done.refs_0_, s32[1,4,256]{2,1,0:T(4,128)S(1)} %slice.45.refs_1_, f32[32,2,2,256,256]{4,3,2,1,0:T(8,128)} %correlate.2.refs_2_), custom_call_target="tpu_custom_call", output_to_operand_aliasing={{}: (2, {})} | custom-call | flops 2000000000 | bytes 5000000 | tf_op jit(solution)/shard_map/correlate/pallas_call | solution.py:477
  (20 shorter events, 0.8 us)
Async XLA Ops:
  11.4 35.1 %all-to-all-start.1 = ((bf16[16,20,16,128]{3,2,1,0:T(8,128)(2,1)}), bf16[16,20,16,128]{3,2,1,0:T(8,128)(2,1)S(1)}, u32[]{:S(2)}, u32[]{:S(2)}) async-start(bf16[16,20,16,128]{3,2,1,0:T(8,128)(2,1)} %get-tuple-element.28), calls=%async_computation.1 | async-start | bytes 2621440 | tf_op jit(solution)/shard_map/all_to_all | solution.py:598
  46.5 7.1 %copy-start = (f32[4,64]{1,0:T(4,128)S(1)}, f32[4,64]{1,0:T(4,128)}, u32[]{:S(2)}) copy-start(f32[4,64]{1,0:T(4,128)} %param.9) | copy-start | bytes 3076
  46.5 8.5 %copy-start.1 = (f32[64]{0:T(128)S(1)}, f32[64]{0:T(128)}, u32[]{:S(2)}) copy-start(f32[64]{0:T(128)} %constant.68.clone) | copy-start | bytes 772
  46.5 103.0 %all-to-all-start.2 = ((bf16[16,64,16,128]{3,2,1,0:T(8,128)(2,1)}), bf16[16,64,16,128]{3,2,1,0:T(8,128)(2,1)}, u32[]{:S(2)}, u32[]{:S(2)}) async-start(bf16[16,64,16,128]{3,2,1,0:T(8,128)(2,1)} %get-tuple-element.29), calls=%async_computation.2 | async-start | bytes 8388608 | tf_op jit(solution)/shard_map/all_to_all | solution.py:598
  78.2 2.4 %collective-permute-start = (f32[8,64,384]{2,1,0:T(8,128)S(1)}, f32[8,64,384]{2,1,0:T(8,128)S(1)}, u32[]{:S(2)}, u32[]{:S(2)}) collective-permute-start(f32[8,64,384]{2,1,0:T(8,128)S(1)} %slice.38), channel_id=1, source_target_pairs={{0,1},{1,0},{2,3},{3,2},{4,5},{5,4},{6,7},{7,6},{8,9},{9,8},{10,11... | collective-permute-start | bytes 2359304 | tf_op jit(solution)/shard_map/ppermute | solution.py:594
  81.9 21.9 %collective-permute-start.1 = (f32[4,64,384]{2,1,0:T(8,128)S(1)}, f32[4,64,384]{2,1,0:T(8,128)S(1)}, u32[]{:S(2)}, u32[]{:S(2)}) collective-permute-start(f32[4,64,384]{2,1,0:T(8,128)S(1)} %slice.40), channel_id=1, source_target_pairs={{0,2},{1,3},{2,0},{3,1},{4,6},{5,7},{6,4},{7,5},{8,10},{9,11},{10,... | collective-permute-start | bytes 1179656 | tf_op jit(solution)/shard_map/ppermute | solution.py:594
  103.9 22.9 %collective-permute-start.2 = (f32[2,64,384]{2,1,0:T(8,128)S(1)}, f32[2,64,384]{2,1,0:T(8,128)S(1)}, u32[]{:S(2)}, u32[]{:S(2)}) collective-permute-start(f32[2,64,384]{2,1,0:T(8,128)S(1)} %slice.42), channel_id=1, source_target_pairs={{0,4},{1,5},{2,6},{3,7},{4,0},{5,1},{6,2},{7,3},{8,12},{9,13},{10,... | collective-permute-start | bytes 589832 | tf_op jit(solution)/shard_map/ppermute | solution.py:594
  126.8 22.0 %collective-permute-start.3 = (bf16[1,64,384]{2,1,0:T(8,128)(2,1)S(1)}, bf16[1,64,384]{2,1,0:T(8,128)(2,1)S(1)}, u32[]{:S(2)}, u32[]{:S(2)}) collective-permute-start(bf16[1,64,384]{2,1,0:T(8,128)(2,1)S(1)} %slice.50), channel_id=1, source_target_pairs={{0,8},{1,9},{2,10},{3,11},{4,12},{5,13},{6,14},{7,15},{8,0},{9,1},... | collective-permute-start | bytes 147464 | tf_op jit(solution)/shard_map/ppermute | solution.py:594
  149.5 23.1 %all-to-all-start = ((bf16[16,12,16,128]{3,2,1,0:T(8,128)(2,1)}), bf16[16,12,16,128]{3,2,1,0:T(8,128)(2,1)S(1)}, u32[]{:S(2)}, u32[]{:S(2)}) async-start(bf16[16,12,16,128]{3,2,1,0:T(8,128)(2,1)} %get-tuple-element.27), calls=%async_computation | async-start | bytes 1572864 | tf_op jit(solution)/shard_map/all_to_all | solution.py:598

commit v14 on v13

--- a/solution.py
+++ b/solution.py
@@ -341,10 +341,18 @@
         )(*operands)
 
 
-def receive_kernel(z, parities, step_pairs, runs, arrays, even_steps, *refs):
+def receive_kernel(z, parities, step_pairs, runs, arrays, even_steps, beams, *refs):
     arr_refs, key_ref = refs[:arrays], refs[arrays]
-    vis_ref, buf_ref, rows_ref, pick_ref, sems = refs[-5:]
+    buf_ref, rows_ref, pick_ref, sems = refs[-4:]
+    vis_ref = refs[-6] if beams else refs[-5]
     g = pl.program_id(0)
+    if beams:
+        kept_ref, away_ref, beams_ref = refs[arrays + 1], refs[arrays + 2], refs[-5]
+
+        @pl.when(g == 0)
+        def _():
+            beams_ref[...] = kept_ref[0] + away_ref[0].astype(jnp.float32)
+
     lf = z.lane_frames
     few = BAND_CH // 2
     steps = few // step_pairs
@@ -449,7 +457,7 @@
         correlate(every)
 
 
-def receive_call(z, chunk, parity, arrived, keys, vis, even_last=False):
+def receive_call(z, chunk, parity, arrived, keys, vis, even_last=False, beams=()):
     parities = 2 if parity is None else 1
     step_pairs = 4
     steps = BAND_CH // 2 // step_pairs
@@ -469,6 +477,18 @@
     operands = arrays + [keys]
     in_specs = [pl.BlockSpec(memory_space=pl.ANY)] * len(arrays) + [whole_spec(keys.shape)]
     aliases = {}
+    out_specs = [
+        pl.BlockSpec(
+            (step_pairs, parities, 2, FSUB, FSUB),
+            lambda g: (chunk * steps + g, at, 0, 0, 0),
+        )
+    ]
+    out_shape = [out_shape]
+    if beams:
+        in_specs += [whole_spec(x.shape) for x in beams]
+        operands += beams
+        out_specs.append(whole_spec(beams[0].shape[1:]))
+        out_shape.append(jax.ShapeDtypeStruct(beams[0].shape[1:], jnp.float32))
     if vis is not None:
         in_specs.append(pl.BlockSpec(memory_space=pl.ANY))
         aliases = {len(operands): 0}
@@ -476,14 +496,12 @@
     share = parities * len(runs)
     return pl.pallas_call(
         functools.partial(
-            receive_kernel, z, parities, step_pairs, runs, len(arrays), steps if even_last else 0
+            receive_kernel, z, parities, step_pairs, runs, len(arrays),
+            steps if even_last else 0, bool(beams),
         ),
         grid=(len(runs) * steps,),
         in_specs=in_specs,
-        out_specs=pl.BlockSpec(
-            (step_pairs, parities, 2, FSUB, FSUB),
-            lambda g: (chunk * steps + g, at, 0, 0, 0),
-        ),
+        out_specs=out_specs,
         out_shape=out_shape,
         input_output_aliases=aliases,
         scratch_shapes=[
@@ -648,22 +666,21 @@
             ]
 
     beams, bit = beam_call(z, me_array, spectra, delays), 1
-    while beams.shape[0] > 1:
+    while beams.shape[0] > 2:
         half = beams.shape[0] // 2
-        kept, away = beams[:half], beams[half:]
-        if half > 1:
-            beams, bit = kept + swap(z, away, bit), 2 * bit
-        else:
-            beams = away = swap(z, away.astype(jnp.bfloat16), bit)
+        beams, bit = beams[:half] + swap(z, beams[half:], bit), 2 * bit
+    kept, away = beams[:1], beams[1:].astype(jnp.bfloat16)
     if len(z.parts) > 1:
         last, kept, away = lax.optimization_barrier((last, kept, away))
         got = exchange(last)
+        away = swap(z, away, bit)
         k = z.chunks - 1
-        vis = receive_call(z, 0, None, arrived, take_key, None, even_last=True)
-        vis = receive_call(z, k, 1, [[(got, 0, z.quads, 0)]], take_key[k:], vis)
+        (vis,) = receive_call(z, 0, None, arrived, take_key, None, even_last=True)
+        odd = [[(got, 0, z.quads, 0)]]
+        vis, beams = receive_call(z, k, 1, odd, take_key[k:], vis, beams=[kept, away])
     else:
-        vis = receive_call(z, 0, None, arrived, take_key, None)
-    beams = (kept + away.astype(jnp.float32)).reshape(z.chan_dev, 2 * BEAMS * FR)
+        (vis,) = receive_call(z, 0, None, arrived, take_key, None)
+        beams = (kept + swap(z, away, bit).astype(jnp.float32)).reshape(z.chan_dev, -1)
     return (vis.reshape(z.chan_dev, 2, FSUB, FSUB), beams)
 
 

time: 178 us -> 177 us (level)
  waiting for transfers between devices: 66.3 us -> 54.8 us
  starting transfers between devices: 22.5 us -> 33.1 us
    ppermute x4, waiting for transfers between devices: 64 us -> 45.1 us  [swap(): return lax.ppermute(x, 'chan', [(i, i ^ offset) for i in range(z.devices)])]
    all_to_all x3, starting transfers between devices: 18.4 us -> 28.9 us  [exchange(): return lax.all_to_all(x, 'chan', split_axis=0, concat_axis=0, tiled=True)]
    all_to_all x3, waiting for transfers between devices: 2.36 us -> 9.64 us  [exchange(): return lax.all_to_all(x, 'chan', split_axis=0, concat_axis=0, tiled=True)]
where the time goes in v14:
time: 177 us; the launch traced here: 174 us
  Pallas kernels  78.6 us (44%)
  waiting for transfers between devices  54.8 us (31%)
  starting transfers between devices  33.1 us (19%)
  other arithmetic  5.4 us (3%)
    ppermute x4, waiting for transfers between devices, swap(): return lax.ppermute(x, 'chan', [(i, i ^ offset) for i in range(z.devices)])  45.1 us
    all_to_all x3, starting transfers between devices, exchange(): return lax.all_to_all(x, 'chan', split_axis=0, concat_axis=0, tiled=True)  28.9 us
    pallas_call x2, Pallas kernels, first(): pl.pallas_call(functools.partial(first_kernel, z, self.scale, chunks, len...  24.5 us
    pallas_call x2, Pallas kernels, receive_call(): pl.pallas_call(functools.partial(receive_kernel, z, parities, step_pairs,...  21.1 us
    pallas_call x1, Pallas kernels, beam_call(): pl.pallas_call(functools.partial(beam_kernel, z), grid_spec=grid_spec, ou...  20.2 us
    pallas_call x1, Pallas kernels, next(): pl.pallas_call(functools.partial(next_kernel, z, self.scale, chunks), in_...  12.8 us
    all_to_all x3, waiting for transfers between devices, exchange(): return lax.all_to_all(x, 'chan', split_axis=0, concat_axis=0, tiled=True)  9.64 us
    ppermute x4, starting transfers between devices, swap(): return lax.ppermute(x, 'chan', [(i, i ^ offset) for i in range(z.devices)])  4.19 us
  transfers between devices with their start and end apart: 7, of which 6 were waited for; matrix products, arithmetic and copies ran while one was open for 4% of the time, Pallas kernels for 37%

profile of v14, /device:TPU:5, one launch (start us, length us, event | category | flops | bytes accessed | tf_op | source)
XLA Modules:
  0.0 174.1 jit_solution(17410518785565806331)
XLA Ops:
  0.6 10.7 %filter_spectra.2 = (bf16[3072,2048]{1,0:T(8,128)(2,1)}, bf16[512,3072]{1,0:T(8,128)(2,1)}, bf16[512,3072]{1,0:T(8,128)(2,1)}, bf16[16,20,16,128]{3,2,1,0:T(8,128)(2,1)}) custom-call(s32[1]{0:T(128)} %bitcast.me_ref, bf16[64,104448]{1,0:T(8,128)(2,1)} %h2_ref.3, bf16[64,104448]{1,0:T(8,128)(2,1)} %h2_ref.3, bf16[64,104448]{1,0:T(8,128)(2,1)} %h2_ref.3, ...), custom_call_target="tpu_custom_call" | custom-call | flops 5368709120 | bytes 15000000 | tf_op jit(solution)/shard_map/filter_spectra/pallas_call | solution.py:293
  11.4 6.7 %all-to-all-start.1 = ((bf16[16,20,16,128]{3,2,1,0:T(8,128)(2,1)}), bf16[16,20,16,128]{3,2,1,0:T(8,128)(2,1)S(1)}, u32[]{:S(2)}, u32[]{:S(2)}) async-start(bf16[16,20,16,128]{3,2,1,0:T(8,128)(2,1)} %get-tuple-element.32), calls=%async_computation.1 | async-start | bytes 2621440 | tf_op jit(solution)/shard_map/all_to_all | solution.py:616
  18.0 13.8 %filter_spectra.3 = (bf16[3072,2048]{1,0:T(8,128)(2,1)}, bf16[512,3072]{1,0:T(8,128)(2,1)}, bf16[512,3072]{1,0:T(8,128)(2,1)}, bf16[16,64,16,128]{3,2,1,0:T(8,128)(2,1)}) custom-call(s32[1]{0:T(128)} %bitcast.me_ref, bf16[64,104448]{1,0:T(8,128)(2,1)} %h2_ref.3, ...), custom_call_target="tpu_custom_call", output_to_operand_aliasing={{0}: (8, {}), {1}: (9, {}), {2}: (10, {})} | custom-call | flops 7516192768 | bytes 21000000 | tf_op jit(solution)/shard_map/filter_spectra/pallas_call | solution.py:293
  31.8 12.8 %spectra_next.1 = (bf16[512,3072]{1,0:T(8,128)(2,1)}, bf16[512,3072]{1,0:T(8,128)(2,1)}, bf16[16,64,16,128]{3,2,1,0:T(8,128)(2,1)}, bf16[16,12,16,128]{3,2,1,0:T(8,128)(2,1)}) custom-call(s32[1]{0:T(128)} %bitcast.me_ref, bf16[3072,2048]{1,0:T(8,128)(2,1)} %get-tuple-element.22.filt_ref, ...), custom_call_target="tpu_custom_call", output_to_operand_aliasing={{2}: (4, {})} | custom-call | flops 6442450944 | bytes 18000000 | tf_op jit(solution)/shard_map/spectra_next/pallas_call | solution.py:322
  44.7 1.8 %all-to-all-done.1.refs_0_ = bf16[16,20,16,128]{3,2,1,0:T(8,128)(2,1)S(1)} async-done(((bf16[16,20,16,128]{3,2,1,0:T(8,128)(2,1)}), bf16[16,20,16,128]{3,2,1,0:T(8,128)(2,1)S(1)}, u32[]{:S(2)}, u32[]{:S(2)}) %all-to-all-start.1) | async-done | bytes 1310752 | tf_op jit(solution)/shard_map/all_to_all | solution.py:616
  46.5 7.1 %all-to-all-start.2 = ((bf16[16,64,16,128]{3,2,1,0:T(8,128)(2,1)}), bf16[16,64,16,128]{3,2,1,0:T(8,128)(2,1)}, u32[]{:S(2)}, u32[]{:S(2)}) async-start(bf16[16,64,16,128]{3,2,1,0:T(8,128)(2,1)} %get-tuple-element.33), calls=%async_computation.2 | async-start | bytes 8388608 | tf_op jit(solution)/shard_map/all_to_all | solution.py:616
  53.8 1.2 fusion.2
  55.0 1.8 %fusion = (f32[4,64,256]{2,1,0:T(8,128)}, f32[4,64,256]{2,1,0:T(8,128)}) fusion(f32[64]{0:T(128)S(1)} %copy-done.1, f32[4,256]{1,0:T(4,128)S(1)} %mul.66), kind=kLoop, calls=%fused_computation.4 | loop fusion | flops 131072 | bytes 528640 | tf_op jit(solution)/shard_map/sin | solution.py:606
  56.8 20.2 %beam_sums.1 = f32[16,64,384]{2,1,0:T(8,128)} custom-call(s32[1]{0:T(128)} %bitcast.me_ref, bf16[512,3072]{1,0:T(8,128)(2,1)} %get-tuple-element.25.refs_0_, bf16[512,3072]{1,0:T(8,128)(2,1)} %get-tuple-element.26.refs_1_, bf16[512,3072]{1,0:T(8,128)(2,1)} %get-tuple-element.27.refs_2_, bf16[512,3072]{1,0:T(8,128)(2,1)} %get-tuple-element.28.refs_3_, ...), custom_call_target="tpu_custom_call" | custom-call | flops 20000000000 | bytes 20000000 | tf_op jit(solution)/shard_map/beam_sums/pallas_call | solution.py:596
  77.0 1.2 slice.38
  78.2 0.4 collective-permute-start
  78.6 1.9 %collective-permute-done = f32[8,64,384]{2,1,0:T(8,128)S(1)} collective-permute-done((f32[8,64,384]{2,1,0:T(8,128)S(1)}, f32[8,64,384]{2,1,0:T(8,128)S(1)}, u32[]{:S(2)}, u32[]{:S(2)}) %collective-permute-start) | collective-permute-done | bytes 786464 | tf_op jit(solution)/shard_map/ppermute | solution.py:612
  80.5 1.2 slice_add_fusion
  81.9 0.7 broadcast_multiply_fusion
  82.6 0.4 convert_reduce_fusion
  83.0 20.6 %collective-permute-done.1 = f32[4,64,384]{2,1,0:T(8,128)S(1)} collective-permute-done((f32[4,64,384]{2,1,0:T(8,128)S(1)}, f32[4,64,384]{2,1,0:T(8,128)S(1)}, u32[]{:S(2)}, u32[]{:S(2)}) %collective-permute-start.1) | collective-permute-done | bytes 393248 | tf_op jit(solution)/shard_map/ppermute | solution.py:612
  103.7 0.4 collective-permute-start.2
  104.1 22.6 %collective-permute-done.2 = f32[2,64,384]{2,1,0:T(8,128)S(1)} collective-permute-done((f32[2,64,384]{2,1,0:T(8,128)S(1)}, f32[2,64,384]{2,1,0:T(8,128)S(1)}, u32[]{:S(2)}, u32[]{:S(2)}) %collective-permute-start.2) | collective-permute-done | bytes 196640 | tf_op jit(solution)/shard_map/ppermute | solution.py:612
  126.8 3.2 %collective-permute-start.3 = (bf16[1,64,384]{2,1,0:T(8,128)(2,1)S(1)}, bf16[1,64,384]{2,1,0:T(8,128)(2,1)S(1)}, u32[]{:S(2)}, u32[]{:S(2)}) collective-permute-start(bf16[1,64,384]{2,1,0:T(8,128)(2,1)S(1)} %slice.50), channel_id=1, source_target_pairs={{0,8},{1,9},{2,10},{3,11},{4,12},{5,13},{6,14},{7,15},{8,0},{9,1},... | collective-permute-start | bytes 147464 | tf_op jit(solution)/shard_map/ppermute | solution.py:612
  130.0 7.3 %all-to-all-done.2.refs_1_ = bf16[16,64,16,128]{3,2,1,0:T(8,128)(2,1)} async-done(((bf16[16,64,16,128]{3,2,1,0:T(8,128)(2,1)}), bf16[16,64,16,128]{3,2,1,0:T(8,128)(2,1)}, u32[]{:S(2)}, u32[]{:S(2)}) %all-to-all-start.2) | async-done | bytes 4194336 | tf_op jit(solution)/shard_map/all_to_all | solution.py:616
  137.3 15.1 %all-to-all-start = ((bf16[16,12,16,128]{3,2,1,0:T(8,128)(2,1)}), bf16[16,12,16,128]{3,2,1,0:T(8,128)(2,1)S(1)}, u32[]{:S(2)}, u32[]{:S(2)}) async-start(bf16[16,12,16,128]{3,2,1,0:T(8,128)(2,1)} %get-tuple-element.29), calls=%async_computation | async-start | bytes 1572864 | tf_op jit(solution)/shard_map/all_to_all | solution.py:616
  152.4 17.9 %correlate.2.refs_4_ = f32[32,2,2,256,256]{4,3,2,1,0:T(8,128)} custom-call(bf16[16,20,16,128]{3,2,1,0:T(8,128)(2,1)S(1)} %all-to-all-done.1.refs_0_, bf16[16,64,16,128]{3,2,1,0:T(8,128)(2,1)} %all-to-all-done.2.refs_1_, s32[4,4,256]{2,1,0:T(4,128)S(1)} %multiply_add_fusion.refs_2_), custom_call_target="tpu_custom_call" | custom-call | flops 16000000000 | bytes 40000000 | tf_op jit(solution)/shard_map/correlate/pallas_call | solution.py:497
  170.4 0.6 all-to-all-done.refs_0_
  170.9 3.2 %correlate.3 = (f32[32,2,2,256,256]{4,3,2,1,0:T(8,128)}, f32[64,384]{1,0:T(8,128)}) custom-call(bf16[16,12,16,128]{3,2,1,0:T(8,128)(2,1)S(1)} %all-to-all-done.refs_0_, s32[1,4,256]{2,1,0:T(4,128)S(1)} %slice.45.refs_1_, f32[1,64,384]{2,1,0:T(8,128)S(1)} %slice.43.refs_2_, ...), custom_call_target="tpu_custom_call", output_to_operand_aliasing={{0}: (4, {})} | custom-call | flops 2000000000 | bytes 5000000 | tf_op jit(solution)/shard_map/correlate/pallas_call | solution.py:497
  (19 shorter events, 0.5 us)
Async XLA Ops:
  11.4 35.1 %all-to-all-start.1 = ((bf16[16,20,16,128]{3,2,1,0:T(8,128)(2,1)}), bf16[16,20,16,128]{3,2,1,0:T(8,128)(2,1)S(1)}, u32[]{:S(2)}, u32[]{:S(2)}) async-start(bf16[16,20,16,128]{3,2,1,0:T(8,128)(2,1)} %get-tuple-element.32), calls=%async_computation.1 | async-start | bytes 2621440 | tf_op jit(solution)/shard_map/all_to_all | solution.py:616
  46.5 7.1 %copy-start = (f32[4,64]{1,0:T(4,128)S(1)}, f32[4,64]{1,0:T(4,128)}, u32[]{:S(2)}) copy-start(f32[4,64]{1,0:T(4,128)} %param.9) | copy-start | bytes 3076
  46.5 8.5 %copy-start.1 = (f32[64]{0:T(128)S(1)}, f32[64]{0:T(128)}, u32[]{:S(2)}) copy-start(f32[64]{0:T(128)} %constant.68.clone) | copy-start | bytes 772
  46.5 90.8 %all-to-all-start.2 = ((bf16[16,64,16,128]{3,2,1,0:T(8,128)(2,1)}), bf16[16,64,16,128]{3,2,1,0:T(8,128)(2,1)}, u32[]{:S(2)}, u32[]{:S(2)}) async-start(bf16[16,64,16,128]{3,2,1,0:T(8,128)(2,1)} %get-tuple-element.33), calls=%async_computation.2 | async-start | bytes 8388608 | tf_op jit(solution)/shard_map/all_to_all | solution.py:616
  78.2 2.4 %collective-permute-start = (f32[8,64,384]{2,1,0:T(8,128)S(1)}, f32[8,64,384]{2,1,0:T(8,128)S(1)}, u32[]{:S(2)}, u32[]{:S(2)}) collective-permute-start(f32[8,64,384]{2,1,0:T(8,128)S(1)} %slice.38), channel_id=1, source_target_pairs={{0,1},{1,0},{2,3},{3,2},{4,5},{5,4},{6,7},{7,6},{8,9},{9,8},{10,11... | collective-permute-start | bytes 2359304 | tf_op jit(solution)/shard_map/ppermute | solution.py:612
  81.8 21.9 %collective-permute-start.1 = (f32[4,64,384]{2,1,0:T(8,128)S(1)}, f32[4,64,384]{2,1,0:T(8,128)S(1)}, u32[]{:S(2)}, u32[]{:S(2)}) collective-permute-start(f32[4,64,384]{2,1,0:T(8,128)S(1)} %slice.40), channel_id=1, source_target_pairs={{0,2},{1,3},{2,0},{3,1},{4,6},{5,7},{6,4},{7,5},{8,10},{9,11},{10,... | collective-permute-start | bytes 1179656 | tf_op jit(solution)/shard_map/ppermute | solution.py:612
  103.7 23.0 %collective-permute-start.2 = (f32[2,64,384]{2,1,0:T(8,128)S(1)}, f32[2,64,384]{2,1,0:T(8,128)S(1)}, u32[]{:S(2)}, u32[]{:S(2)}) collective-permute-start(f32[2,64,384]{2,1,0:T(8,128)S(1)} %slice.42), channel_id=1, source_target_pairs={{0,4},{1,5},{2,6},{3,7},{4,0},{5,1},{6,2},{7,3},{8,12},{9,13},{10,... | collective-permute-start | bytes 589832 | tf_op jit(solution)/shard_map/ppermute | solution.py:612
  126.8 43.6 %collective-permute-start.3 = (bf16[1,64,384]{2,1,0:T(8,128)(2,1)S(1)}, bf16[1,64,384]{2,1,0:T(8,128)(2,1)S(1)}, u32[]{:S(2)}, u32[]{:S(2)}) collective-permute-start(bf16[1,64,384]{2,1,0:T(8,128)(2,1)S(1)} %slice.50), channel_id=1, source_target_pairs={{0,8},{1,9},{2,10},{3,11},{4,12},{5,13},{6,14},{7,15},{8,0},{9,1},... | collective-permute-start | bytes 147464 | tf_op jit(solution)/shard_map/ppermute | solution.py:612
  137.3 33.6 %all-to-all-start = ((bf16[16,12,16,128]{3,2,1,0:T(8,128)(2,1)}), bf16[16,12,16,128]{3,2,1,0:T(8,128)(2,1)S(1)}, u32[]{:S(2)}, u32[]{:S(2)}) async-start(bf16[16,12,16,128]{3,2,1,0:T(8,128)(2,1)} %get-tuple-element.29), calls=%async_computation | async-start | bytes 1572864 | tf_op jit(solution)/shard_map/all_to_all | solution.py:616

commit v15 on v14

--- a/solution.py
+++ b/solution.py
@@ -183,8 +183,16 @@
     z, scale, chunks, held, me_ref, main_ref, h0_ref, h1_ref, h2_ref, win_ref, basis_ref,
     lists_ref, *refs,
 ):
-    filt_ref, spec_refs, send_ref, loc_ref = refs[held], refs[held + 1 : -2], refs[-2], refs[-1]
+    filt_ref, spec_refs, send_ref = refs[held], refs[held + 1 : -4], refs[-4]
+    loc_ref, table_ref, sem = refs[-3:]
     halo = (h0_ref, h1_ref, h2_ref)
+    fetch = pltpu.make_async_copy(basis_ref, table_ref, sem)
+    begin = pl.program_id(0) == 0
+
+    @pl.when(begin)
+    def _():
+        fetch.start()
+
     loc_ref[...] = find_places(z, me_ref[0], lists_ref[...])
 
     def emit(quad, spectra):
@@ -204,8 +212,14 @@
         samples = [jnp.concatenate([tile[p] for tile in tiles], axis=1) for p in range(2)]
         if before is not None:
             emit(quad - 1, before)
+        else:
+
+            @pl.when(begin)
+            def _():
+                fetch.wait()
+
         before = [
-            [product(z, basis_ref, p, c, samples[p]) for p in range(2)]
+            [product(z, table_ref, p, c, samples[p]) for p in range(2)]
             for c in range(len(chunks))
         ]
     emit(z.step_quads - 1, before)
@@ -265,12 +279,12 @@
     def message(self, units):
         return jax.ShapeDtypeStruct((self.z.devices, units, BAND_CH, LANES), jnp.bfloat16)
 
-    def common(self, steps, chunks):
+    def common(self, steps, chunks, scratch=()):
         z = self.z
         flops = len(chunks) * z.rows * NFFT * z.step_lanes * steps
         return dict(
             grid=(steps,),
-            scratch_shapes=[pltpu.VMEM((BANDS, LANES), jnp.int32)],
+            scratch_shapes=[pltpu.VMEM((BANDS, LANES), jnp.int32), *scratch],
             compiler_params=pltpu.CompilerParams(vmem_limit_bytes=VMEM),
             cost_estimate=pl.CostEstimate(
                 flops=flops, bytes_accessed=3_000_000 * steps, transcendentals=0
@@ -299,7 +313,7 @@
                 halo_spec(1),
                 halo_spec(2),
                 whole_spec((TAPS, NFFT)),
-                whole_spec(basis.shape),
+                pl.BlockSpec(memory_space=pltpu.HBM),
                 whole_spec(self.lists.shape),
             ]
             + [pl.BlockSpec(memory_space=pl.ANY)] * len(held),
@@ -311,7 +325,9 @@
             out_shape=[self.filt_shape] + [self.spec_shape] * count + [self.message(units)],
             input_output_aliases=aliases,
             name="filter_spectra",
-            **self.common(steps, chunks),
+            **self.common(
+                steps, chunks, [pltpu.VMEM(basis.shape, basis.dtype), pltpu.SemaphoreType.DMA]
+            ),
         )(*operands, *held)
 
     def next(self, chunks, filt, held):
@@ -506,7 +522,9 @@
         input_output_aliases=aliases,
         scratch_shapes=[
             pltpu.VMEM((slots, z.devices, units, BAND_CH, LANES), jnp.bfloat16),
-            pltpu.VMEM((FSUB // LANES, z.lane_frames * units * BAND_CH, LANES), jnp.float32),
+            pltpu.VMEM(
+                (FSUB // LANES, z.lane_frames * units * BAND_CH + z.rows_dev, LANES), jnp.float32
+            ),
             pltpu.VMEM((z.lane_frames, z.groups * LANES, FSUB), jnp.bfloat16),
             pltpu.SemaphoreType.DMA((slots, max(len(x) for x in runs))),
         ],
@@ -549,7 +567,7 @@
             first = i // 2 * BAND_CH + i % 2
             top = j * count + i * few
             row_ref[j, pl.ds(first, few, stride=2), :] = sums[top : top + few]
-        out_ref[0, :, j * FR : (j + 1) * FR] = row_ref[j][:, :FR]
+        out_ref[0, :, j * FR : (j + 1) * FR] = row_ref[j, :count, :FR]
 
 
 def beam_call(z, me, spectra, delays):
@@ -590,7 +608,7 @@
         ),
         scratch_shapes=[
             pltpu.VMEM((2 * BEAMS * z.chan_dev, FR * z.cap), jnp.bfloat16),
-            pltpu.VMEM((2 * BEAMS, z.chan_dev, LANES), jnp.float32),
+            pltpu.VMEM((2 * BEAMS, z.chan_dev + BAND_CH, LANES), jnp.float32),
         ],
     )
     return pl.pallas_call(

time: 177 us -> 178 us (level)
  Pallas kernels: 78.6 us -> 83.5 us
  waiting for transfers between devices: 54.8 us -> 53 us
    pallas_call x2, Pallas kernels: 24.5 us -> 29.4 us  [first(): pl.pallas_call(functools.partial(first_kernel, z, self.scale, chunks, len...]
    all_to_all x3, waiting for transfers between devices: 9.64 us -> 7.86 us  [exchange(): return lax.all_to_all(x, 'chan', split_axis=0, concat_axis=0, tiled=True)]
  transfers between devices with their start and end apart: 7 -> 7, of which waited for: 6 -> 5; matrix products, arithmetic and copies ran while one was open for 4% -> 4% of each run, Pallas kernels for 37% -> 38%
where the time goes in v15:
time: 178 us; the launch traced here: 176 us
  Pallas kernels  83.5 us (47%)
  waiting for transfers between devices  53 us (30%)
  starting transfers between devices  32.2 us (18%)
  other arithmetic  5.4 us (3%)
    ppermute x4, waiting for transfers between devices, swap(): return lax.ppermute(x, 'chan', [(i, i ^ offset) for i in range(z.devices)])  45.1 us
    pallas_call x2, Pallas kernels, first(): pl.pallas_call(functools.partial(first_kernel, z, self.scale, chunks, len...  29.4 us
    all_to_all x3, starting transfers between devices, exchange(): return lax.all_to_all(x, 'chan', split_axis=0, concat_axis=0, tiled=True)  28 us
    pallas_call x2, Pallas kernels, receive_call(): pl.pallas_call(functools.partial(receive_kernel, z, parities, step_pairs,...  21.1 us
    pallas_call x1, Pallas kernels, beam_call(): pl.pallas_call(functools.partial(beam_kernel, z), grid_spec=grid_spec, ou...  20.2 us
    pallas_call x1, Pallas kernels, next(): pl.pallas_call(functools.partial(next_kernel, z, self.scale, chunks), in_...  12.8 us
    all_to_all x3, waiting for transfers between devices, exchange(): return lax.all_to_all(x, 'chan', split_axis=0, concat_axis=0, tiled=True)  7.86 us
    ppermute x4, starting transfers between devices, swap(): return lax.ppermute(x, 'chan', [(i, i ^ offset) for i in range(z.devices)])  4.19 us
  transfers between devices with their start and end apart: 7, of which 5 were waited for; matrix products, arithmetic and copies ran while one was open for 4% of the time, Pallas kernels for 38%

profile of v15, /device:TPU:5, one launch (start us, length us, event | category | flops | bytes accessed | tf_op | source)
XLA Modules:
  0.0 176.3 jit_solution(11854939137287439474)
XLA Ops:
  0.6 12.7 %filter_spectra.2 = (bf16[3072,2048]{1,0:T(8,128)(2,1)}, bf16[512,3072]{1,0:T(8,128)(2,1)}, bf16[512,3072]{1,0:T(8,128)(2,1)}, bf16[16,20,16,128]{3,2,1,0:T(8,128)(2,1)}) custom-call(s32[1]{0:T(128)} %bitcast.me_ref, bf16[64,104448]{1,0:T(8,128)(2,1)} %h2_ref.3, bf16[64,104448]{1,0:T(8,128)(2,1)} %h2_ref.3, bf16[64,104448]{1,0:T(8,128)(2,1)} %h2_ref.3, ...), custom_call_target="tpu_custom_call" | custom-call | flops 5368709120 | bytes 15000000 | tf_op jit(solution)/shard_map/filter_spectra/pallas_call | solution.py:307
  13.4 6.7 %all-to-all-start.1 = ((bf16[16,20,16,128]{3,2,1,0:T(8,128)(2,1)}), bf16[16,20,16,128]{3,2,1,0:T(8,128)(2,1)S(1)}, u32[]{:S(2)}, u32[]{:S(2)}) async-start(bf16[16,20,16,128]{3,2,1,0:T(8,128)(2,1)} %get-tuple-element.32), calls=%async_computation.1 | async-start | bytes 2621440 | tf_op jit(solution)/shard_map/all_to_all | solution.py:634
  20.1 16.7 %filter_spectra.3 = (bf16[3072,2048]{1,0:T(8,128)(2,1)}, bf16[512,3072]{1,0:T(8,128)(2,1)}, bf16[512,3072]{1,0:T(8,128)(2,1)}, bf16[16,64,16,128]{3,2,1,0:T(8,128)(2,1)}) custom-call(s32[1]{0:T(128)} %bitcast.me_ref, bf16[64,104448]{1,0:T(8,128)(2,1)} %h2_ref.3, ...), custom_call_target="tpu_custom_call", output_to_operand_aliasing={{0}: (8, {}), {1}: (9, {}), {2}: (10, {})} | custom-call | flops 7516192768 | bytes 21000000 | tf_op jit(solution)/shard_map/filter_spectra/pallas_call | solution.py:307
  36.8 12.8 %spectra_next.1 = (bf16[512,3072]{1,0:T(8,128)(2,1)}, bf16[512,3072]{1,0:T(8,128)(2,1)}, bf16[16,64,16,128]{3,2,1,0:T(8,128)(2,1)}, bf16[16,12,16,128]{3,2,1,0:T(8,128)(2,1)}) custom-call(s32[1]{0:T(128)} %bitcast.me_ref, bf16[3072,2048]{1,0:T(8,128)(2,1)} %get-tuple-element.22.filt_ref, ...), custom_call_target="tpu_custom_call", output_to_operand_aliasing={{2}: (4, {})} | custom-call | flops 6442450944 | bytes 18000000 | tf_op jit(solution)/shard_map/spectra_next/pallas_call | solution.py:338
  49.6 6.2 %all-to-all-start.2 = ((bf16[16,64,16,128]{3,2,1,0:T(8,128)(2,1)}), bf16[16,64,16,128]{3,2,1,0:T(8,128)(2,1)}, u32[]{:S(2)}, u32[]{:S(2)}) async-start(bf16[16,64,16,128]{3,2,1,0:T(8,128)(2,1)} %get-tuple-element.33), calls=%async_computation.2 | async-start | bytes 8388608 | tf_op jit(solution)/shard_map/all_to_all | solution.py:634
  56.0 1.2 fusion.2
  57.2 1.8 %fusion = (f32[4,64,256]{2,1,0:T(8,128)}, f32[4,64,256]{2,1,0:T(8,128)}) fusion(f32[64]{0:T(128)S(1)} %copy-done.1, f32[4,256]{1,0:T(4,128)S(1)} %mul.66), kind=kLoop, calls=%fused_computation.4 | loop fusion | flops 131072 | bytes 528640 | tf_op jit(solution)/shard_map/sin | solution.py:624
  59.0 20.2 %beam_sums.1 = f32[16,64,384]{2,1,0:T(8,128)} custom-call(s32[1]{0:T(128)} %bitcast.me_ref, bf16[512,3072]{1,0:T(8,128)(2,1)} %get-tuple-element.25.refs_0_, bf16[512,3072]{1,0:T(8,128)(2,1)} %get-tuple-element.26.refs_1_, bf16[512,3072]{1,0:T(8,128)(2,1)} %get-tuple-element.27.refs_2_, bf16[512,3072]{1,0:T(8,128)(2,1)} %get-tuple-element.28.refs_3_, ...), custom_call_target="tpu_custom_call" | custom-call | flops 20000000000 | bytes 20000000 | tf_op jit(solution)/shard_map/beam_sums/pallas_call | solution.py:614
  79.2 1.2 slice.38
  80.4 0.4 collective-permute-start
  80.8 1.9 %collective-permute-done = f32[8,64,384]{2,1,0:T(8,128)S(1)} collective-permute-done((f32[8,64,384]{2,1,0:T(8,128)S(1)}, f32[8,64,384]{2,1,0:T(8,128)S(1)}, u32[]{:S(2)}, u32[]{:S(2)}) %collective-permute-start) | collective-permute-done | bytes 786464 | tf_op jit(solution)/shard_map/ppermute | solution.py:630
  82.7 1.2 slice_add_fusion
  84.0 0.1 collective-permute-start.1
  84.1 0.7 broadcast_multiply_fusion
  84.8 0.4 convert_reduce_fusion
  85.2 20.6 %collective-permute-done.1 = f32[4,64,384]{2,1,0:T(8,128)S(1)} collective-permute-done((f32[4,64,384]{2,1,0:T(8,128)S(1)}, f32[4,64,384]{2,1,0:T(8,128)S(1)}, u32[]{:S(2)}, u32[]{:S(2)}) %collective-permute-start.1) | collective-permute-done | bytes 393248 | tf_op jit(solution)/shard_map/ppermute | solution.py:630
  105.9 0.4 collective-permute-start.2
  106.3 22.6 %collective-permute-done.2 = f32[2,64,384]{2,1,0:T(8,128)S(1)} collective-permute-done((f32[2,64,384]{2,1,0:T(8,128)S(1)}, f32[2,64,384]{2,1,0:T(8,128)S(1)}, u32[]{:S(2)}, u32[]{:S(2)}) %collective-permute-start.2) | collective-permute-done | bytes 196640 | tf_op jit(solution)/shard_map/ppermute | solution.py:630
  129.0 3.2 %collective-permute-start.3 = (bf16[1,64,384]{2,1,0:T(8,128)(2,1)S(1)}, bf16[1,64,384]{2,1,0:T(8,128)(2,1)S(1)}, u32[]{:S(2)}, u32[]{:S(2)}) collective-permute-start(bf16[1,64,384]{2,1,0:T(8,128)(2,1)S(1)} %slice.50), channel_id=1, source_target_pairs={{0,8},{1,9},{2,10},{3,11},{4,12},{5,13},{6,14},{7,15},{8,0},{9,1},... | collective-permute-start | bytes 147464 | tf_op jit(solution)/shard_map/ppermute | solution.py:630
  132.2 7.3 %all-to-all-done.2.refs_1_ = bf16[16,64,16,128]{3,2,1,0:T(8,128)(2,1)} async-done(((bf16[16,64,16,128]{3,2,1,0:T(8,128)(2,1)}), bf16[16,64,16,128]{3,2,1,0:T(8,128)(2,1)}, u32[]{:S(2)}, u32[]{:S(2)}) %all-to-all-start.2) | async-done | bytes 4194336 | tf_op jit(solution)/shard_map/all_to_all | solution.py:634
  139.5 15.1 %all-to-all-start = ((bf16[16,12,16,128]{3,2,1,0:T(8,128)(2,1)}), bf16[16,12,16,128]{3,2,1,0:T(8,128)(2,1)S(1)}, u32[]{:S(2)}, u32[]{:S(2)}) async-start(bf16[16,12,16,128]{3,2,1,0:T(8,128)(2,1)} %get-tuple-element.29), calls=%async_computation | async-start | bytes 1572864 | tf_op jit(solution)/shard_map/all_to_all | solution.py:634
  154.6 17.9 %correlate.2.refs_4_ = f32[32,2,2,256,256]{4,3,2,1,0:T(8,128)} custom-call(bf16[16,20,16,128]{3,2,1,0:T(8,128)(2,1)S(1)} %all-to-all-done.1.refs_0_, bf16[16,64,16,128]{3,2,1,0:T(8,128)(2,1)} %all-to-all-done.2.refs_1_, s32[4,4,256]{2,1,0:T(4,128)S(1)} %multiply_add_fusion.refs_2_), custom_call_target="tpu_custom_call" | custom-call | flops 16000000000 | bytes 40000000 | tf_op jit(solution)/shard_map/correlate/pallas_call | solution.py:513
  172.6 0.6 all-to-all-done.refs_0_
  173.1 3.1 %correlate.3 = (f32[32,2,2,256,256]{4,3,2,1,0:T(8,128)}, f32[64,384]{1,0:T(8,128)}) custom-call(bf16[16,12,16,128]{3,2,1,0:T(8,128)(2,1)S(1)} %all-to-all-done.refs_0_, s32[1,4,256]{2,1,0:T(4,128)S(1)} %slice.45.refs_1_, f32[1,64,384]{2,1,0:T(8,128)S(1)} %slice.43.refs_2_, ...), custom_call_target="tpu_custom_call", output_to_operand_aliasing={{0}: (4, {})} | custom-call | flops 2000000000 | bytes 5000000 | tf_op jit(solution)/shard_map/correlate/pallas_call | solution.py:513
  (19 shorter events, 0.4 us)
Async XLA Ops:
  13.4 36.2 %all-to-all-start.1 = ((bf16[16,20,16,128]{3,2,1,0:T(8,128)(2,1)}), bf16[16,20,16,128]{3,2,1,0:T(8,128)(2,1)S(1)}, u32[]{:S(2)}, u32[]{:S(2)}) async-start(bf16[16,20,16,128]{3,2,1,0:T(8,128)(2,1)} %get-tuple-element.32), calls=%async_computation.1 | async-start | bytes 2621440 | tf_op jit(solution)/shard_map/all_to_all | solution.py:634
  49.6 6.2 %copy-start = (f32[4,64]{1,0:T(4,128)S(1)}, f32[4,64]{1,0:T(4,128)}, u32[]{:S(2)}) copy-start(f32[4,64]{1,0:T(4,128)} %param.9) | copy-start | bytes 3076
  49.6 7.6 %copy-start.1 = (f32[64]{0:T(128)S(1)}, f32[64]{0:T(128)}, u32[]{:S(2)}) copy-start(f32[64]{0:T(128)} %constant.68.clone) | copy-start | bytes 772
  49.6 89.9 %all-to-all-start.2 = ((bf16[16,64,16,128]{3,2,1,0:T(8,128)(2,1)}), bf16[16,64,16,128]{3,2,1,0:T(8,128)(2,1)}, u32[]{:S(2)}, u32[]{:S(2)}) async-start(bf16[16,64,16,128]{3,2,1,0:T(8,128)(2,1)} %get-tuple-element.33), calls=%async_computation.2 | async-start | bytes 8388608 | tf_op jit(solution)/shard_map/all_to_all | solution.py:634
  80.4 2.4 %collective-permute-start = (f32[8,64,384]{2,1,0:T(8,128)S(1)}, f32[8,64,384]{2,1,0:T(8,128)S(1)}, u32[]{:S(2)}, u32[]{:S(2)}) collective-permute-start(f32[8,64,384]{2,1,0:T(8,128)S(1)} %slice.38), channel_id=1, source_target_pairs={{0,1},{1,0},{2,3},{3,2},{4,5},{5,4},{6,7},{7,6},{8,9},{9,8},{10,11... | collective-permute-start | bytes 2359304 | tf_op jit(solution)/shard_map/ppermute | solution.py:630
  84.0 21.8 %collective-permute-start.1 = (f32[4,64,384]{2,1,0:T(8,128)S(1)}, f32[4,64,384]{2,1,0:T(8,128)S(1)}, u32[]{:S(2)}, u32[]{:S(2)}) collective-permute-start(f32[4,64,384]{2,1,0:T(8,128)S(1)} %slice.40), channel_id=1, source_target_pairs={{0,2},{1,3},{2,0},{3,1},{4,6},{5,7},{6,4},{7,5},{8,10},{9,11},{10,... | collective-permute-start | bytes 1179656 | tf_op jit(solution)/shard_map/ppermute | solution.py:630
  105.9 23.0 %collective-permute-start.2 = (f32[2,64,384]{2,1,0:T(8,128)S(1)}, f32[2,64,384]{2,1,0:T(8,128)S(1)}, u32[]{:S(2)}, u32[]{:S(2)}) collective-permute-start(f32[2,64,384]{2,1,0:T(8,128)S(1)} %slice.42), channel_id=1, source_target_pairs={{0,4},{1,5},{2,6},{3,7},{4,0},{5,1},{6,2},{7,3},{8,12},{9,13},{10,... | collective-permute-start | bytes 589832 | tf_op jit(solution)/shard_map/ppermute | solution.py:630
  129.0 43.6 %collective-permute-start.3 = (bf16[1,64,384]{2,1,0:T(8,128)(2,1)S(1)}, bf16[1,64,384]{2,1,0:T(8,128)(2,1)S(1)}, u32[]{:S(2)}, u32[]{:S(2)}) collective-permute-start(bf16[1,64,384]{2,1,0:T(8,128)(2,1)S(1)} %slice.50), channel_id=1, source_target_pairs={{0,8},{1,9},{2,10},{3,11},{4,12},{5,13},{6,14},{7,15},{8,0},{9,1},... | collective-permute-start | bytes 147464 | tf_op jit(solution)/shard_map/ppermute | solution.py:630
  139.5 33.6 %all-to-all-start = ((bf16[16,12,16,128]{3,2,1,0:T(8,128)(2,1)}), bf16[16,12,16,128]{3,2,1,0:T(8,128)(2,1)S(1)}, u32[]{:S(2)}, u32[]{:S(2)}) async-start(bf16[16,12,16,128]{3,2,1,0:T(8,128)(2,1)} %get-tuple-element.29), calls=%async_computation | async-start | bytes 1572864 | tf_op jit(solution)/shard_map/all_to_all | solution.py:634

commit v16 on v14

--- a/solution.py
+++ b/solution.py
@@ -506,7 +506,9 @@
         input_output_aliases=aliases,
         scratch_shapes=[
             pltpu.VMEM((slots, z.devices, units, BAND_CH, LANES), jnp.bfloat16),
-            pltpu.VMEM((FSUB // LANES, z.lane_frames * units * BAND_CH, LANES), jnp.float32),
+            pltpu.VMEM(
+                (FSUB // LANES, z.lane_frames * units * BAND_CH + z.rows_dev, LANES), jnp.float32
+            ),
             pltpu.VMEM((z.lane_frames, z.groups * LANES, FSUB), jnp.bfloat16),
             pltpu.SemaphoreType.DMA((slots, max(len(x) for x in runs))),
         ],
@@ -549,7 +551,7 @@
             first = i // 2 * BAND_CH + i % 2
             top = j * count + i * few
             row_ref[j, pl.ds(first, few, stride=2), :] = sums[top : top + few]
-        out_ref[0, :, j * FR : (j + 1) * FR] = row_ref[j][:, :FR]
+        out_ref[0, :, j * FR : (j + 1) * FR] = row_ref[j, :count, :FR]
 
 
 def beam_call(z, me, spectra, delays):
@@ -590,7 +592,7 @@
         ),
         scratch_shapes=[
             pltpu.VMEM((2 * BEAMS * z.chan_dev, FR * z.cap), jnp.bfloat16),
-            pltpu.VMEM((2 * BEAMS, z.chan_dev, LANES), jnp.float32),
+            pltpu.VMEM((2 * BEAMS, z.chan_dev + BAND_CH, LANES), jnp.float32),
         ],
     )
     return pl.pallas_call(

time: 177 us -> 177 us (level)
  no operation moved by 1% of the time
where the time goes in v16:
time: 177 us; the launch traced here: 174 us
  Pallas kernels  78.6 us (44%)
  waiting for transfers between devices  54.8 us (31%)
  starting transfers between devices  33.1 us (19%)
  other arithmetic  5.4 us (3%)
    ppermute x4, waiting for transfers between devices, swap(): return lax.ppermute(x, 'chan', [(i, i ^ offset) for i in range(z.devices)])  45.1 us
    all_to_all x3, starting transfers between devices, exchange(): return lax.all_to_all(x, 'chan', split_axis=0, concat_axis=0, tiled=True)  28.9 us
    pallas_call x2, Pallas kernels, first(): pl.pallas_call(functools.partial(first_kernel, z, self.scale, chunks, len...  24.5 us
    pallas_call x2, Pallas kernels, receive_call(): pl.pallas_call(functools.partial(receive_kernel, z, parities, step_pairs,...  21.1 us
    pallas_call x1, Pallas kernels, beam_call(): pl.pallas_call(functools.partial(beam_kernel, z), grid_spec=grid_spec, ou...  20.2 us
    pallas_call x1, Pallas kernels, next(): pl.pallas_call(functools.partial(next_kernel, z, self.scale, chunks), in_...  12.8 us
    all_to_all x3, waiting for transfers between devices, exchange(): return lax.all_to_all(x, 'chan', split_axis=0, concat_axis=0, tiled=True)  9.64 us
    ppermute x4, starting transfers between devices, swap(): return lax.ppermute(x, 'chan', [(i, i ^ offset) for i in range(z.devices)])  4.19 us
  transfers between devices with their start and end apart: 7, of which 6 were waited for; matrix products, arithmetic and copies ran while one was open for 4% of the time, Pallas kernels for 37%

profile of v16, /device:TPU:5, one launch (start us, length us, event | category | flops | bytes accessed | tf_op | source)
XLA Modules:
  0.0 174.1 jit_solution(9836375617378199731)
XLA Ops:
  0.6 10.7 %filter_spectra.2 = (bf16[3072,2048]{1,0:T(8,128)(2,1)}, bf16[512,3072]{1,0:T(8,128)(2,1)}, bf16[512,3072]{1,0:T(8,128)(2,1)}, bf16[16,20,16,128]{3,2,1,0:T(8,128)(2,1)}) custom-call(s32[1]{0:T(128)} %bitcast.me_ref, bf16[64,104448]{1,0:T(8,128)(2,1)} %h2_ref.3, bf16[64,104448]{1,0:T(8,128)(2,1)} %h2_ref.3, bf16[64,104448]{1,0:T(8,128)(2,1)} %h2_ref.3, ...), custom_call_target="tpu_custom_call" | custom-call | flops 5368709120 | bytes 15000000 | tf_op jit(solution)/shard_map/filter_spectra/pallas_call | solution.py:293
  11.4 6.7 %all-to-all-start.1 = ((bf16[16,20,16,128]{3,2,1,0:T(8,128)(2,1)}), bf16[16,20,16,128]{3,2,1,0:T(8,128)(2,1)S(1)}, u32[]{:S(2)}, u32[]{:S(2)}) async-start(bf16[16,20,16,128]{3,2,1,0:T(8,128)(2,1)} %get-tuple-element.32), calls=%async_computation.1 | async-start | bytes 2621440 | tf_op jit(solution)/shard_map/all_to_all | solution.py:618
  18.0 13.8 %filter_spectra.3 = (bf16[3072,2048]{1,0:T(8,128)(2,1)}, bf16[512,3072]{1,0:T(8,128)(2,1)}, bf16[512,3072]{1,0:T(8,128)(2,1)}, bf16[16,64,16,128]{3,2,1,0:T(8,128)(2,1)}) custom-call(s32[1]{0:T(128)} %bitcast.me_ref, bf16[64,104448]{1,0:T(8,128)(2,1)} %h2_ref.3, ...), custom_call_target="tpu_custom_call", output_to_operand_aliasing={{0}: (8, {}), {1}: (9, {}), {2}: (10, {})} | custom-call | flops 7516192768 | bytes 21000000 | tf_op jit(solution)/shard_map/filter_spectra/pallas_call | solution.py:293
  31.8 12.8 %spectra_next.1 = (bf16[512,3072]{1,0:T(8,128)(2,1)}, bf16[512,3072]{1,0:T(8,128)(2,1)}, bf16[16,64,16,128]{3,2,1,0:T(8,128)(2,1)}, bf16[16,12,16,128]{3,2,1,0:T(8,128)(2,1)}) custom-call(s32[1]{0:T(128)} %bitcast.me_ref, bf16[3072,2048]{1,0:T(8,128)(2,1)} %get-tuple-element.22.filt_ref, ...), custom_call_target="tpu_custom_call", output_to_operand_aliasing={{2}: (4, {})} | custom-call | flops 6442450944 | bytes 18000000 | tf_op jit(solution)/shard_map/spectra_next/pallas_call | solution.py:322
  44.7 1.8 %all-to-all-done.1.refs_0_ = bf16[16,20,16,128]{3,2,1,0:T(8,128)(2,1)S(1)} async-done(((bf16[16,20,16,128]{3,2,1,0:T(8,128)(2,1)}), bf16[16,20,16,128]{3,2,1,0:T(8,128)(2,1)S(1)}, u32[]{:S(2)}, u32[]{:S(2)}) %all-to-all-start.1) | async-done | bytes 1310752 | tf_op jit(solution)/shard_map/all_to_all | solution.py:618
  46.5 7.1 %all-to-all-start.2 = ((bf16[16,64,16,128]{3,2,1,0:T(8,128)(2,1)}), bf16[16,64,16,128]{3,2,1,0:T(8,128)(2,1)}, u32[]{:S(2)}, u32[]{:S(2)}) async-start(bf16[16,64,16,128]{3,2,1,0:T(8,128)(2,1)} %get-tuple-element.33), calls=%async_computation.2 | async-start | bytes 8388608 | tf_op jit(solution)/shard_map/all_to_all | solution.py:618
  53.8 1.2 fusion.2
  55.0 1.8 %fusion = (f32[4,64,256]{2,1,0:T(8,128)}, f32[4,64,256]{2,1,0:T(8,128)}) fusion(f32[64]{0:T(128)S(1)} %copy-done.1, f32[4,256]{1,0:T(4,128)S(1)} %mul.66), kind=kLoop, calls=%fused_computation.4 | loop fusion | flops 131072 | bytes 528640 | tf_op jit(solution)/shard_map/sin | solution.py:608
  56.8 20.2 %beam_sums.1 = f32[16,64,384]{2,1,0:T(8,128)} custom-call(s32[1]{0:T(128)} %bitcast.me_ref, bf16[512,3072]{1,0:T(8,128)(2,1)} %get-tuple-element.25.refs_0_, bf16[512,3072]{1,0:T(8,128)(2,1)} %get-tuple-element.26.refs_1_, bf16[512,3072]{1,0:T(8,128)(2,1)} %get-tuple-element.27.refs_2_, bf16[512,3072]{1,0:T(8,128)(2,1)} %get-tuple-element.28.refs_3_, ...), custom_call_target="tpu_custom_call" | custom-call | flops 20000000000 | bytes 20000000 | tf_op jit(solution)/shard_map/beam_sums/pallas_call | solution.py:598
  77.0 1.2 slice.38
  78.2 0.4 collective-permute-start
  78.6 1.9 %collective-permute-done = f32[8,64,384]{2,1,0:T(8,128)S(1)} collective-permute-done((f32[8,64,384]{2,1,0:T(8,128)S(1)}, f32[8,64,384]{2,1,0:T(8,128)S(1)}, u32[]{:S(2)}, u32[]{:S(2)}) %collective-permute-start) | collective-permute-done | bytes 786464 | tf_op jit(solution)/shard_map/ppermute | solution.py:614
  80.5 1.2 slice_add_fusion
  81.9 0.7 broadcast_multiply_fusion
  82.6 0.4 convert_reduce_fusion
  83.0 20.6 %collective-permute-done.1 = f32[4,64,384]{2,1,0:T(8,128)S(1)} collective-permute-done((f32[4,64,384]{2,1,0:T(8,128)S(1)}, f32[4,64,384]{2,1,0:T(8,128)S(1)}, u32[]{:S(2)}, u32[]{:S(2)}) %collective-permute-start.1) | collective-permute-done | bytes 393248 | tf_op jit(solution)/shard_map/ppermute | solution.py:614
  103.7 0.4 collective-permute-start.2
  104.1 22.6 %collective-permute-done.2 = f32[2,64,384]{2,1,0:T(8,128)S(1)} collective-permute-done((f32[2,64,384]{2,1,0:T(8,128)S(1)}, f32[2,64,384]{2,1,0:T(8,128)S(1)}, u32[]{:S(2)}, u32[]{:S(2)}) %collective-permute-start.2) | collective-permute-done | bytes 196640 | tf_op jit(solution)/shard_map/ppermute | solution.py:614
  126.8 3.2 %collective-permute-start.3 = (bf16[1,64,384]{2,1,0:T(8,128)(2,1)S(1)}, bf16[1,64,384]{2,1,0:T(8,128)(2,1)S(1)}, u32[]{:S(2)}, u32[]{:S(2)}) collective-permute-start(bf16[1,64,384]{2,1,0:T(8,128)(2,1)S(1)} %slice.50), channel_id=1, source_target_pairs={{0,8},{1,9},{2,10},{3,11},{4,12},{5,13},{6,14},{7,15},{8,0},{9,1},... | collective-permute-start | bytes 147464 | tf_op jit(solution)/shard_map/ppermute | solution.py:614
  130.0 7.3 %all-to-all-done.2.refs_1_ = bf16[16,64,16,128]{3,2,1,0:T(8,128)(2,1)} async-done(((bf16[16,64,16,128]{3,2,1,0:T(8,128)(2,1)}), bf16[16,64,16,128]{3,2,1,0:T(8,128)(2,1)}, u32[]{:S(2)}, u32[]{:S(2)}) %all-to-all-start.2) | async-done | bytes 4194336 | tf_op jit(solution)/shard_map/all_to_all | solution.py:618
  137.3 15.1 %all-to-all-start = ((bf16[16,12,16,128]{3,2,1,0:T(8,128)(2,1)}), bf16[16,12,16,128]{3,2,1,0:T(8,128)(2,1)S(1)}, u32[]{:S(2)}, u32[]{:S(2)}) async-start(bf16[16,12,16,128]{3,2,1,0:T(8,128)(2,1)} %get-tuple-element.29), calls=%async_computation | async-start | bytes 1572864 | tf_op jit(solution)/shard_map/all_to_all | solution.py:618
  152.4 17.9 %correlate.2.refs_4_ = f32[32,2,2,256,256]{4,3,2,1,0:T(8,128)} custom-call(bf16[16,20,16,128]{3,2,1,0:T(8,128)(2,1)S(1)} %all-to-all-done.1.refs_0_, bf16[16,64,16,128]{3,2,1,0:T(8,128)(2,1)} %all-to-all-done.2.refs_1_, s32[4,4,256]{2,1,0:T(4,128)S(1)} %multiply_add_fusion.refs_2_), custom_call_target="tpu_custom_call" | custom-call | flops 16000000000 | bytes 40000000 | tf_op jit(solution)/shard_map/correlate/pallas_call | solution.py:497
  170.4 0.6 all-to-all-done.refs_0_
  170.9 3.2 %correlate.3 = (f32[32,2,2,256,256]{4,3,2,1,0:T(8,128)}, f32[64,384]{1,0:T(8,128)}) custom-call(bf16[16,12,16,128]{3,2,1,0:T(8,128)(2,1)S(1)} %all-to-all-done.refs_0_, s32[1,4,256]{2,1,0:T(4,128)S(1)} %slice.45.refs_1_, f32[1,64,384]{2,1,0:T(8,128)S(1)} %slice.43.refs_2_, ...), custom_call_target="tpu_custom_call", output_to_operand_aliasing={{0}: (4, {})} | custom-call | flops 2000000000 | bytes 5000000 | tf_op jit(solution)/shard_map/correlate/pallas_call | solution.py:497
  (19 shorter events, 0.5 us)
Async XLA Ops:
  11.4 35.1 %all-to-all-start.1 = ((bf16[16,20,16,128]{3,2,1,0:T(8,128)(2,1)}), bf16[16,20,16,128]{3,2,1,0:T(8,128)(2,1)S(1)}, u32[]{:S(2)}, u32[]{:S(2)}) async-start(bf16[16,20,16,128]{3,2,1,0:T(8,128)(2,1)} %get-tuple-element.32), calls=%async_computation.1 | async-start | bytes 2621440 | tf_op jit(solution)/shard_map/all_to_all | solution.py:618
  46.5 7.1 %copy-start = (f32[4,64]{1,0:T(4,128)S(1)}, f32[4,64]{1,0:T(4,128)}, u32[]{:S(2)}) copy-start(f32[4,64]{1,0:T(4,128)} %param.9) | copy-start | bytes 3076
  46.5 8.5 %copy-start.1 = (f32[64]{0:T(128)S(1)}, f32[64]{0:T(128)}, u32[]{:S(2)}) copy-start(f32[64]{0:T(128)} %constant.68.clone) | copy-start | bytes 772
  46.5 90.8 %all-to-all-start.2 = ((bf16[16,64,16,128]{3,2,1,0:T(8,128)(2,1)}), bf16[16,64,16,128]{3,2,1,0:T(8,128)(2,1)}, u32[]{:S(2)}, u32[]{:S(2)}) async-start(bf16[16,64,16,128]{3,2,1,0:T(8,128)(2,1)} %get-tuple-element.33), calls=%async_computation.2 | async-start | bytes 8388608 | tf_op jit(solution)/shard_map/all_to_all | solution.py:618
  78.2 2.4 %collective-permute-start = (f32[8,64,384]{2,1,0:T(8,128)S(1)}, f32[8,64,384]{2,1,0:T(8,128)S(1)}, u32[]{:S(2)}, u32[]{:S(2)}) collective-permute-start(f32[8,64,384]{2,1,0:T(8,128)S(1)} %slice.38), channel_id=1, source_target_pairs={{0,1},{1,0},{2,3},{3,2},{4,5},{5,4},{6,7},{7,6},{8,9},{9,8},{10,11... | collective-permute-start | bytes 2359304 | tf_op jit(solution)/shard_map/ppermute | solution.py:614
  81.8 21.9 %collective-permute-start.1 = (f32[4,64,384]{2,1,0:T(8,128)S(1)}, f32[4,64,384]{2,1,0:T(8,128)S(1)}, u32[]{:S(2)}, u32[]{:S(2)}) collective-permute-start(f32[4,64,384]{2,1,0:T(8,128)S(1)} %slice.40), channel_id=1, source_target_pairs={{0,2},{1,3},{2,0},{3,1},{4,6},{5,7},{6,4},{7,5},{8,10},{9,11},{10,... | collective-permute-start | bytes 1179656 | tf_op jit(solution)/shard_map/ppermute | solution.py:614
  103.7 23.0 %collective-permute-start.2 = (f32[2,64,384]{2,1,0:T(8,128)S(1)}, f32[2,64,384]{2,1,0:T(8,128)S(1)}, u32[]{:S(2)}, u32[]{:S(2)}) collective-permute-start(f32[2,64,384]{2,1,0:T(8,128)S(1)} %slice.42), channel_id=1, source_target_pairs={{0,4},{1,5},{2,6},{3,7},{4,0},{5,1},{6,2},{7,3},{8,12},{9,13},{10,... | collective-permute-start | bytes 589832 | tf_op jit(solution)/shard_map/ppermute | solution.py:614
  126.8 43.6 %collective-permute-start.3 = (bf16[1,64,384]{2,1,0:T(8,128)(2,1)S(1)}, bf16[1,64,384]{2,1,0:T(8,128)(2,1)S(1)}, u32[]{:S(2)}, u32[]{:S(2)}) collective-permute-start(bf16[1,64,384]{2,1,0:T(8,128)(2,1)S(1)} %slice.50), channel_id=1, source_target_pairs={{0,8},{1,9},{2,10},{3,11},{4,12},{5,13},{6,14},{7,15},{8,0},{9,1},... | collective-permute-start | bytes 147464 | tf_op jit(solution)/shard_map/ppermute | solution.py:614
  137.3 33.6 %all-to-all-start = ((bf16[16,12,16,128]{3,2,1,0:T(8,128)(2,1)}), bf16[16,12,16,128]{3,2,1,0:T(8,128)(2,1)S(1)}, u32[]{:S(2)}, u32[]{:S(2)}) async-start(bf16[16,12,16,128]{3,2,1,0:T(8,128)(2,1)} %get-tuple-element.29), calls=%async_computation | async-start | bytes 1572864 | tf_op jit(solution)/shard_map/all_to_all | solution.py:618
